TPU v7x, 32 devices: a whole 2x2x4 slice. The times are simulated.
32 devices in a mesh: dp: 8 (over z, x), hst: 4 (over y, core).
Axes of the slice: x: 2, y: 2, z: 4, core: 2. Of those that a mesh axis runs over, the one named last changes fastest.
Arguments:
- pixels: bfloat16 [4, 128, 128, 2048], P(None, ('dp', 'hst')), may hold values from -6 to 6
- crop_map: int32 [4, 128, 128], P(None, ('dp', 'hst')), may hold values from 0 to 4, as said below
- queue_rows: bfloat16 [512, 128], P(('dp', 'hst')), may hold values from -0.5390625 to 0.5390625
- conv_in: bfloat16 [2048, 512], replicated, may hold values from -0.125 to 0.125
- gain_one: float32 [512], replicated, may hold values from 0.25 to 1.75
- shift_one: float32 [512], replicated, may hold values from -1.5 to 1.5
- conv_mid: bfloat16 [4608, 512], replicated, may hold values from -0.09375 to 0.09375
- gain_two: float32 [512], replicated, may hold values from 0.25 to 1.75
- shift_two: float32 [512], replicated, may hold values from -1.5 to 1.5
- conv_out: bfloat16 [512, 2048], replicated, may hold values from -0.25 to 0.25
- gain_three: float32 [2048], replicated, may hold values from 0.25 to 1.75
- shift_three: float32 [2048], replicated, may hold values from -1.5 to 1.5
- head_weight: bfloat16 [2048, 2048], replicated, may hold values from -0.125 to 0.125
- head_gain: float32 [2048], replicated, may hold values from 0.25 to 1.75
- head_shift: float32 [2048], replicated, may hold values from -1.5 to 1.5
- embed_weight: bfloat16 [2048, 128], replicated, may hold values from -0.125 to 0.125
- embed_bias: float32 [128], replicated, may hold values from -1.5 to 1.5
- prototypes: bfloat16 [128, 3000], replicated, may hold values from -0.75 to 0.75
Outputs:
- total_loss: float32 [], replicated
- grad_pixels: bfloat16 [4, 128, 128, 2048], P(None, ('dp', 'hst'))
- grad_conv_in: float32 [2048, 512], P('dp')
- grad_gain_one: float32 [512], P('dp')
- grad_shift_one: float32 [512], P('dp')
- grad_conv_mid: float32 [4608, 512], P('dp')
- grad_gain_two: float32 [512], P('dp')
- grad_shift_two: float32 [512], P('dp')
- grad_conv_out: float32 [512, 2048], P('dp')
- grad_gain_three: float32 [2048], P('dp')
- grad_shift_three: float32 [2048], P('dp')
- grad_head_weight: float32 [2048, 2048], P('dp')
- grad_head_gain: float32 [2048], P('dp')
- grad_head_shift: float32 [2048], P('dp')
- grad_embed_weight: float32 [2048, 128], P('dp')
- grad_embed_bias: float32 [128], P('dp')
- grad_prototypes: float32 [128, 3000], P('dp')
Inputs may be any that keep to these rules, and one draw needn't show every extreme that they name: `crop_map`: canvas pixels are row-major over 8 rows and 16 columns. Crop k of a canvas covers its top 3 to 8 rows in 2 to 4 columns starting at column 4 * k (the last crop at most 3 columns); other pixels hold 4. Crops 2 * j and 2 * j + 1 of a canvas are two views of one image.
All inputs are finite; a program needn't handle non-finite values.
Results may differ from a plain program's by a relative error of at most 0.024.
Values sent between devices are 32-bit elements; how exact they have to be, the bound alone decides.
No kernel may reach another device: no remote copies, remote signals or barrier semaphores. Data moves between devices by JAX's collectives and lax.ppermute only.
A program may use at most 320 MiB of HBM per device.

v0:
```python
import jax
import jax.numpy as jnp
from jax import lax
from jax.sharding import PartitionSpec as P

ROWS = 8
COLS = 16
SLOTS = 4
SINK_ITERS = 3


eps_norm = 1e-05
eps_unit = 1e-06
transport_epsilon = 0.05
softmax_sharpness = 0.1
highest = lax.Precision.HIGHEST
tap_offsets = ((-1, -1), (-1, 0), (-1, 1), (0, -1), (0, 0), (0, 1), (1, -1), (1, 0), (1, 1))


def shift_map(field, row_step, col_step, fill):
    widths = [(0, 0), (1, 1), (1, 1)] + [(0, 0)] * (field.ndim - 3)
    padded = jnp.pad(field, widths, constant_values=fill)
    height = field.shape[1]
    breadth = field.shape[2]
    return padded[:, 1 + row_step : 1 + row_step + height, 1 + col_step : 1 + col_step + breadth]


def tap_masks(crop_ids):
    crop_grid = crop_ids.reshape(crop_ids.shape[0], ROWS, COLS)
    result = []
    for row_step, col_step in tap_offsets:
        nearby = shift_map(crop_grid, row_step, col_step, -1)
        result.append(((nearby == crop_grid) & (crop_grid < SLOTS)).reshape(-1, 1))
    return result


def silu_slope(value):
    sigma = jax.nn.sigmoid(value)
    return sigma * (1.0 + value * (1.0 - sigma))


def normalize(values, valid_mask, total, gain, shift):
    first_sum = lax.psum(jnp.sum(values * valid_mask, 0), ("dp", "hst"))
    mean_value = first_sum / total
    centered = values - mean_value
    variance = lax.psum(jnp.sum(centered * centered * valid_mask, 0), ("dp", "hst")) / total
    scaled = lax.rsqrt(variance + eps_norm)
    normal = (values - mean_value) * scaled
    return (normal, scaled, normal * gain + shift)


def normalize_back(grad_out, normal, scaled, gain, valid_mask, total):
    first_sum, second_sum = lax.psum(
        (jnp.sum(grad_out, 0), jnp.sum(grad_out * normal, 0)), ("dp", "hst")
    )
    grad_in = gain * scaled * (grad_out - valid_mask * (first_sum + normal * second_sum) / total)
    return (grad_in, second_sum, first_sum)


def reduce_end(terms):
    shards = (
        lax.psum_scatter(terms[0], "dp", scatter_dimension=0, tiled=True),
        lax.psum_scatter(terms[1], "dp", scatter_dimension=0, tiled=True),
        lax.psum_scatter(terms[2], "dp", scatter_dimension=0, tiled=True),
        lax.psum_scatter(terms[3], "dp", scatter_dimension=0, tiled=True),
        lax.psum_scatter(terms[4], "dp", scatter_dimension=0, tiled=True),
        lax.psum_scatter(terms[5], "dp", scatter_dimension=0, tiled=True),
        lax.psum_scatter(terms[6], "dp", scatter_dimension=0, tiled=True),
    )
    return lax.psum(
        (shards[0], shards[1], shards[2], shards[3], shards[4], shards[5], shards[6]), "hst"
    )


def own_shard(vector):
    piece_size = vector.shape[0] // lax.axis_size("dp")
    return lax.dynamic_slice_in_dim(vector, lax.axis_index("dp") * piece_size, piece_size, 0)


def on_device(
    pixels,
    crop_map,
    queue_rows,
    conv_in,
    gain_one,
    shift_one,
    conv_mid,
    gain_two,
    shift_two,
    conv_out,
    gain_three,
    shift_three,
    head_weight,
    head_gain,
    head_shift,
    embed_weight,
    embed_bias,
    prototypes,
):
    micro_count = pixels.shape[0]
    canvas = pixels.shape[1]
    pixel_count = pixels.shape[2]
    channels = pixels.shape[3]
    middle = conv_in.shape[1]
    crop_rows = canvas * SLOTS
    total_crops = crop_rows * lax.axis_size("dp") * lax.axis_size("hst") * 1.0
    loss_scale = 1.0 / (micro_count * total_crops)
    valid_all = (crop_map < SLOTS).astype(jnp.float32)
    pixel_totals = lax.psum(jnp.sum(valid_all, (1, 2)), ("dp", "hst"))
    queued_logits = jnp.dot(queue_rows, prototypes, preferred_element_type=jnp.float32)
    proto_wide = prototypes.astype(jnp.float32)
    embed_wide = embed_weight.astype(jnp.float32)
    all_rows = jnp.ones((crop_rows, 1), jnp.float32)
    side_grads = [
        jnp.zeros(gain_one.shape, jnp.float32),
        jnp.zeros(gain_one.shape, jnp.float32),
        jnp.zeros(gain_two.shape, jnp.float32),
        jnp.zeros(gain_two.shape, jnp.float32),
        jnp.zeros(gain_three.shape, jnp.float32),
        jnp.zeros(gain_three.shape, jnp.float32),
        jnp.zeros(head_gain.shape, jnp.float32),
        jnp.zeros(head_gain.shape, jnp.float32),
    ]
    total_loss = jnp.zeros((), jnp.float32)
    summed = None
    grad_list = []
    for micro_index in range(micro_count):
        crop_ids = crop_map[micro_index]
        valid_mask = valid_all[micro_index].reshape(-1, 1)
        pixel_total = pixel_totals[micro_index]
        flat_pixels = pixels[micro_index].reshape(canvas * pixel_count, channels)
        norm_one, scale_one, pre_one = normalize(
            jnp.dot(flat_pixels, conv_in, preferred_element_type=jnp.float32),
            valid_mask,
            pixel_total,
            gain_one,
            shift_one,
        )
        act_one = (jax.nn.silu(pre_one) * valid_mask).astype(jnp.bfloat16)
        act_grid = act_one.reshape(canvas, ROWS, COLS, middle)
        mask_list = tap_masks(crop_ids)
        pieces = []
        for mask_now, offset in zip(mask_list, tap_offsets):
            moved = shift_map(act_grid, offset[0], offset[1], 0).reshape(-1, middle)
            pieces.append(jnp.where(mask_now, moved, jnp.zeros((), jnp.bfloat16)))
        columns = jnp.concatenate(pieces, 1)
        norm_two, scale_two, pre_two = normalize(
            jnp.dot(columns, conv_mid, preferred_element_type=jnp.float32),
            valid_mask,
            pixel_total,
            gain_two,
            shift_two,
        )
        act_two = (jax.nn.silu(pre_two) * valid_mask).astype(jnp.bfloat16)
        norm_three, scale_three, pre_three = normalize(
            jnp.dot(act_two, conv_out, preferred_element_type=jnp.float32),
            valid_mask,
            pixel_total,
            gain_three,
            shift_three,
        )
        residual = pre_three + flat_pixels.astype(jnp.float32)
        block_out = (jax.nn.silu(residual) * valid_mask).astype(jnp.bfloat16)
        onehot_wide = (
            crop_ids[:, None, :] == jnp.arange(SLOTS, dtype=jnp.int32)[None, :, None]
        ).astype(jnp.float32)
        crop_sizes = jnp.sum(onehot_wide, 2)
        pooled = jnp.einsum(
            "cqp,cpd->cqd",
            onehot_wide.astype(jnp.bfloat16),
            block_out.reshape(canvas, pixel_count, channels),
            preferred_element_type=jnp.float32,
        )
        features = (
            (pooled / crop_sizes[:, :, None]).reshape(crop_rows, channels).astype(jnp.bfloat16)
        )
        norm_four, scale_four, pre_four = normalize(
            jnp.dot(features, head_weight, preferred_element_type=jnp.float32),
            all_rows,
            total_crops,
            head_gain,
            head_shift,
        )
        act_four = jax.nn.silu(pre_four).astype(jnp.bfloat16)
        embedded = jnp.dot(act_four, embed_weight, preferred_element_type=jnp.float32) + embed_bias
        inverse = lax.rsqrt(jnp.sum(embedded * embedded, 1, keepdims=True) + eps_unit)
        unit_rows = (embedded * inverse).astype(jnp.bfloat16)
        prototype_logits = jnp.dot(unit_rows, prototypes, preferred_element_type=jnp.float32)
        batch_marginal = jnp.exp(prototype_logits / transport_epsilon)
        queue_marginal = jnp.exp(queued_logits / transport_epsilon)
        for sweep in range(SINK_ITERS):
            column_total = lax.psum(
                jnp.sum(batch_marginal, 0) + jnp.sum(queue_marginal, 0), ("dp", "hst")
            )
            batch_marginal = batch_marginal / column_total
            batch_marginal = batch_marginal / jnp.sum(batch_marginal, 1, keepdims=True)
            if sweep + 1 < SINK_ITERS:
                queue_marginal = queue_marginal / column_total
                queue_marginal = queue_marginal / jnp.sum(queue_marginal, 1, keepdims=True)
        partner = batch_marginal.reshape(canvas, 2, 2, -1)[:, :, ::-1].reshape(crop_rows, -1)
        log_likelihoods = jax.nn.log_softmax(prototype_logits / softmax_sharpness, -1)
        loss_local = -jnp.sum(partner * log_likelihoods) * loss_scale
        grad_scores = (
            loss_scale
            * (jnp.sum(partner, 1, keepdims=True) * jnp.exp(log_likelihoods) - partner)
            / softmax_sharpness
        )
        unit_wide = unit_rows.astype(jnp.float32)
        grad_protos = jnp.dot(
            unit_wide.T, grad_scores, precision=highest, preferred_element_type=jnp.float32
        )
        grad_unit = jnp.dot(
            grad_scores, proto_wide.T, precision=highest, preferred_element_type=jnp.float32
        )
        grad_embedded = inverse * grad_unit - embedded * inverse * inverse * inverse * jnp.sum(
            embedded * grad_unit, 1, keepdims=True
        )
        grad_bias = jnp.sum(grad_embedded, 0)
        grad_embed = jnp.dot(
            act_four.astype(jnp.float32).T,
            grad_embedded,
            precision=highest,
            preferred_element_type=jnp.float32,
        )
        grad_act_four = jnp.dot(
            grad_embedded, embed_wide.T, precision=highest, preferred_element_type=jnp.float32
        )
        grad_pre_four = grad_act_four * silu_slope(pre_four)
        first_four, second_four, loss_part = lax.psum(
            (jnp.sum(grad_pre_four, 0), jnp.sum(grad_pre_four * norm_four, 0), loss_local),
            ("dp", "hst"),
        )
        grad_hidden = (
            head_gain
            * scale_four
            * (grad_pre_four - (first_four + norm_four * second_four) / total_crops)
        ).astype(jnp.bfloat16)
        grad_head = jnp.dot(features.T, grad_hidden, preferred_element_type=jnp.float32)
        grad_features = jnp.dot(grad_hidden, head_weight.T, preferred_element_type=jnp.float32)
        per_crop = (grad_features / crop_sizes.reshape(-1, 1)).reshape(canvas, SLOTS, channels)
        grad_block = jnp.einsum("cqp,cqd->cpd", onehot_wide, per_crop, precision=highest).reshape(
            -1, channels
        )
        grad_resid = grad_block * silu_slope(residual) * valid_mask
        grad_three, gain_part, shift_part = normalize_back(
            grad_resid, norm_three, scale_three, gain_three, valid_mask, pixel_total
        )
        side_grads[4] = side_grads[4] + gain_part
        side_grads[5] = side_grads[5] + shift_part
        grad_three = grad_three.astype(jnp.bfloat16)
        grad_conv_out = jnp.dot(act_two.T, grad_three, preferred_element_type=jnp.float32)
        grad_act_two = jnp.dot(grad_three, conv_out.T, preferred_element_type=jnp.float32)
        grad_two, gain_part, shift_part = normalize_back(
            grad_act_two * valid_mask * silu_slope(pre_two),
            norm_two,
            scale_two,
            gain_two,
            valid_mask,
            pixel_total,
        )
        side_grads[2] = side_grads[2] + gain_part
        side_grads[3] = side_grads[3] + shift_part
        grad_two = grad_two.astype(jnp.bfloat16)
        grad_conv_mid = jnp.dot(columns.T, grad_two, preferred_element_type=jnp.float32)
        back_columns = jnp.dot(grad_two, conv_mid.T, preferred_element_type=jnp.float32)
        grad_act_one = jnp.zeros((canvas * pixel_count, middle), jnp.float32)
        for tap_index in range(len(tap_offsets)):
            offset = tap_offsets[tap_index]
            piece_cols = back_columns[:, tap_index * middle : (tap_index + 1) * middle]
            masked = jnp.where(mask_list[tap_index], piece_cols, 0.0).reshape(
                canvas, ROWS, COLS, middle
            )
            grad_act_one = grad_act_one + shift_map(masked, -offset[0], -offset[1], 0.0).reshape(
                -1, middle
            )
        grad_one, gain_part, shift_part = normalize_back(
            grad_act_one * valid_mask * silu_slope(pre_one),
            norm_one,
            scale_one,
            gain_one,
            valid_mask,
            pixel_total,
        )
        side_grads[0] = side_grads[0] + gain_part
        side_grads[1] = side_grads[1] + shift_part
        side_grads[6] = side_grads[6] + second_four
        side_grads[7] = side_grads[7] + first_four
        grad_one = grad_one.astype(jnp.bfloat16)
        grad_conv_in = jnp.dot(flat_pixels.T, grad_one, preferred_element_type=jnp.float32)
        grad_flat = jnp.dot(grad_one, conv_in.T, preferred_element_type=jnp.float32) + grad_resid
        grad_list.append(grad_flat.astype(jnp.bfloat16).reshape(canvas, pixel_count, channels))
        total_loss = total_loss + loss_part
        local_terms = (
            grad_conv_in,
            grad_conv_mid,
            grad_conv_out,
            grad_head,
            grad_embed,
            grad_bias,
            grad_protos,
        )
        summed = (
            local_terms
            if summed is None
            else tuple((earlier + latest for earlier, latest in zip(summed, local_terms)))
        )
    summed = reduce_end(summed)
    return (
        total_loss,
        jnp.stack(grad_list),
        summed[0],
        own_shard(side_grads[0]),
        own_shard(side_grads[1]),
        summed[1],
        own_shard(side_grads[2]),
        own_shard(side_grads[3]),
        summed[2],
        own_shard(side_grads[4]),
        own_shard(side_grads[5]),
        summed[3],
        own_shard(side_grads[6]),
        own_shard(side_grads[7]),
        summed[4],
        summed[5],
        summed[6],
    )


def solution(mesh):
    placed = (
        P(None, ("dp", "hst"), None, None),
        P(None, ("dp", "hst"), None),
        P(("dp", "hst"), None),
        P(),
        P(),
        P(),
        P(),
        P(),
        P(),
        P(),
        P(),
        P(),
        P(),
        P(),
        P(),
        P(),
        P(),
        P(),
    )
    return jax.shard_map(
        on_device,
        mesh=mesh,
        in_specs=placed,
        out_specs=(
            P(),
            P(None, ("dp", "hst"), None, None),
            P("dp", None),
            P("dp"),
            P("dp"),
            P("dp", None),
            P("dp"),
            P("dp"),
            P("dp", None),
            P("dp"),
            P("dp"),
            P("dp", None),
            P("dp"),
            P("dp"),
            P("dp", None),
            P("dp"),
            P("dp", None),
        ),
        check_vma=False,
    )
```

profile of v0, /device:TPU:0, one launch (start us, length us, event | category | flops | bytes accessed | tf_op | source)
XLA Modules:
  0.0 1917.0 jit_solution(4018500225140370743)
XLA Ops:
  37.9 42.1 %all-reduce.55 = (f32[512]{0:T(512)S(1)}, f32[4]{0:T(128)S(1)}, f32[512]{0:T(512)S(1)}, f32[512]{0:T(512)S(1)}, f32[512]{0:T(512)S(1)}) all-reduce(f32[512]{0:T(512)S(1)} %get-tuple-element.430, f32[4]{0:T(128)S(1)} %fusion.206, f32[512]{0:T(512)S(1)} %get-tuple-element.432, ...), channel_id=1, replica_groups=mesh['dp'=8,'hst'=4] {'dp','hst'}, use_global_device_ids=true, to_apply=%region_105.107 | all-reduce | flops 2052 | bytes 16416 | tf_op jit(solution)/shard_map/psum | solution.py:43
  87.7 40.2 %all-reduce.54 = (f32[512]{0:T(512)S(1)}, f32[512]{0:T(512)S(1)}, f32[512]{0:T(512)S(1)}, f32[512]{0:T(512)S(1)}) all-reduce(f32[512]{0:T(512)S(1)} %multiply_reduce_fusion.22, f32[512]{0:T(512)S(1)} %multiply_reduce_fusion.26, f32[512]{0:T(512)S(1)} %multiply_reduce_fusion.30, ...), channel_id=1, replica_groups=mesh['dp'=8,'hst'=4] {'dp','hst'}, use_global_device_ids=true, to_apply=%region_107.109 | all-reduce | flops 2048 | bytes 16384 | tf_op jit(solution)/shard_map/psum | solution.py:46
  169.7 40.1 %all-reduce.53 = (f32[512]{0:T(512)S(1)}, f32[512]{0:T(512)S(1)}, f32[512]{0:T(512)S(1)}, f32[512]{0:T(512)S(1)}) all-reduce(f32[512]{0:T(512)S(1)} %get-tuple-element.438, f32[512]{0:T(512)S(1)} %get-tuple-element.440, f32[512]{0:T(512)S(1)} %get-tuple-element.442, ...), channel_id=1, replica_groups=mesh['dp'=8,'hst'=4] {'dp','hst'}, use_global_device_ids=true, to_apply=%region_109.111 | all-reduce | flops 2048 | bytes 16384 | tf_op jit(solution)/shard_map/psum | solution.py:43
  216.8 40.2 %all-reduce.52 = (f32[512]{0:T(512)S(1)}, f32[512]{0:T(512)S(1)}, f32[512]{0:T(512)S(1)}, f32[512]{0:T(512)S(1)}) all-reduce(f32[512]{0:T(512)S(1)} %multiply_reduce_fusion.20, f32[512]{0:T(512)S(1)} %multiply_reduce_fusion.24, f32[512]{0:T(512)S(1)} %multiply_reduce_fusion.28, ...), channel_id=1, replica_groups=mesh['dp'=8,'hst'=4] {'dp','hst'}, use_global_device_ids=true, to_apply=%region_111.113 | all-reduce | flops 2048 | bytes 16384 | tf_op jit(solution)/shard_map/psum | solution.py:46
  275.4 40.3 %all-reduce.51 = (f32[2048]{0:T(1024)S(1)}, f32[2048]{0:T(1024)S(1)}, f32[2048]{0:T(1024)S(1)}, f32[2048]{0:T(1024)S(1)}) all-reduce(f32[2048]{0:T(1024)S(1)} %get-tuple-element.446, f32[2048]{0:T(1024)S(1)} %get-tuple-element.448, f32[2048]{0:T(1024)S(1)} %get-tuple-element.450, ...), channel_id=1, replica_groups=mesh['dp'=8,'hst'=4] {'dp','hst'}, use_global_device_ids=true, to_apply=%region_113.115 | all-reduce | flops 8192 | bytes 65536 | tf_op jit(solution)/shard_map/psum | solution.py:43
  324.5 40.7 %all-reduce.50 = (f32[2048]{0:T(1024)S(1)}, f32[2048]{0:T(1024)S(1)}, f32[2048]{0:T(1024)S(1)}, f32[2048]{0:T(1024)S(1)}) all-reduce(f32[2048]{0:T(1024)S(1)} %multiply_reduce_fusion.4, f32[2048]{0:T(1024)S(1)} %multiply_reduce_fusion.6, f32[2048]{0:T(1024)S(1)} %multiply_reduce_fusion.8, ...), channel_id=1, replica_groups=mesh['dp'=8,'hst'=4] {'dp','hst'}, use_global_device_ids=true, to_apply=%region_115.117 | all-reduce | flops 8192 | bytes 65536 | tf_op jit(solution)/shard_map/psum | solution.py:46
  372.8 11.0 multiply_convert_fusion.7
  401.1 40.7 %all-reduce.49 = (f32[2048]{0:T(1024)S(1)}, f32[2048]{0:T(1024)S(1)}, f32[2048]{0:T(1024)S(1)}, f32[2048]{0:T(1024)S(1)}) all-reduce(f32[2048]{0:T(1024)S(1)} %get-tuple-element.454, f32[2048]{0:T(1024)S(1)} %get-tuple-element.456, f32[2048]{0:T(1024)S(1)} %get-tuple-element.458, ...), channel_id=1, replica_groups=mesh['dp'=8,'hst'=4] {'dp','hst'}, use_global_device_ids=true, to_apply=%region_118.120 | all-reduce | flops 8192 | bytes 65536 | tf_op jit(solution)/shard_map/psum | solution.py:43
  442.1 40.6 %all-reduce.48 = (f32[2048]{0:T(1024)S(1)}, f32[2048]{0:T(1024)S(1)}, f32[2048]{0:T(1024)S(1)}, f32[2048]{0:T(1024)S(1)}) all-reduce(f32[2048]{0:T(1024)S(1)} %multiply_reduce_fusion.48, f32[2048]{0:T(1024)S(1)} %multiply_reduce_fusion.49, f32[2048]{0:T(1024)S(1)} %multiply_reduce_fusion.50, ...), channel_id=1, replica_groups=mesh['dp'=8,'hst'=4] {'dp','hst'}, use_global_device_ids=true, to_apply=%region_120.122 | all-reduce | flops 8192 | bytes 65536 | tf_op jit(solution)/shard_map/psum | solution.py:46
  495.6 40.8 %all-reduce.47 = (f32[3000]{0:T(1024)S(1)}, f32[3000]{0:T(1024)S(1)}, f32[3000]{0:T(1024)S(1)}, f32[3000]{0:T(1024)S(1)}) all-reduce(f32[3000]{0:T(1024)} %get-tuple-element.377, f32[3000]{0:T(1024)} %get-tuple-element.378, f32[3000]{0:T(1024)} %get-tuple-element.379, ...), channel_id=1, replica_groups=mesh['dp'=8,'hst'=4] {'dp','hst'}, use_global_device_ids=true, to_apply=%region_123.125 | all-reduce | flops 12000 | bytes 96000 | tf_op jit(solution)/shard_map/psum | solution.py:192
  547.5 42.1 %all-reduce.46 = (f32[3000]{0:T(1024)S(1)}, f32[3000]{0:T(1024)S(1)}, f32[3000]{0:T(1024)}, f32[3000]{0:T(1024)S(1)}) all-reduce(f32[3000]{0:T(1024)} %add.1137, f32[3000]{0:T(1024)} %add.1118, f32[3000]{0:T(1024)} %add.1099, f32[3000]{0:T(1024)} %add.1081), channel_id=1, replica_groups=mesh['dp'=8,'hst'=4] {'dp','hst'}, use_global_device_ids=true, to_apply=%region_128.130 | all-reduce | flops 12000 | bytes 96000 | tf_op jit(solution)/shard_map/psum | solution.py:192
  599.1 41.1 %all-reduce.45 = (f32[3000]{0:T(1024)}, f32[3000]{0:T(1024)}, f32[3000]{0:T(1024)}, f32[3000]{0:T(1024)}) all-reduce(f32[3000]{0:T(1024)} %add.1082, f32[3000]{0:T(1024)} %add.1100, f32[3000]{0:T(1024)} %add.1119, f32[3000]{0:T(1024)} %add.1138), channel_id=1, replica_groups=mesh['dp'=8,'hst'=4] {'dp','hst'}, use_global_device_ids=true, to_apply=%region_32.33 | all-reduce | flops 12000 | bytes 96000 | tf_op jit(solution)/shard_map/psum | solution.py:192
  646.4 11.3 rev.15
  664.3 11.3 rev.14
  683.2 11.3 rev.13
  702.0 11.3 rev.12
  754.2 112.9 %all-reduce.63.cloned.1.call-done = (f32[2048]{0:T(1024)}, f32[2048]{0:T(1024)}, f32[2048]{0:T(1024)}, f32[2048]{0:T(1024)}, f32[2048]{0:T(1024)}, /*index=5*/f32[2048]{0:T(1024)}, f32[2048]{0:T(1024)}, f32[2048]{0:T(1024)}) async-done(((f32[2048]{0:T(1024)}, f32[2048]{0:T(1024)}, f32[2048]{0:T(1024)}, f32[2048]{0:T(1024)}, f32[2048]{0:T(1024)}, /*index=5*/f32[2048]{0:T(1024)}, f32[2048]{0:T(1024)}, ...) | async-done | bytes 65552 | tf_op jit(solution)/shard_map/psum | solution.py:229
  909.6 10.7 fusion.223
  920.4 10.8 fusion.225
  950.6 104.8 %all-reduce.61.cloned.1.call-done = (f32[2048]{0:T(1024)}, f32[2048]{0:T(1024)}, f32[2048]{0:T(1024)}, f32[2048]{0:T(1024)}, f32[2048]{0:T(1024)}, /*index=5*/f32[2048]{0:T(1024)}, f32[2048]{0:T(1024)}, f32[2048]{0:T(1024)}) async-done(((f32[2048]{0:T(1024)}, f32[2048]{0:T(1024)}, f32[2048]{0:T(1024)}, f32[2048]{0:T(1024)}, f32[2048]{0:T(1024)}, /*index=5*/f32[2048]{0:T(1024)}, f32[2048]{0:T(1024)}, ...) | async-done | bytes 65552 | tf_op jit(solution)/shard_map/psum | solution.py:53
  1055.5 8.8 multiply_convert_fusion
  1087.0 41.7 %all-reduce.42 = (f32[512]{0:T(512)S(1)}, f32[512]{0:T(512)S(1)}, f32[512]{0:T(512)S(1)}, f32[512]{0:T(512)S(1)}, f32[512]{0:T(512)S(1)}, /*index=5*/f32[512]{0:T(512)S(1)}, f32[512]{0:T(512)S(1)}, f32[512]{0:T(512)S(1)}) all-reduce(f32[512]{0:T(512)S(1)} %get-tuple-element.92, ...), channel_id=1, replica_groups=mesh['dp'=8,'hst'=4] {'dp','hst'}, use_global_device_ids=true, to_apply=%region_204.206 | all-reduce | flops 4096 | bytes 32768 | tf_op jit(solution)/shard_map/psum | solution.py:53
  1209.8 39.8 %all-reduce.41 = (f32[]{:T(128)}, f32[512]{0:T(512)S(1)}, f32[512]{0:T(512)S(1)}, f32[512]{0:T(512)S(1)}, f32[512]{0:T(512)S(1)}, /*index=5*/f32[512]{0:T(512)S(...) all-reduce(f32[]{:T(128)S(6)} %multiply.163, ...), channel_id=1, replica_groups=mesh['dp'=8,'hst'=4] {'dp','hst'}, use_global_device_ids=true, to_apply=%region_37.39 | all-reduce | flops 4097 | bytes 32776 | tf_op jit(solution)/shard_map/psum | solution.py:229
  1271.3 7.6 fusion.279
  1284.0 12.7 add_add_fusion.1
  1300.0 8.1 fusion.282
  1308.1 8.1 fusion.283
  1316.2 18.1 add_add_fusion
  1336.3 22.6 %all-reduce.40 = f32[128]{0:T(128)S(1)} all-reduce(f32[128]{0:T(128)S(1)} %add_add_fusion.7), channel_id=7, replica_groups=mesh['dp'=8,'hst'=4] {'dp'}, use_global_device_ids=true, to_apply=%region_223.225.clone | all-reduce | flops 128 | bytes 1024
  1373.9 150.8 %reduce-scatter.9.cloned.1.call-done = f32[576,512]{1,0:T(8,128)} async-done(((f32[4608,512]{1,0:T(8,128)}), f32[576,512]{1,0:T(8,128)}) %reduce-scatter.9.cloned.1.call-update) | async-done | bytes 1179664 | tf_op jit(solution)/shard_map/reduce_scatter | solution.py:63
  1524.6 282.7 %reduce-scatter.13.cloned.1.call-done = f32[256,2048]{1,0:T(8,128)} async-done(((f32[2048,2048]{1,0:T(8,128)}), f32[256,2048]{1,0:T(8,128)}) %reduce-scatter.13.cloned.1.call-update) | async-done | bytes 2097168 | tf_op jit(solution)/shard_map/reduce_scatter | solution.py:65
  1820.4 80.0 %all-reduce.65.cloned.1.call-done = (f32[256,512]{0,1:T(8,128)}, f32[576,512]{1,0:T(8,128)}, f32[64,2048]{1,0:T(8,128)}, f32[256,2048]{1,0:T(8,128)}, f32[256,128]{1,0:T(8,128)}, /*index=5*/f32[16,3000]{1,0:T(8,128)}) async-done(((f32[256,512]{0,1:T(8,128)}, f32[576,512]{1,0:T(8,128)}, f32[64,2048]{1,0:T(8,128)}, f32[256,2048]{1,0:T(8,128)}, f32[256,128]{1,0:T(8,128)}, /*index=5*/f32[16,3000]{1,0:T(8,128)}), ...) | async-done | bytes 4648464 | tf_op jit(solution)/shard_map/psum | solution.py:70
  (1093 shorter events, 468.3 us)
Async XLA Ops:
  8.0 252.1 %copy-start = (bf16[512,2048]{1,0:T(8,128)(2,1)S(1)}, bf16[512,2048]{1,0:T(8,128)(2,1)}, u32[]{:S(2)}) copy-start(bf16[512,2048]{1,0:T(8,128)(2,1)} %param.28) | copy-start | bytes 6291460
  8.0 859.1 %all-reduce.63.cloned.1.call-start = ((), (), s32[]{:S(2)}) async-start(), calls=%async_computation.13 | async-start | bytes 131072 | tf_op jit(solution)/shard_map/psum | solution.py:229
  11.8 360.5 %copy-start.238 = (s32[4,128]{1,0:T(4,128)}, s32[4,128]{1,0:T(4,128)S(1)}, u32[]{:S(2)}) copy-start(s32[4,128]{1,0:T(4,128)S(1)} %get-tuple-element.389) | copy-start | bytes 6148
  11.8 372.0 %copy-start.240 = (s32[4,128]{1,0:T(4,128)}, s32[4,128]{1,0:T(4,128)S(1)}, u32[]{:S(2)}) copy-start(s32[4,128]{1,0:T(4,128)S(1)} %get-tuple-element.388) | copy-start | bytes 6148
  11.8 373.1 %copy-start.234 = (s32[4,128]{1,0:T(4,128)}, s32[4,128]{1,0:T(4,128)S(1)}, u32[]{:S(2)}) copy-start(s32[4,128]{1,0:T(4,128)S(1)} %get-tuple-element.391) | copy-start | bytes 6148
  11.8 375.2 %copy-start.236 = (s32[4,128]{1,0:T(4,128)}, s32[4,128]{1,0:T(4,128)S(1)}, u32[]{:S(2)}) copy-start(s32[4,128]{1,0:T(4,128)S(1)} %get-tuple-element.390) | copy-start | bytes 6148
  11.8 356.7 %copy-start.137 = (f32[512]{0:T(512)}, f32[512]{0:T(512)S(1)}, u32[]{:S(2)}) copy-start(f32[512]{0:T(512)S(1)} %get-tuple-element.408) | copy-start | bytes 6148
  11.8 360.9 %copy-start.135 = (f32[512]{0:T(512)}, f32[512]{0:T(512)S(1)}, u32[]{:S(2)}) copy-start(f32[512]{0:T(512)S(1)} %get-tuple-element.407) | copy-start | bytes 6148
  11.8 360.9 %copy-start.139 = (f32[512]{0:T(512)}, f32[512]{0:T(512)S(1)}, u32[]{:S(2)}) copy-start(f32[512]{0:T(512)S(1)} %get-tuple-element.406) | copy-start | bytes 6148
  12.6 359.7 %copy-start.254 = (f32[4,4]{1,0:T(4,128)}, f32[4,4]{1,0:T(4,128)S(1)}, u32[]{:S(2)}) copy-start(f32[4,4]{1,0:T(4,128)S(1)} %convert_reduce_fusion.2) | copy-start | bytes 196
  14.5 141.4 %copy-start.299 = (pred[512]{0:T(512)(128)(4,1)}, pred[512]{0:T(512)(128)(4,1)S(1)}, u32[]{:S(2)}) copy-start(pred[512]{0:T(512)(128)(4,1)S(1)} %broadcast_in_dim.680) | copy-start | bytes 1540
  14.6 140.9 %copy-start.301 = (pred[512]{0:T(512)(128)(4,1)}, pred[512]{0:T(512)(128)(4,1)S(1)}, u32[]{:S(2)}) copy-start(pred[512]{0:T(512)(128)(4,1)S(1)} %broadcast_in_dim.676) | copy-start | bytes 1540
  14.7 140.6 %copy-start.303 = (pred[512]{0:T(512)(128)(4,1)}, pred[512]{0:T(512)(128)(4,1)S(1)}, u32[]{:S(2)}) copy-start(pred[512]{0:T(512)(128)(4,1)S(1)} %broadcast_in_dim.674) | copy-start | bytes 1540
  14.8 139.4 %copy-start.305 = (pred[512]{0:T(512)(128)(4,1)}, pred[512]{0:T(512)(128)(4,1)S(1)}, u32[]{:S(2)}) copy-start(pred[512]{0:T(512)(128)(4,1)S(1)} %broadcast_in_dim.671) | copy-start | bytes 1540
  14.9 139.1 %copy-start.307 = (pred[512]{0:T(512)(128)(4,1)}, pred[512]{0:T(512)(128)(4,1)S(1)}, u32[]{:S(2)}) copy-start(pred[512]{0:T(512)(128)(4,1)S(1)} %broadcast_in_dim.669) | copy-start | bytes 1540
  14.9 138.8 %copy-start.309 = (pred[512]{0:T(512)(128)(4,1)}, pred[512]{0:T(512)(128)(4,1)S(1)}, u32[]{:S(2)}) copy-start(pred[512]{0:T(512)(128)(4,1)S(1)} %broadcast_in_dim.667) | copy-start | bytes 1540
  15.0 140.6 %copy-start.311 = (pred[512]{0:T(512)(128)(4,1)}, pred[512]{0:T(512)(128)(4,1)S(1)}, u32[]{:S(2)}) copy-start(pred[512]{0:T(512)(128)(4,1)S(1)} %broadcast_in_dim.678) | copy-start | bytes 1540
  15.1 138.4 %copy-start.313 = (pred[512]{0:T(512)(128)(4,1)}, pred[512]{0:T(512)(128)(4,1)S(1)}, u32[]{:S(2)}) copy-start(pred[512]{0:T(512)(128)(4,1)S(1)} %broadcast_in_dim.665) | copy-start | bytes 1540
  24.4 125.3 %copy-start.315 = (pred[512]{0:T(512)(128)(4,1)}, pred[512]{0:T(512)(128)(4,1)S(1)}, u32[]{:S(2)}) copy-start(pred[512]{0:T(512)(128)(4,1)S(1)} %broadcast_in_dim.663) | copy-start | bytes 1540
  740.1 127.0 %copy-start.179 = (f32[2048]{0:T(1024)S(1)}, f32[2048]{0:T(1024)}, u32[]{:S(2)}) copy-start(f32[2048]{0:T(1024)} %copy-done.178) | copy-start | bytes 24580
  740.1 127.0 %copy-start.194 = (f32[2048]{0:T(1024)S(1)}, f32[2048]{0:T(1024)}, u32[]{:S(2)}) copy-start(f32[2048]{0:T(1024)} %copy-done.193) | copy-start | bytes 24580
  742.4 124.8 %copy-start.100 = (f32[16,2048]{1,0:T(8,128)S(1)}, f32[16,2048]{1,0:T(8,128)}, u32[]{:S(2)}) copy-start(f32[16,2048]{1,0:T(8,128)} %copy-done.99) | copy-start | bytes 393220
  742.4 124.8 %copy-start.187 = (f32[16,2048]{1,0:T(8,128)S(1)}, f32[16,2048]{1,0:T(8,128)}, u32[]{:S(2)}) copy-start(f32[16,2048]{1,0:T(8,128)} %get-tuple-element.480) | copy-start | bytes 393220
  746.0 309.4 %all-reduce.61.cloned.1.call-start = ((), (), s32[]{:S(2)}) async-start(), calls=%async_computation.12 | async-start | bytes 131072 | tf_op jit(solution)/shard_map/psum | solution.py:53
  931.2 442.6 %reduce-scatter.15.cloned.1.call-start = ((), (), s32[]{:S(2)}) async-start(), calls=%async_computation.10 | async-start | bytes 1179648 | tf_op jit(solution)/shard_map/reduce_scatter | solution.py:66
  934.4 439.4 %reduce-scatter.17.cloned.1.call-start = ((), (), s32[]{:S(2)}) async-start(), calls=%async_computation.11 | async-start | bytes 1769472 | tf_op jit(solution)/shard_map/reduce_scatter | solution.py:68
  941.9 431.9 %reduce-scatter.11.cloned.1.call-start = ((), (), s32[]{:S(2)}) async-start(), calls=%async_computation.8 | async-start | bytes 4718592 | tf_op jit(solution)/shard_map/reduce_scatter | solution.py:64
  1177.6 196.2 %reduce-scatter.7.cloned.1.call-start = ((), (), s32[]{:S(2)}) async-start(), calls=%async_computation.6 | async-start | bytes 4718592 | tf_op jit(solution)/shard_map/reduce_scatter | solution.py:62
  1265.1 259.5 %reduce-scatter.9.cloned.1.call-start = ((), (), s32[]{:S(2)}) async-start(), calls=%async_computation.7 | async-start | bytes 10616832 | tf_op jit(solution)/shard_map/reduce_scatter | solution.py:63
  1296.8 510.6 %reduce-scatter.13.cloned.1.call-start = ((), (), s32[]{:S(2)}) async-start(), calls=%async_computation.9 | async-start | bytes 18874368 | tf_op jit(solution)/shard_map/reduce_scatter | solution.py:65
  1334.5 566.0 %all-reduce.65.cloned.1.call-start = ((), (), s32[]{:S(2)}) async-start(), calls=%async_computation.14 | async-start | bytes 9306112 | tf_op jit(solution)/shard_map/psum | solution.py:70
  1373.8 434.9 %copy-start.58 = (bf16[512,512]{1,0:T(8,128)(2,1)S(1)}, bf16[512,512]{1,0:T(8,128)(2,1)}, u32[]{:S(2)}) copy-start(bf16[512,512]{1,0:T(8,128)(2,1)} %copy-done.57) | copy-start | bytes 1572868
  (340 other events, 6754.4 us)
Sparse Core Ops, SparseCore 0:
  746.1 121.0 all-reduce.62
  931.3 123.9 all-reduce.60
  1807.5 92.9 all-reduce.64
Sparse Core Ops, SparseCore 1:
  935.1 64.6 reduce-scatter.14
  1003.4 64.1 reduce-scatter.16
  1177.7 88.0 reduce-scatter.10
  1269.8 88.1 reduce-scatter.6
  1361.6 163.0 reduce-scatter.8
  1528.4 278.9 reduce-scatter.12
where the time goes:
time: 1930 us; the launch traced here: 1920 us
  waiting for transfers between devices  731 us (38%)
  blocking collectives  559 us (29%)
  matrix products  259 us (13%)
  other arithmetic  209 us (11%)
  local copies, waits for them, and re-layouts  134 us (7%)
  between operations  23.7 us (1%)
    reduce_scatter x1, waiting for transfers between devices, reduce_end(): lax.psum_scatter(terms[3], 'dp', scatter_dimension=0, tiled=True)  283 us
    psum x4, blocking collectives, normalize(): first_sum = lax.psum(jnp.sum(values * valid_mask, 0), ('dp', 'hst'))  163 us
    psum x4, blocking collectives, normalize(): lax.psum(jnp.sum(centered * centered * valid_mask, 0), ('dp', 'hst'))  162 us
    reduce_scatter x1, waiting for transfers between devices, reduce_end(): lax.psum_scatter(terms[1], 'dp', scatter_dimension=0, tiled=True)  151 us
    psum x3, blocking collectives, on_device(): lax.psum(jnp.sum(batch_marginal, 0) + jnp.sum(queue_marginal, 0), ('dp',...  124 us
    psum x1, waiting for transfers between devices, on_device(): lax.psum((jnp.sum(grad_pre_four, 0), jnp.sum(grad_pre_four * norm_four, 0...  113 us
    psum x1, waiting for transfers between devices, normalize_back(): lax.psum((jnp.sum(grad_out, 0), jnp.sum(grad_out * normal, 0)), ('dp', 'h...  105 us
    psum x1, waiting for transfers between devices, reduce_end(): lax.psum((shards[0], shards[1], shards[2], shards[3], shards[4], shards[5...  80 us
  transfers between devices with their start and end apart: 9, of which 5 were waited for; matrix products, arithmetic and copies ran while one was open for 12% of the time, Pallas kernels for 0%

commit v1 on v0

v1 whole, which is shorter than its diff:
```python
import functools

import jax
import jax.numpy as jnp
from jax import lax
from jax.experimental import pallas as pl
from jax.experimental.pallas import tpu as pltpu
from jax.sharding import PartitionSpec as P

ROWS = 8
COLS = 16
SLOTS = 4
CELL = COLS // SLOTS
PIX = ROWS * COLS
SINK_ITERS = 3
TAPS = 9

eps_norm = 1e-05
eps_unit = 1e-06
transport_epsilon = 0.05
softmax_sharpness = 0.1
highest = lax.Precision.HIGHEST
F32 = jnp.float32
BF16 = jnp.bfloat16
AXES = ("dp", "hst")
MIB = 1 << 20


def swap(value, mask):
    count = lax.axis_size("dp") * lax.axis_size("hst")
    return lax.ppermute(value, AXES, [(i, i ^ mask) for i in range(count)])


def sync_groups():
    bits = (lax.axis_size("dp") * lax.axis_size("hst")).bit_length() - 1
    groups = [(1,)]
    bit = 1
    while bit < bits:
        if bit + 1 < bits:
            groups.append((1 << bit, 2 << bit, 3 << bit))
            bit += 2
        else:
            groups.append((1 << bit,))
            bit += 1
    return groups


def tree(parts):
    while len(parts) > 1:
        parts = [parts[i] + parts[i + 1] for i in range(0, len(parts), 2)]
    return parts[0]


def total_sum(value):
    for group in sync_groups():
        value = tree([value] + [swap(value, mask) for mask in group])
    return value


def merge_moments(moments, counts):
    for group, members in zip(sync_groups(), counts):
        parts = [moments] + [swap(moments, mask) for mask in group]
        whole = tree(list(members))
        mean = tree([n * part[:, 0] for n, part in zip(members, parts)]) / whole
        spread = tree(
            [part[:, 1] + n * (part[:, 0] - mean) ** 2 for n, part in zip(members, parts)]
        )
        moments = jnp.stack([mean, spread], 1)
    return moments[:, 0], moments[:, 1]


def first_merge(moments):
    counts = []
    for group in sync_groups():
        parts = [moments] + [swap(moments, mask) for mask in group]
        members = [part[:, 2] for part in parts]
        whole = tree(members)
        mean = tree([n * part[:, 0] for n, part in zip(members, parts)]) / whole
        spread = tree(
            [part[:, 1] + n * (part[:, 0] - mean) ** 2 for n, part in zip(members, parts)]
        )
        counts.append([n[:, :1] for n in members])
        moments = jnp.stack([mean, spread, whole], 1)
    return moments[:, 0], moments[:, 1], moments[:, 2, :1], counts


def bit_of(mask):
    index = lax.axis_index("dp") * lax.axis_size("hst") + lax.axis_index("hst")
    return (index // mask) % 2


def halve(value, axis, mask):
    bit = bit_of(mask)
    keep = lax.dynamic_index_in_dim(value, bit, axis, keepdims=False)
    send = lax.dynamic_index_in_dim(value, 1 - bit, axis, keepdims=False)
    return keep + swap(send, mask)


def joined(value, axis, mask):
    other = swap(value, mask)
    low = bit_of(mask) == 0
    return jnp.concatenate([jnp.where(low, value, other), jnp.where(low, other, value)], axis)


def split_rows(value, order):
    devices = lax.axis_size("dp")
    dp_bits = devices.bit_length() - 1
    base = lax.axis_size("hst")
    inner = 2 in order
    dims = [("dp", j) for j in reversed(range(dp_bits))] + ([("row", 0)] if inner else [])
    rest = value.shape[0] // (devices * (2 if inner else 1))
    value = value.reshape((2,) * len(dims) + (rest, value.shape[1]))
    for mask in order:
        key = ("row", 0) if mask == 2 else ("dp", (mask // base).bit_length() - 1)
        place = dims.index(key)
        value = halve(value, place, mask)
        dims.pop(place)
    return value


def dp_masks():
    base = lax.axis_size("hst")
    return [base << j for j in range(lax.axis_size("dp").bit_length() - 1)]


def reduce_weight(keep, send):
    value = keep + swap(send, 1)
    width = value.shape[1]
    masks = dp_masks()
    if width % 256 == 0:
        half = width // 2
        left = split_rows(value[:, :half], [2] + masks)
        right = split_rows(value[:, half:], masks[:1] + [2] + masks[1:])
        value = jnp.concatenate([left, right], 1)
    else:
        value = split_rows(value, [2] + masks)
    value = joined(value, 0, 2)
    return joined(value, 1, 1)


def own_shard(vector):
    piece_size = vector.shape[0] // lax.axis_size("dp")
    return lax.dynamic_slice_in_dim(vector, lax.axis_index("dp") * piece_size, piece_size, 0)


def run(body, grid, in_specs, out_specs, out_shape, scratch=(), flops=0, bytes_accessed=0, prefetch=0):
    return pl.pallas_call(
        body,
        grid_spec=pltpu.PrefetchScalarGridSpec(
            num_scalar_prefetch=prefetch,
            grid=grid,
            in_specs=in_specs,
            out_specs=out_specs,
            scratch_shapes=list(scratch),
        ),
        out_shape=out_shape,
        compiler_params=pltpu.CompilerParams(
            vmem_limit_bytes=56 * MIB, dimension_semantics=("arbitrary",) * len(grid)
        ),
        cost_estimate=pl.CostEstimate(
            flops=flops, bytes_accessed=bytes_accessed, transcendentals=0
        ),
    )


def shape(dims, dtype=F32):
    return jax.ShapeDtypeStruct(tuple(dims), dtype)


def sigmoid(u):
    return 0.5 * jnp.tanh(0.5 * u) + 0.5


def slope_of(u):
    s = sigmoid(u)
    return s * (1.0 + u * (1.0 - s))


def nt_dot(left, right):
    return lax.dot_general(left, right, (((1,), (1,)), ((), ())), preferred_element_type=F32)


def tn_dot(left, right):
    return lax.dot_general(left, right, (((0,), (0,)), ((), ())), preferred_element_type=F32)


def put_moments(stats_ref, h_ref, v, chunk, with_count):
    rows = h_ref.shape[0]
    count = jnp.sum(v, axis=0, keepdims=True)
    total = jnp.zeros((1, h_ref.shape[1]), F32)
    for i in range(0, rows, chunk):
        total += jnp.sum(h_ref[i : i + chunk] * v[i : i + chunk], axis=0, keepdims=True)
    mean = total / count
    spread = jnp.zeros((1, h_ref.shape[1]), F32)
    for i in range(0, rows, chunk):
        off = (h_ref[i : i + chunk] - mean) * v[i : i + chunk]
        spread += jnp.sum(off * off, axis=0, keepdims=True)
    stats_ref[0, 0:1, :] = mean
    stats_ref[0, 1:2, :] = spread
    if with_count:
        stats_ref[0, 2:3, :] = jnp.broadcast_to(count, mean.shape)


def first_body(x_ref, w_ref, v_ref, h_ref, stats_ref):
    h_ref[...] = jnp.dot(x_ref[...], w_ref[...], preferred_element_type=F32)
    put_moments(stats_ref, h_ref, v_ref[...], 64, True)


def first_product(x, weight, valid, micro):
    rows = x.shape[0] // micro
    depth, width = weight.shape
    return run(
        first_body,
        (micro,),
        [
            pl.BlockSpec((rows, depth), lambda m: (m, 0)),
            pl.BlockSpec((depth, width), lambda m: (0, 0)),
            pl.BlockSpec((rows, 1), lambda m: (m, 0)),
        ],
        [
            pl.BlockSpec((rows, width), lambda m: (m, 0)),
            pl.BlockSpec((1, 3, width), lambda m: (m, 0, 0)),
        ],
        [shape((micro * rows, width)), shape((micro, 3, width))],
        flops=2 * micro * rows * depth * width,
        bytes_accessed=2 * x.size,
    )(x, weight, valid)


def cell_column(rows):
    return lax.broadcasted_iota(jnp.int32, (rows, 1), 0) % CELL


def second_body(h_ref, v_ref, coef_ref, w_ref, a_ref, h2_ref, stats_ref, cols_ref):
    rows, width = h_ref.shape
    v = v_ref[...]
    mean = coef_ref[0, 0:1, :]
    factor = coef_ref[0, 1:2, :]
    shift = coef_ref[0, 2:3, :]
    pre = (h_ref[...] - mean) * factor + shift
    act = (pre * sigmoid(pre) * v).astype(BF16)
    a_ref[...] = act
    wide = act.astype(F32)
    place = cell_column(rows)
    sides = (
        jnp.where(place >= 1, pltpu.roll(wide, 1, 0), 0.0).astype(BF16),
        act,
        jnp.where(place <= CELL - 2, pltpu.roll(wide, rows - 1, 0), 0.0).astype(BF16),
    )
    blank = jnp.zeros((COLS, width), BF16)
    for c in range(3):
        side = sides[c]
        cols_ref[:, pl.ds((3 + c) * width, width)] = side
        for k in range(0, rows, PIX):
            cols_ref[k : k + COLS, pl.ds(c * width, width)] = blank
            cols_ref[k + COLS : k + PIX, pl.ds(c * width, width)] = side[k : k + PIX - COLS]
            cols_ref[k : k + PIX - COLS, pl.ds((6 + c) * width, width)] = side[k + COLS : k + PIX]
            cols_ref[k + PIX - COLS : k + PIX, pl.ds((6 + c) * width, width)] = blank
    h2_ref[...] = jnp.dot(cols_ref[...], w_ref[...], preferred_element_type=F32)
    put_moments(stats_ref, h2_ref, v, 64, False)


def second_product(h1, valid, coef, weight, micro):
    rows, width = h1.shape[0] // micro, h1.shape[1]
    return run(
        second_body,
        (micro,),
        [
            pl.BlockSpec((rows, width), lambda m: (m, 0)),
            pl.BlockSpec((rows, 1), lambda m: (m, 0)),
            pl.BlockSpec((1, 3, width), lambda m: (m, 0, 0)),
            pl.BlockSpec(weight.shape, lambda m: (0, 0)),
        ],
        [
            pl.BlockSpec((rows, width), lambda m: (m, 0)),
            pl.BlockSpec((rows, width), lambda m: (m, 0)),
            pl.BlockSpec((1, 2, width), lambda m: (m, 0, 0)),
        ],
        [
            shape((micro * rows, width), BF16),
            shape((micro * rows, width)),
            shape((micro, 2, width)),
        ],
        [pltpu.VMEM((rows, weight.shape[0]), BF16)],
        flops=2 * micro * rows * weight.size,
        bytes_accessed=10 * h1.size,
    )(h1, valid, coef, weight)


def third_body(h_ref, v_ref, coef_ref, w_ref, a_ref, h3_ref, stats_ref):
    v = v_ref[...]
    pre = (h_ref[...] - coef_ref[0, 0:1, :]) * coef_ref[0, 1:2, :] + coef_ref[0, 2:3, :]
    act = (pre * sigmoid(pre) * v).astype(BF16)
    a_ref[...] = act
    h3_ref[...] = jnp.dot(act, w_ref[...], preferred_element_type=F32)
    put_moments(stats_ref, h3_ref, v, 16, False)


def third_product(h2, valid, coef, weight, micro):
    rows, depth = h2.shape[0] // micro, h2.shape[1]
    width = weight.shape[1]
    return run(
        third_body,
        (micro,),
        [
            pl.BlockSpec((rows, depth), lambda m: (m, 0)),
            pl.BlockSpec((rows, 1), lambda m: (m, 0)),
            pl.BlockSpec((1, 3, depth), lambda m: (m, 0, 0)),
            pl.BlockSpec(weight.shape, lambda m: (0, 0)),
        ],
        [
            pl.BlockSpec((rows, depth), lambda m: (m, 0)),
            pl.BlockSpec((rows, width), lambda m: (m, 0)),
            pl.BlockSpec((1, 2, width), lambda m: (m, 0, 0)),
        ],
        [
            shape((micro * rows, depth), BF16),
            shape((micro * rows, width)),
            shape((micro, 2, width)),
        ],
        flops=2 * micro * rows * weight.size,
        bytes_accessed=4 * micro * rows * width,
    )(h2, valid, coef, weight)


def pool_body(h_ref, x_ref, v_ref, coef_ref, size_ref, feat_ref, first_ref, second_ref, slope_ref, norm_ref, sums_ref):
    rows, width = h_ref.shape
    mean = coef_ref[0, 0:1, :]
    scaled = coef_ref[0, 1:2, :]
    gain = coef_ref[0, 2:3, :]
    shift = coef_ref[0, 3:4, :]
    for k in range(rows // PIX):
        acc_out = jnp.zeros((COLS, width), F32)
        acc_first = jnp.zeros((COLS, width), F32)
        acc_second = jnp.zeros((COLS, width), F32)
        for r in range(ROWS):
            at = pl.ds(k * PIX + r * COLS, COLS)
            v = v_ref[at, :]
            normal = (h_ref[at, :] - mean) * scaled
            resid = normal * gain + shift + x_ref[at, :].astype(F32)
            sig = sigmoid(resid)
            kept = sig * v
            out = (resid * kept).astype(BF16).astype(F32)
            slope = kept * (1.0 + resid * (1.0 - sig))
            acc_out += out
            acc_first += slope
            acc_second += slope * normal
            slope_ref[at, :] = slope.astype(BF16)
            norm_ref[at, :] = normal.astype(BF16)
        place = pl.ds(k * COLS, COLS)
        sums_ref[0, place, :] = acc_out
        sums_ref[1, place, :] = acc_first
        sums_ref[2, place, :] = acc_second
    crops = size_ref.shape[0]
    lines = sums_ref.shape[1]
    pick = (
        lax.broadcasted_iota(jnp.int32, (crops, lines), 1) // CELL
        == lax.broadcasted_iota(jnp.int32, (crops, lines), 0)
    ).astype(F32)
    gather = functools.partial(jnp.dot, precision=highest, preferred_element_type=F32)
    feat_ref[...] = (gather(pick, sums_ref[0]) / size_ref[...]).astype(BF16).astype(F32)
    first_ref[...] = gather(pick, sums_ref[1])
    second_ref[...] = gather(pick, sums_ref[2])


def pool(h3, x, valid, coef, sizes, micro):
    rows, channels = h3.shape[0] // micro, h3.shape[1]
    crops = sizes.shape[0] // micro
    width = 512
    tile = pl.BlockSpec((rows, width), lambda m, c: (m, c))
    small = pl.BlockSpec((crops, width), lambda m, c: (m, c))
    return run(
        pool_body,
        (micro, channels // width),
        [
            tile,
            tile,
            pl.BlockSpec((rows, 1), lambda m, c: (m, 0)),
            pl.BlockSpec((1, 4, width), lambda m, c: (m, 0, c)),
            pl.BlockSpec((crops, 1), lambda m, c: (m, 0)),
        ],
        [small, small, small, tile, tile],
        [shape((micro * crops, channels))] * 3 + [shape(h3.shape, BF16)] * 2,
        [pltpu.VMEM((3, rows // ROWS, width), F32)],
        flops=40 * h3.size,
        bytes_accessed=10 * h3.size,
    )(h3, x, valid, coef, sizes)


def head_body(feat_ref, w_ref, g_ref, stats_ref):
    g = jnp.dot(feat_ref[...].astype(BF16), w_ref[...], preferred_element_type=F32)
    g_ref[...] = g
    micro = stats_ref.shape[0]
    crops = g.shape[0] // micro
    for m in range(micro):
        part = g[m * crops : (m + 1) * crops]
        mean = jnp.sum(part, axis=0, keepdims=True) / crops
        stats_ref[m, 0:1, :] = mean
        stats_ref[m, 1:2, :] = jnp.sum((part - mean) ** 2, axis=0, keepdims=True)


def head_product(feat, weight, micro):
    lines = feat.shape[0]
    depth, width = weight.shape
    tile = 512
    return run(
        head_body,
        (width // tile,),
        [
            pl.BlockSpec((lines, depth), lambda c: (0, 0)),
            pl.BlockSpec((depth, tile), lambda c: (0, c)),
        ],
        [
            pl.BlockSpec((lines, tile), lambda c: (0, c)),
            pl.BlockSpec((micro, 2, tile), lambda c: (0, 0, c)),
        ],
        [shape((lines, width)), shape((micro, 2, width))],
        flops=2 * lines * weight.size,
        bytes_accessed=2 * weight.size,
    )(feat, weight)


def head_back_body(dy_ref, g_ref, coef_ref, w_ref, size_ref, first_ref, second_ref, dg_ref, wide_ref, stats_ref, low_ref):
    micro = stats_ref.shape[0]
    lines = dy_ref.shape[0]
    crops = lines // micro

    @pl.when(pl.program_id(0) == 0)
    def _():
        for m in range(micro):
            at = pl.ds(m * crops, crops)
            normal = (g_ref[at, :] - coef_ref[m, 0:1, :]) * coef_ref[m, 1:2, :]
            dg = coef_ref[m, 2:3, :] * (
                dy_ref[at, :] - (coef_ref[m, 3:4, :] + normal * coef_ref[m, 4:5, :])
            )
            low = dg.astype(BF16)
            low_ref[at, :] = low
            dg_ref[at, :] = low.astype(F32)

    per_crop = nt_dot(low_ref[...], w_ref[...]) / size_ref[...]
    lift = (
        lax.broadcasted_iota(jnp.int32, (lines * CELL, lines), 0) // CELL
        == lax.broadcasted_iota(jnp.int32, (lines * CELL, lines), 1)
    ).astype(F32)
    wide_ref[...] = jnp.dot(lift, per_crop, precision=highest, preferred_element_type=F32)
    one = per_crop * first_ref[...]
    two = per_crop * second_ref[...]
    for m in range(micro):
        at = slice(m * crops, (m + 1) * crops)
        stats_ref[m, 0:1, :] = jnp.sum(one[at], axis=0, keepdims=True)
        stats_ref[m, 1:2, :] = jnp.sum(two[at], axis=0, keepdims=True)


def head_back(dy, g, coef, weight, sizes, first, second, micro):
    lines, width = dy.shape
    channels = weight.shape[0]
    tile = 512
    full = pl.BlockSpec((lines, width), lambda c: (0, 0))
    part = pl.BlockSpec((lines, tile), lambda c: (0, c))
    return run(
        head_back_body,
        (channels // tile,),
        [
            full,
            full,
            pl.BlockSpec((micro, 5, width), lambda c: (0, 0, 0)),
            pl.BlockSpec((tile, width), lambda c: (c, 0)),
            pl.BlockSpec((lines, 1), lambda c: (0, 0)),
            part,
            part,
        ],
        [
            full,
            pl.BlockSpec((lines * CELL, tile), lambda c: (0, c)),
            pl.BlockSpec((micro, 2, tile), lambda c: (0, 0, c)),
        ],
        [shape((lines, width)), shape((lines * CELL, channels)), shape((micro, 2, channels))],
        [pltpu.VMEM((lines, width), BF16)],
        flops=2 * lines * weight.size,
        bytes_accessed=2 * weight.size,
    )(dy, g, coef, weight, sizes, first, second)


def third_back_body(wide_ref, slope_ref, norm_ref, v_ref, coef_ref, w_ref, h2_ref, coef2_ref, d_ref, dy_ref, stats_ref):
    rows, channels = slope_ref.shape
    factor = coef_ref[0, 0:1, :]
    one = coef_ref[0, 1:2, :]
    two = coef_ref[0, 2:3, :]
    for k in range(rows // PIX):
        for r in range(ROWS):
            at = pl.ds(k * PIX + r * COLS, COLS)
            v = v_ref[at, :]
            dy = wide_ref[pl.ds(k * COLS, COLS), :] * slope_ref[at, :].astype(F32)
            d = factor * (dy - v * (one + norm_ref[at, :].astype(F32) * two))
            d_ref[at, :] = d.astype(BF16)
    d_act = nt_dot(d_ref[...], w_ref[...])
    normal = (h2_ref[...] - coef2_ref[0, 0:1, :]) * coef2_ref[0, 1:2, :]
    pre = normal * coef2_ref[0, 2:3, :] + coef2_ref[0, 3:4, :]
    dy = d_act * v_ref[...] * slope_of(pre)
    dy_ref[...] = dy
    stats_ref[0, 0:1, :] = jnp.sum(dy, axis=0, keepdims=True)
    stats_ref[0, 1:2, :] = jnp.sum(dy * normal, axis=0, keepdims=True)


def third_back(wide, slope, norm, valid, coef, weight, h2, coef2, micro):
    rows, channels = slope.shape[0] // micro, slope.shape[1]
    middle = weight.shape[0]
    lines = wide.shape[0] // micro
    big = pl.BlockSpec((rows, channels), lambda m: (m, 0))
    mid = pl.BlockSpec((rows, middle), lambda m: (m, 0))
    return run(
        third_back_body,
        (micro,),
        [
            pl.BlockSpec((lines, channels), lambda m: (m, 0)),
            big,
            big,
            pl.BlockSpec((rows, 1), lambda m: (m, 0)),
            pl.BlockSpec((1, 3, channels), lambda m: (m, 0, 0)),
            pl.BlockSpec(weight.shape, lambda m: (0, 0)),
            mid,
            pl.BlockSpec((1, 4, middle), lambda m: (m, 0, 0)),
        ],
        [big, mid, pl.BlockSpec((1, 2, middle), lambda m: (m, 0, 0))],
        [shape(slope.shape, BF16), shape(h2.shape), shape((micro, 2, middle))],
        flops=2 * slope.shape[0] * weight.size,
        bytes_accessed=6 * slope.size,
    )(wide, slope, norm, valid, coef, weight, h2, coef2)


def grad_body(which_ref, left_ref, right_ref, out_ref):
    out_ref[...] = tn_dot(left_ref[...], right_ref[...])


def half_grad(which, left, right, tile):
    rows, depth = left.shape
    half = right.shape[1] // 2
    return run(
        grad_body,
        (depth // tile,),
        [
            pl.BlockSpec((rows, tile), lambda c, w: (0, c)),
            pl.BlockSpec((rows, half), lambda c, w: (0, w[0])),
        ],
        pl.BlockSpec((tile, half), lambda c, w: (c, 0)),
        shape((depth, half)),
        flops=2 * rows * depth * half,
        bytes_accessed=2 * left.size + right.size + 4 * depth * half,
        prefetch=1,
    )(which, left, right)


def norm_back_body(dy_ref, h_ref, v_ref, coef_ref, d_ref):
    normal = (h_ref[...] - coef_ref[0, 0:1, :]) * coef_ref[0, 1:2, :]
    d = coef_ref[0, 2:3, :] * (
        dy_ref[...] - v_ref[...] * (coef_ref[0, 3:4, :] + normal * coef_ref[0, 4:5, :])
    )
    d_ref[...] = d.astype(BF16)


def norm_back(dy, h, valid, coef, micro):
    rows, width = dy.shape[0] // micro, dy.shape[1]
    mid = pl.BlockSpec((rows, width), lambda m: (m, 0))
    return run(
        norm_back_body,
        (micro,),
        [
            mid,
            mid,
            pl.BlockSpec((rows, 1), lambda m: (m, 0)),
            pl.BlockSpec((1, 5, width), lambda m: (m, 0, 0)),
        ],
        mid,
        shape(dy.shape, BF16),
        bytes_accessed=10 * dy.size,
    )(dy, h, valid, coef)


def taps_body(which_ref, a_ref, d_ref, out_ref, sides_ref, left_ref):
    rows, width = a_ref.shape
    tap = pl.program_id(0)

    @pl.when(tap == 0)
    def _():
        blank = jnp.zeros((COLS, width), BF16)
        place = cell_column(PIX)
        for k in range(rows // PIX):
            act = a_ref[k * PIX : (k + 1) * PIX, :]
            wide = act.astype(F32)
            sides = (
                jnp.where(place >= 1, pltpu.roll(wide, 1, 0), 0.0).astype(BF16),
                act,
                jnp.where(place <= CELL - 2, pltpu.roll(wide, PIX - 1, 0), 0.0).astype(BF16),
            )
            for c in range(3):
                sides_ref[c, k, 0:COLS, :] = blank
                sides_ref[c, k, COLS : COLS + PIX, :] = sides[c]
                sides_ref[c, k, COLS + PIX :, :] = blank

    row = tap // 3
    col = tap % 3
    start = pl.multiple_of(row * COLS, COLS)
    for k in range(rows // PIX):
        left_ref[k * PIX : (k + 1) * PIX, :] = sides_ref[col, k, pl.ds(start, PIX), :]
    out_ref[...] = tn_dot(left_ref[...], d_ref[...])


def taps_grad(which, act, d, tile=None):
    rows, width = act.shape
    half = d.shape[1] // 2
    return run(
        taps_body,
        (TAPS,),
        [
            pl.BlockSpec((rows, width), lambda t, w: (0, 0)),
            pl.BlockSpec((rows, half), lambda t, w: (0, w[0])),
        ],
        pl.BlockSpec((width, half), lambda t, w: (t, 0)),
        shape((TAPS * width, half)),
        [
            pltpu.VMEM((3, rows // PIX, PIX + 2 * COLS, width), BF16),
            pltpu.VMEM((rows, width), BF16),
        ],
        flops=2 * rows * TAPS * width * half,
        bytes_accessed=4 * TAPS * width * half,
        prefetch=1,
    )(which, act, d)


def second_back_body(d_ref, w_ref, v_ref, h1_ref, coef_ref, dy_ref, stats_ref, moved_ref):
    rows, width = d_ref.shape
    blank = jnp.zeros((COLS, width), BF16)
    for k in range(0, rows, PIX):
        moved_ref[0, k : k + PIX - COLS, :] = d_ref[k + COLS : k + PIX, :]
        moved_ref[0, k + PIX - COLS : k + PIX, :] = blank
        moved_ref[1, k : k + COLS, :] = blank
        moved_ref[1, k + COLS : k + PIX, :] = d_ref[k : k + PIX - COLS, :]
    sources = (moved_ref[0], d_ref[...], moved_ref[1])
    parts = []
    for c in range(3):
        part = None
        for r in range(3):
            tap = 3 * r + c
            term = nt_dot(sources[r], w_ref[tap * width : (tap + 1) * width, :])
            part = term if part is None else part + term
        parts.append(part)
    place = cell_column(rows)
    d_act = (
        parts[1]
        + jnp.where(place >= 1, pltpu.roll(parts[2], 1, 0), 0.0)
        + jnp.where(place <= CELL - 2, pltpu.roll(parts[0], rows - 1, 0), 0.0)
    )
    normal = (h1_ref[...] - coef_ref[0, 0:1, :]) * coef_ref[0, 1:2, :]
    pre = normal * coef_ref[0, 2:3, :] + coef_ref[0, 3:4, :]
    dy = d_act * v_ref[...] * slope_of(pre)
    dy_ref[...] = dy
    stats_ref[0, 0:1, :] = jnp.sum(dy, axis=0, keepdims=True)
    stats_ref[0, 1:2, :] = jnp.sum(dy * normal, axis=0, keepdims=True)


def second_back(d, weight, valid, h1, coef, micro):
    rows, width = d.shape[0] // micro, d.shape[1]
    mid = pl.BlockSpec((rows, width), lambda m: (m, 0))
    return run(
        second_back_body,
        (micro,),
        [
            mid,
            pl.BlockSpec(weight.shape, lambda m: (0, 0)),
            pl.BlockSpec((rows, 1), lambda m: (m, 0)),
            mid,
            pl.BlockSpec((1, 4, width), lambda m: (m, 0, 0)),
        ],
        [mid, pl.BlockSpec((1, 2, width), lambda m: (m, 0, 0))],
        [shape(d.shape), shape((micro, 2, width))],
        [pltpu.VMEM((2, rows, width), BF16)],
        flops=2 * micro * rows * weight.size,
        bytes_accessed=10 * d.size,
    )(d, weight, valid, h1, coef)


def pixels_body(d_ref, w_ref, wide_ref, slope_ref, out_ref):
    rows, channels = out_ref.shape
    width = 512
    for j in range(0, channels, width):
        lane = pl.ds(j, width)
        grad = nt_dot(d_ref[...], w_ref[lane, :])
        for k in range(rows // PIX):
            wide = wide_ref[pl.ds(k * COLS, COLS), lane]
            for r in range(ROWS):
                first = k * PIX + r * COLS
                at = pl.ds(first, COLS)
                out_ref[at, lane] = (
                    grad[first : first + COLS] + wide * slope_ref[at, lane].astype(F32)
                ).astype(BF16)


def pixels_grad(d, weight, wide, slope, micro):
    rows, channels = slope.shape[0] // micro, slope.shape[1]
    lines = wide.shape[0] // micro
    big = pl.BlockSpec((rows, channels), lambda m: (m, 0))
    return run(
        pixels_body,
        (micro,),
        [
            pl.BlockSpec((rows, d.shape[1]), lambda m: (m, 0)),
            pl.BlockSpec(weight.shape, lambda m: (0, 0)),
            pl.BlockSpec((lines, channels), lambda m: (m, 0)),
            big,
        ],
        big,
        shape(slope.shape, BF16),
        flops=2 * slope.shape[0] * weight.size,
        bytes_accessed=4 * slope.size,
    )(d, weight, wide, slope)


def factor_body(which_ref, *refs):
    lefts, rights, out_ref = refs[:-1][0::2], refs[:-1][1::2], refs[-1]
    left = jnp.concatenate([ref[...] for ref in lefts], 0).astype(BF16)
    right = jnp.concatenate([ref[...] for ref in rights], 0).astype(BF16)
    out_ref[...] = tn_dot(left, right)


def factor_grad(which, pairs):
    lines, depth = pairs[0][0].shape
    width = pairs[0][1].shape[1]
    quarter = width // 4
    tile = 512
    specs = []
    for _ in pairs:
        specs.append(pl.BlockSpec((lines, tile), lambda c, w: (0, c)))
        specs.append(pl.BlockSpec((lines, quarter), lambda c, w: (0, w[0])))
    return run(
        factor_body,
        (depth // tile,),
        specs,
        pl.BlockSpec((tile, quarter), lambda c, w: (c, 0)),
        shape((depth, quarter)),
        flops=2 * lines * len(pairs) * depth * quarter,
        bytes_accessed=4 * depth * quarter,
        prefetch=1,
    )(which, *[array for pair in pairs for array in pair])


def on_device(
    pixels,
    crop_map,
    queue_rows,
    conv_in,
    gain_one,
    shift_one,
    conv_mid,
    gain_two,
    shift_two,
    conv_out,
    gain_three,
    shift_three,
    head_weight,
    head_gain,
    head_shift,
    embed_weight,
    embed_bias,
    prototypes,
):
    micro, canvas, pixel_count, channels = pixels.shape
    devices = lax.axis_size("dp") * lax.axis_size("hst")
    crops = canvas * SLOTS
    total_crops = crops * devices * 1.0
    loss_scale = 1.0 / (micro * total_crops)
    half = lax.axis_index("hst") % 2
    keep_half = half.astype(jnp.int32).reshape(1)
    send_half = 1 - keep_half
    quarter = lax.axis_index("hst").astype(jnp.int32).reshape(1)

    x = pixels.reshape(micro * canvas * pixel_count, channels)
    valid = (crop_map < SLOTS).astype(F32).reshape(-1, 1)
    sizes = jnp.sum(
        (crop_map[:, :, None, :] == jnp.arange(SLOTS, dtype=jnp.int32)[:, None]).astype(F32), 3
    ).reshape(-1, 1)

    def across(vector):
        return jnp.broadcast_to(vector, (micro,) + vector.shape)

    h1, stats = first_product(x, conv_in, valid, micro)
    mean_one, spread, count, counts = first_merge(stats)
    scaled_one = lax.rsqrt(spread / count + eps_norm)
    coef = jnp.stack([mean_one, scaled_one * gain_one, across(shift_one)], 1)
    act_one, h2, stats = second_product(h1, valid, coef, conv_mid, micro)
    mean_two, spread = merge_moments(stats, counts)
    scaled_two = lax.rsqrt(spread / count + eps_norm)
    coef = jnp.stack([mean_two, scaled_two * gain_two, across(shift_two)], 1)
    act_two, h3, stats = third_product(h2, valid, coef, conv_out, micro)
    mean_three, spread = merge_moments(stats, counts)
    scaled_three = lax.rsqrt(spread / count + eps_norm)
    coef = jnp.stack([mean_three, scaled_three, across(gain_three), across(shift_three)], 1)
    feat, slope_first, slope_second, slope, norm_three = pool(h3, x, valid, coef, sizes, micro)
    g, stats = head_product(feat, head_weight, micro)
    crop_counts = []
    members = crops * 1.0
    for group in sync_groups():
        crop_counts.append([members] * (len(group) + 1))
        members = members * (len(group) + 1)
    mean_four, spread = merge_moments(stats, crop_counts)
    scaled_four = lax.rsqrt(spread / total_crops + eps_norm)

    shaped = g.reshape(micro, crops, -1)
    norm_four = (shaped - mean_four[:, None]) * scaled_four[:, None]
    pre_four = norm_four * head_gain + head_shift
    act_four = jax.nn.silu(pre_four).astype(BF16).reshape(micro * crops, -1)
    embedded = jnp.dot(act_four, embed_weight, preferred_element_type=F32) + embed_bias
    inverse = lax.rsqrt(jnp.sum(embedded * embedded, 1, keepdims=True) + eps_unit)
    unit_rows = (embedded * inverse).astype(BF16)
    logits = jnp.dot(unit_rows, prototypes, preferred_element_type=F32)
    queued = jnp.dot(queue_rows, prototypes, preferred_element_type=F32)
    batch = jnp.exp(logits / transport_epsilon).reshape(micro, crops, -1)
    queue = jnp.broadcast_to(
        jnp.exp(queued / transport_epsilon)[None], (micro,) + queued.shape
    )
    for sweep in range(SINK_ITERS):
        column = total_sum(jnp.sum(batch, 1) + jnp.sum(queue, 1))[:, None]
        batch = batch / column
        batch = batch / jnp.sum(batch, 2, keepdims=True)
        if sweep + 1 < SINK_ITERS:
            queue = queue / column
            queue = queue / jnp.sum(queue, 2, keepdims=True)
    pairs = batch.reshape(micro * crops // 2, 2, -1)
    partner = jnp.stack([pairs[:, 1], pairs[:, 0]], 1).reshape(micro * crops, -1)
    log_likelihoods = jax.nn.log_softmax(logits / softmax_sharpness, -1)
    loss_local = -jnp.sum(partner * log_likelihoods) * loss_scale
    grad_scores = (
        loss_scale
        * (jnp.sum(partner, 1, keepdims=True) * jnp.exp(log_likelihoods) - partner)
        / softmax_sharpness
    )
    grad_protos = jnp.dot(
        unit_rows.astype(F32).T, grad_scores, precision=highest, preferred_element_type=F32
    )
    grad_unit = jnp.dot(
        grad_scores, prototypes.astype(F32).T, precision=highest, preferred_element_type=F32
    )
    grad_embedded = inverse * grad_unit - embedded * inverse * inverse * inverse * jnp.sum(
        embedded * grad_unit, 1, keepdims=True
    )
    grad_embed = jnp.dot(
        act_four.astype(F32).T, grad_embedded, precision=highest, preferred_element_type=F32
    )
    grad_act_four = jnp.dot(
        grad_embedded, embed_weight.astype(F32).T, precision=highest, preferred_element_type=F32
    )
    dy_four = grad_act_four.reshape(micro, crops, -1) * slope_of(pre_four)
    width = dy_four.shape[-1]
    tail = jnp.zeros((1, width), F32)
    tail = tail.at[0, : embed_bias.shape[0]].set(jnp.sum(grad_embedded, 0))
    tail = tail.at[0, embed_bias.shape[0]].set(loss_local)
    payload = jnp.concatenate(
        [jnp.sum(dy_four, 1), jnp.sum(dy_four * norm_four, 1), tail], 0
    )
    payload = total_sum(payload)
    first_four, second_four = payload[:micro], payload[micro : 2 * micro]
    grad_bias = payload[2 * micro, : embed_bias.shape[0]]
    total_loss = payload[2 * micro, embed_bias.shape[0]]

    coef = jnp.stack(
        [
            mean_four,
            scaled_four,
            head_gain * scaled_four,
            first_four / total_crops,
            second_four / total_crops,
        ],
        1,
    )
    dg, wide, sums = head_back(
        dy_four.reshape(micro * crops, -1),
        g,
        coef,
        head_weight,
        sizes,
        slope_first,
        slope_second,
        micro,
    )
    sums = total_sum(sums)
    first_three, second_three = sums[:, 0], sums[:, 1]
    coef = jnp.stack(
        [gain_three * scaled_three, first_three / count, second_three / count], 1
    )
    coef2 = jnp.stack([mean_two, scaled_two, across(gain_two), across(shift_two)], 1)
    d_three, dy, sums = third_back(
        wide, slope, norm_three, valid, coef, conv_out, h2, coef2, micro
    )

    mine = jnp.concatenate([feat, dg], 0)
    across_y = swap(mine, 2)
    both = jnp.concatenate([mine, across_y], 0)
    other = swap(both, 1)
    lines = feat.shape[0]
    sets = [both[:2 * lines], both[2 * lines :], other[: 2 * lines], other[2 * lines :]]
    partial = factor_grad(quarter, [(s[:lines], s[lines:]) for s in sets])

    sums = total_sum(sums)
    first_two, second_two = sums[:, 0], sums[:, 1]
    coef = jnp.stack(
        [mean_two, scaled_two, gain_two * scaled_two, first_two / count, second_two / count], 1
    )
    d_two = norm_back(dy, h2, valid, coef, micro)
    coef1 = jnp.stack([mean_one, scaled_one, across(gain_one), across(shift_one)], 1)
    send_mid = taps_grad(send_half, act_one, d_two)
    keep_mid = taps_grad(keep_half, act_one, d_two)
    dy, sums = second_back(d_two, conv_mid, valid, h1, coef1, micro)
    sums = total_sum(sums)
    first_one, second_one = sums[:, 0], sums[:, 1]
    coef = jnp.stack(
        [mean_one, scaled_one, gain_one * scaled_one, first_one / count, second_one / count], 1
    )
    d_one = norm_back(dy, h1, valid, coef, micro)
    send_in = half_grad(send_half, x, d_one, 512)
    keep_in = half_grad(keep_half, x, d_one, 512)
    grad_x = pixels_grad(d_one, conv_in, wide, slope, micro)

    send_out = half_grad(send_half, act_two, d_three, 256)
    keep_out = half_grad(keep_half, act_two, d_three, 256)

    masks = dp_masks()
    grad_head = joined(joined(split_rows(partial, masks), 1, 1), 1, 2)
    grad_conv_out = reduce_weight(keep_out, send_out)
    grad_conv_mid = reduce_weight(keep_mid, send_mid)
    grad_conv_in = reduce_weight(keep_in, send_in)
    shards = lax.axis_size("dp")
    embed_rows = grad_embed.reshape(shards, 2, -1, grad_embed.shape[1])
    embed_part = halve(embed_rows, 1, 1).reshape(-1, grad_embed.shape[1])
    embed_part = joined(split_rows(embed_part, [2] + masks), 0, 2)
    grad_embed = joined(embed_part, 0, 1)
    protos = grad_protos.shape[1]
    padded = jnp.pad(grad_protos, ((0, 0), (0, -protos % 256)))
    folded = padded.reshape(padded.shape[0], 2, -1).swapaxes(0, 1)
    protos_part = joined(split_rows(halve(folded, 0, 1), [2] + masks), 0, 2)
    grad_protos = joined(protos_part, 1, 1)[:, :protos]

    return (
        total_loss,
        grad_x.reshape(pixels.shape),
        grad_conv_in,
        own_shard(jnp.sum(second_one, 0)),
        own_shard(jnp.sum(first_one, 0)),
        grad_conv_mid,
        own_shard(jnp.sum(second_two, 0)),
        own_shard(jnp.sum(first_two, 0)),
        grad_conv_out,
        own_shard(jnp.sum(second_three, 0)),
        own_shard(jnp.sum(first_three, 0)),
        grad_head,
        own_shard(jnp.sum(second_four, 0)),
        own_shard(jnp.sum(first_four, 0)),
        grad_embed,
        own_shard(grad_bias),
        grad_protos,
    )


def solution(mesh):
    placed = (
        P(None, ("dp", "hst"), None, None),
        P(None, ("dp", "hst"), None),
        P(("dp", "hst"), None),
    ) + (P(),) * 15
    return jax.shard_map(
        on_device,
        mesh=mesh,
        in_specs=placed,
        out_specs=(
            P(),
            P(None, ("dp", "hst"), None, None),
            P("dp", None),
            P("dp"),
            P("dp"),
            P("dp", None),
            P("dp"),
            P("dp"),
            P("dp", None),
            P("dp"),
            P("dp"),
            P("dp", None),
            P("dp"),
            P("dp"),
            P("dp", None),
            P("dp"),
            P("dp", None),
        ),
        check_vma=False,
    )
```

time: 1930 us -> 662 us (0.34)
  blocking collectives: 559 us -> 0 us
  waiting for transfers between devices: 731 us -> 234 us
  matrix products: 259 us -> 5.82 us
  Pallas kernels: 0 us -> 192 us
  other arithmetic: 209 us -> 46.7 us
  starting transfers between devices: 0.74 us -> 134 us
  local copies, waits for them, and re-layouts: 134 us -> 35.8 us
  between operations: 23.7 us -> 4.07 us
    psum x14 -> x0, blocking collectives: 537 us -> none  [the longest x4 163 us: normalize(): first_sum = lax.psum(jnp.sum(values * valid_mask, 0), ('dp', 'hst'))]
    reduce_scatter x6 -> x0, waiting for transfers between devices: 434 us -> none  [the longest x1 283 us: reduce_end(): lax.psum_scatter(terms[3], 'dp', scatter_dimension=0, tiled=True)]
    psum x3 -> x0, waiting for transfers between devices: 298 us -> none  [the longest x1 113 us: on_device(): lax.psum((jnp.sum(grad_pre_four, 0), jnp.sum(grad_pre_four * norm_four, 0...]
    dot_general x81 -> x7, matrix products: 259 us -> 5.82 us  [the longest x1 2.16 us: on_device(): jnp.dot(unit_rows.astype(F32).T, grad_scores, precision=highest, preferre...]
    ppermute x0 -> x131, waiting for transfers between devices: none -> 234 us  [swap(): return lax.ppermute(value, AXES, [(i, i ^ mask) for i in range(count)])]
    pallas_call x0 -> x18, Pallas kernels: none -> 192 us  [the longest x4 26.3 us: half_grad(): run(grad_body, (depth // tile,), [pl.BlockSpec((rows, tile), lambda c, w:...]
    ppermute x0 -> x131, starting transfers between devices: none -> 134 us  [swap(): return lax.ppermute(value, AXES, [(i, i ^ mask) for i in range(count)])]
    reduce_sum x48 -> x12, other arithmetic: 76.5 us -> 2.56 us  [the longest x3 0.89 us: on_device(): column = total_sum(jnp.sum(batch, 1) + jnp.sum(queue, 1))[:, None]]
  transfers between devices with their start and end apart: 9 -> 131, of which waited for: 5 -> 80; matrix products, arithmetic and copies ran while one was open for 12% -> 7% of each run, Pallas kernels for 0% -> 17%
where the time goes in v1:
time: 662 us; the launch traced here: 652 us
  waiting for transfers between devices  234 us (35%)
  Pallas kernels  192 us (29%)
  starting transfers between devices  134 us (20%)
  other arithmetic  46.7 us (7%)
  local copies, waits for them, and re-layouts  35.8 us (5%)
    ppermute x131, waiting for transfers between devices, swap(): return lax.ppermute(value, AXES, [(i, i ^ mask) for i in range(count)])  234 us
    ppermute x131, starting transfers between devices, swap(): return lax.ppermute(value, AXES, [(i, i ^ mask) for i in range(count)])  134 us
    pallas_call x4, Pallas kernels, half_grad(): run(grad_body, (depth // tile,), [pl.BlockSpec((rows, tile), lambda c, w:...  26.3 us
    pallas_call x1, Pallas kernels, pool(): run(pool_body, (micro, channels // width), [tile, tile, pl.BlockSpec((row...  24.8 us
    pallas_call x2, Pallas kernels, taps_grad(): run(taps_body, (TAPS,), [pl.BlockSpec((rows, width), lambda t, w: (0, 0))...  22.4 us
    pallas_call x1, Pallas kernels, second_back(): run(second_back_body, (micro,), [mid, pl.BlockSpec(weight.shape, lambda m...  17.4 us
    pallas_call x1, Pallas kernels, third_back(): run(third_back_body, (micro,), [pl.BlockSpec((lines, channels), lambda m:...  16.8 us
    pallas_call x1, Pallas kernels, second_product(): run(second_body, (micro,), [pl.BlockSpec((rows, width), lambda m: (m, 0))...  16 us
  transfers between devices with their start and end apart: 131, of which 80 were waited for; matrix products, arithmetic and copies ran while one was open for 7% of the time, Pallas kernels for 17%

profile of v1, /device:TPU:0, one launch (start us, length us, event | category | flops | bytes accessed | tf_op | source)
XLA Modules:
  0.0 652.0 jit_solution(4839905147981269277)
XLA Ops:
  2.8 9.4 %shard_map.305 = (f32[2048,512]{1,0:T(8,128)}, f32[4,3,512]{2,1,0:T(4,128)}) custom-call(bf16[2048,2048]{1,0:T(8,128)(2,1)} %bitcast.322, bf16[2048,512]{1,0:T(8,128)(2,1)} %w_ref.15, f32[2048,1]{1,0:T(8,128)} %copy.185.v_ref), custom_call_target="tpu_custom_call" | custom-call | flops 4294967296 | bytes 8388608 | tf_op jit(solution)/shard_map/pallas_call | solution.py:212
  28.2 5.3 collective-permute-done.6
  35.2 16.0 %shard_map.306 = (bf16[2048,512]{1,0:T(8,128)(2,1)}, f32[2048,512]{1,0:T(8,128)}, f32[4,2,512]{2,1,0:T(2,128)}) custom-call(f32[2048,512]{1,0:T(8,128)} %get-tuple-element.64.h_ref.h1_ref, f32[2048,1]{1,0:T(8,128)} %copy.185.v_ref, f32[4,3,512]{2,1,0:T(4,128)} %pad_maximum_fusion.25.coef_ref, bf16[4608,512]{1,0:T(8,128)(2,1)} %w_ref.14), custom_call_target="tpu_custom_call" | custom-call | flops 9663676416 | bytes 10485760 | tf_op jit(solution)/shard_map/pallas_call | solution.py:265
  67.9 15.5 %shard_map.307 = (bf16[2048,512]{1,0:T(8,128)(2,1)}, f32[2048,2048]{1,0:T(8,128)}, f32[4,2,2048]{2,1,0:T(2,128)}) custom-call(f32[2048,512]{1,0:T(8,128)} %get-tuple-element.66.h_ref.h2_ref, f32[2048,1]{1,0:T(8,128)} %copy.185.v_ref, f32[4,3,512]{2,1,0:T(4,128)} %pad_maximum_fusion.26.coef_ref, bf16[512,2048]{1,0:T(8,128)(2,1)} %w_ref.13), custom_call_target="tpu_custom_call" | custom-call | flops 4294967296 | bytes 16777216 | tf_op jit(solution)/shard_map/pallas_call | solution.py:302
  105.8 24.8 %shard_map.308 = (f32[64,2048]{1,0:T(8,128)}, f32[64,2048]{1,0:T(8,128)}, f32[64,2048]{1,0:T(8,128)}, bf16[2048,2048]{1,0:T(8,128)(2,1)}, bf16[2048,2048]{1,0:T(8,128)(2,1)}) custom-call(f32[2048,2048]{1,0:T(8,128)} %get-tuple-element.68.h_ref, bf16[2048,2048]{1,0:T(8,128)(2,1)} %bitcast.323, f32[2048,1]{1,0:T(8,128)} %copy.185.v_ref, ...), custom_call_target="tpu_custom_call" | custom-call | flops 167772160 | bytes 41943040 | tf_op jit(solution)/shard_map/pallas_call | solution.py:372
  130.7 6.0 shard_map.309
  255.6 9.4 %shard_map.310 = (f32[64,2048]{1,0:T(8,128)}, f32[256,2048]{1,0:T(8,128)}, f32[4,2,2048]{2,1,0:T(2,128)}) custom-call(f32[64,2048]{1,0:T(8,128)} %multiply_multiply_fusion.1.dy_ref, f32[64,2048]{1,0:T(8,128)} %get-tuple-element.71.g_ref, f32[4,5,2048]{2,1,0:T(8,128)} %stack.54.coef_ref, bf16[2048,2048]{1,0:T(8,128)(2,1)} %w_ref.12, ...), custom_call_target="tpu_custom_call" | custom-call | flops 536870912 | bytes 8388608 | tf_op jit(solution)/shard_map/pallas_call | solution.py:460
  286.6 16.8 %shard_map.311 = (bf16[2048,2048]{1,0:T(8,128)(2,1)}, f32[2048,512]{1,0:T(8,128)}, f32[4,2,512]{2,1,0:T(2,128)}) custom-call(f32[256,2048]{1,0:T(8,128)} %get-tuple-element.75.wide_ref, bf16[2048,2048]{1,0:T(8,128)(2,1)} %get-tuple-element.76.slope_ref, bf16[2048,2048]{1,0:T(8,128)(2,1)} %get-tuple-element.77.norm_ref, f32[2048,1]{1,0:T(8,128)} %copy.185.v_ref, ...), custom_call_target="tpu_custom_call" | custom-call | flops 4294967296 | bytes 25165824 | tf_op jit(solution)/shard_map/pallas_call | solution.py:511
  314.6 6.1 shard_map.320
  321.5 5.7 shard_map.312.d_ref
  327.2 17.4 %shard_map.313 = (f32[2048,512]{1,0:T(8,128)}, f32[4,2,512]{2,1,0:T(2,128)}) custom-call(bf16[2048,512]{1,0:T(8,128)(2,1)} %shard_map.312.d_ref, bf16[4608,512]{1,0:T(8,128)(2,1)} %w_ref.14, f32[2048,1]{1,0:T(8,128)} %copy.185.v_ref, f32[2048,512]{1,0:T(8,128)} %get-tuple-element.64.h_ref.h1_ref, f32[4,4,512]{2,1,0:T(4,128)} %pad_maximum_fusion.28.coef_ref), custom_call_target="tpu_custom_call" | custom-call | flops 9663676416 | bytes 10485760 | tf_op jit(solution)/shard_map/pallas_call | solution.py:664
  344.7 6.1 shard_map.321
  355.6 11.3 %shard_map.319 = f32[4608,256]{1,0:T(8,128)} custom-call(s32[1]{0:T(128)S(6)} %sub.446.which_ref, bf16[2048,512]{1,0:T(8,128)(2,1)} %get-tuple-element.83.a_ref, bf16[2048,512]{1,0:T(8,128)(2,1)} %shard_map.312.d_ref), custom_call_target="tpu_custom_call" | custom-call | flops 4831838208 | bytes 4718592 | tf_op jit(solution)/shard_map/pallas_call | solution.py:611
  370.6 11.1 %shard_map.318 = f32[4608,256]{1,0:T(8,128)} custom-call(s32[1]{0:T(128)} %bitcast.27.which_ref, bf16[2048,512]{1,0:T(8,128)(2,1)} %get-tuple-element.83.a_ref, bf16[2048,512]{1,0:T(8,128)(2,1)} %shard_map.312.d_ref), custom_call_target="tpu_custom_call" | custom-call | flops 4831838208 | bytes 4718592 | tf_op jit(solution)/shard_map/pallas_call | solution.py:611
  385.4 5.7 shard_map.314.d_ref.right_ref
  393.2 11.5 %shard_map.315 = bf16[2048,2048]{1,0:T(8,128)(2,1)} custom-call(bf16[2048,512]{1,0:T(8,128)(2,1)} %shard_map.314.d_ref.right_ref, bf16[2048,512]{1,0:T(8,128)(2,1)} %w_ref.15, f32[256,2048]{1,0:T(8,128)} %get-tuple-element.75.wide_ref, bf16[2048,2048]{1,0:T(8,128)(2,1)} %get-tuple-element.76.slope_ref), custom_call_target="tpu_custom_call" | custom-call | flops 4294967296 | bytes 16777216 | tf_op jit(solution)/shard_map/pallas_call | solution.py:702
  404.7 7.0 %shard_map.317 = f32[2048,256]{1,0:T(8,128)} custom-call(s32[1]{0:T(128)S(6)} %sub.446.which_ref, bf16[2048,2048]{1,0:T(8,128)(2,1)} %bitcast.324, bf16[2048,512]{1,0:T(8,128)(2,1)} %shard_map.314.d_ref.right_ref), custom_call_target="tpu_custom_call" | custom-call | flops 2147483648 | bytes 11534336 | tf_op jit(solution)/shard_map/pallas_call | solution.py:538
  424.9 7.1 %shard_map.316 = f32[2048,256]{1,0:T(8,128)} custom-call(s32[1]{0:T(128)} %bitcast.27.which_ref, bf16[2048,2048]{1,0:T(8,128)(2,1)} %bitcast.325, bf16[2048,512]{1,0:T(8,128)(2,1)} %shard_map.314.d_ref.right_ref), custom_call_target="tpu_custom_call" | custom-call | flops 2147483648 | bytes 11534336 | tf_op jit(solution)/shard_map/pallas_call | solution.py:538
  438.5 5.6 collective-permute-done.126
  445.4 4.8 collective-permute-done.127
  468.3 10.7 %collective-permute-done.100 = f32[2,2,2,32,512]{4,3,1,0,2:T(8,128)S(1)} collective-permute-done((f32[2,2,2,32,512]{4,3,1,0,2:T(8,128)S(1)}, f32[2,2,2,32,512]{4,3,1,0,2:T(8,128)S(1)}, u32[]{:S(2)}, u32[]{:S(2)}) %collective-permute-start.100) | collective-permute-done | bytes 524320 | tf_op jit(solution)/shard_map/ppermute | solution.py:31
  481.4 8.2 %collective-permute-done.78 = f32[2,2,2,128,128]{4,3,1,0,2:T(8,128)S(1)} collective-permute-done((f32[2,2,2,128,128]{4,3,1,0,2:T(8,128)S(1)}, f32[2,2,2,128,128]{4,3,1,0,2:T(8,128)S(1)}, u32[]{:S(2)}, u32[]{:S(2)}) %collective-permute-start.78) | collective-permute-done | bytes 524320 | tf_op jit(solution)/shard_map/ppermute | solution.py:31
  504.2 5.2 shard_map.322
  515.6 5.1 collective-permute-done.103
  521.4 5.1 collective-permute-done.107
  541.0 19.0 %collective-permute-done.112 = f32[2,2,256,512]{3,2,1,0:T(8,128)S(1)} collective-permute-done((f32[2,2,256,512]{3,2,1,0:T(8,128)S(1)}, f32[2,2,256,512]{3,2,1,0:T(8,128)S(1)}, u32[]{:S(2)}, u32[]{:S(2)}) %collective-permute-start.112) | collective-permute-done | bytes 2097184 | tf_op jit(solution)/shard_map/ppermute | solution.py:31
  560.7 6.2 collective-permute-done.89
  568.0 16.9 %collective-permute-done.93 = f32[2,2,2,288,128]{4,3,1,0,2:T(8,128)S(1)} collective-permute-done((f32[2,2,2,288,128]{4,3,1,0,2:T(8,128)S(1)}, f32[2,2,2,288,128]{4,3,1,0,2:T(8,128)S(1)}, u32[]{:S(2)}, u32[]{:S(2)}) %collective-permute-start.93) | collective-permute-done | bytes 1179680 | tf_op jit(solution)/shard_map/ppermute | solution.py:31
  595.6 6.8 %collective-permute-done.114 = f32[256,512]{1,0:T(8,128)S(1)} collective-permute-done((f32[256,512]{1,0:T(8,128)S(1)}, f32[256,512]{1,0:T(8,128)S(1)}, u32[]{:S(2)}, u32[]{:S(2)}) %collective-permute-start.114) | collective-permute-done | bytes 524320 | tf_op jit(solution)/shard_map/ppermute | solution.py:31
  608.7 8.0 %collective-permute-done.92 = f32[288,128]{1,0:T(8,128)S(1)} collective-permute-done((f32[288,128]{1,0:T(8,128)S(1)}, f32[288,128]{1,0:T(8,128)S(1)}, u32[]{:S(2)}, u32[]{:S(2)}) %collective-permute-start.92) | collective-permute-done | bytes 147488 | tf_op jit(solution)/shard_map/ppermute | solution.py:31
  621.4 7.7 %collective-permute-done.97 = f32[288,256]{1,0:T(8,128)S(1)} collective-permute-done((f32[288,256]{1,0:T(8,128)S(1)}, f32[288,256]{1,0:T(8,128)S(1)}, u32[]{:S(2)}, u32[]{:S(2)}) %collective-permute-start.97) | collective-permute-done | bytes 294944 | tf_op jit(solution)/shard_map/ppermute | solution.py:31
  632.5 17.3 %collective-permute-done.116 = f32[256,1024]{1,0:T(8,128)S(1)} collective-permute-done((f32[256,1024]{1,0:T(8,128)S(1)}, f32[256,1024]{1,0:T(8,128)S(1)}, u32[]{:S(2)}, u32[]{:S(2)}) %collective-permute-start.116) | collective-permute-done | bytes 1048608 | tf_op jit(solution)/shard_map/ppermute | solution.py:31
  (649 shorter events, 329.1 us)
Async XLA Ops:
  268.6 145.6 %collective-permute-start.124 = (f32[128,1536]{1,0:T(8,128)}, f32[128,1536]{1,0:T(8,128)}, u32[]{:S(2)}, u32[]{:S(2)}) collective-permute-start(f32[128,1536]{1,0:T(8,128)} %bitcast.107), channel_id=1, source_target_pairs={{0,1},{1,0},{2,3},{3,2},{4,5},{5,4},{6,7},{7,6},{8,9},{9,8},{10,11... | collective-permute-start | bytes 2359304 | tf_op jit(solution)/shard_map/ppermute | solution.py:31
  281.9 109.3 %collective-permute-start.117 = (f32[8,128,128]{2,1,0:T(8,128)}, f32[8,128,128]{2,1,0:T(8,128)}, u32[]{:S(2)}, u32[]{:S(2)}) collective-permute-start(f32[8,128,128]{2,1,0:T(8,128)} %dynamic-slice_bitcast_fusion.4), channel_id=1, source_target_pairs={{0,1},{1,0},{2,3},{3,2},{4,5},{5,4},{6,7},{7,6},{8,9},{9,8},{10,11... | collective-permute-start | bytes 1572872 | tf_op jit(solution)/shard_map/ppermute | solution.py:31
  352.1 14.9 %collective-permute-start.72 = (f32[4,2,512]{2,1,0:T(2,128)S(1)}, f32[4,2,512]{2,1,0:T(2,128)S(1)}, u32[]{:S(2)}, u32[]{:S(2)}) collective-permute-start(f32[4,2,512]{2,1,0:T(2,128)S(1)} %add.1500), channel_id=1, source_target_pairs={{0,4},{1,5},{2,6},{3,7},{4,0},{5,1},{6,2},{7,3},{8,12},{9,13},{10,... | collective-permute-start | bytes 49160 | tf_op jit(solution)/shard_map/ppermute | solution.py:31
  353.2 13.7 %collective-permute-start.73 = (f32[4,2,512]{2,1,0:T(2,128)S(1)}, f32[4,2,512]{2,1,0:T(2,128)S(1)}, u32[]{:S(2)}, u32[]{:S(2)}) collective-permute-start(f32[4,2,512]{2,1,0:T(2,128)S(1)} %add.1500), channel_id=1, source_target_pairs={{0,6},{1,7},{2,4},{3,5},{4,2},{5,3},{6,0},{7,1},{8,14},{9,15},{10,... | collective-permute-start | bytes 49160 | tf_op jit(solution)/shard_map/ppermute | solution.py:31
  367.0 15.9 %collective-permute-start.75 = (f32[4,2,512]{2,1,0:T(2,128)S(1)}, f32[4,2,512]{2,1,0:T(2,128)S(1)}, u32[]{:S(2)}, u32[]{:S(2)}) collective-permute-start(f32[4,2,512]{2,1,0:T(2,128)S(1)} %bitcast.360), channel_id=1, source_target_pairs={{0,16},{1,17},{2,18},{3,19},{4,20},{5,21},{6,22},{7,23},{8,24},{9,... | collective-permute-start | bytes 49160 | tf_op jit(solution)/shard_map/ppermute | solution.py:31
  368.8 15.3 %collective-permute-start.76 = (f32[4,2,512]{2,1,0:T(2,128)S(1)}, f32[4,2,512]{2,1,0:T(2,128)S(1)}, u32[]{:S(2)}, u32[]{:S(2)}) collective-permute-start(f32[4,2,512]{2,1,0:T(2,128)S(1)} %bitcast.361), channel_id=1, source_target_pairs={{0,24},{1,25},{2,26},{3,27},{4,28},{5,29},{6,30},{7,31},{8,16},{9,... | collective-permute-start | bytes 49160 | tf_op jit(solution)/shard_map/ppermute | solution.py:31
  370.6 13.5 %collective-permute-start.74 = (f32[4,2,512]{2,1,0:T(2,128)S(1)}, f32[4,2,512]{2,1,0:T(2,128)S(1)}, u32[]{:S(2)}, u32[]{:S(2)}) collective-permute-start(f32[4,2,512]{2,1,0:T(2,128)S(1)} %bitcast.362), channel_id=1, source_target_pairs={{0,8},{1,9},{2,10},{3,11},{4,12},{5,13},{6,14},{7,15},{8,0},{9,1},... | collective-permute-start | bytes 49160 | tf_op jit(solution)/shard_map/ppermute | solution.py:31
  382.9 73.7 %collective-permute-start.110 = (f32[128,2048]{1,0:T(8,128)}, f32[128,2048]{1,0:T(8,128)S(1)}, u32[]{:S(2)}, u32[]{:S(2)}) collective-permute-start(f32[128,2048]{1,0:T(8,128)} %pad_maximum_fusion.3), channel_id=1, source_target_pairs={{0,2},{1,3},{2,0},{3,1},{4,6},{5,7},{6,4},{7,5},{8,10},{9,11},{10,... | collective-permute-start | bytes 3145736 | tf_op jit(solution)/shard_map/ppermute | solution.py:31
  384.1 77.8 %collective-permute-start.99 = (f32[512,1024]{1,0:T(8,128)}, f32[512,1024]{1,0:T(8,128)}, u32[]{:S(2)}, u32[]{:S(2)}) collective-permute-start(f32[512,1024]{1,0:T(8,128)} %shard_map.321), channel_id=1, source_target_pairs={{0,1},{1,0},{2,3},{3,2},{4,5},{5,4},{6,7},{7,6},{8,9},{9,8},{10,11... | collective-permute-start | bytes 6291464 | tf_op jit(solution)/shard_map/ppermute | solution.py:31
  384.1 150.8 %collective-permute-start.88 = (f32[4608,256]{1,0:T(8,128)}, f32[4608,256]{1,0:T(8,128)}, u32[]{:S(2)}, u32[]{:S(2)}) collective-permute-start(f32[4608,256]{1,0:T(8,128)} %shard_map.319), channel_id=1, source_target_pairs={{0,1},{1,0},{2,3},{3,2},{4,5},{5,4},{6,7},{7,6},{8,9},{9,8},{10,11... | collective-permute-start | bytes 14155784 | tf_op jit(solution)/shard_map/ppermute | solution.py:31
  392.3 20.6 %collective-permute-start.118 = (f32[2,2,2,64,128]{4,3,2,1,0:T(8,128)S(1)}, f32[2,2,2,64,128]{4,3,2,1,0:T(8,128)S(1)}, u32[]{:S(2)}, u32[]{:S(2)}) collective-permute-start(f32[2,2,2,64,128]{4,3,2,1,0:T(8,128)S(1)} %dynamic-slice_bitcast_fusion.9), channel_id=1, source_target_pairs={{0,2},{1,3},{2,0},{3,1},{4,6},{5,7},{6,4},{7,5},{8,10},{9,11},{10,... | collective-permute-start | bytes 786440 | tf_op jit(solution)/shard_map/ppermute | solution.py:31
  433.3 33.2 %collective-permute-start.77 = (f32[2048,256]{1,0:T(8,128)S(1)}, f32[2048,256]{1,0:T(8,128)S(1)}, u32[]{:S(2)}, u32[]{:S(2)}) collective-permute-start(f32[2048,256]{1,0:T(8,128)S(1)} %copy-done.10), channel_id=1, source_target_pairs={{0,1},{1,0},{2,3},{3,2},{4,5},{5,4},{6,7},{7,6},{8,9},{9,8},{10,11... | collective-permute-start | bytes 6291464 | tf_op jit(solution)/shard_map/ppermute | solution.py:31
  456.8 44.0 %collective-permute-start.111 = (f32[256,2048]{1,0:T(8,128)S(1)}, f32[256,2048]{1,0:T(8,128)S(1)}, u32[]{:S(2)}, u32[]{:S(2)}) collective-permute-start(f32[256,2048]{1,0:T(8,128)S(1)} %pad_maximum_fusion), channel_id=1, source_target_pairs={{0,1},{1,0},{2,3},{3,2},{4,5},{5,4},{6,7},{7,6},{8,9},{9,8},{10,11... | collective-permute-start | bytes 6291464 | tf_op jit(solution)/shard_map/ppermute | solution.py:31
  464.2 14.8 %collective-permute-start.100 = (f32[2,2,2,32,512]{4,3,1,0,2:T(8,128)S(1)}, f32[2,2,2,32,512]{4,3,1,0,2:T(8,128)S(1)}, u32[]{:S(2)}, u32[]{:S(2)}) collective-permute-start(f32[2,2,2,32,512]{4,3,1,0,2:T(8,128)S(1)} %bitcast.346), channel_id=1, source_target_pairs={{0,2},{1,3},{2,0},{3,1},{4,6},{5,7},{6,4},{7,5},{8,10},{9,11},{10,... | collective-permute-start | bytes 1572872 | tf_op jit(solution)/shard_map/ppermute | solution.py:31
  465.4 14.8 %collective-permute-start.104 = (f32[2,2,2,32,512]{4,3,1,0,2:T(8,128)S(1)}, f32[2,2,2,32,512]{4,3,1,0,2:T(8,128)S(1)}, u32[]{:S(2)}, u32[]{:S(2)}) collective-permute-start(f32[2,2,2,32,512]{4,3,1,0,2:T(8,128)S(1)} %bitcast.345), channel_id=1, source_target_pairs={{0,4},{1,5},{2,6},{3,7},{4,0},{5,1},{6,2},{7,3},{8,12},{9,13},{10,... | collective-permute-start | bytes 1572872 | tf_op jit(solution)/shard_map/ppermute | solution.py:31
  467.1 22.5 %collective-permute-start.78 = (f32[2,2,2,128,128]{4,3,1,0,2:T(8,128)S(1)}, f32[2,2,2,128,128]{4,3,1,0,2:T(8,128)S(1)}, u32[]{:S(2)}, u32[]{:S(2)}) collective-permute-start(f32[2,2,2,128,128]{4,3,1,0,2:T(8,128)S(1)} %bitcast.348), channel_id=1, source_target_pairs={{0,2},{1,3},{2,0},{3,1},{4,6},{5,7},{6,4},{7,5},{8,10},{9,11},{10,... | collective-permute-start | bytes 1572872 | tf_op jit(solution)/shard_map/ppermute | solution.py:31
  479.0 14.9 %collective-permute-start.82 = (f32[2,2,2,128,128]{4,3,1,0,2:T(8,128)S(1)}, f32[2,2,2,128,128]{4,3,1,0,2:T(8,128)S(1)}, u32[]{:S(2)}, u32[]{:S(2)}) collective-permute-start(f32[2,2,2,128,128]{4,3,1,0,2:T(8,128)S(1)} %bitcast.347), channel_id=1, source_target_pairs={{0,4},{1,5},{2,6},{3,7},{4,0},{5,1},{6,2},{7,3},{8,12},{9,13},{10,... | collective-permute-start | bytes 1572872 | tf_op jit(solution)/shard_map/ppermute | solution.py:31
  480.2 19.3 %collective-permute-start.101 = (f32[2,2,32,512]{3,2,1,0:T(8,128)S(1)}, f32[2,2,32,512]{3,2,1,0:T(8,128)S(1)}, u32[]{:S(2)}, u32[]{:S(2)}) collective-permute-start(f32[2,2,32,512]{3,2,1,0:T(8,128)S(1)} %dynamic-slice_bitcast_fusion.11), channel_id=1, source_target_pairs={{0,4},{1,5},{2,6},{3,7},{4,0},{5,1},{6,2},{7,3},{8,12},{9,13},{10,... | collective-permute-start | bytes 786440 | tf_op jit(solution)/shard_map/ppermute | solution.py:31
  493.9 17.4 %collective-permute-start.79 = (f32[2,2,128,128]{3,2,1,0:T(8,128)S(1)}, f32[2,2,128,128]{3,2,1,0:T(8,128)S(1)}, u32[]{:S(2)}, u32[]{:S(2)}) collective-permute-start(f32[2,2,128,128]{3,2,1,0:T(8,128)S(1)} %dynamic-slice_bitcast_fusion.13), channel_id=1, source_target_pairs={{0,4},{1,5},{2,6},{3,7},{4,0},{5,1},{6,2},{7,3},{8,12},{9,13},{10,... | collective-permute-start | bytes 786440 | tf_op jit(solution)/shard_map/ppermute | solution.py:31
  500.8 13.9 %collective-permute-start.106 = (f32[2,32,512]{2,1,0:T(8,128)S(1)}, f32[2,32,512]{2,1,0:T(8,128)S(1)}, u32[]{:S(2)}, u32[]{:S(2)}) collective-permute-start(f32[2,32,512]{2,1,0:T(8,128)S(1)} %dynamic-slice_bitcast_fusion.18), channel_id=1, source_target_pairs={{0,8},{1,9},{2,10},{3,11},{4,12},{5,13},{6,14},{7,15},{8,0},{9,1},... | collective-permute-start | bytes 393224 | tf_op jit(solution)/shard_map/ppermute | solution.py:31
  511.3 48.6 %collective-permute-start.112 = (f32[2,2,256,512]{3,2,1,0:T(8,128)S(1)}, f32[2,2,256,512]{3,2,1,0:T(8,128)S(1)}, u32[]{:S(2)}, u32[]{:S(2)}) collective-permute-start(f32[2,2,256,512]{3,2,1,0:T(8,128)S(1)} %dynamic-slice_bitcast_fusion), channel_id=1, source_target_pairs={{0,4},{1,5},{2,6},{3,7},{4,0},{5,1},{6,2},{7,3},{8,12},{9,13},{10,... | collective-permute-start | bytes 6291464 | tf_op jit(solution)/shard_map/ppermute | solution.py:31
  512.5 15.3 %collective-permute-start.80 = (f32[2,128,128]{2,1,0:T(8,128)S(1)}, f32[2,128,128]{2,1,0:T(8,128)S(1)}, u32[]{:S(2)}, u32[]{:S(2)}) collective-permute-start(f32[2,128,128]{2,1,0:T(8,128)S(1)} %dynamic-slice_bitcast_fusion.21), channel_id=1, source_target_pairs={{0,8},{1,9},{2,10},{3,11},{4,12},{5,13},{6,14},{7,15},{8,0},{9,1},... | collective-permute-start | bytes 393224 | tf_op jit(solution)/shard_map/ppermute | solution.py:31
  512.6 15.5 %collective-permute-start.84 = (f32[2,128,128]{2,1,0:T(8,128)S(1)}, f32[2,128,128]{2,1,0:T(8,128)S(1)}, u32[]{:S(2)}, u32[]{:S(2)}) collective-permute-start(f32[2,128,128]{2,1,0:T(8,128)S(1)} %dynamic-slice_bitcast_fusion.20), channel_id=1, source_target_pairs={{0,8},{1,9},{2,10},{3,11},{4,12},{5,13},{6,14},{7,15},{8,0},{9,1},... | collective-permute-start | bytes 393224 | tf_op jit(solution)/shard_map/ppermute | solution.py:31
  534.8 25.9 %collective-permute-start.109 = (f32[64,1024]{1,0:T(8,128)S(1)}, f32[64,1024]{1,0:T(8,128)S(1)}, u32[]{:S(2)}, u32[]{:S(2)}) collective-permute-start(f32[64,1024]{1,0:T(8,128)S(1)} %pad_maximum_fusion.11), channel_id=1, source_target_pairs={{0,1},{1,0},{2,3},{3,2},{4,5},{5,4},{6,7},{7,6},{8,9},{9,8},{10,11... | collective-permute-start | bytes 786440 | tf_op jit(solution)/shard_map/ppermute | solution.py:31
  538.4 28.4 %collective-permute-start.89 = (f32[2,2,2,288,128]{4,3,1,0,2:T(8,128)S(1)}, f32[2,2,2,288,128]{4,3,1,0,2:T(8,128)S(1)}, u32[]{:S(2)}, u32[]{:S(2)}) collective-permute-start(f32[2,2,2,288,128]{4,3,1,0,2:T(8,128)S(1)} %bitcast.343), channel_id=1, source_target_pairs={{0,2},{1,3},{2,0},{3,1},{4,6},{5,7},{6,4},{7,5},{8,10},{9,11},{10,... | collective-permute-start | bytes 3538952 | tf_op jit(solution)/shard_map/ppermute | solution.py:31
  539.9 45.0 %collective-permute-start.93 = (f32[2,2,2,288,128]{4,3,1,0,2:T(8,128)S(1)}, f32[2,2,2,288,128]{4,3,1,0,2:T(8,128)S(1)}, u32[]{:S(2)}, u32[]{:S(2)}) collective-permute-start(f32[2,2,2,288,128]{4,3,1,0,2:T(8,128)S(1)} %bitcast.344), channel_id=1, source_target_pairs={{0,4},{1,5},{2,6},{3,7},{4,0},{5,1},{6,2},{7,3},{8,12},{9,13},{10,... | collective-permute-start | bytes 3538952 | tf_op jit(solution)/shard_map/ppermute | solution.py:31
  540.9 89.2 %collective-permute-start.87 = (f32[256,256]{1,0:T(8,128)S(1)}, f32[256,256]{1,0:T(8,128)S(1)}, u32[]{:S(2)}, u32[]{:S(2)}) collective-permute-start(f32[256,256]{1,0:T(8,128)S(1)} %pad_maximum_fusion.10), channel_id=1, source_target_pairs={{0,1},{1,0},{2,3},{3,2},{4,5},{5,4},{6,7},{7,6},{8,9},{9,8},{10,11... | collective-permute-start | bytes 786440 | tf_op jit(solution)/shard_map/ppermute | solution.py:31
  560.5 25.8 %collective-permute-start.113 = (f32[2,256,512]{2,1,0:T(8,128)S(1)}, f32[2,256,512]{2,1,0:T(8,128)S(1)}, u32[]{:S(2)}, u32[]{:S(2)}) collective-permute-start(f32[2,256,512]{2,1,0:T(8,128)S(1)} %dynamic-slice_bitcast_fusion.1), channel_id=1, source_target_pairs={{0,8},{1,9},{2,10},{3,11},{4,12},{5,13},{6,14},{7,15},{8,0},{9,1},... | collective-permute-start | bytes 3145736 | tf_op jit(solution)/shard_map/ppermute | solution.py:31
  567.1 24.2 %collective-permute-start.90 = (f32[2,2,288,128]{3,2,1,0:T(8,128)S(1)}, f32[2,2,288,128]{3,2,1,0:T(8,128)S(1)}, u32[]{:S(2)}, u32[]{:S(2)}) collective-permute-start(f32[2,2,288,128]{3,2,1,0:T(8,128)S(1)} %dynamic-slice_bitcast_fusion.3), channel_id=1, source_target_pairs={{0,4},{1,5},{2,6},{3,7},{4,0},{5,1},{6,2},{7,3},{8,12},{9,13},{10,... | collective-permute-start | bytes 1769480 | tf_op jit(solution)/shard_map/ppermute | solution.py:31
  586.6 15.7 %collective-permute-start.114 = (f32[256,512]{1,0:T(8,128)S(1)}, f32[256,512]{1,0:T(8,128)S(1)}, u32[]{:S(2)}, u32[]{:S(2)}) collective-permute-start(f32[256,512]{1,0:T(8,128)S(1)} %dynamic-slice_bitcast_fusion.5), channel_id=1, source_target_pairs={{0,16},{1,17},{2,18},{3,19},{4,20},{5,21},{6,22},{7,23},{8,24},{9,... | collective-permute-start | bytes 1572872 | tf_op jit(solution)/shard_map/ppermute | solution.py:31
  602.4 17.7 %collective-permute-start.115 = (f32[256,512]{1,0:T(8,128)S(1)}, f32[256,512]{1,0:T(8,128)S(1)}, u32[]{:S(2)}, u32[]{:S(2)}) collective-permute-start(f32[256,512]{1,0:T(8,128)S(1)} %bitcast_add_fusion.8), channel_id=1, source_target_pairs={{0,1},{1,0},{2,3},{3,2},{4,5},{5,4},{6,7},{7,6},{8,9},{9,8},{10,11... | collective-permute-start | bytes 1572872 | tf_op jit(solution)/shard_map/ppermute | solution.py:31
  620.4 29.5 %collective-permute-start.116 = (f32[256,1024]{1,0:T(8,128)S(1)}, f32[256,1024]{1,0:T(8,128)S(1)}, u32[]{:S(2)}, u32[]{:S(2)}) collective-permute-start(f32[256,1024]{1,0:T(8,128)S(1)} %pad_maximum_fusion.4), channel_id=1, source_target_pairs={{0,2},{1,3},{2,0},{3,1},{4,6},{5,7},{6,4},{7,5},{8,10},{9,11},{10,... | collective-permute-start | bytes 3145736 | tf_op jit(solution)/shard_map/ppermute | solution.py:31
  (170 other events, 2306.0 us)

commit v2 on v1

v2 whole, which is shorter than its diff:
```python
import functools

import jax
import jax.numpy as jnp
from jax import lax
from jax.experimental import pallas as pl
from jax.experimental.pallas import tpu as pltpu
from jax.sharding import PartitionSpec as P

ROWS = 8
COLS = 16
SLOTS = 4
CELL = COLS // SLOTS
PIX = ROWS * COLS
SINK_ITERS = 3
TAPS = 9

eps_norm = 1e-05
eps_unit = 1e-06
transport_epsilon = 0.05
softmax_sharpness = 0.1
highest = lax.Precision.HIGHEST
F32 = jnp.float32
BF16 = jnp.bfloat16
AXES = ("dp", "hst")
MIB = 1 << 20


def swap(value, mask):
    count = lax.axis_size("dp") * lax.axis_size("hst")
    return lax.ppermute(value, AXES, [(i, i ^ mask) for i in range(count)])


def sync_groups():
    bits = (lax.axis_size("dp") * lax.axis_size("hst")).bit_length() - 1
    groups = [(1,)]
    bit = 1
    while bit < bits:
        if bit + 1 < bits:
            groups.append((1 << bit, 2 << bit, 3 << bit))
            bit += 2
        else:
            groups.append((1 << bit,))
            bit += 1
    return groups


def tree(parts):
    while len(parts) > 1:
        parts = [parts[i] + parts[i + 1] for i in range(0, len(parts), 2)]
    return parts[0]


def between(parts, gate, fillers):
    for filler in fillers:
        parts = list(tie(*parts, *filler(gate)))[: len(parts)]
    return parts


def pick(fillers, step):
    return fillers[step] if step < len(fillers) else ()


def sum_parts(value, fillers=()):
    groups = sync_groups()
    for step, group in enumerate(groups):
        parts = [value] + [swap(value, mask) for mask in group]
        parts = between(parts, value, pick(fillers, step))
        value = tree(parts)
    return parts


def merge(parts, members):
    whole = tree(list(members))
    mean = tree([n * part[:, 0] for n, part in zip(members, parts)]) / whole
    spread = tree(
        [part[:, 1] + n * (part[:, 0] - mean) ** 2 for n, part in zip(members, parts)]
    )
    return mean, spread, whole


def moment_parts(moments, counts, fillers=()):
    groups = sync_groups()
    for step, group in enumerate(groups):
        parts = [moments] + [swap(moments, mask) for mask in group]
        parts = between(parts, moments, pick(fillers, step))
        if step + 1 < len(groups):
            moments = jnp.stack(merge(parts, counts[step])[:2], 1)
    return parts


def first_parts(moments):
    groups = sync_groups()
    counts = []
    for step, group in enumerate(groups):
        parts = [moments] + [swap(moments, mask) for mask in group]
        if step + 1 < len(groups):
            members = [part[:, 2] for part in parts]
            moments = jnp.stack(merge(parts, members), 1)
            counts.append([n[:, :1] for n in members])
    return parts, counts


def bit_of(mask):
    index = lax.axis_index("dp") * lax.axis_size("hst") + lax.axis_index("hst")
    return (index // mask) % 2


def dp_masks():
    base = lax.axis_size("hst")
    return [base << j for j in range(lax.axis_size("dp").bit_length() - 1)]


def tie(first, *others):
    return lax.optimization_barrier((first,) + others)


def at(view, place, axis):
    return lax.dynamic_index_in_dim(view, place, axis, keepdims=False)


def core_swap(value, low, high):
    count = lax.axis_size("dp") * lax.axis_size("hst")
    pairs = [(i, i ^ (high if i % 2 else low)) for i in range(count)]
    return lax.ppermute(value, AXES, pairs)


def dp_halves(addends, mask, axis):
    bit = bit_of(mask)
    send = sum(at(array, 1 - bit, axis) for array in addends)
    return [at(array, bit, axis) for array in addends] + [swap(send, mask)]


def run(body, grid, in_specs, out_specs, out_shape, scratch=(), flops=0, bytes_accessed=0, prefetch=0, aliases=None):
    return pl.pallas_call(
        body,
        grid_spec=pltpu.PrefetchScalarGridSpec(
            num_scalar_prefetch=prefetch,
            grid=grid,
            in_specs=in_specs,
            out_specs=out_specs,
            scratch_shapes=list(scratch),
        ),
        out_shape=out_shape,
        name=body.__name__,
        input_output_aliases=aliases or {},
        compiler_params=pltpu.CompilerParams(
            vmem_limit_bytes=56 * MIB, dimension_semantics=("arbitrary",) * len(grid)
        ),
        cost_estimate=pl.CostEstimate(
            flops=flops, bytes_accessed=bytes_accessed, transcendentals=0
        ),
    )


def shape(dims, dtype=F32):
    return jax.ShapeDtypeStruct(tuple(dims), dtype)


def sigmoid(u):
    return 0.5 * jnp.tanh(0.5 * u) + 0.5


def norm_of(part_refs, members, m=0, lane=slice(None)):
    whole = tree(list(members))
    means = [ref[m, 0:1, lane] for ref in part_refs]
    mean = tree([n * one for n, one in zip(members, means)]) / whole
    spread = tree(
        [ref[m, 1:2, lane] + n * (one - mean) ** 2 for n, ref, one in zip(members, part_refs, means)]
    )
    return mean, lax.rsqrt(spread / whole + eps_norm)


def sums_of(part_refs, first, second, m=0):
    return (
        tree([ref[m, first : first + 1, :] for ref in part_refs]),
        tree([ref[m, second : second + 1, :] for ref in part_refs]),
    )


def counts_of(count_refs, m=0):
    return [ref[m, 2:3, 0:1] for ref in count_refs]


def whole(array):
    return pl.BlockSpec(array.shape, lambda *_: (0,) * len(array.shape))


def per_micro(array):
    return pl.BlockSpec((1,) + array.shape[1:], lambda m, *_: (m,) + (0,) * (array.ndim - 1))


def slope_of(u):
    s = sigmoid(u)
    return s * (1.0 + u * (1.0 - s))


def nt_dot(left, right):
    return lax.dot_general(left, right, (((1,), (1,)), ((), ())), preferred_element_type=F32)


def tn_dot(left, right):
    return lax.dot_general(left, right, (((0,), (0,)), ((), ())), preferred_element_type=F32)


def fold(y):
    return jnp.sum(y.reshape(y.shape[0] // 8, 8, y.shape[1]), 0)


def put_moments(stats_ref, h_ref, v_ref, with_count):
    rows, width = h_ref.shape
    chunk = 32
    lanes = 512
    v = v_ref[...]
    count = jnp.sum(v, axis=0, keepdims=True)
    first = jnp.sum(v[:PIX], axis=0, keepdims=True)
    for j in range(0, width, lanes):
        lane = slice(j, j + lanes)
        acc = jnp.zeros((8, lanes), F32)
        for i in range(0, PIX, chunk):
            acc += fold(h_ref[i : i + chunk, lane].astype(F32) * v_ref[i : i + chunk, :])
        pivot = jnp.sum(acc, axis=0, keepdims=True) / first
        line = jnp.zeros((8, lanes), F32)
        square = jnp.zeros((8, lanes), F32)
        for i in range(0, rows, chunk):
            off = (h_ref[i : i + chunk, lane].astype(F32) - pivot) * v_ref[i : i + chunk, :]
            line += fold(off)
            square += fold(off * off)
        total = jnp.sum(line, axis=0, keepdims=True)
        stats_ref[0, 0:1, lane] = pivot + total / count
        stats_ref[0, 1:2, lane] = (
            jnp.sum(square, axis=0, keepdims=True) - total * total / count
        )
        if with_count:
            stats_ref[0, 2:3, lane] = jnp.broadcast_to(count, (1, lanes))


def first_body(x_ref, w_ref, v_ref, h_ref, stats_ref):
    h_ref[...] = jnp.dot(x_ref[...], w_ref[...], preferred_element_type=F32)
    put_moments(stats_ref, h_ref, v_ref, True)


def first_product(x, weight, valid, micro):
    rows = x.shape[0] // micro
    depth, width = weight.shape
    return run(
        first_body,
        (micro,),
        [
            pl.BlockSpec((rows, depth), lambda m: (m, 0)),
            pl.BlockSpec((depth, width), lambda m: (0, 0)),
            pl.BlockSpec((rows, 1), lambda m: (m, 0)),
        ],
        [
            pl.BlockSpec((rows, width), lambda m: (m, 0)),
            pl.BlockSpec((1, 3, width), lambda m: (m, 0, 0)),
        ],
        [shape((micro * rows, width)), shape((micro, 3, width))],
        flops=2 * micro * rows * depth * width,
        bytes_accessed=2 * x.size,
    )(x, weight, valid)


def cell_column(rows):
    return lax.broadcasted_iota(jnp.int32, (rows, 1), 0) % CELL


def second_body(counts, refs):
    part_refs, (h_ref, v_ref, gain_ref, shift_ref, w_ref, a_ref, h2_ref, stats_ref, info_ref, cols_ref) = refs[:counts], refs[counts:]
    rows, width = h_ref.shape
    members = counts_of(part_refs)
    mean, scaled = norm_of(part_refs, members)
    info_ref[0, 0:1, :] = mean
    info_ref[0, 1:2, :] = scaled
    info_ref[0, 2:3, :] = jnp.broadcast_to(tree(list(members)), mean.shape)
    factor = scaled * gain_ref[...]
    shift = shift_ref[...]
    place = cell_column(COLS)
    has_left = (place >= 1).astype(F32)
    has_right = (place <= CELL - 2).astype(F32)
    blank = jnp.zeros((COLS, width), BF16)
    for i in range(0, rows, COLS):
        at = slice(i, i + COLS)
        pre = (h_ref[at, :] - mean) * factor + shift
        act = (pre * sigmoid(pre) * v_ref[at, :]).astype(BF16)
        a_ref[at, :] = act
        wide = act.astype(F32)
        sides = (
            (pltpu.roll(wide, 1, 0) * has_left).astype(BF16),
            act,
            (pltpu.roll(wide, COLS - 1, 0) * has_right).astype(BF16),
        )
        for c in range(3):
            cols_ref[at, (3 + c) * width : (4 + c) * width] = sides[c]
            if i % PIX < PIX - COLS:
                cols_ref[i + COLS : i + 2 * COLS, c * width : (c + 1) * width] = sides[c]
            else:
                cols_ref[at, (6 + c) * width : (7 + c) * width] = blank
            if i % PIX > 0:
                cols_ref[i - COLS : i, (6 + c) * width : (7 + c) * width] = sides[c]
            else:
                cols_ref[at, c * width : (c + 1) * width] = blank
    h2_ref[...] = jnp.dot(cols_ref[...], w_ref[...], preferred_element_type=F32)
    put_moments(stats_ref, h2_ref, v_ref, False)


def named(name, body, *fixed):
    def kernel(*refs):
        body(*fixed, refs)

    kernel.__name__ = name
    return kernel


def second_product(parts, h1, valid, gain, shift, weight, micro):
    rows, width = h1.shape[0] // micro, h1.shape[1]
    mid = pl.BlockSpec((rows, width), lambda m: (m, 0))
    return run(
        named("second_product", second_body, len(parts)),
        (micro,),
        [per_micro(part) for part in parts]
        + [
            mid,
            pl.BlockSpec((rows, 1), lambda m: (m, 0)),
            whole(gain),
            whole(shift),
            whole(weight),
        ],
        [
            mid,
            mid,
            pl.BlockSpec((1, 2, width), lambda m: (m, 0, 0)),
            pl.BlockSpec((1, 3, width), lambda m: (m, 0, 0)),
        ],
        [
            shape((micro * rows, width), BF16),
            shape((micro * rows, width)),
            shape((micro, 2, width)),
            shape((micro, 3, width)),
        ],
        [pltpu.VMEM((rows, weight.shape[0]), BF16)],
        flops=2 * micro * rows * weight.size,
        bytes_accessed=10 * h1.size,
    )(*parts, h1, valid, gain, shift, weight)


def third_body(counts, refs):
    part_refs, count_refs = refs[:counts], refs[counts : 2 * counts]
    h_ref, v_ref, gain_ref, shift_ref, w_ref, a_ref, h3_ref, stats_ref, info_ref, wide_ref = refs[2 * counts :]
    rows = h_ref.shape[0]
    mean, scaled = norm_of(part_refs, counts_of(count_refs))
    info_ref[0, 0:1, :] = mean
    info_ref[0, 1:2, :] = scaled
    factor = scaled * gain_ref[...]
    shift = shift_ref[...]
    for i in range(0, rows, 32):
        at = slice(i, i + 32)
        pre = (h_ref[at, :] - mean) * factor + shift
        a_ref[at, :] = (pre * sigmoid(pre) * v_ref[at, :]).astype(BF16)
    wide_ref[...] = jnp.dot(a_ref[...], w_ref[...], preferred_element_type=F32)
    h3_ref[...] = wide_ref[...].astype(BF16)
    put_moments(stats_ref, wide_ref, v_ref, False)


def third_product(parts, members, h2, valid, gain, shift, weight, micro):
    rows, depth = h2.shape[0] // micro, h2.shape[1]
    width = weight.shape[1]
    mid = pl.BlockSpec((rows, depth), lambda m: (m, 0))
    return run(
        named("third_product", third_body, len(parts)),
        (micro,),
        [per_micro(part) for part in parts + members]
        + [
            mid,
            pl.BlockSpec((rows, 1), lambda m: (m, 0)),
            whole(gain),
            whole(shift),
            whole(weight),
        ],
        [
            mid,
            pl.BlockSpec((rows, width), lambda m: (m, 0)),
            pl.BlockSpec((1, 2, width), lambda m: (m, 0, 0)),
            pl.BlockSpec((1, 2, depth), lambda m: (m, 0, 0)),
        ],
        [
            shape((micro * rows, depth), BF16),
            shape((micro * rows, width), BF16),
            shape((micro, 2, width)),
            shape((micro, 2, depth)),
        ],
        [pltpu.VMEM((rows, width), F32)],
        flops=2 * micro * rows * weight.size,
        bytes_accessed=4 * micro * rows * width,
    )(*parts, *members, h2, valid, gain, shift, weight)


def crop_sums(lines):
    crops = lines.shape[0] // CELL
    chosen = (
        lax.broadcasted_iota(jnp.int32, (crops, lines.shape[0]), 1) // CELL
        == lax.broadcasted_iota(jnp.int32, (crops, lines.shape[0]), 0)
    ).astype(F32)
    return jnp.dot(chosen, lines, precision=highest, preferred_element_type=F32)


def pool_body(counts, refs):
    part_refs, count_refs = refs[:counts], refs[counts : 2 * counts]
    h_ref, x_ref, v_ref, gain_ref, shift_ref, size_ref, feat_ref, info_ref, sums_ref = refs[2 * counts :]
    rows, width = h_ref.shape
    mean, scaled = norm_of(part_refs, counts_of(count_refs))
    info_ref[0, 0:1, :] = mean
    info_ref[0, 1:2, :] = scaled
    factor = scaled * gain_ref[...]
    shift = shift_ref[...]
    for j in range(0, width, 512):
        lane = slice(j, j + 512)
        for k in range(rows // PIX):
            acc = jnp.zeros((COLS, 512), F32)
            for r in range(ROWS):
                at = pl.ds(k * PIX + r * COLS, COLS)
                resid = (
                    (h_ref[at, lane].astype(F32) - mean[:, lane]) * factor[:, lane]
                    + shift[:, lane]
                    + x_ref[at, lane].astype(F32)
                )
                out = resid * (sigmoid(resid) * v_ref[at, :])
                acc += out.astype(BF16).astype(F32)
            sums_ref[pl.ds(k * COLS, COLS), lane] = acc
    feat_ref[...] = (crop_sums(sums_ref[...]) / size_ref[...]).astype(BF16).astype(F32)


def pool(parts, members, h3, x, valid, gain, shift, sizes, micro):
    rows, channels = h3.shape[0] // micro, h3.shape[1]
    crops = sizes.shape[0] // micro
    width = 1024
    tile = pl.BlockSpec((rows, width), lambda m, c: (m, c))
    line = pl.BlockSpec((1, width), lambda m, c: (0, c))
    pair = pl.BlockSpec((1, 2, width), lambda m, c: (m, 0, c))
    return run(
        named("pool", pool_body, len(parts)),
        (micro, channels // width),
        [pair] * len(parts)
        + [per_micro(part) for part in members]
        + [
            tile,
            tile,
            pl.BlockSpec((rows, 1), lambda m, c: (m, 0)),
            line,
            line,
            pl.BlockSpec((crops, 1), lambda m, c: (m, 0)),
        ],
        [pl.BlockSpec((crops, width), lambda m, c: (m, c)), pair],
        [shape((micro * crops, channels)), shape((micro, 2, channels))],
        [pltpu.VMEM((rows // ROWS, width), F32)],
        flops=20 * h3.size,
        bytes_accessed=4 * h3.size,
    )(*parts, *members, h3, x, valid, gain, shift, sizes)


def slope_body(*refs):
    h_ref, x_ref, v_ref, info_ref, gain_ref, shift_ref = refs[:6]
    slope_ref, first_ref, second_ref, sums_ref = refs[-4:]
    rows, width = h_ref.shape
    mean = info_ref[0, 0:1, :]
    scaled = info_ref[0, 1:2, :]
    factor = scaled * gain_ref[...]
    shift = shift_ref[...]
    for j in range(0, width, 512):
        lane = slice(j, j + 512)
        for k in range(rows // PIX):
            acc_first = jnp.zeros((COLS, 512), F32)
            acc_second = jnp.zeros((COLS, 512), F32)
            for r in range(ROWS):
                at = pl.ds(k * PIX + r * COLS, COLS)
                centred = h_ref[at, lane].astype(F32) - mean[:, lane]
                resid = centred * factor[:, lane] + shift[:, lane] + x_ref[at, lane].astype(F32)
                sig = sigmoid(resid)
                kept = sig * v_ref[at, :]
                slope = kept + resid * kept * (1.0 - sig)
                acc_first += slope
                acc_second += slope * centred
                slope_ref[at, lane] = slope.astype(BF16)
            place = pl.ds(k * COLS, COLS)
            sums_ref[0, place, lane] = acc_first
            sums_ref[1, place, lane] = acc_second * scaled[:, lane]
    first_ref[...] = crop_sums(sums_ref[0])
    second_ref[...] = crop_sums(sums_ref[1])


def slope_part(h3, x, valid, info, gain, shift, micro, index, earlier):
    rows, channels = h3.shape[0] // micro, h3.shape[1]
    crops = rows // PIX * SLOTS
    width = 1024
    tile = pl.BlockSpec((rows, width), lambda c: (index, c))
    small = pl.BlockSpec((crops, width), lambda c: (index, c))
    return run(
        slope_body,
        (channels // width,),
        [
            tile,
            tile,
            pl.BlockSpec((rows, 1), lambda c: (index, 0)),
            pl.BlockSpec((1, 2, width), lambda c: (index, 0, c)),
            pl.BlockSpec((1, width), lambda c: (0, c)),
            pl.BlockSpec((1, width), lambda c: (0, c)),
        ]
        + [pl.BlockSpec(memory_space=pl.ANY)] * len(earlier),
        [tile, small, small],
        [
            shape(h3.shape, BF16),
            shape((micro * crops, channels)),
            shape((micro * crops, channels)),
        ],
        [pltpu.VMEM((2, rows // ROWS, width), F32)],
        flops=30 * rows * channels,
        bytes_accessed=6 * rows * channels,
        aliases={6 + i: i for i in range(len(earlier))},
    )(h3, x, valid, info, gain, shift, *earlier)


def head_body(feat_ref, w_ref, g_ref, stats_ref):
    g = jnp.dot(feat_ref[...].astype(BF16), w_ref[...], preferred_element_type=F32)
    g_ref[...] = g
    micro = stats_ref.shape[0]
    crops = g.shape[0] // micro
    for m in range(micro):
        part = g[m * crops : (m + 1) * crops]
        mean = jnp.sum(part, axis=0, keepdims=True) / crops
        stats_ref[m, 0:1, :] = mean
        stats_ref[m, 1:2, :] = jnp.sum((part - mean) ** 2, axis=0, keepdims=True)


def head_product(feat, weight, micro):
    lines = feat.shape[0]
    depth, width = weight.shape
    tile = 512
    return run(
        head_body,
        (width // tile,),
        [
            pl.BlockSpec((lines, depth), lambda c: (0, 0)),
            pl.BlockSpec((depth, tile), lambda c: (0, c)),
        ],
        [
            pl.BlockSpec((lines, tile), lambda c: (0, c)),
            pl.BlockSpec((micro, 2, tile), lambda c: (0, 0, c)),
        ],
        [shape((lines, width)), shape((micro, 2, width))],
        flops=2 * lines * weight.size,
        bytes_accessed=2 * weight.size,
    )(feat, weight)


def head_back_body(total_crops, counts, refs):
    part_refs = refs[:counts]
    dy_ref, g_ref, info_ref, gain_ref, w_ref, size_ref, first_ref, second_ref, dg_ref, wide_ref, stats_ref, low_ref = refs[counts:]
    micro = stats_ref.shape[0]
    lines = dy_ref.shape[0]
    crops = lines // micro

    @pl.when(pl.program_id(0) == 0)
    def _():
        for m in range(micro):
            at = pl.ds(m * crops, crops)
            one = tree([ref[m : m + 1, :] for ref in part_refs]) / total_crops
            two = tree([ref[micro + m : micro + m + 1, :] for ref in part_refs]) / total_crops
            scaled = info_ref[m, 1:2, :]
            normal = (g_ref[at, :] - info_ref[m, 0:1, :]) * scaled
            dg = gain_ref[...] * scaled * (dy_ref[at, :] - (one + normal * two))
            low = dg.astype(BF16)
            low_ref[at, :] = low
            dg_ref[at, :] = low.astype(F32)

    per_crop = nt_dot(low_ref[...], w_ref[...]) / size_ref[...]
    lift = (
        lax.broadcasted_iota(jnp.int32, (lines * CELL, lines), 0) // CELL
        == lax.broadcasted_iota(jnp.int32, (lines * CELL, lines), 1)
    ).astype(F32)
    wide_ref[...] = jnp.dot(lift, per_crop, precision=highest, preferred_element_type=F32)
    one = per_crop * first_ref[...]
    two = per_crop * second_ref[...]
    for m in range(micro):
        at = slice(m * crops, (m + 1) * crops)
        stats_ref[m, 0:1, :] = jnp.sum(one[at], axis=0, keepdims=True)
        stats_ref[m, 1:2, :] = jnp.sum(two[at], axis=0, keepdims=True)


def head_back(parts, dy, g, info, gain, weight, sizes, first, second, total_crops):
    lines, width = dy.shape
    channels = weight.shape[0]
    micro = info.shape[0]
    tile = 512
    part = pl.BlockSpec((lines, tile), lambda c: (0, c))
    return run(
        named("head_back", head_back_body, total_crops, len(parts)),
        (channels // tile,),
        [whole(a) for a in parts]
        + [
            whole(dy),
            whole(g),
            whole(info),
            whole(gain),
            pl.BlockSpec((tile, width), lambda c: (c, 0)),
            whole(sizes),
            part,
            part,
        ],
        [
            whole(dy),
            pl.BlockSpec((lines * CELL, tile), lambda c: (0, c)),
            pl.BlockSpec((micro, 2, tile), lambda c: (0, 0, c)),
        ],
        [shape((lines, width)), shape((lines * CELL, channels)), shape((micro, 2, channels))],
        [pltpu.VMEM((lines, width), BF16)],
        flops=2 * lines * weight.size,
        bytes_accessed=2 * weight.size,
    )(*parts, dy, g, info, gain, weight, sizes, first, second)


def third_back_body(counts, refs):
    part_refs = refs[:counts]
    wide_ref, slope_ref, h3_ref, v_ref, info3_ref, gain3_ref, info1_ref, w_ref, h2_ref, info2_ref, gain2_ref, shift2_ref, d_ref, dy_ref, stats_ref = refs[counts:]
    rows, channels = slope_ref.shape
    number = info1_ref[0, 2:3, 0:1]
    first, second = sums_of(part_refs, 0, 1)
    mean = info3_ref[0, 0:1, :]
    scaled = info3_ref[0, 1:2, :]
    factor = gain3_ref[...] * scaled
    one = factor * first / number
    two = factor * scaled * second / number
    for j in range(0, channels, 512):
        lane = slice(j, j + 512)
        for k in range(rows // PIX):
            wide = wide_ref[pl.ds(k * COLS, COLS), lane] * factor[:, lane]
            for r in range(ROWS):
                at = pl.ds(k * PIX + r * COLS, COLS)
                back = one[:, lane] + (h3_ref[at, lane].astype(F32) - mean[:, lane]) * two[:, lane]
                d = wide * slope_ref[at, lane].astype(F32) - v_ref[at, :] * back
                d_ref[at, lane] = d.astype(BF16)
    dy_ref[...] = nt_dot(d_ref[...], w_ref[...])
    put_back(dy_ref, h2_ref, v_ref, info2_ref, gain2_ref, shift2_ref, stats_ref)


def put_back(dy_ref, h_ref, v_ref, info_ref, gain_ref, shift_ref, stats_ref):
    rows, width = dy_ref.shape
    first = jnp.zeros((8, width), F32)
    second = jnp.zeros((8, width), F32)
    for i in range(0, rows, 32):
        at = slice(i, i + 32)
        normal = (h_ref[at, :] - info_ref[0, 0:1, :]) * info_ref[0, 1:2, :]
        pre = normal * gain_ref[...] + shift_ref[...]
        dy = dy_ref[at, :] * v_ref[at, :] * slope_of(pre)
        dy_ref[at, :] = dy
        first += fold(dy)
        second += fold(dy * normal)
    stats_ref[0, 0:1, :] = jnp.sum(first, axis=0, keepdims=True)
    stats_ref[0, 1:2, :] = jnp.sum(second, axis=0, keepdims=True)


def third_back(parts, wide, slope, h3, valid, info3, gain3, info1, weight, h2, info2, gain2, shift2, micro):
    rows, channels = slope.shape[0] // micro, slope.shape[1]
    middle = weight.shape[0]
    lines = wide.shape[0] // micro
    big = pl.BlockSpec((rows, channels), lambda m: (m, 0))
    mid = pl.BlockSpec((rows, middle), lambda m: (m, 0))
    return run(
        named("third_back", third_back_body, len(parts)),
        (micro,),
        [per_micro(part) for part in parts]
        + [
            pl.BlockSpec((lines, channels), lambda m: (m, 0)),
            big,
            big,
            pl.BlockSpec((rows, 1), lambda m: (m, 0)),
            per_micro(info3),
            whole(gain3),
            per_micro(info1),
            whole(weight),
            mid,
            per_micro(info2),
            whole(gain2),
            whole(shift2),
        ],
        [big, mid, pl.BlockSpec((1, 2, middle), lambda m: (m, 0, 0))],
        [shape(slope.shape, BF16), shape(h2.shape), shape((micro, 2, middle))],
        flops=2 * slope.shape[0] * weight.size,
        bytes_accessed=6 * slope.size,
    )(*parts, wide, slope, h3, valid, info3, gain3, info1, weight, h2, info2, gain2, shift2)


def out_grad_body(which_ref, left_ref, right_ref, out_ref, turned_ref):
    @pl.when(pl.program_id(0) == 0)
    def _():
        turned_ref[...] = left_ref[...].T

    grad = jnp.dot(turned_ref[...], right_ref[...], preferred_element_type=F32)
    out_ref[0] = grad.reshape(out_ref.shape[1:])


def out_grad(which, left, right, shards):
    rows, depth = left.shape
    half = right.shape[1] // 2
    tile = 512
    steps = half // tile
    lines = depth // shards

    def column(c, w):
        return jnp.where(c // steps == 0, w[0], 1 - w[0]) * steps + c % steps

    return run(
        out_grad_body,
        (2 * steps,),
        [
            pl.BlockSpec(left.shape, lambda c, w: (0, 0)),
            pl.BlockSpec((rows, tile), lambda c, w: (0, column(c, w))),
        ],
        pl.BlockSpec((1, shards, lines, tile), lambda c, w: (c // steps, 0, c % steps, 0)),
        shape((2, shards, steps * lines, tile)),
        [pltpu.VMEM((depth, rows), BF16)],
        flops=2 * rows * depth * right.shape[1],
        bytes_accessed=2 * left.size + 2 * right.size + 8 * depth * half,
        prefetch=1,
    )(which, left, right)


def put_norm_back(part_refs, dy_ref, h_ref, v_ref, info_ref, number_ref, gain_ref, d_ref):
    micro = info_ref.shape[0]
    rows = dy_ref.shape[0] // micro
    for m in range(micro):
        number = number_ref[m, 2:3, 0:1]
        first, second = sums_of(part_refs, 0, 1, m)
        scaled = info_ref[m, 1:2, :]
        factor = gain_ref[...] * scaled
        one = factor * first / number
        two = factor * scaled * second / number
        mean = info_ref[m, 0:1, :]
        for i in range(m * rows, (m + 1) * rows, 32):
            at = slice(i, i + 32)
            back = one + (h_ref[at, :] - mean) * two
            d_ref[at, :] = (factor * dy_ref[at, :] - v_ref[at, :] * back).astype(BF16)


def put_sides(a_ref, sides_ref):
    rows, width = a_ref.shape
    blank = jnp.zeros((COLS, width), BF16)
    place = cell_column(COLS)
    has_left = (place >= 1).astype(F32)
    has_right = (place <= CELL - 2).astype(F32)
    for k in range(rows // PIX):
        for c in range(3):
            sides_ref[c, k, 0:COLS, :] = blank
            sides_ref[c, k, COLS + PIX :, :] = blank
        for r in range(ROWS):
            act = a_ref[k * PIX + r * COLS : k * PIX + (r + 1) * COLS, :]
            wide = act.astype(F32)
            at = slice((r + 1) * COLS, (r + 2) * COLS)
            sides_ref[0, k, at, :] = (pltpu.roll(wide, 1, 0) * has_left).astype(BF16)
            sides_ref[1, k, at, :] = act
            sides_ref[2, k, at, :] = (pltpu.roll(wide, COLS - 1, 0) * has_right).astype(BF16)


def put_tap(out_ref, sides_ref, turned_ref):
    tap = pl.program_id(0)
    _, canvases, _, width = sides_ref.shape
    start = pl.multiple_of(tap // 3 * COLS, COLS)
    left = sides_ref[tap % 3, :, pl.ds(start, PIX), :].reshape(canvases * PIX, width)
    out_ref[...] = jnp.dot(turned_ref[...], left, preferred_element_type=F32).T


def half_of(which_ref, d_ref):
    half = d_ref.shape[1] // 2
    return d_ref[:, pl.ds(pl.multiple_of(which_ref[0] * half, half), half)]


def mid_first_body(counts, refs):
    which_ref, part_refs = refs[0], refs[1 : 1 + counts]
    dy_ref, h_ref, v_ref, info_ref, number_ref, gain_ref, a_ref, d_ref, out_ref, sides_ref, turned_ref = refs[1 + counts :]

    @pl.when(pl.program_id(0) == 0)
    def _():
        put_norm_back(part_refs, dy_ref, h_ref, v_ref, info_ref, number_ref, gain_ref, d_ref)
        turned_ref[...] = half_of(which_ref, d_ref).T
        put_sides(a_ref, sides_ref)

    put_tap(out_ref, sides_ref, turned_ref)


def mid_second_body(refs):
    which_ref, d_ref, a_ref, out_ref, sides_ref, turned_ref = refs

    @pl.when(pl.program_id(0) == 0)
    def _():
        turned_ref[...] = half_of(which_ref, d_ref).T
        put_sides(a_ref, sides_ref)

    put_tap(out_ref, sides_ref, turned_ref)


def mid_grad(name, body, which, ins, act, with_d):
    rows, width = act.shape
    half = width // 2
    grad = pl.BlockSpec((width, half), lambda t, w: (t, 0))
    return run(
        named(name, body, *([len(ins) - 7] if with_d else [])),
        (TAPS,),
        [whole(a) for a in ins],
        [whole(act), grad] if with_d else grad,
        [shape(act.shape, BF16), shape((TAPS * width, half))]
        if with_d
        else shape((TAPS * width, half)),
        [
            pltpu.VMEM((3, rows // PIX, PIX + 2 * COLS, width), BF16),
            pltpu.VMEM((half, rows), BF16),
        ],
        flops=2 * rows * TAPS * width * half,
        bytes_accessed=4 * TAPS * width * half,
        prefetch=1,
    )(which, *ins)


def in_grad_body(counts, refs):
    which_ref, part_refs = refs[0], refs[1 : 1 + counts]
    dy_ref, h_ref, v_ref, info_ref, number_ref, gain_ref, x_ref, d_ref, send_ref, keep_ref, turned_ref = refs[1 + counts :]

    @pl.when(pl.program_id(0) == 0)
    def _():
        put_norm_back(part_refs, dy_ref, h_ref, v_ref, info_ref, number_ref, gain_ref, d_ref)
        turned_ref[...] = d_ref[...].T

    grad = jnp.dot(turned_ref[...], x_ref[...], preferred_element_type=F32).T
    half = grad.shape[1] // 2
    low = which_ref[0] == 0
    left, right = grad[:, :half], grad[:, half:]
    send_ref[...] = jnp.where(low, left, right)
    keep_ref[...] = jnp.where(low, right, left)


def in_grad(which, parts, dy, h, valid, info, number, gain, x):
    rows, width = dy.shape
    depth = x.shape[1]
    half = width // 2
    tile = 512
    ins = [*parts, dy, h, valid, info, number, gain]
    grad = pl.BlockSpec((tile, half), lambda c, w: (c, 0))
    return run(
        named("in_grad", in_grad_body, len(parts)),
        (depth // tile,),
        [whole(a) for a in ins] + [pl.BlockSpec((rows, tile), lambda c, w: (0, c))],
        [whole(dy), grad, grad],
        [shape(dy.shape, BF16), shape((depth, half)), shape((depth, half))],
        [pltpu.VMEM((width, rows), BF16)],
        flops=2 * rows * depth * width,
        bytes_accessed=2 * x.size + 4 * depth * width + 10 * dy.size,
        prefetch=1,
    )(which, *ins, x)


def second_back_body(d_ref, w_ref, v_ref, h1_ref, info_ref, gain_ref, shift_ref, dy_ref, stats_ref, moved_ref, packed_ref):
    rows, width = d_ref.shape

    @pl.when(pl.program_id(0) == 0)
    def _():
        for r in range(3):
            for c in range(3):
                tap = 3 * r + c
                packed_ref[c, :, r * width : (r + 1) * width] = w_ref[
                    tap * width : (tap + 1) * width, :
                ]

    blank = jnp.zeros((COLS, width), BF16)
    for k in range(0, rows, PIX):
        moved_ref[k : k + PIX - COLS, 0:width] = d_ref[k + COLS : k + PIX, :]
        moved_ref[k + PIX - COLS : k + PIX, 0:width] = blank
        moved_ref[k : k + COLS, 2 * width :] = blank
        moved_ref[k + COLS : k + PIX, 2 * width :] = d_ref[k : k + PIX - COLS, :]
    moved_ref[:, width : 2 * width] = d_ref[...]
    parts = [nt_dot(moved_ref[...], packed_ref[c]) for c in range(3)]
    place = cell_column(rows)
    dy_ref[...] = (
        parts[1]
        + pltpu.roll(parts[2], 1, 0) * (place >= 1).astype(F32)
        + pltpu.roll(parts[0], rows - 1, 0) * (place <= CELL - 2).astype(F32)
    )
    put_back(dy_ref, h1_ref, v_ref, info_ref, gain_ref, shift_ref, stats_ref)


def second_back(d, weight, valid, h1, info, gain, shift, micro):
    rows, width = d.shape[0] // micro, d.shape[1]
    mid = pl.BlockSpec((rows, width), lambda m: (m, 0))
    return run(
        second_back_body,
        (micro,),
        [
            mid,
            whole(weight),
            pl.BlockSpec((rows, 1), lambda m: (m, 0)),
            mid,
            per_micro(info),
            whole(gain),
            whole(shift),
        ],
        [mid, pl.BlockSpec((1, 2, width), lambda m: (m, 0, 0))],
        [shape(d.shape), shape((micro, 2, width))],
        [pltpu.VMEM((rows, 3 * width), BF16), pltpu.VMEM((3, width, 3 * width), BF16)],
        flops=2 * micro * rows * weight.size,
        bytes_accessed=10 * d.size,
    )(d, weight, valid, h1, info, gain, shift)


def pixels_body(d_ref, w_ref, wide_ref, slope_ref, out_ref):
    rows, channels = out_ref.shape
    width = 512
    for j in range(0, channels, width):
        lane = pl.ds(j, width)
        grad = nt_dot(d_ref[...], w_ref[lane, :])
        for k in range(rows // PIX):
            wide = wide_ref[pl.ds(k * COLS, COLS), lane]
            for r in range(ROWS):
                first = k * PIX + r * COLS
                at = pl.ds(first, COLS)
                out_ref[at, lane] = (
                    grad[first : first + COLS] + wide * slope_ref[at, lane].astype(F32)
                ).astype(BF16)


def pixels_grad(d, weight, wide, slope, micro):
    rows, channels = slope.shape[0] // micro, slope.shape[1]
    lines = wide.shape[0] // micro
    big = pl.BlockSpec((rows, channels), lambda m: (m, 0))
    return run(
        pixels_body,
        (micro,),
        [
            pl.BlockSpec((rows, d.shape[1]), lambda m: (m, 0)),
            pl.BlockSpec(weight.shape, lambda m: (0, 0)),
            pl.BlockSpec((lines, channels), lambda m: (m, 0)),
            big,
        ],
        big,
        shape(slope.shape, BF16),
        flops=2 * slope.shape[0] * weight.size,
        bytes_accessed=4 * slope.size,
    )(d, weight, wide, slope)


def factor_body(feat_ref, other_feat_ref, dg_ref, far_ref, near_ref, both_ref, out_ref):
    left = jnp.concatenate([feat_ref[...], other_feat_ref[...]], 0).astype(BF16)
    lines = dg_ref.shape[0] // 2
    right = jnp.concatenate(
        [
            ref[c * lines : (c + 1) * lines, :]
            for c in range(2)
            for ref in (dg_ref, near_ref, far_ref, both_ref)
        ],
        0,
    ).astype(BF16)
    out_ref[...] = tn_dot(left, right)


def factor_grad(feat, other_feat, dg, far, near, both):
    lines, depth = feat.shape
    width = dg.shape[1]
    tile = 512
    left = pl.BlockSpec((lines, tile), lambda c: (0, c))
    return run(
        factor_body,
        (depth // tile,),
        [left, left] + [whole(dg)] * 4,
        pl.BlockSpec((tile, width), lambda c: (c, 0)),
        shape((depth, width)),
        flops=4 * lines * depth * width,
        bytes_accessed=4 * depth * width,
    )(feat, other_feat, dg, far, near, both)


def embed_body(protos, counts, members, refs):
    part_refs = refs[:counts]
    g_ref, gain_ref, shift_ref, w_ref, bias_ref, table_ref, queue_ref, act_ref, z_ref, inverse_ref, unit_ref, logits_ref, batch_ref, line_ref, sums_ref, info_ref = refs[counts:]
    micro = info_ref.shape[0]
    crops = g_ref.shape[0] // micro
    for m in range(micro):
        at = slice(m * crops, (m + 1) * crops)
        mean, scaled = norm_of(part_refs, members, m)
        info_ref[m, 0:1, :] = mean
        info_ref[m, 1:2, :] = scaled
        pre = (g_ref[at, :] - mean) * scaled * gain_ref[...] + shift_ref[...]
        act_ref[at, :] = (pre * sigmoid(pre)).astype(BF16)
    z = jnp.dot(act_ref[...], w_ref[...], preferred_element_type=F32) + bias_ref[...]
    inverse = lax.rsqrt(jnp.sum(z * z, 1, keepdims=True) + eps_unit)
    unit = (z * inverse).astype(BF16)
    z_ref[...] = z
    inverse_ref[...] = inverse
    unit_ref[...] = unit
    logits = jnp.dot(unit, table_ref[...], preferred_element_type=F32)
    logits_ref[...] = logits
    real = lax.broadcasted_iota(jnp.int32, (1, logits.shape[1]), 1) < protos
    batch = jnp.where(real, jnp.exp(logits / transport_epsilon), 0.0)
    batch_ref[...] = batch
    queued = jnp.dot(queue_ref[...], table_ref[...], preferred_element_type=F32)
    line = jnp.where(real, jnp.exp(queued / transport_epsilon), 0.0)
    line_ref[...] = line
    queue_sum = jnp.sum(line, axis=0, keepdims=True)
    for m in range(micro):
        at = slice(m * crops, (m + 1) * crops)
        sums_ref[m : m + 1, :] = jnp.sum(batch[at], axis=0, keepdims=True) + queue_sum


def embed_product(parts, members, protos, g, gain, shift, weight, bias, table, queue):
    lines = g.shape[0]
    micro = parts[0].shape[0]
    feat = weight.shape[1]
    wide = table.shape[1]
    outs = [
        shape(g.shape, BF16),
        shape((lines, feat)),
        shape((lines, 1)),
        shape((lines, feat), BF16),
        shape((lines, wide)),
        shape((lines, wide)),
        shape((queue.shape[0], wide)),
        shape((micro, wide)),
        shape((micro, 2, g.shape[1])),
    ]
    ins = [*parts, g, gain, shift, weight, bias, table, queue]
    return run(
        named("embed", embed_body, protos, len(parts), members),
        (1,),
        [whole(a) for a in ins],
        [whole(a) for a in outs],
        outs,
        flops=2 * lines * table.size,
        bytes_accessed=8 * lines * wide,
    )(*ins)


def sweep_body(protos, counts, refs):
    part_refs = refs[:counts]
    batch_ref, queue_ref, new_batch_ref, new_queue_ref, sums_ref = refs[counts:]
    micro, wide = sums_ref.shape
    crops = batch_ref.shape[0] // micro
    lines = new_queue_ref.shape[0] // micro
    shared = queue_ref.shape[0] == lines
    real = lax.broadcasted_iota(jnp.int32, (1, wide), 1) < protos
    for m in range(micro):
        column = jnp.where(real, tree([ref[m : m + 1, :] for ref in part_refs]), 1.0)
        at = slice(m * crops, (m + 1) * crops)
        batch = batch_ref[at, :] / column
        batch = batch / jnp.sum(batch, 1, keepdims=True)
        new_batch_ref[at, :] = batch
        own = slice(m * lines, (m + 1) * lines)
        queue = queue_ref[slice(0, lines) if shared else own, :] / column
        queue = queue / jnp.sum(queue, 1, keepdims=True)
        new_queue_ref[own, :] = queue
        sums_ref[m : m + 1, :] = jnp.sum(batch, axis=0, keepdims=True) + jnp.sum(
            queue, axis=0, keepdims=True
        )


def sweep(parts, protos, batch, queue, lines):
    micro, wide = parts[0].shape
    outs = [shape(batch.shape), shape((micro * lines, wide)), shape(parts[0].shape)]
    ins = [*parts, batch, queue]
    return run(
        named("sweep", sweep_body, protos, len(parts)),
        (1,),
        [whole(a) for a in ins],
        [whole(a) for a in outs],
        outs,
        flops=20 * batch.size,
        bytes_accessed=16 * batch.size,
    )(*ins)


def split_dot(dot, left, right, wide_left):
    value = left if wide_left else right
    high = value.astype(BF16)
    low = (value - high.astype(F32)).astype(BF16)
    if wide_left:
        return dot(high, right) + dot(low, right)
    return dot(left, high) + dot(left, low)


def pack_small(packed_ref, protos, embed):
    _, shards, _, lines, width = packed_ref.shape
    rows = protos.shape[0] // shards // 2
    half = protos.shape[1] // 2
    groups = half // width
    lane = embed.shape[1]
    below = lines - groups * rows
    for c in range(2):
        for d in range(shards):
            for y in range(2):
                first = (2 * d + y) * rows
                for q in range(groups):
                    packed_ref[c, d, y, q * rows : (q + 1) * rows, :] = protos[
                        first : first + rows, c * half + q * width : c * half + (q + 1) * width
                    ]
                for q in range(width // lane):
                    first = (((2 * d + c) * 2 + y) * (width // lane) + q) * below
                    packed_ref[c, d, y, groups * rows :, q * lane : (q + 1) * lane] = embed[
                        first : first + below
                    ]


def unpack_small(packed, protos, embed):
    _, shards, _, lines, width = packed.shape
    rows = protos[0] // shards // 2
    groups = protos[1] // 2 // width
    lane = embed[1]
    above = packed[:, :, :, : groups * rows].reshape(2, shards, 2, groups, rows, width)
    below = packed[:, :, :, groups * rows :]
    below = below.reshape(2, shards, 2, lines - groups * rows, width // lane, lane)
    return (
        above.transpose(1, 2, 4, 0, 3, 5).reshape(protos),
        below.transpose(1, 0, 2, 4, 3, 5).reshape(embed),
    )


def packed_shape(protos, embed, shards):
    width = 512
    lines = protos[0] // shards // 2 * (protos[1] // 2 // width)
    return (2, shards, 2, lines + embed[0] * embed[1] // shards // 4 // width, width)


def loss_body(protos, scale, counts, refs):
    part_refs = refs[:counts]
    batch_ref, logits_ref, unit_ref, z_ref, inverse_ref, act_ref, g_ref, info_ref, gain_ref, shift_ref, w_ref, table_ref, packed_ref, dy_ref, sums_ref = refs[counts:]
    micro, wide = part_refs[0].shape
    lines = batch_ref.shape[0]
    crops = lines // micro
    real = lax.broadcasted_iota(jnp.int32, (1, wide), 1) < protos
    odd = lax.broadcasted_iota(jnp.int32, (crops, 1), 0) % 2 == 1
    parts = []
    loss = jnp.zeros((1, 1), F32)
    for m in range(micro):
        at = slice(m * crops, (m + 1) * crops)
        codes = batch_ref[at, :] / jnp.where(
            real, tree([ref[m : m + 1, :] for ref in part_refs]), 1.0
        )
        codes = codes / jnp.sum(codes, 1, keepdims=True)
        partner = jnp.where(odd, pltpu.roll(codes, 1, 0), pltpu.roll(codes, crops - 1, 0))
        sharp = logits_ref[at, :] / softmax_sharpness
        top = jnp.max(jnp.where(real, sharp, -jnp.inf), 1, keepdims=True)
        shifted = sharp - top
        mass = jnp.where(real, jnp.exp(shifted), 0.0)
        total = jnp.sum(mass, 1, keepdims=True)
        chance = shifted - jnp.log(total)
        loss += jnp.sum(jnp.sum(partner * chance, 1, keepdims=True), 0, keepdims=True)
        weight = jnp.sum(partner, 1, keepdims=True)
        parts.append((scale / softmax_sharpness) * (weight * (mass / total) - partner))
    d_scores = jnp.concatenate(parts, 0)
    unit = unit_ref[...]
    grad_protos = split_dot(tn_dot, unit, d_scores, False)
    d_unit = split_dot(nt_dot, d_scores, table_ref[...], True)
    z = z_ref[...]
    inverse = inverse_ref[...]
    dz = inverse * d_unit - z * (inverse * inverse * inverse) * jnp.sum(
        z * d_unit, 1, keepdims=True
    )
    grad_embed = split_dot(tn_dot, act_ref[...], dz, False)
    pack_small(packed_ref, grad_protos, grad_embed)
    d_act = split_dot(nt_dot, dz, w_ref[...], True)
    for m in range(micro):
        at = slice(m * crops, (m + 1) * crops)
        normal = (g_ref[at, :] - info_ref[m, 0:1, :]) * info_ref[m, 1:2, :]
        pre = normal * gain_ref[...] + shift_ref[...]
        dy = d_act[at] * slope_of(pre)
        dy_ref[at, :] = dy
        sums_ref[m : m + 1, :] = jnp.sum(dy, axis=0, keepdims=True)
        sums_ref[micro + m : micro + m + 1, :] = jnp.sum(dy * normal, axis=0, keepdims=True)
    feat = z.shape[1]
    sums_ref[2 * micro : 2 * micro + 1, :] = jnp.zeros((1, sums_ref.shape[1]), F32)
    sums_ref[2 * micro : 2 * micro + 1, 0:feat] = jnp.sum(dz, axis=0, keepdims=True)
    sums_ref[2 * micro : 2 * micro + 1, feat : 2 * feat] = jnp.broadcast_to(
        -scale * loss, (1, feat)
    )


def loss_grads(parts, protos, scale, batch, logits, unit, z, inverse, act, g, info, gain, shift, weight, table, shards):
    ins = [*parts, batch, logits, unit, z, inverse, act, g, info, gain, shift, weight, table]
    micro = info.shape[0]
    outs = [
        shape(packed_shape(table.shape, weight.shape, shards)),
        shape(g.shape),
        shape((2 * micro + 1, g.shape[1])),
    ]
    return run(
        named("loss", loss_body, protos, scale, len(parts)),
        (1,),
        [whole(a) for a in ins],
        [whole(a) for a in outs],
        outs,
        flops=8 * table.size * batch.shape[0],
        bytes_accessed=16 * batch.size,
    )(*ins)


def pick_block(rows, width, cell):
    return pl.BlockSpec((1, rows, width), lambda g, w: cell(g, w[0], w[1], w[2]) + (0,))


def sent_first(g, core, x, y):
    z, b = g // 2, g % 2
    return (2 * z + (1 - core) * (1 - x) + core * b, (1 - core) * b + core * (1 - y))


def kept_second(g, core, x, y):
    return (2 * g + x, y)


def sent_second(g, core, x, y):
    return (2 * g + (1 - core) * x + core * (1 - x), (1 - core) * (1 - y) + core * y)


def add_groups(refs, sizes, out_ref, extra=None):
    start = 0
    place = 0
    for count, rows in sizes:
        value = refs[place][0]
        for ref in refs[place + 1 : place + count]:
            value = value + ref[0]
        if extra is not None:
            value = value + extra[0, start : start + rows, :]
        out_ref[0, start : start + rows, :] = value
        place += count
        start += rows


def first_send(scalars, groups):
    sizes = [(len(addends), addends[0].shape[1] // 2) for addends in groups]
    shards, _, width = groups[0][0].shape
    lines = sum(rows for _, rows in sizes)
    specs = []
    for (count, rows), addends in zip(sizes, groups):
        specs += [pick_block(rows, width, sent_first)] * count
    flat = [array for addends in groups for array in addends]

    def body(refs):
        add_groups(refs[1:-1], sizes, refs[-1])

    return run(
        named("first_send", body),
        (shards,),
        specs,
        pl.BlockSpec((1, lines, width), lambda g, w: (g, 0, 0)),
        shape((shards, lines, width)),
        bytes_accessed=4 * lines * width * shards * 3,
        prefetch=1,
    )(scalars, *flat)


def second_send(scalars, groups, came):
    sizes = [(len(addends), addends[0].shape[1] // 2) for addends in groups]
    shards, _, width = groups[0][0].shape
    lines = sum(rows for _, rows in sizes)
    flat = [array for addends in groups for array in addends]
    specs = []
    for cell in (sent_second, kept_second):
        for (count, rows), addends in zip(sizes, groups):
            specs += [pick_block(rows, width, cell)] * count

    def bit(w):
        return (1 - w[0]) * w[2] + w[0] * w[1]

    specs.append(pl.BlockSpec((1, lines, width), lambda g, w: (2 * g + 1 - bit(w), 0, 0)))
    specs.append(pl.BlockSpec((1, lines, width), lambda g, w: (2 * g + bit(w), 0, 0)))
    out = pl.BlockSpec((1, lines, width), lambda g, w: (g, 0, 0))

    def body(refs):
        refs = refs[1:]
        add_groups(refs[: len(flat)], sizes, refs[-2], refs[2 * len(flat)])
        add_groups(refs[len(flat) : 2 * len(flat)], sizes, refs[-1], refs[2 * len(flat) + 1])

    return run(
        named("second_send", body),
        (shards // 2,),
        specs,
        [out, out],
        [shape((shards // 2, lines, width))] * 2,
        bytes_accessed=4 * lines * width * shards * 4,
        prefetch=1,
    )(scalars, *flat, *flat, came, came)


def place_early_body(scalars_ref, mine_ref, far_ref, mine_core_ref, far_core_ref, out_ref, embed_ref, protos_ref, head_ref):
    lines = out_ref.shape[0]
    rows = protos_ref.shape[0] // 2
    wide = 512
    groups = protos_ref.shape[1] // 2 // wide
    lane = embed_ref.shape[1]
    below = embed_ref.shape[0] // 4 // (wide // lane)
    start = lines + groups * rows + below
    for c, y, ref in ((0, 0, mine_ref), (0, 1, far_ref), (1, 0, mine_core_ref), (1, 1, far_core_ref)):
        c = scalars_ref[0] if c == 0 else 1 - scalars_ref[0]
        y = scalars_ref[2] if y == 0 else 1 - scalars_ref[2]
        column = pl.multiple_of((2 * c + y) * wide, wide)
        out_ref[:, pl.ds(column, wide)] = ref[0:lines, :]
        head_ref[:, pl.ds(column, wide)] = ref[start:, :]
        at = pl.ds(pl.multiple_of(y * rows, rows), rows)
        for q in range(groups):
            column = pl.multiple_of((c * groups + q) * wide, wide)
            protos_ref[at, pl.ds(column, wide)] = ref[lines + q * rows : lines + (q + 1) * rows, :]
        for q in range(wide // lane):
            first = pl.multiple_of(((2 * c + y) * (wide // lane) + q) * below, below)
            embed_ref[pl.ds(first, below), :] = ref[
                lines + groups * rows : start, q * lane : (q + 1) * lane
            ]


def place_late_body(scalars_ref, mine_ref, far_ref, mine_core_ref, far_core_ref, *out_refs):
    for c, y, ref in ((0, 0, mine_ref), (0, 1, far_ref), (1, 0, mine_core_ref), (1, 1, far_core_ref)):
        c = scalars_ref[0] if c == 0 else 1 - scalars_ref[0]
        y = scalars_ref[2] if y == 0 else 1 - scalars_ref[2]
        start = 0
        for out_ref in out_refs:
            rows, width = out_ref.shape[0] // 2, out_ref.shape[1] // 2
            out_ref[
                pl.ds(pl.multiple_of(y * rows, rows), rows),
                pl.ds(pl.multiple_of(c * width, width), width),
            ] = ref[start : start + rows, :]
            start += rows


def placed_pieces(body, scalars, pieces, outs):
    return run(
        body,
        (1,),
        [whole(a) for a in pieces],
        [whole(a) for a in outs],
        outs,
        prefetch=1,
    )(scalars, *pieces)


def gathered(mine):
    far = swap(mine, 2)
    return [mine, far, swap(mine, 1), swap(far, 1)]


def on_device(
    pixels,
    crop_map,
    queue_rows,
    conv_in,
    gain_one,
    shift_one,
    conv_mid,
    gain_two,
    shift_two,
    conv_out,
    gain_three,
    shift_three,
    head_weight,
    head_gain,
    head_shift,
    embed_weight,
    embed_bias,
    prototypes,
):
    micro, canvas, pixel_count, channels = pixels.shape
    devices = lax.axis_size("dp") * lax.axis_size("hst")
    crops = canvas * SLOTS
    total_crops = crops * devices * 1.0
    loss_scale = 1.0 / (micro * total_crops)
    x = pixels.reshape(micro * canvas * pixel_count, channels)
    valid = (crop_map < SLOTS).astype(F32).reshape(-1, 1)
    sizes = jnp.sum(
        (crop_map[:, :, None, :] == jnp.arange(SLOTS, dtype=jnp.int32)[:, None]).astype(F32), 3
    ).reshape(-1, 1)

    shards = lax.axis_size("dp")
    quick = shards == 8 and lax.axis_size("hst") == 4
    packs = 8
    protos = prototypes.shape[1]
    table = jnp.pad(prototypes, ((0, 0), (0, -protos % 1024)))

    def row(vector):
        return vector.reshape(1, -1)

    masks = dp_masks()
    near, far = masks[0], masks[1:]
    core = bit_of(1)
    side = bit_of(2)
    scalars = jnp.stack([core, bit_of(near), side]).astype(jnp.int32)
    keep_half = core.astype(jnp.int32).reshape(1)
    send_half = 1 - keep_half

    h1, stats = first_product(x, conv_in, valid, micro)
    members, counts = first_parts(stats)
    act_one, h2, stats, info_one = second_product(
        members, h1, valid, row(gain_one), row(shift_one), conv_mid, micro
    )
    parts = moment_parts(stats, counts)
    act_two, h3, stats, info_two = third_product(
        parts, members, h2, valid, row(gain_two), row(shift_two), conv_out, micro
    )
    parts = moment_parts(stats, counts)
    feat, info_three = pool(
        parts, members, h3, x, valid, row(gain_three), row(shift_three), sizes, micro
    )

    lines = feat.shape[0]
    if quick:
        by_bit = feat.reshape(lines, shards // 2, 2, -1)
        bit = bit_of(near)
        feat_keep = at(by_bit, bit, 2).reshape(lines, -1)
        feat_send = at(by_bit, 1 - bit, 2).reshape(lines, -1)
        feat_near = swap(feat_send, near)
    g, stats = head_product(feat, head_weight, micro)
    if quick:
        stats, feat_near = tie(stats, feat_near)

    crop_counts = []
    crop_members = []
    number = crops * 1.0
    for group in sync_groups():
        crop_members = [number] * (len(group) + 1)
        crop_counts.append(crop_members)
        number = number * (len(group) + 1)
    slopes = []

    def slope_filler(index):
        def fill(gate):
            source = tie(h3, gate)[0]
            slopes[:] = slope_part(
                source, x, valid, info_three, row(gain_three), row(shift_three), micro, index, slopes
            )
            return slopes

        return fill

    parts = moment_parts(stats, crop_counts, ((), (slope_filler(0),), (slope_filler(1),)))

    act_four, embedded, inverse, unit_rows, logits, batch, queue, column, info_four = embed_product(
        parts,
        crop_members,
        protos,
        g,
        row(head_gain),
        row(head_shift),
        embed_weight,
        row(embed_bias),
        table,
        queue_rows,
    )
    fillers = ((), (slope_filler(2),), (slope_filler(3),))
    for _ in range(SINK_ITERS - 1):
        parts = sum_parts(column, fillers)
        fillers = ()
        batch, queue, column = sweep(parts, protos, batch, queue, queue_rows.shape[0])
    parts = sum_parts(column, fillers)
    slope, slope_first, slope_second = slopes
    packed, dy_four, payload = loss_grads(
        parts,
        protos,
        loss_scale,
        batch,
        logits,
        unit_rows,
        embedded,
        inverse,
        act_four,
        g,
        info_four,
        row(head_gain),
        row(head_shift),
        embed_weight,
        table,
        packs,
    )
    if quick:
        small_recv = swap(at(packed, 1 - core, 0), 1)
    parts = sum_parts(payload)
    if quick:
        *parts, small_recv = tie(*parts, small_recv)
        small = [at(packed, core, 0), small_recv]
    payload = tree(list(parts))
    first_four, second_four = payload[:micro], payload[micro : 2 * micro]
    grad_bias = payload[2 * micro, : embed_bias.shape[0]]
    total_loss = payload[2 * micro, embed_bias.shape[0]]

    if quick:
        feat_keep, feat_near, *parts = tie(feat_keep, feat_near, *parts)
        feat_near = jnp.concatenate([feat_keep, feat_near], 0)
        feat_far = swap(feat_near, 2)
    dg, wide, sums = head_back(
        parts,
        dy_four,
        g,
        info_four,
        row(head_gain),
        head_weight,
        sizes,
        slope_first,
        slope_second,
        total_crops,
    )
    first_norm = (h1, valid, info_one, info_one, row(gain_one))
    second_norm = (h2, valid, info_two, info_one, row(gain_two))

    def from_third(parts):
        return third_back(
            parts,
            wide,
            slope,
            h3,
            valid,
            info_three,
            row(gain_three),
            info_one,
            conv_out,
            h2,
            info_two,
            row(gain_two),
            row(shift_two),
            micro,
        )

    def from_second(d):
        return second_back(
            d, conv_mid, valid, h1, info_one, row(gain_one), row(shift_one), micro
        )

    if quick:
        sums, dg, feat_far = tie(sums, dg, feat_far)
        feat_both = jnp.concatenate([feat_near, feat_far], 0)
        feat_other = swap(feat_both, 1)
        split = dg.reshape(lines, 2, -1)
        dg_other = swap(at(split, 1 - core, 1), 1)
        parts_three = sum_parts(sums)
        *parts_three, dg_other, feat_other = tie(*parts_three, dg_other, feat_other)
        split = jnp.concatenate([at(split, core, 1), dg_other], 0).reshape(2 * lines, 2, -1)
        dg_here, dg_there = at(split, side, 1), at(split, 1 - side, 1)
        *parts_three, dg_here, dg_there = tie(*parts_three, dg_here, dg_there)
        dg_far, dg_near, dg_both = swap(dg_there, 2), swap(dg_here, near), swap(dg_there, 2 + near)
        d_three, dy, sums = from_third(parts_three)
        sums, dy, d_three, dg_far, dg_near, dg_both = tie(sums, dy, d_three, dg_far, dg_near, dg_both)
        grads = {}

        def out_filler(gate):
            source = tie(d_three, gate)[0]
            grads["out"] = out_grad(send_half, act_two, source, shards)
            return [grads["out"]]

        def head_filler(gate):
            grads["out_recv"] = swap(grads["out"][0], 1)
            source = tie(dg_near, gate)[0]
            grads["head"] = factor_grad(feat_both, feat_other, dg_here, dg_far, source, dg_both)
            return [grads["head"], grads["out_recv"]]

        parts_two = sum_parts(sums, ((), (out_filler,), (head_filler,)))

        small = [array.reshape(shards, -1, array.shape[-1]) for array in small]
        early = [[grads["out"][1], grads["out_recv"]], small]
        early_out = first_send(scalars, early)
        *parts_two, early_out, partial = tie(*parts_two, early_out, grads["head"])
        came = core_swap(early_out, near, 2)
        partial = partial.reshape(2, 2, -1, partial.shape[1])
        head = dp_halves([partial], far[0], 1)
        d_two, mid_send = mid_grad(
            "mid_first",
            mid_first_body,
            send_half,
            [*parts_two, dy, *second_norm, act_one],
            act_one,
            True,
        )
        d_two, mid_send, early_came, head[-1] = tie(d_two, mid_send, came, head[-1])
        mid_recv = swap(mid_send, 1)
        early_send, early_keep = second_send(scalars, early, early_came)
        early_came = core_swap(early_send, 2, near)
        mid_keep = mid_grad(
            "mid_second", mid_second_body, keep_half, [d_two, act_one], act_one, False
        )
        mid_keep, mid_recv, early_came = tie(mid_keep, mid_recv, early_came)

        def sharded(array):
            return array.reshape(shards, -1, array.shape[-1])

        def by_bits(array):
            return array.reshape((2, 2) + array.shape[1:])

        late = [[sharded(mid_keep), sharded(mid_recv)]]
        mid_came = core_swap(first_send(scalars, late), near, 2)
        early = dp_halves([by_bits(early_keep), by_bits(early_came)], far[0], 1)
        d_two = tie(d_two, mid_keep)[0]
        dy, sums = from_second(d_two)
        dy, sums, mid_came, early[-1] = tie(dy, sums, mid_came, early[-1])
        parts_one = sum_parts(sums)
        mid_out, mid_keep = second_send(scalars, late, mid_came)
        *parts_one, mid_out = tie(*parts_one, mid_out)
        mid_came = core_swap(mid_out, 2, near)
        head = dp_halves(head, far[1], 0)
        d_one, in_send, in_keep = in_grad(send_half, parts_one, dy, *first_norm, x)
        d_one, in_send, in_keep, mid_came, head[-1] = tie(d_one, in_send, in_keep, mid_came, head[-1])
        in_recv = swap(in_send, 1)
        mid = dp_halves([by_bits(mid_keep), by_bits(mid_came)], far[0], 1)
        early = dp_halves(early, far[1], 0)
        inner = [[sharded(in_keep), sharded(in_recv)]]
        in_out = first_send(scalars, inner)
        in_came = core_swap(in_out, near, 2)
        d_one = tie(d_one, in_out)[0]
        grad_x = pixels_grad(d_one, conv_in, wide, slope, micro)
        grad_x, in_came, mid[-1], early[-1] = tie(grad_x, in_came, mid[-1], early[-1])
        in_out, in_keep = second_send(scalars, inner, in_came)
        in_came = core_swap(in_out, 2, near)
        mid = dp_halves(mid, far[1], 0)
        early_pieces = gathered(jnp.concatenate([sum(early), sum(head)], 0))
        inner = dp_halves([by_bits(in_keep), by_bits(in_came)], far[0], 1)
        inner = dp_halves(inner, far[1], 0)
        late_pieces = gathered(jnp.concatenate([sum(mid), sum(inner)], 0))

        channel = channels // shards
        grad_conv_out, grad_embed, grad_protos, grad_head = placed_pieces(
            place_early_body,
            scalars,
            early_pieces,
            [
                shape((conv_out.shape[0] // shards, channels)),
                shape((embed_weight.shape[0] // shards, embed_weight.shape[1])),
                shape((table.shape[0] // shards, table.shape[1])),
                shape((channel, head_weight.shape[1])),
            ],
        )
        grad_protos = grad_protos[:, :protos]
        grad_conv_mid, grad_conv_in = placed_pieces(
            place_late_body,
            scalars,
            late_pieces,
            [
                shape((conv_mid.shape[0] // shards, conv_mid.shape[1])),
                shape((channel, conv_in.shape[1])),
            ],
        )
    else:
        low, high = jnp.zeros((1,), jnp.int32), jnp.ones((1,), jnp.int32)

        def reduced(array):
            return lax.psum(lax.psum_scatter(array, "dp", scatter_dimension=0, tiled=True), "hst")

        parts_three = sum_parts(sums)
        d_three, dy, sums = from_third(parts_three)
        parts_two = sum_parts(sums)
        ins = [*parts_two, dy, *second_norm, act_one]
        d_two, mid_low = mid_grad("mid_first", mid_first_body, low, ins, act_one, True)
        mid_high = mid_grad("mid_second", mid_second_body, high, [d_two, act_one], act_one, False)
        dy, sums = from_second(d_two)
        parts_one = sum_parts(sums)
        d_one, in_low, in_high = in_grad(low, parts_one, dy, *first_norm, x)
        grad_x = pixels_grad(d_one, conv_in, wide, slope, micro)
        out = out_grad(low, act_two, d_three, shards)
        out = out.reshape(2, shards, -1, conv_out.shape[0] // shards, out.shape[-1])
        small_protos, small_embed = unpack_small(packed, table.shape, embed_weight.shape)
        grad_conv_out = reduced(out.transpose(1, 3, 0, 2, 4).reshape(conv_out.shape))
        grad_conv_mid = reduced(jnp.concatenate([mid_low, mid_high], 1))
        grad_conv_in = reduced(jnp.concatenate([in_low, in_high], 1))
        grad_head = reduced(
            jnp.dot(feat.astype(BF16).T, dg.astype(BF16), preferred_element_type=F32)
        )
        grad_embed = reduced(small_embed)
        grad_protos = reduced(small_protos)[:, :protos]

    def own_rows(vectors):
        sums = [jnp.sum(vector, 0) for vector in vectors]
        piece = sums[0].shape[0] // shards
        stacked = jnp.stack(sums)
        found = lax.dynamic_slice_in_dim(stacked, lax.axis_index("dp") * piece, piece, 1)
        return [found[i] for i in range(len(vectors))]

    def both_sums(parts):
        total = tree(list(parts))
        return [total[:, 1], total[:, 0]]

    small_ones = own_rows(both_sums(parts_one) + both_sums(parts_two))
    large_ones = own_rows(both_sums(parts_three) + [second_four, first_four])

    return (
        total_loss,
        grad_x.reshape(pixels.shape),
        grad_conv_in,
        small_ones[0],
        small_ones[1],
        grad_conv_mid,
        small_ones[2],
        small_ones[3],
        grad_conv_out,
        large_ones[0],
        large_ones[1],
        grad_head,
        large_ones[2],
        large_ones[3],
        grad_embed,
        lax.dynamic_slice_in_dim(
            grad_bias,
            lax.axis_index("dp") * (grad_bias.shape[0] // shards),
            grad_bias.shape[0] // shards,
            0,
        ),
        grad_protos,
    )


def solution(mesh):
    placed = (
        P(None, ("dp", "hst"), None, None),
        P(None, ("dp", "hst"), None),
        P(("dp", "hst"), None),
    ) + (P(),) * 15
    return jax.shard_map(
        on_device,
        mesh=mesh,
        in_specs=placed,
        out_specs=(
            P(),
            P(None, ("dp", "hst"), None, None),
            P("dp", None),
            P("dp"),
            P("dp"),
            P("dp", None),
            P("dp"),
            P("dp"),
            P("dp", None),
            P("dp"),
            P("dp"),
            P("dp", None),
            P("dp"),
            P("dp"),
            P("dp", None),
            P("dp"),
            P("dp", None),
        ),
        check_vma=False,
    )
```

time: 662 us -> 574 us (0.87)
  waiting for transfers between devices: 234 us -> 144 us
  Pallas kernels: 192 us -> 252 us
  other arithmetic: 46.7 us -> 15.5 us
  starting transfers between devices: 134 us -> 113 us
    ppermute x131 -> x102, waiting for transfers between devices: 234 us -> 130 us  [swap(): return lax.ppermute(value, AXES, [(i, i ^ mask) for i in range(count)])]
    pallas_call x15 -> x27, Pallas kernels: 165 us -> 225 us  [the longest x2 28.1 us: mid_grad(): run(named(name, body, *([len(ins) - 7] if with_d else [])), (TAPS,), [who...]
    ppermute x131 -> x102, starting transfers between devices: 134 us -> 107 us  [swap(): return lax.ppermute(value, AXES, [(i, i ^ mask) for i in range(count)])]
    unnamed x143 -> x204, local copies, waits for them, and re-layouts: 2.8 us -> 16.9 us
    ppermute x0 -> x6, waiting for transfers between devices: none -> 14.1 us  [core_swap(): return lax.ppermute(value, AXES, pairs)]
    another operation x14 -> x1, local copies, waits for them, and re-layouts: 7.81 us -> 0.01 us  [first_parts(): moments = jnp.stack(merge(parts, members), 1)]
    concatenate x18 -> x3, other arithmetic: 7.14 us -> 0.12 us  [the longest x1 0.05 us: on_device(): early_pieces = gathered(jnp.concatenate([sum(early), sum(head)], 0))]
    add x43 -> x11, other arithmetic: 10.6 us -> 3.97 us  [the longest x7 2.46 us: dp_halves(): send = sum((at(array, 1 - bit, axis) for array in addends))]
  transfers between devices with their start and end apart: 131 -> 108, of which waited for: 80 -> 59; matrix products, arithmetic and copies ran while one was open for 7% -> 2% of each run, Pallas kernels for 17% -> 26%
where the time goes in v2:
time: 574 us; the launch traced here: 564 us
  Pallas kernels  252 us (44%)
  waiting for transfers between devices  144 us (25%)
  starting transfers between devices  113 us (20%)
  local copies, waits for them, and re-layouts  36.8 us (6%)
  other arithmetic  15.5 us (3%)
    ppermute x102, waiting for transfers between devices, swap(): return lax.ppermute(value, AXES, [(i, i ^ mask) for i in range(count)])  130 us
    ppermute x102, starting transfers between devices, swap(): return lax.ppermute(value, AXES, [(i, i ^ mask) for i in range(count)])  107 us
    pallas_call x2, Pallas kernels, mid_grad(): run(named(name, body, *([len(ins) - 7] if with_d else [])), (TAPS,), [who...  28.1 us
    pallas_call x4, Pallas kernels, slope_part(): run(slope_body, (channels // width,), [tile, tile, pl.BlockSpec((rows, 1)...  24.3 us
    pallas_call x3, Pallas kernels, first_send(): run(named('first_send', body), (shards,), specs, pl.BlockSpec((1, lines,...  20.2 us
    pallas_call x1, Pallas kernels, third_back(): run(named('third_back', third_back_body, len(parts)), (micro,), [per_micr...  17.3 us
    pallas_call x1, Pallas kernels, second_back(): run(second_back_body, (micro,), [mid, whole(weight), pl.BlockSpec((rows,...  17.2 us
    unnamed x204, local copies, waits for them, and re-layouts  16.9 us
  transfers between devices with their start and end apart: 108, of which 59 were waited for; matrix products, arithmetic and copies ran while one was open for 2% of the time, Pallas kernels for 26%

profile of v2, /device:TPU:0, one launch (start us, length us, event | category | flops | bytes accessed | tf_op | source)
XLA Modules:
  0.0 564.0 jit_solution(2896727456367926572)
XLA Ops:
  2.8 9.3 %first_body.1 = (f32[2048,512]{1,0:T(8,128)}, f32[4,3,512]{2,1,0:T(4,128)}) custom-call(bf16[2048,2048]{1,0:T(8,128)(2,1)} %bitcast.157, bf16[2048,512]{1,0:T(8,128)(2,1)} %w_ref.7, f32[2048,1]{1,0:T(8,128)} %copy.139.v_ref.refs_5_.refs_9_.refs_10_.refs_2_.refs_7_), custom_call_target="tpu_custom_call" | custom-call | flops 4294967296 | bytes 8388608 | tf_op jit(solution)/shard_map/first_body/pallas_call | solution.py:246
  34.4 16.6 %second_product.1 = (bf16[2048,512]{1,0:T(8,128)(2,1)}, f32[2048,512]{1,0:T(8,128)}, f32[4,2,512]{2,1,0:T(2,128)}, f32[4,3,512]{2,1,0:T(4,128)}) custom-call(f32[4,3,512]{2,1,0:T(4,128)} %copy-done.58, f32[4,3,512]{2,1,0:T(4,128)} %copy-done.84, f32[4,3,512]{2,1,0:T(4,128)} %copy-done.85, f32[4,3,512]{2,1,0:T(4,128)} %copy-done.86, ...), custom_call_target="tpu_custom_call" | custom-call | flops 9663676416 | bytes 10485760 | tf_op jit(solution)/shard_map/second_product/pallas_call | solution.py:318
  66.5 12.1 %third_product.1 = (bf16[2048,512]{1,0:T(8,128)(2,1)}, bf16[2048,2048]{1,0:T(8,128)(2,1)}, f32[4,2,2048]{2,1,0:T(2,128)}, f32[4,2,512]{2,1,0:T(2,128)}) custom-call(f32[4,2,512]{2,1,0:T(2,128)} %copy-done.94, f32[4,2,512]{2,1,0:T(2,128)} %copy-done.95, f32[4,2,512]{2,1,0:T(2,128)} %copy-done.96, f32[4,2,512]{2,1,0:T(2,128)} %copy-done.97, ...), custom_call_target="tpu_custom_call" | custom-call | flops 4294967296 | bytes 16777216 | tf_op jit(solution)/shard_map/third_product/pallas_call | solution.py:369
  99.8 14.3 %pool.1 = (f32[64,2048]{1,0:T(8,128)}, f32[4,2,2048]{2,1,0:T(2,128)}) custom-call(f32[4,2,2048]{2,1,0:T(2,128)} %copy-done.46, f32[4,2,2048]{2,1,0:T(2,128)} %copy-done.60, f32[4,2,2048]{2,1,0:T(2,128)} %copy-done.61, f32[4,2,2048]{2,1,0:T(2,128)} %copy-done.62, f32[4,3,512]{2,1,0:T(4,128)} %copy-done.58, f32[4,3,512]{2,1,0:T(4,128)} %copy-done.84, ...), custom_call_target="tpu_custom_call" | custom-call | flops 83886080 | bytes 16777216 | tf_op jit(solution)/shard_map/pool/pallas_call | solution.py:440
  117.8 6.3 %head_body.1 = (f32[64,2048]{1,0:T(8,128)}, f32[4,2,2048]{2,1,0:T(2,128)}) custom-call(f32[64,2048]{1,0:T(8,128)} %get-tuple-element.188.feat_ref, bf16[2048,2048]{1,0:T(8,128)(2,1)} %refs_8_.3), custom_call_target="tpu_custom_call" | custom-call | flops 536870912 | bytes 8388608 | tf_op jit(solution)/shard_map/head_body/pallas_call | solution.py:538
  130.3 6.1 %slope_body.4 = (bf16[2048,2048]{1,0:T(8,128)(2,1)}, f32[64,2048]{1,0:T(8,128)}, f32[64,2048]{1,0:T(8,128)}) custom-call(bf16[2048,2048]{1,0:T(8,128)(2,1)} %get-tuple-element.218.refs_8_.refs_0_.refs_6_, bf16[2048,2048]{1,0:T(8,128)(2,1)} %bitcast.159, f32[2048,1]{1,0:T(8,128)} %copy.139.v_ref.refs_5_.refs_9_.refs_10_.refs_2_.refs_7_, ...), custom_call_target="tpu_custom_call" | custom-call | flops 31457280 | bytes 6291456 | tf_op jit(solution)/shard_map/slope_body/pallas_call | solution.py:497
  142.5 6.0 %slope_body.5 = (bf16[2048,2048]{1,0:T(8,128)(2,1)}, f32[64,2048]{1,0:T(8,128)}, f32[64,2048]{1,0:T(8,128)}) custom-call(bf16[2048,2048]{1,0:T(8,128)(2,1)} %get-tuple-element.218.refs_8_.refs_0_.refs_6_, bf16[2048,2048]{1,0:T(8,128)(2,1)} %bitcast.160, ...), custom_call_target="tpu_custom_call", output_to_operand_aliasing={{0}: (6, {}), {1}: (7, {}), {2}: (8, {})} | custom-call | flops 31457280 | bytes 6291456 | tf_op jit(solution)/shard_map/slope_body/pallas_call | solution.py:497
  158.5 6.0 %slope_body.6 = (bf16[2048,2048]{1,0:T(8,128)(2,1)}, f32[64,2048]{1,0:T(8,128)}, f32[64,2048]{1,0:T(8,128)}) custom-call(bf16[2048,2048]{1,0:T(8,128)(2,1)} %get-tuple-element.218.refs_8_.refs_0_.refs_6_, bf16[2048,2048]{1,0:T(8,128)(2,1)} %bitcast.161, ...), custom_call_target="tpu_custom_call", output_to_operand_aliasing={{0}: (6, {}), {1}: (7, {}), {2}: (8, {})} | custom-call | flops 31457280 | bytes 6291456 | tf_op jit(solution)/shard_map/slope_body/pallas_call | solution.py:497
  169.1 6.2 %slope_body.7 = (bf16[2048,2048]{1,0:T(8,128)(2,1)}, f32[64,2048]{1,0:T(8,128)}, f32[64,2048]{1,0:T(8,128)}) custom-call(bf16[2048,2048]{1,0:T(8,128)(2,1)} %get-tuple-element.218.refs_8_.refs_0_.refs_6_, bf16[2048,2048]{1,0:T(8,128)(2,1)} %bitcast.162, ...), custom_call_target="tpu_custom_call", output_to_operand_aliasing={{0}: (6, {}), {1}: (7, {}), {2}: (8, {})} | custom-call | flops 31457280 | bytes 6291456 | tf_op jit(solution)/shard_map/slope_body/pallas_call | solution.py:497
  217.9 6.5 %loss.1 = (f32[2,8,2,40,512]{4,3,2,1,0:T(8,128)}, f32[64,2048]{1,0:T(8,128)}, f32[9,2048]{1,0:T(8,128)}) custom-call(f32[4,3072]{1,0:T(4,128)} %copy-done.53, f32[4,3072]{1,0:T(4,128)} %copy-done.75, f32[4,3072]{1,0:T(4,128)} %copy-done.76, f32[4,3072]{1,0:T(4,128)} %copy-done.77, f32[64,3072]{1,0:T(8,128)} %get-tuple-element.232.refs_4_, ...), custom_call_target="tpu_custom_call" | custom-call | flops 201326592 | bytes 3145728 | tf_op jit(solution)/shard_map/loss/pallas_call | solution.py:1188
  248.2 5.7 %collective-permute-done.55.refs_2_ = f32[9,2048]{1,0:T(8,128)S(1)} collective-permute-done((f32[9,2048]{1,0:T(8,128)S(1)}, f32[9,2048]{1,0:T(8,128)S(1)}, u32[]{:S(2)}, u32[]{:S(2)}) %collective-permute-start.55) | collective-permute-done | bytes 73760 | tf_op jit(solution)/shard_map/ppermute | solution.py:31
  254.8 9.4 %head_back.1 = (f32[64,2048]{1,0:T(8,128)}, f32[256,2048]{1,0:T(8,128)}, f32[4,2,2048]{2,1,0:T(2,128)}) custom-call(f32[9,2048]{1,0:T(8,128)} %copy-done.10, f32[9,2048]{1,0:T(8,128)} %copy-done.27, f32[9,2048]{1,0:T(8,128)} %copy-done.29, f32[9,2048]{1,0:T(8,128)} %copy-done.30, f32[64,2048]{1,0:T(8,128)} %get-tuple-element.250.refs_4_, ...), custom_call_target="tpu_custom_call" | custom-call | flops 536870912 | bytes 8388608 | tf_op jit(solution)/shard_map/head_back/pallas_call | solution.py:595
  280.7 5.2 collective-permute-done.64.refs_2_
  291.4 17.3 %third_back.1 = (bf16[2048,2048]{1,0:T(8,128)(2,1)}, f32[2048,512]{1,0:T(8,128)}, f32[4,2,512]{2,1,0:T(2,128)}) custom-call(f32[4,2,2048]{2,1,0:T(2,128)} %bitcast.205, f32[4,2,2048]{2,1,0:T(2,128)} %copy-done.40, f32[4,2,2048]{2,1,0:T(2,128)} %copy-done.42, f32[4,2,2048]{2,1,0:T(2,128)} %copy-done.44, f32[256,2048]{1,0:T(8,128)} %get-tuple-element.267.refs_4_.wide_ref, ...), custom_call_target="tpu_custom_call" | custom-call | flops 4294967296 | bytes 25165824 | tf_op jit(solution)/shard_map/third_back/pallas_call | solution.py:667
  311.0 9.8 %out_grad_body.1 = f32[2,8,128,512]{3,2,1,0:T(8,128)} custom-call(s32[1]{0:T(128)S(6)} %sub.185.which_ref.refs_0_, bf16[2048,512]{1,0:T(8,128)(2,1)} %get-tuple-element.276.left_ref, bf16[2048,2048]{1,0:T(8,128)(2,1)} %get-tuple-element.278.right_ref), custom_call_target="tpu_custom_call" | custom-call | flops 4294967296 | bytes 14680064 | tf_op jit(solution)/shard_map/out_grad_body/pallas_call | solution.py:711
  341.5 6.8 %first_send.3 = f32[8,104,512]{2,1,0:T(8,128)} custom-call(s32[3]{0:T(128)} %pad_add_fusion.refs_0_.scalars_ref, f32[8,128,512]{2,1,0:T(8,128)} %get-tuple-element.381.refs_1_.refs_5_, f32[8,128,512]{2,1,0:T(8,128)} %copy-done.1, f32[8,80,512]{2,1,0:T(8,128)} %bitcast.170, f32[8,80,512]{2,1,0:T(8,128)} %bitcast.179), custom_call_target="tpu_custom_call" | custom-call | bytes 5111808 | tf_op jit(solution)/shard_map/first_send/pallas_call | solution.py:1242
  350.0 15.8 %mid_first.1 = (bf16[2048,512]{1,0:T(8,128)(2,1)}, f32[4608,256]{1,0:T(8,128)}) custom-call(s32[1]{0:T(128)S(6)} %sub.185.which_ref.refs_0_, f32[4,2,512]{2,1,0:T(2,128)} %bitcast.242, f32[4,2,512]{2,1,0:T(2,128)} %copy-done.88, f32[4,2,512]{2,1,0:T(2,128)} %copy-done.90, f32[4,2,512]{2,1,0:T(2,128)} %copy-done.92, f32[2048,512]{1,0:T(8,128)} %get-tuple-element.297.refs_5_, ...), custom_call_target="tpu_custom_call" | custom-call | flops 4831838208 | bytes 4718592 | tf_op jit(solution)/shard_map/mid_first/pallas_call | solution.py:804
  365.8 6.4 %collective-permute-done.80 = f32[2,256,512]{2,1,0:T(8,128)S(1)} collective-permute-done((f32[2,256,512]{2,1,0:T(8,128)S(1)}, f32[2,256,512]{2,1,0:T(8,128)S(1)}, u32[]{:S(2)}, u32[]{:S(2)}) %collective-permute-start.80) | collective-permute-done | bytes 1048608 | tf_op jit(solution)/shard_map/ppermute | solution.py:31
  373.2 5.1 second_send.3
  379.0 12.3 %mid_second.1 = f32[4608,256]{1,0:T(8,128)} custom-call(s32[1]{0:T(128)} %bitcast.17.refs_0_, bf16[2048,512]{1,0:T(8,128)(2,1)} %get-tuple-element.308.refs_1_.d_ref, bf16[2048,512]{1,0:T(8,128)(2,1)} %get-tuple-element.298.refs_11_.refs_2_), custom_call_target="tpu_custom_call" | custom-call | flops 4831838208 | bytes 4718592 | tf_op jit(solution)/shard_map/mid_second/pallas_call | solution.py:804
  393.8 7.1 %first_send.4 = f32[8,288,256]{2,1,0:T(8,128)} custom-call(s32[3]{0:T(128)} %pad_add_fusion.refs_0_.scalars_ref, f32[8,576,256]{2,1,0:T(8,128)} %bitcast.167, f32[8,576,256]{2,1,0:T(8,128)} %bitcast.164), custom_call_target="tpu_custom_call" | custom-call | bytes 7077888 | tf_op jit(solution)/shard_map/first_send/pallas_call | solution.py:1242
  403.7 17.2 %second_back_body.1 = (f32[2048,512]{1,0:T(8,128)}, f32[4,2,512]{2,1,0:T(2,128)}) custom-call(bf16[2048,512]{1,0:T(8,128)(2,1)} %get-tuple-element.308.refs_1_.d_ref, bf16[4608,512]{1,0:T(8,128)(2,1)} %w_ref.6, f32[2048,1]{1,0:T(8,128)} %copy.139.v_ref.refs_5_.refs_9_.refs_10_.refs_2_.refs_7_, f32[2048,512]{1,0:T(8,128)} %get-tuple-element.183.refs_4_.h1_ref.refs_6_, ...), custom_call_target="tpu_custom_call" | custom-call | flops 9663676416 | bytes 10485760 | tf_op jit(solution)/shard_map/second_back_body/pallas_call | solution.py:891
  421.0 8.9 %collective-permute-done.83.refs_5_.refs_6_ = f32[8,288,256]{2,1,0:T(8,128)S(1)} collective-permute-done((f32[8,288,256]{2,1,0:T(8,128)}, f32[8,288,256]{2,1,0:T(8,128)S(1)}, u32[]{:S(2)}, u32[]{:S(2)}) %collective-permute-start.83) | collective-permute-done | bytes 2359328 | tf_op jit(solution)/shard_map/ppermute | solution.py:125
  443.1 5.6 second_send.4
  450.7 13.9 %in_grad.1 = (bf16[2048,512]{1,0:T(8,128)(2,1)}, f32[2048,256]{1,0:T(8,128)}, f32[2048,256]{1,0:T(8,128)}) custom-call(s32[1]{0:T(128)S(6)} %sub.185.which_ref.refs_0_, f32[4,2,512]{2,1,0:T(2,128)} %bitcast.232, f32[4,2,512]{2,1,0:T(2,128)} %copy-done.69, f32[4,2,512]{2,1,0:T(2,128)} %copy-done.71, f32[4,2,512]{2,1,0:T(2,128)} %copy-done.73, ...), custom_call_target="tpu_custom_call" | custom-call | flops 4294967296 | bytes 23068672 | tf_op jit(solution)/shard_map/in_grad/pallas_call | solution.py:846
  464.6 8.6 %collective-permute-done.93 = f32[256,512]{1,0:T(8,128)S(1)} collective-permute-done((f32[256,512]{1,0:T(8,128)S(1)}, f32[256,512]{1,0:T(8,128)S(1)}, u32[]{:S(2)}, u32[]{:S(2)}) %collective-permute-start.93) | collective-permute-done | bytes 524320 | tf_op jit(solution)/shard_map/ppermute | solution.py:31
  479.7 6.3 %first_send.5 = f32[8,128,256]{2,1,0:T(8,128)} custom-call(s32[3]{0:T(128)} %pad_add_fusion.refs_0_.scalars_ref, f32[8,256,256]{2,1,0:T(8,128)} %bitcast.173, f32[8,256,256]{2,1,0:T(8,128)} %bitcast.176), custom_call_target="tpu_custom_call" | custom-call | bytes 3145728 | tf_op jit(solution)/shard_map/first_send/pallas_call | solution.py:1242
  490.5 11.5 %pixels_body.1 = bf16[2048,2048]{1,0:T(8,128)(2,1)} custom-call(bf16[2048,512]{1,0:T(8,128)(2,1)} %get-tuple-element.330.d_ref, bf16[2048,512]{1,0:T(8,128)(2,1)} %w_ref.7, f32[256,2048]{1,0:T(8,128)} %get-tuple-element.267.refs_4_.wide_ref, bf16[2048,2048]{1,0:T(8,128)(2,1)} %get-tuple-element.219.refs_5_.slope_ref), custom_call_target="tpu_custom_call" | custom-call | flops 4294967296 | bytes 16777216 | tf_op jit(solution)/shard_map/pixels_body/pallas_call | solution.py:931
  517.0 5.1 collective-permute-done.99
  524.5 9.9 %collective-permute-done.100 = f32[2,128,256]{2,1,0:T(8,128)S(1)} collective-permute-done((f32[2,128,256]{2,1,0:T(8,128)S(1)}, f32[2,128,256]{2,1,0:T(8,128)S(1)}, u32[]{:S(2)}, u32[]{:S(2)}) %collective-permute-start.100) | collective-permute-done | bytes 262176 | tf_op jit(solution)/shard_map/ppermute | solution.py:31
  534.9 6.5 %collective-permute-done.101 = f32[128,256]{1,0:T(8,128)S(1)} collective-permute-done((f32[128,256]{1,0:T(8,128)S(1)}, f32[128,256]{1,0:T(8,128)S(1)}, u32[]{:S(2)}, u32[]{:S(2)}) %collective-permute-start.101) | collective-permute-done | bytes 131104 | tf_op jit(solution)/shard_map/ppermute | solution.py:31
  543.1 9.0 %collective-permute-done.102.far_ref = f32[416,256]{1,0:T(8,128)S(1)} collective-permute-done((f32[416,256]{1,0:T(8,128)S(1)}, f32[416,256]{1,0:T(8,128)S(1)}, u32[]{:S(2)}, u32[]{:S(2)}) %collective-permute-start.102) | collective-permute-done | bytes 426016 | tf_op jit(solution)/shard_map/ppermute | solution.py:31
  (504 shorter events, 268.8 us)
Async XLA Ops:
  136.8 11.7 %collective-permute-start.26 = (f32[4,2,2048]{2,1,0:T(2,128)S(1)}, f32[4,2,2048]{2,1,0:T(2,128)S(1)}, u32[]{:S(2)}, u32[]{:S(2)}) collective-permute-start(f32[4,2,2048]{2,1,0:T(2,128)S(1)} %pad_maximum_fusion.6.refs_0_), channel_id=1, source_target_pairs={{0,8},{1,9},{2,10},{3,11},{4,12},{5,13},{6,14},{7,15},{8,0},{9,1},... | collective-permute-start | bytes 196616 | tf_op jit(solution)/shard_map/ppermute | solution.py:31
  136.8 11.6 %collective-permute-start.27 = (f32[4,2,2048]{2,1,0:T(2,128)S(1)}, f32[4,2,2048]{2,1,0:T(2,128)S(1)}, u32[]{:S(2)}, u32[]{:S(2)}) collective-permute-start(f32[4,2,2048]{2,1,0:T(2,128)S(1)} %pad_maximum_fusion.6.refs_0_), channel_id=1, source_target_pairs={{0,16},{1,17},{2,18},{3,19},{4,20},{5,21},{6,22},{7,23},{8,24},{9,... | collective-permute-start | bytes 196616 | tf_op jit(solution)/shard_map/ppermute | solution.py:31
  164.6 10.7 %collective-permute-start.33 = (f32[4,3072]{1,0:T(4,128)S(1)}, f32[4,3072]{1,0:T(4,128)S(1)}, u32[]{:S(2)}, u32[]{:S(2)}) collective-permute-start(f32[4,3072]{1,0:T(4,128)S(1)} %add_add_fusion.6.refs_0_), channel_id=1, source_target_pairs={{0,8},{1,9},{2,10},{3,11},{4,12},{5,13},{6,14},{7,15},{8,0},{9,1},... | collective-permute-start | bytes 147464 | tf_op jit(solution)/shard_map/ppermute | solution.py:31
  164.7 10.6 %collective-permute-start.34 = (f32[4,3072]{1,0:T(4,128)S(1)}, f32[4,3072]{1,0:T(4,128)S(1)}, u32[]{:S(2)}, u32[]{:S(2)}) collective-permute-start(f32[4,3072]{1,0:T(4,128)S(1)} %add_add_fusion.6.refs_0_), channel_id=1, source_target_pairs={{0,16},{1,17},{2,18},{3,19},{4,20},{5,21},{6,22},{7,23},{8,24},{9,... | collective-permute-start | bytes 147464 | tf_op jit(solution)/shard_map/ppermute | solution.py:31
  227.5 26.5 %collective-permute-start.57 = (f32[8,2,40,512]{3,2,1,0:T(8,128)S(1)}, f32[8,2,40,512]{3,2,1,0:T(8,128)S(1)}, u32[]{:S(2)}, u32[]{:S(2)}) collective-permute-start(f32[8,2,40,512]{3,2,1,0:T(8,128)S(1)} %get-tuple-element.384), channel_id=1, source_target_pairs={{0,1},{1,0},{2,3},{3,2},{4,5},{5,4},{6,7},{7,6},{8,9},{9,8},{10,11... | collective-permute-start | bytes 3932168 | tf_op jit(solution)/shard_map/ppermute | solution.py:31
  241.4 12.5 %collective-permute-start.55 = (f32[9,2048]{1,0:T(8,128)S(1)}, f32[9,2048]{1,0:T(8,128)S(1)}, u32[]{:S(2)}, u32[]{:S(2)}) collective-permute-start(f32[9,2048]{1,0:T(8,128)S(1)} %add_add_fusion.1.refs_0_), channel_id=1, source_target_pairs={{0,16},{1,17},{2,18},{3,19},{4,20},{5,21},{6,22},{7,23},{8,24},{9,... | collective-permute-start | bytes 221192 | tf_op jit(solution)/shard_map/ppermute | solution.py:31
  242.9 11.0 %collective-permute-start.56 = (f32[9,2048]{1,0:T(8,128)S(1)}, f32[9,2048]{1,0:T(8,128)S(1)}, u32[]{:S(2)}, u32[]{:S(2)}) collective-permute-start(f32[9,2048]{1,0:T(8,128)S(1)} %add_add_fusion.1.refs_0_), channel_id=1, source_target_pairs={{0,24},{1,25},{2,26},{3,27},{4,28},{5,29},{6,30},{7,31},{8,16},{9,... | collective-permute-start | bytes 221192 | tf_op jit(solution)/shard_map/ppermute | solution.py:31
  254.0 11.2 %collective-permute-start.58 = (f32[128,1024]{1,0:T(8,128)S(1)}, f32[128,1024]{1,0:T(8,128)S(1)}, u32[]{:S(2)}, u32[]{:S(2)}) collective-permute-start(f32[128,1024]{1,0:T(8,128)S(1)} %pad_maximum_fusion.1), channel_id=1, source_target_pairs={{0,2},{1,3},{2,0},{3,1},{4,6},{5,7},{6,4},{7,5},{8,10},{9,11},{10,... | collective-permute-start | bytes 1572872 | tf_op jit(solution)/shard_map/ppermute | solution.py:31
  265.2 20.7 %collective-permute-start.67 = (f32[256,1024]{1,0:T(8,128)S(1)}, f32[256,1024]{1,0:T(8,128)S(1)}, u32[]{:S(2)}, u32[]{:S(2)}) collective-permute-start(f32[256,1024]{1,0:T(8,128)S(1)} %constant_dynamic-update-slice_fusion.feat_ref), channel_id=1, source_target_pairs={{0,1},{1,0},{2,3},{3,2},{4,5},{5,4},{6,7},{7,6},{8,9},{9,8},{10,11... | collective-permute-start | bytes 3145736 | tf_op jit(solution)/shard_map/ppermute | solution.py:31
  273.4 12.6 %collective-permute-start.66 = (f32[64,1024]{1,0:T(8,128)}, f32[64,1024]{1,0:T(8,128)}, u32[]{:S(2)}, u32[]{:S(2)}) collective-permute-start(f32[64,1024]{1,0:T(8,128)} %bitcast.125), channel_id=1, source_target_pairs={{0,1},{1,0},{2,3},{3,2},{4,5},{5,4},{6,7},{7,6},{8,9},{9,8},{10,11... | collective-permute-start | bytes 786440 | tf_op jit(solution)/shard_map/ppermute | solution.py:31
  287.9 20.9 %collective-permute-start.68 = (f32[128,512]{1,0:T(8,128)S(1)}, f32[128,512]{1,0:T(8,128)S(1)}, u32[]{:S(2)}, u32[]{:S(2)}) collective-permute-start(f32[128,512]{1,0:T(8,128)S(1)} %get-tuple-element.273), channel_id=1, source_target_pairs={{0,2},{1,3},{2,0},{3,1},{4,6},{5,7},{6,4},{7,5},{8,10},{9,11},{10,... | collective-permute-start | bytes 786440 | tf_op jit(solution)/shard_map/ppermute | solution.py:31
  289.5 19.3 %collective-permute-start.70 = (f32[128,512]{1,0:T(8,128)S(1)}, f32[128,512]{1,0:T(8,128)S(1)}, u32[]{:S(2)}, u32[]{:S(2)}) collective-permute-start(f32[128,512]{1,0:T(8,128)S(1)} %get-tuple-element.273), channel_id=1, source_target_pairs={{0,6},{1,7},{2,4},{3,5},{4,2},{5,3},{6,0},{7,1},{8,14},{9,15},{10,... | collective-permute-start | bytes 786440 | tf_op jit(solution)/shard_map/ppermute | solution.py:31
  290.9 17.9 %collective-permute-start.69 = (f32[128,512]{1,0:T(8,128)S(1)}, f32[128,512]{1,0:T(8,128)S(1)}, u32[]{:S(2)}, u32[]{:S(2)}) collective-permute-start(f32[128,512]{1,0:T(8,128)S(1)} %get-tuple-element.274.dg_ref), channel_id=1, source_target_pairs={{0,4},{1,5},{2,6},{3,7},{4,0},{5,1},{6,2},{7,3},{8,12},{9,13},{10,... | collective-permute-start | bytes 786440 | tf_op jit(solution)/shard_map/ppermute | solution.py:31
  325.0 15.1 %collective-permute-start.78 = (f32[8,128,512]{2,1,0:T(8,128)S(1)}, f32[8,128,512]{2,1,0:T(8,128)S(1)}, u32[]{:S(2)}, u32[]{:S(2)}) collective-permute-start(f32[8,128,512]{2,1,0:T(8,128)S(1)} %get-tuple-element.382), channel_id=1, source_target_pairs={{0,1},{1,0},{2,3},{3,2},{4,5},{5,4},{6,7},{7,6},{8,9},{9,8},{10,11... | collective-permute-start | bytes 6291464 | tf_op jit(solution)/shard_map/ppermute | solution.py:31
  348.3 23.9 %collective-permute-start.79 = (f32[8,104,512]{2,1,0:T(8,128)}, f32[8,104,512]{2,1,0:T(8,128)}, u32[]{:S(2)}, u32[]{:S(2)}) collective-permute-start(f32[8,104,512]{2,1,0:T(8,128)} %first_send.3), channel_id=1, source_target_pairs={{0,4},{1,3},{2,6},{3,1},{4,0},{5,7},{6,2},{7,5},{8,12},{9,11},{10,... | collective-permute-start | bytes 5111816 | tf_op jit(solution)/shard_map/ppermute | solution.py:125
  349.6 22.6 %collective-permute-start.80 = (f32[2,256,512]{2,1,0:T(8,128)S(1)}, f32[2,256,512]{2,1,0:T(8,128)S(1)}, u32[]{:S(2)}, u32[]{:S(2)}) collective-permute-start(f32[2,256,512]{2,1,0:T(8,128)S(1)} %dynamic-slice_bitcast_fusion.1), channel_id=1, source_target_pairs={{0,8},{1,9},{2,10},{3,11},{4,12},{5,13},{6,14},{7,15},{8,0},{9,1},... | collective-permute-start | bytes 3145736 | tf_op jit(solution)/shard_map/ppermute | solution.py:31
  373.2 18.2 %collective-permute-start.81 = (f32[4608,256]{1,0:T(8,128)}, f32[4608,256]{1,0:T(8,128)S(1)}, u32[]{:S(2)}, u32[]{:S(2)}) collective-permute-start(f32[4608,256]{1,0:T(8,128)} %get-tuple-element.304), channel_id=1, source_target_pairs={{0,1},{1,0},{2,3},{3,2},{4,5},{5,4},{6,7},{7,6},{8,9},{9,8},{10,11... | collective-permute-start | bytes 14155784 | tf_op jit(solution)/shard_map/ppermute | solution.py:31
  378.3 13.0 %collective-permute-start.82 = (f32[4,104,512]{2,1,0:T(8,128)}, f32[4,104,512]{2,1,0:T(8,128)S(1)}, u32[]{:S(2)}, u32[]{:S(2)}) collective-permute-start(f32[4,104,512]{2,1,0:T(8,128)} %get-tuple-element.306), channel_id=1, source_target_pairs={{0,2},{1,5},{2,0},{3,7},{4,6},{5,1},{6,4},{7,3},{8,10},{9,13},{10,... | collective-permute-start | bytes 2555912 | tf_op jit(solution)/shard_map/ppermute | solution.py:125
  400.9 29.1 %collective-permute-start.83 = (f32[8,288,256]{2,1,0:T(8,128)}, f32[8,288,256]{2,1,0:T(8,128)S(1)}, u32[]{:S(2)}, u32[]{:S(2)}) collective-permute-start(f32[8,288,256]{2,1,0:T(8,128)} %first_send.4), channel_id=1, source_target_pairs={{0,4},{1,3},{2,6},{3,1},{4,0},{5,7},{6,2},{7,5},{8,12},{9,11},{10,... | collective-permute-start | bytes 7077896 | tf_op jit(solution)/shard_map/ppermute | solution.py:125
  403.3 17.7 %collective-permute-start.84 = (f32[2,104,512]{2,1,0:T(8,128)S(1)}, f32[2,104,512]{2,1,0:T(8,128)S(1)}, u32[]{:S(2)}, u32[]{:S(2)}) collective-permute-start(f32[2,104,512]{2,1,0:T(8,128)S(1)} %add_bitcast_fusion.1), channel_id=1, source_target_pairs={{0,8},{1,9},{2,10},{3,11},{4,12},{5,13},{6,14},{7,15},{8,0},{9,1},... | collective-permute-start | bytes 1277960 | tf_op jit(solution)/shard_map/ppermute | solution.py:31
  448.8 24.5 %collective-permute-start.92 = (f32[4,288,256]{2,1,0:T(8,128)}, f32[4,288,256]{2,1,0:T(8,128)S(1)}, u32[]{:S(2)}, u32[]{:S(2)}) collective-permute-start(f32[4,288,256]{2,1,0:T(8,128)} %get-tuple-element.325), channel_id=1, source_target_pairs={{0,2},{1,5},{2,0},{3,7},{4,6},{5,1},{6,4},{7,3},{8,10},{9,13},{10,... | collective-permute-start | bytes 3538952 | tf_op jit(solution)/shard_map/ppermute | solution.py:125
  450.7 22.6 %collective-permute-start.93 = (f32[256,512]{1,0:T(8,128)S(1)}, f32[256,512]{1,0:T(8,128)S(1)}, u32[]{:S(2)}, u32[]{:S(2)}) collective-permute-start(f32[256,512]{1,0:T(8,128)S(1)} %bitcast_add_fusion.1), channel_id=1, source_target_pairs={{0,16},{1,17},{2,18},{3,19},{4,20},{5,21},{6,22},{7,23},{8,24},{9,... | collective-permute-start | bytes 1572872 | tf_op jit(solution)/shard_map/ppermute | solution.py:31
  486.1 21.1 %collective-permute-start.95 = (f32[8,128,256]{2,1,0:T(8,128)}, f32[8,128,256]{2,1,0:T(8,128)S(1)}, u32[]{:S(2)}, u32[]{:S(2)}) collective-permute-start(f32[8,128,256]{2,1,0:T(8,128)} %first_send.5), channel_id=1, source_target_pairs={{0,4},{1,3},{2,6},{3,1},{4,0},{5,7},{6,2},{7,5},{8,12},{9,11},{10,... | collective-permute-start | bytes 3145736 | tf_op jit(solution)/shard_map/ppermute | solution.py:125
  487.4 19.7 %collective-permute-start.96 = (f32[2,288,256]{2,1,0:T(8,128)S(1)}, f32[2,288,256]{2,1,0:T(8,128)S(1)}, u32[]{:S(2)}, u32[]{:S(2)}) collective-permute-start(f32[2,288,256]{2,1,0:T(8,128)S(1)} %add_bitcast_fusion), channel_id=1, source_target_pairs={{0,8},{1,9},{2,10},{3,11},{4,12},{5,13},{6,14},{7,15},{8,0},{9,1},... | collective-permute-start | bytes 1769480 | tf_op jit(solution)/shard_map/ppermute | solution.py:31
  487.7 17.3 %collective-permute-start.97 = (f32[104,512]{1,0:T(8,128)S(1)}, f32[104,512]{1,0:T(8,128)S(1)}, u32[]{:S(2)}, u32[]{:S(2)}) collective-permute-start(f32[104,512]{1,0:T(8,128)S(1)} %bitcast_add_fusion.5), channel_id=1, source_target_pairs={{0,16},{1,17},{2,18},{3,19},{4,20},{5,21},{6,22},{7,23},{8,24},{9,... | collective-permute-start | bytes 638984 | tf_op jit(solution)/shard_map/ppermute | solution.py:31
  515.7 19.1 %collective-permute-start.98 = (f32[288,256]{1,0:T(8,128)S(1)}, f32[288,256]{1,0:T(8,128)S(1)}, u32[]{:S(2)}, u32[]{:S(2)}) collective-permute-start(f32[288,256]{1,0:T(8,128)S(1)} %bitcast_add_fusion.2), channel_id=1, source_target_pairs={{0,16},{1,17},{2,18},{3,19},{4,20},{5,21},{6,22},{7,23},{8,24},{9,... | collective-permute-start | bytes 884744 | tf_op jit(solution)/shard_map/ppermute | solution.py:31
  522.2 12.1 %collective-permute-start.100 = (f32[2,128,256]{2,1,0:T(8,128)S(1)}, f32[2,128,256]{2,1,0:T(8,128)S(1)}, u32[]{:S(2)}, u32[]{:S(2)}) collective-permute-start(f32[2,128,256]{2,1,0:T(8,128)S(1)} %add_bitcast_fusion.2), channel_id=1, source_target_pairs={{0,8},{1,9},{2,10},{3,11},{4,12},{5,13},{6,14},{7,15},{8,0},{9,1},... | collective-permute-start | bytes 786440 | tf_op jit(solution)/shard_map/ppermute | solution.py:31
  523.6 18.8 %collective-permute-start.105 = (f32[360,512]{1,0:T(8,128)S(1)}, f32[360,512]{1,0:T(8,128)S(1)}, u32[]{:S(2)}, u32[]{:S(2)}) collective-permute-start(f32[360,512]{1,0:T(8,128)S(1)} %pad_maximum_fusion.mine_ref), channel_id=1, source_target_pairs={{0,2},{1,3},{2,0},{3,1},{4,6},{5,7},{6,4},{7,5},{8,10},{9,11},{10,... | collective-permute-start | bytes 2211848 | tf_op jit(solution)/shard_map/ppermute | solution.py:31
  541.5 10.6 %collective-permute-start.102 = (f32[416,256]{1,0:T(8,128)S(1)}, f32[416,256]{1,0:T(8,128)S(1)}, u32[]{:S(2)}, u32[]{:S(2)}) collective-permute-start(f32[416,256]{1,0:T(8,128)S(1)} %pad_maximum_fusion.2.mine_ref), channel_id=1, source_target_pairs={{0,2},{1,3},{2,0},{3,1},{4,6},{5,7},{6,4},{7,5},{8,10},{9,11},{10,... | collective-permute-start | bytes 1277960 | tf_op jit(solution)/shard_map/ppermute | solution.py:31
  542.3 10.4 %collective-permute-start.106 = (f32[360,512]{1,0:T(8,128)S(1)}, f32[360,512]{1,0:T(8,128)S(1)}, u32[]{:S(2)}, u32[]{:S(2)}) collective-permute-start(f32[360,512]{1,0:T(8,128)S(1)} %pad_maximum_fusion.mine_ref), channel_id=1, source_target_pairs={{0,1},{1,0},{2,3},{3,2},{4,5},{5,4},{6,7},{7,6},{8,9},{9,8},{10,11... | collective-permute-start | bytes 2211848 | tf_op jit(solution)/shard_map/ppermute | solution.py:31
  542.4 10.4 %collective-permute-start.107 = (f32[360,512]{1,0:T(8,128)S(1)}, f32[360,512]{1,0:T(8,128)S(1)}, u32[]{:S(2)}, u32[]{:S(2)}) collective-permute-start(f32[360,512]{1,0:T(8,128)S(1)} %collective-permute-done.105.far_ref), channel_id=1, source_target_pairs={{0,1},{1,0},{2,3},{3,2},{4,5},{5,4},{6,7},{7,6},{8,9},{9,8},{10,11... | collective-permute-start | bytes 2211848 | tf_op jit(solution)/shard_map/ppermute | solution.py:31
  543.0 15.7 %collective-permute-start.103 = (f32[416,256]{1,0:T(8,128)S(1)}, f32[416,256]{1,0:T(8,128)S(1)}, u32[]{:S(2)}, u32[]{:S(2)}) collective-permute-start(f32[416,256]{1,0:T(8,128)S(1)} %pad_maximum_fusion.2.mine_ref), channel_id=1, source_target_pairs={{0,1},{1,0},{2,3},{3,2},{4,5},{5,4},{6,7},{7,6},{8,9},{9,8},{10,11... | collective-permute-start | bytes 1277960 | tf_op jit(solution)/shard_map/ppermute | solution.py:31
  (174 other events, 1204.7 us)

commit v3 on v2

--- a/solution.py
+++ b/solution.py
@@ -24,6 +24,7 @@
 BF16 = jnp.bfloat16
 AXES = ("dp", "hst")
 MIB = 1 << 20
+LANES = 128
 
 
 def swap(value, mask):
@@ -395,13 +396,18 @@
     )(*parts, *members, h2, valid, gain, shift, weight)
 
 
-def crop_sums(lines):
-    crops = lines.shape[0] // CELL
-    chosen = (
-        lax.broadcasted_iota(jnp.int32, (crops, lines.shape[0]), 1) // CELL
-        == lax.broadcasted_iota(jnp.int32, (crops, lines.shape[0]), 0)
-    ).astype(F32)
-    return jnp.dot(chosen, lines, precision=highest, preferred_element_type=F32)
+def crop_sums(ref, *index):
+    crops = ref.shape[-2] // CELL
+    slabs = [
+        tree([ref[(*index, j, pl.ds(i, crops, CELL), slice(None))] for i in range(CELL)])
+        for j in range(ref.shape[-3])
+    ]
+    return jnp.concatenate(slabs, 1)
+
+
+def put_lanes(ref, place, first, value, *index):
+    for j in range(0, value.shape[1], LANES):
+        ref[(*index, (first + j) // LANES, place, slice(None))] = value[:, j : j + LANES]
 
 
 def pool_body(counts, refs):
@@ -426,8 +432,8 @@
                 )
                 out = resid * (sigmoid(resid) * v_ref[at, :])
                 acc += out.astype(BF16).astype(F32)
-            sums_ref[pl.ds(k * COLS, COLS), lane] = acc
-    feat_ref[...] = (crop_sums(sums_ref[...]) / size_ref[...]).astype(BF16).astype(F32)
+            put_lanes(sums_ref, pl.ds(k * COLS, COLS), j, acc)
+    feat_ref[...] = (crop_sums(sums_ref) / size_ref[...]).astype(BF16).astype(F32)
 
 
 def pool(parts, members, h3, x, valid, gain, shift, sizes, micro):
@@ -452,7 +458,7 @@
         ],
         [pl.BlockSpec((crops, width), lambda m, c: (m, c)), pair],
         [shape((micro * crops, channels)), shape((micro, 2, channels))],
-        [pltpu.VMEM((rows // ROWS, width), F32)],
+        [pltpu.VMEM((width // LANES, rows // ROWS, LANES), F32)],
         flops=20 * h3.size,
         bytes_accessed=4 * h3.size,
     )(*parts, *members, h3, x, valid, gain, shift, sizes)
@@ -482,10 +488,10 @@
                 acc_second += slope * centred
                 slope_ref[at, lane] = slope.astype(BF16)
             place = pl.ds(k * COLS, COLS)
-            sums_ref[0, place, lane] = acc_first
-            sums_ref[1, place, lane] = acc_second * scaled[:, lane]
-    first_ref[...] = crop_sums(sums_ref[0])
-    second_ref[...] = crop_sums(sums_ref[1])
+            put_lanes(sums_ref, place, j, acc_first, 0)
+            put_lanes(sums_ref, place, j, acc_second * scaled[:, lane], 1)
+    first_ref[...] = crop_sums(sums_ref, 0)
+    second_ref[...] = crop_sums(sums_ref, 1)
 
 
 def slope_part(h3, x, valid, info, gain, shift, micro, index, earlier):
@@ -512,7 +518,7 @@
             shape((micro * crops, channels)),
             shape((micro * crops, channels)),
         ],
-        [pltpu.VMEM((2, rows // ROWS, width), F32)],
+        [pltpu.VMEM((2, width // LANES, rows // ROWS, LANES), F32)],
         flops=30 * rows * channels,
         bytes_accessed=6 * rows * channels,
         aliases={6 + i: i for i in range(len(earlier))},
@@ -554,17 +560,17 @@
 
 def head_back_body(total_crops, counts, refs):
     part_refs = refs[:counts]
-    dy_ref, g_ref, info_ref, gain_ref, w_ref, size_ref, first_ref, second_ref, dg_ref, wide_ref, stats_ref, low_ref = refs[counts:]
+    dy_ref, g_ref, info_ref, gain_ref, w_ref, size_ref, first_ref, second_ref, dg_ref, wide_ref, stats_ref, low_ref, spread_ref = refs[counts:]
     micro = stats_ref.shape[0]
-    lines = dy_ref.shape[0]
+    lines, width = dy_ref.shape
     crops = lines // micro
 
     @pl.when(pl.program_id(0) == 0)
     def _():
         for m in range(micro):
             at = pl.ds(m * crops, crops)
-            one = tree([ref[m : m + 1, :] for ref in part_refs]) / total_crops
-            two = tree([ref[micro + m : micro + m + 1, :] for ref in part_refs]) / total_crops
+            one = tree([ref[m : m + 1, :width] for ref in part_refs]) / total_crops
+            two = tree([ref[micro + m : micro + m + 1, :width] for ref in part_refs]) / total_crops
             scaled = info_ref[m, 1:2, :]
             normal = (g_ref[at, :] - info_ref[m, 0:1, :]) * scaled
             dg = gain_ref[...] * scaled * (dy_ref[at, :] - (one + normal * two))
@@ -573,11 +579,11 @@
             dg_ref[at, :] = low.astype(F32)
 
     per_crop = nt_dot(low_ref[...], w_ref[...]) / size_ref[...]
-    lift = (
-        lax.broadcasted_iota(jnp.int32, (lines * CELL, lines), 0) // CELL
-        == lax.broadcasted_iota(jnp.int32, (lines * CELL, lines), 1)
-    ).astype(F32)
-    wide_ref[...] = jnp.dot(lift, per_crop, precision=highest, preferred_element_type=F32)
+    for j in range(wide_ref.shape[1] // LANES):
+        lane = slice(j * LANES, (j + 1) * LANES)
+        for i in range(CELL):
+            spread_ref[j, pl.ds(i, lines, CELL), :] = per_crop[:, lane]
+        wide_ref[:, lane] = spread_ref[j]
     one = per_crop * first_ref[...]
     two = per_crop * second_ref[...]
     for m in range(micro):
@@ -612,16 +618,20 @@
             pl.BlockSpec((micro, 2, tile), lambda c: (0, 0, c)),
         ],
         [shape((lines, width)), shape((lines * CELL, channels)), shape((micro, 2, channels))],
-        [pltpu.VMEM((lines, width), BF16)],
+        [
+            pltpu.VMEM((lines, width), BF16),
+            pltpu.VMEM((tile // LANES, lines * CELL, LANES), F32),
+        ],
         flops=2 * lines * weight.size,
         bytes_accessed=2 * weight.size,
     )(*parts, dy, g, info, gain, weight, sizes, first, second)
 
 
 def third_back_body(counts, refs):
-    part_refs = refs[:counts]
-    wide_ref, slope_ref, h3_ref, v_ref, info3_ref, gain3_ref, info1_ref, w_ref, h2_ref, info2_ref, gain2_ref, shift2_ref, d_ref, dy_ref, stats_ref = refs[counts:]
+    which_ref, part_refs = refs[0], refs[1 : 1 + counts]
+    wide_ref, slope_ref, h3_ref, v_ref, info3_ref, gain3_ref, info1_ref, w_ref, act_ref, h2_ref, info2_ref, gain2_ref, shift2_ref, dy_ref, stats_ref, send_ref, keep_ref, d_ref, sum_ref = refs[1 + counts :]
     rows, channels = slope_ref.shape
+    step = pl.program_id(0)
     number = info1_ref[0, 2:3, 0:1]
     first, second = sums_of(part_refs, 0, 1)
     mean = info3_ref[0, 0:1, :]
@@ -629,8 +639,15 @@
     factor = gain3_ref[...] * scaled
     one = factor * first / number
     two = factor * scaled * second / number
-    for j in range(0, channels, 512):
-        lane = slice(j, j + 512)
+    act = act_ref[...].T
+
+    @pl.when(step == 0)
+    def _():
+        sum_ref[...] = jnp.zeros(sum_ref.shape, F32)
+
+    tile = sum_ref.shape[2]
+    for j in range(0, channels, tile):
+        lane = slice(j, j + tile)
         for k in range(rows // PIX):
             wide = wide_ref[pl.ds(k * COLS, COLS), lane] * factor[:, lane]
             for r in range(ROWS):
@@ -638,8 +655,25 @@
                 back = one[:, lane] + (h3_ref[at, lane].astype(F32) - mean[:, lane]) * two[:, lane]
                 d = wide * slope_ref[at, lane].astype(F32) - v_ref[at, :] * back
                 d_ref[at, lane] = d.astype(BF16)
-    dy_ref[...] = nt_dot(d_ref[...], w_ref[...])
+        part = nt_dot(d_ref[:, lane], w_ref[:, lane])
+        if j == 0:
+            dy_ref[...] = part
+        else:
+            dy_ref[...] += part
+        sum_ref[j // tile] += jnp.dot(act, d_ref[:, lane], preferred_element_type=F32)
     put_back(dy_ref, h2_ref, v_ref, info2_ref, gain2_ref, shift2_ref, stats_ref)
+
+    @pl.when(step == pl.num_programs(0) - 1)
+    def _():
+        low = which_ref[0] == 0
+        steps = sum_ref.shape[0] // 2
+        lines = send_ref.shape[1] // steps
+        for q in range(steps):
+            place = slice(q * lines, (q + 1) * lines)
+            left = sum_ref[q].reshape(-1, lines, tile)
+            right = sum_ref[steps + q].reshape(-1, lines, tile)
+            send_ref[:, place, :] = jnp.where(low, left, right)
+            keep_ref[:, place, :] = jnp.where(low, right, left)
 
 
 def put_back(dy_ref, h_ref, v_ref, info_ref, gain_ref, shift_ref, stats_ref):
@@ -658,70 +692,48 @@
     stats_ref[0, 1:2, :] = jnp.sum(second, axis=0, keepdims=True)
 
 
-def third_back(parts, wide, slope, h3, valid, info3, gain3, info1, weight, h2, info2, gain2, shift2, micro):
+def third_back(which, parts, wide, slope, h3, valid, info3, gain3, info1, weight, act, h2, info2, gain2, shift2, micro, shards):
     rows, channels = slope.shape[0] // micro, slope.shape[1]
     middle = weight.shape[0]
     lines = wide.shape[0] // micro
-    big = pl.BlockSpec((rows, channels), lambda m: (m, 0))
-    mid = pl.BlockSpec((rows, middle), lambda m: (m, 0))
+    tile = 512
+    big = pl.BlockSpec((rows, channels), lambda m, w: (m, 0))
+    mid = pl.BlockSpec((rows, middle), lambda m, w: (m, 0))
+    half = shape((shards, middle // shards * (channels // tile // 2), tile))
     return run(
         named("third_back", third_back_body, len(parts)),
         (micro,),
         [per_micro(part) for part in parts]
         + [
-            pl.BlockSpec((lines, channels), lambda m: (m, 0)),
+            pl.BlockSpec((lines, channels), lambda m, w: (m, 0)),
             big,
             big,
-            pl.BlockSpec((rows, 1), lambda m: (m, 0)),
+            pl.BlockSpec((rows, 1), lambda m, w: (m, 0)),
             per_micro(info3),
             whole(gain3),
             per_micro(info1),
             whole(weight),
             mid,
+            mid,
             per_micro(info2),
             whole(gain2),
             whole(shift2),
         ],
-        [big, mid, pl.BlockSpec((1, 2, middle), lambda m: (m, 0, 0))],
-        [shape(slope.shape, BF16), shape(h2.shape), shape((micro, 2, middle))],
-        flops=2 * slope.shape[0] * weight.size,
+        [
+            mid,
+            pl.BlockSpec((1, 2, middle), lambda m, w: (m, 0, 0)),
+            whole(half),
+            whole(half),
+        ],
+        [shape(h2.shape), shape((micro, 2, middle)), half, half],
+        [
+            pltpu.VMEM((rows, channels), BF16),
+            pltpu.VMEM((channels // tile, middle, tile), F32),
+        ],
+        flops=4 * slope.shape[0] * weight.size,
         bytes_accessed=6 * slope.size,
-    )(*parts, wide, slope, h3, valid, info3, gain3, info1, weight, h2, info2, gain2, shift2)
-
-
-def out_grad_body(which_ref, left_ref, right_ref, out_ref, turned_ref):
-    @pl.when(pl.program_id(0) == 0)
-    def _():
-        turned_ref[...] = left_ref[...].T
-
-    grad = jnp.dot(turned_ref[...], right_ref[...], preferred_element_type=F32)
-    out_ref[0] = grad.reshape(out_ref.shape[1:])
-
-
-def out_grad(which, left, right, shards):
-    rows, depth = left.shape
-    half = right.shape[1] // 2
-    tile = 512
-    steps = half // tile
-    lines = depth // shards
-
-    def column(c, w):
-        return jnp.where(c // steps == 0, w[0], 1 - w[0]) * steps + c % steps
-
-    return run(
-        out_grad_body,
-        (2 * steps,),
-        [
-            pl.BlockSpec(left.shape, lambda c, w: (0, 0)),
-            pl.BlockSpec((rows, tile), lambda c, w: (0, column(c, w))),
-        ],
-        pl.BlockSpec((1, shards, lines, tile), lambda c, w: (c // steps, 0, c % steps, 0)),
-        shape((2, shards, steps * lines, tile)),
-        [pltpu.VMEM((depth, rows), BF16)],
-        flops=2 * rows * depth * right.shape[1],
-        bytes_accessed=2 * left.size + 2 * right.size + 8 * depth * half,
         prefetch=1,
-    )(which, left, right)
+    )(which, *parts, wide, slope, h3, valid, info3, gain3, info1, weight, act, h2, info2, gain2, shift2)
 
 
 def put_norm_back(part_refs, dy_ref, h_ref, v_ref, info_ref, number_ref, gain_ref, d_ref):
@@ -760,12 +772,12 @@
             sides_ref[2, k, at, :] = (pltpu.roll(wide, COLS - 1, 0) * has_right).astype(BF16)
 
 
-def put_tap(out_ref, sides_ref, turned_ref):
+def put_tap(out_ref, sides_ref, half_ref):
     tap = pl.program_id(0)
     _, canvases, _, width = sides_ref.shape
     start = pl.multiple_of(tap // 3 * COLS, COLS)
     left = sides_ref[tap % 3, :, pl.ds(start, PIX), :].reshape(canvases * PIX, width)
-    out_ref[...] = jnp.dot(turned_ref[...], left, preferred_element_type=F32).T
+    out_ref[...] = tn_dot(left, half_ref[...])
 
 
 def half_of(which_ref, d_ref):
@@ -775,26 +787,26 @@
 
 def mid_first_body(counts, refs):
     which_ref, part_refs = refs[0], refs[1 : 1 + counts]
-    dy_ref, h_ref, v_ref, info_ref, number_ref, gain_ref, a_ref, d_ref, out_ref, sides_ref, turned_ref = refs[1 + counts :]
+    dy_ref, h_ref, v_ref, info_ref, number_ref, gain_ref, a_ref, d_ref, out_ref, sides_ref, half_ref = refs[1 + counts :]
 
     @pl.when(pl.program_id(0) == 0)
     def _():
         put_norm_back(part_refs, dy_ref, h_ref, v_ref, info_ref, number_ref, gain_ref, d_ref)
-        turned_ref[...] = half_of(which_ref, d_ref).T
+        half_ref[...] = half_of(which_ref, d_ref)
         put_sides(a_ref, sides_ref)
 
-    put_tap(out_ref, sides_ref, turned_ref)
+    put_tap(out_ref, sides_ref, half_ref)
 
 
 def mid_second_body(refs):
-    which_ref, d_ref, a_ref, out_ref, sides_ref, turned_ref = refs
+    which_ref, d_ref, a_ref, out_ref, sides_ref, half_ref = refs
 
     @pl.when(pl.program_id(0) == 0)
     def _():
-        turned_ref[...] = half_of(which_ref, d_ref).T
+        half_ref[...] = half_of(which_ref, d_ref)
         put_sides(a_ref, sides_ref)
 
-    put_tap(out_ref, sides_ref, turned_ref)
+    put_tap(out_ref, sides_ref, half_ref)
 
 
 def mid_grad(name, body, which, ins, act, with_d):
@@ -811,7 +823,7 @@
         else shape((TAPS * width, half)),
         [
             pltpu.VMEM((3, rows // PIX, PIX + 2 * COLS, width), BF16),
-            pltpu.VMEM((half, rows), BF16),
+            pltpu.VMEM((rows, half), BF16),
         ],
         flops=2 * rows * TAPS * width * half,
         bytes_accessed=4 * TAPS * width * half,
@@ -821,14 +833,13 @@
 
 def in_grad_body(counts, refs):
     which_ref, part_refs = refs[0], refs[1 : 1 + counts]
-    dy_ref, h_ref, v_ref, info_ref, number_ref, gain_ref, x_ref, d_ref, send_ref, keep_ref, turned_ref = refs[1 + counts :]
+    dy_ref, h_ref, v_ref, info_ref, number_ref, gain_ref, x_ref, d_ref, send_ref, keep_ref = refs[1 + counts :]
 
     @pl.when(pl.program_id(0) == 0)
     def _():
         put_norm_back(part_refs, dy_ref, h_ref, v_ref, info_ref, number_ref, gain_ref, d_ref)
-        turned_ref[...] = d_ref[...].T
-
-    grad = jnp.dot(turned_ref[...], x_ref[...], preferred_element_type=F32).T
+
+    grad = tn_dot(x_ref[...], d_ref[...])
     half = grad.shape[1] // 2
     low = which_ref[0] == 0
     left, right = grad[:, :half], grad[:, half:]
@@ -849,7 +860,6 @@
         [whole(a) for a in ins] + [pl.BlockSpec((rows, tile), lambda c, w: (0, c))],
         [whole(dy), grad, grad],
         [shape(dy.shape, BF16), shape((depth, half)), shape((depth, half))],
-        [pltpu.VMEM((width, rows), BF16)],
         flops=2 * rows * depth * width,
         bytes_accessed=2 * x.size + 4 * depth * width + 10 * dy.size,
         prefetch=1,
@@ -1081,30 +1091,44 @@
     return dot(left, high) + dot(left, low)
 
 
-def pack_small(packed_ref, protos, embed):
-    _, shards, _, lines, width = packed_ref.shape
+def pack_small(low, send_ref, keep_ref, protos, embed):
+    shards, lines, width = send_ref.shape
+    lines = lines // 2
     rows = protos.shape[0] // shards // 2
     half = protos.shape[1] // 2
     groups = half // width
     lane = embed.shape[1]
     below = lines - groups * rows
-    for c in range(2):
-        for d in range(shards):
-            for y in range(2):
-                first = (2 * d + y) * rows
-                for q in range(groups):
-                    packed_ref[c, d, y, q * rows : (q + 1) * rows, :] = protos[
-                        first : first + rows, c * half + q * width : c * half + (q + 1) * width
+
+    def put(d, place, columns, one, two):
+        keep_ref[d, place, columns] = jnp.where(low, one, two)
+        send_ref[d, place, columns] = jnp.where(low, two, one)
+
+    for d in range(shards):
+        for y in range(2):
+            first = (2 * d + y) * rows
+            for q in range(groups):
+                start = y * lines + q * rows
+                one, two = [
+                    protos[first : first + rows, c * half + q * width : c * half + (q + 1) * width]
+                    for c in range(2)
+                ]
+                put(d, slice(start, start + rows), slice(None), one, two)
+            for q in range(width // lane):
+                one, two = [
+                    embed[first : first + below]
+                    for first in [
+                        (((2 * d + c) * 2 + y) * (width // lane) + q) * below for c in range(2)
                     ]
-                for q in range(width // lane):
-                    first = (((2 * d + c) * 2 + y) * (width // lane) + q) * below
-                    packed_ref[c, d, y, groups * rows :, q * lane : (q + 1) * lane] = embed[
-                        first : first + below
-                    ]
-
-
-def unpack_small(packed, protos, embed):
-    _, shards, _, lines, width = packed.shape
+                ]
+                start = y * lines + groups * rows
+                put(d, slice(start, start + below), slice(q * lane, (q + 1) * lane), one, two)
+
+
+def unpack_small(halves, protos, embed):
+    shards, lines, width = halves[0].shape
+    lines = lines // 2
+    packed = jnp.stack(halves).reshape(2, shards, 2, lines, width)
     rows = protos[0] // shards // 2
     groups = protos[1] // 2 // width
     lane = embed[1]
@@ -1120,12 +1144,12 @@
 def packed_shape(protos, embed, shards):
     width = 512
     lines = protos[0] // shards // 2 * (protos[1] // 2 // width)
-    return (2, shards, 2, lines + embed[0] * embed[1] // shards // 4 // width, width)
+    return (shards, 2 * (lines + embed[0] * embed[1] // shards // 4 // width), width)
 
 
 def loss_body(protos, scale, counts, refs):
-    part_refs = refs[:counts]
-    batch_ref, logits_ref, unit_ref, z_ref, inverse_ref, act_ref, g_ref, info_ref, gain_ref, shift_ref, w_ref, table_ref, packed_ref, dy_ref, sums_ref = refs[counts:]
+    which_ref, part_refs = refs[0], refs[1 : 1 + counts]
+    batch_ref, logits_ref, unit_ref, z_ref, inverse_ref, act_ref, g_ref, info_ref, gain_ref, shift_ref, w_ref, table_ref, send_ref, keep_ref, dy_ref, sums_ref = refs[1 + counts :]
     micro, wide = part_refs[0].shape
     lines = batch_ref.shape[0]
     crops = lines // micro
@@ -1159,7 +1183,7 @@
         z * d_unit, 1, keepdims=True
     )
     grad_embed = split_dot(tn_dot, act_ref[...], dz, False)
-    pack_small(packed_ref, grad_protos, grad_embed)
+    pack_small(which_ref[0] == 0, send_ref, keep_ref, grad_protos, grad_embed)
     d_act = split_dot(nt_dot, dz, w_ref[...], True)
     for m in range(micro):
         at = slice(m * crops, (m + 1) * crops)
@@ -1167,23 +1191,26 @@
         pre = normal * gain_ref[...] + shift_ref[...]
         dy = d_act[at] * slope_of(pre)
         dy_ref[at, :] = dy
-        sums_ref[m : m + 1, :] = jnp.sum(dy, axis=0, keepdims=True)
-        sums_ref[micro + m : micro + m + 1, :] = jnp.sum(dy * normal, axis=0, keepdims=True)
+        sums_ref[m : m + 1, : dy.shape[1]] = jnp.sum(dy, axis=0, keepdims=True)
+        sums_ref[micro + m : micro + m + 1, : dy.shape[1]] = jnp.sum(
+            dy * normal, axis=0, keepdims=True
+        )
     feat = z.shape[1]
-    sums_ref[2 * micro : 2 * micro + 1, :] = jnp.zeros((1, sums_ref.shape[1]), F32)
-    sums_ref[2 * micro : 2 * micro + 1, 0:feat] = jnp.sum(dz, axis=0, keepdims=True)
-    sums_ref[2 * micro : 2 * micro + 1, feat : 2 * feat] = jnp.broadcast_to(
-        -scale * loss, (1, feat)
+    wide = dy_ref.shape[1]
+    extra = jnp.concatenate(
+        [jnp.sum(dz, axis=0, keepdims=True), jnp.broadcast_to(-scale * loss, (1, feat))], 1
     )
-
-
-def loss_grads(parts, protos, scale, batch, logits, unit, z, inverse, act, g, info, gain, shift, weight, table, shards):
+    sums_ref[:, wide:] = jnp.broadcast_to(extra, (2 * micro, 2 * feat))
+
+
+def loss_grads(which, parts, protos, scale, batch, logits, unit, z, inverse, act, g, info, gain, shift, weight, table, shards):
     ins = [*parts, batch, logits, unit, z, inverse, act, g, info, gain, shift, weight, table]
     micro = info.shape[0]
     outs = [
         shape(packed_shape(table.shape, weight.shape, shards)),
+        shape(packed_shape(table.shape, weight.shape, shards)),
         shape(g.shape),
-        shape((2 * micro + 1, g.shape[1])),
+        shape((2 * micro, g.shape[1] + 2 * weight.shape[1])),
     ]
     return run(
         named("loss", loss_body, protos, scale, len(parts)),
@@ -1193,27 +1220,29 @@
         outs,
         flops=8 * table.size * batch.shape[0],
         bytes_accessed=16 * batch.size,
-    )(*ins)
-
-
-def pick_block(rows, width, cell):
-    return pl.BlockSpec((1, rows, width), lambda g, w: cell(g, w[0], w[1], w[2]) + (0,))
-
-
-def sent_first(g, core, x, y):
-    z, b = g // 2, g % 2
+        prefetch=1,
+    )(which, *ins)
+
+
+def pick_block(rows, width, cell, *fixed):
+    return pl.BlockSpec((1, rows, width), lambda g, w: cell(g, *fixed, w[0], w[1], w[2]) + (0,))
+
+
+def sent_first(g, i, core, x, y):
+    z, b = 2 * g + i // 2, i % 2
     return (2 * z + (1 - core) * (1 - x) + core * b, (1 - core) * b + core * (1 - y))
 
 
-def kept_second(g, core, x, y):
-    return (2 * g + x, y)
-
-
-def sent_second(g, core, x, y):
-    return (2 * g + (1 - core) * x + core * (1 - x), (1 - core) * (1 - y) + core * y)
-
-
-def add_groups(refs, sizes, out_ref, extra=None):
+def kept_second(g, i, core, x, y):
+    return (2 * (2 * g + i) + x, y)
+
+
+def sent_second(g, i, core, x, y):
+    z = 2 * g + i
+    return (2 * z + (1 - core) * x + core * (1 - x), (1 - core) * (1 - y) + core * y)
+
+
+def add_groups(refs, sizes, out_ref, index, extra=None):
     start = 0
     place = 0
     for count, rows in sizes:
@@ -1222,65 +1251,89 @@
             value = value + ref[0]
         if extra is not None:
             value = value + extra[0, start : start + rows, :]
-        out_ref[0, start : start + rows, :] = value
+        out_ref[index, start : start + rows, :] = value
         place += count
         start += rows
 
 
+def group_sizes(groups):
+    return [(len(addends), addends[0].shape[1] // 2) for addends in groups]
+
+
 def first_send(scalars, groups):
-    sizes = [(len(addends), addends[0].shape[1] // 2) for addends in groups]
+    sizes = group_sizes(groups)
     shards, _, width = groups[0][0].shape
     lines = sum(rows for _, rows in sizes)
+    flat = [array for addends in groups for array in addends]
     specs = []
-    for (count, rows), addends in zip(sizes, groups):
-        specs += [pick_block(rows, width, sent_first)] * count
-    flat = [array for addends in groups for array in addends]
+    for i in range(4):
+        for array in flat:
+            specs.append(pick_block(array.shape[1] // 2, width, sent_first, i))
 
     def body(refs):
-        add_groups(refs[1:-1], sizes, refs[-1])
+        refs = refs[1:]
+        for i in range(4):
+            add_groups(refs[i * len(flat) : (i + 1) * len(flat)], sizes, refs[-1], i)
 
     return run(
         named("first_send", body),
-        (shards,),
+        (shards // 4,),
         specs,
-        pl.BlockSpec((1, lines, width), lambda g, w: (g, 0, 0)),
+        pl.BlockSpec((4, lines, width), lambda g, w: (g, 0, 0)),
         shape((shards, lines, width)),
         bytes_accessed=4 * lines * width * shards * 3,
         prefetch=1,
-    )(scalars, *flat)
+    )(scalars, *(flat * 4))
 
 
 def second_send(scalars, groups, came):
-    sizes = [(len(addends), addends[0].shape[1] // 2) for addends in groups]
+    sizes = group_sizes(groups)
     shards, _, width = groups[0][0].shape
     lines = sum(rows for _, rows in sizes)
     flat = [array for addends in groups for array in addends]
     specs = []
     for cell in (sent_second, kept_second):
-        for (count, rows), addends in zip(sizes, groups):
-            specs += [pick_block(rows, width, cell)] * count
+        for i in range(2):
+            for array in flat:
+                specs.append(pick_block(array.shape[1] // 2, width, cell, i))
 
     def bit(w):
         return (1 - w[0]) * w[2] + w[0] * w[1]
 
-    specs.append(pl.BlockSpec((1, lines, width), lambda g, w: (2 * g + 1 - bit(w), 0, 0)))
-    specs.append(pl.BlockSpec((1, lines, width), lambda g, w: (2 * g + bit(w), 0, 0)))
-    out = pl.BlockSpec((1, lines, width), lambda g, w: (g, 0, 0))
+    for flip in (1, 0):
+        for i in range(2):
+            specs.append(
+                pl.BlockSpec(
+                    (1, lines, width),
+                    lambda g, w, i=i, flip=flip: (2 * (2 * g + i) + (1 - bit(w) if flip else bit(w)), 0, 0),
+                )
+            )
+    out = pl.BlockSpec((2, lines, width), lambda g, w: (g, 0, 0))
 
     def body(refs):
         refs = refs[1:]
-        add_groups(refs[: len(flat)], sizes, refs[-2], refs[2 * len(flat)])
-        add_groups(refs[len(flat) : 2 * len(flat)], sizes, refs[-1], refs[2 * len(flat) + 1])
+        count = len(flat)
+        came_refs = refs[4 * count : 4 * count + 4]
+        for side in range(2):
+            for i in range(2):
+                place = 2 * side + i
+                add_groups(
+                    refs[place * count : (place + 1) * count],
+                    sizes,
+                    refs[-2 + side],
+                    i,
+                    came_refs[place],
+                )
 
     return run(
         named("second_send", body),
-        (shards // 2,),
+        (shards // 4,),
         specs,
         [out, out],
         [shape((shards // 2, lines, width))] * 2,
         bytes_accessed=4 * lines * width * shards * 4,
         prefetch=1,
-    )(scalars, *flat, *flat, came, came)
+    )(scalars, *(flat * 4), *([came] * 4))
 
 
 def place_early_body(scalars_ref, mine_ref, far_ref, mine_core_ref, far_core_ref, out_ref, embed_ref, protos_ref, head_ref):
@@ -1331,11 +1384,6 @@
         outs,
         prefetch=1,
     )(scalars, *pieces)
-
-
-def gathered(mine):
-    far = swap(mine, 2)
-    return [mine, far, swap(mine, 1), swap(far, 1)]
 
 
 def on_device(
@@ -1451,7 +1499,9 @@
         batch, queue, column = sweep(parts, protos, batch, queue, queue_rows.shape[0])
     parts = sum_parts(column, fillers)
     slope, slope_first, slope_second = slopes
-    packed, dy_four, payload = loss_grads(
+    which = (1 - send_half) if quick else jnp.zeros((1,), jnp.int32)
+    small_send, small_keep, dy_four, payload = loss_grads(
+        which,
         parts,
         protos,
         loss_scale,
@@ -1469,21 +1519,18 @@
         table,
         packs,
     )
+    parts = sum_parts(payload)
+    payload = tree(list(parts))
+    channel_sums = payload[:, : head_gain.shape[0]]
+    first_four, second_four = channel_sums[:micro], channel_sums[micro:]
+    extra = payload[0, head_gain.shape[0] :]
+    grad_bias, total_loss = extra[: embed_bias.shape[0]], extra[embed_bias.shape[0]]
+
     if quick:
-        small_recv = swap(at(packed, 1 - core, 0), 1)
-    parts = sum_parts(payload)
-    if quick:
-        *parts, small_recv = tie(*parts, small_recv)
-        small = [at(packed, core, 0), small_recv]
-    payload = tree(list(parts))
-    first_four, second_four = payload[:micro], payload[micro : 2 * micro]
-    grad_bias = payload[2 * micro, : embed_bias.shape[0]]
-    total_loss = payload[2 * micro, embed_bias.shape[0]]
-
-    if quick:
-        feat_keep, feat_near, *parts = tie(feat_keep, feat_near, *parts)
+        feat_keep, feat_near, small_send, *parts = tie(feat_keep, feat_near, small_send, *parts)
         feat_near = jnp.concatenate([feat_keep, feat_near], 0)
         feat_far = swap(feat_near, 2)
+        small_recv = swap(small_send, 1)
     dg, wide, sums = head_back(
         parts,
         dy_four,
@@ -1499,8 +1546,9 @@
     first_norm = (h1, valid, info_one, info_one, row(gain_one))
     second_norm = (h2, valid, info_two, info_one, row(gain_two))
 
-    def from_third(parts):
+    def from_third(which, parts):
         return third_back(
+            which,
             parts,
             wide,
             slope,
@@ -1510,11 +1558,13 @@
             row(gain_three),
             info_one,
             conv_out,
+            act_two,
             h2,
             info_two,
             row(gain_two),
             row(shift_two),
             micro,
+            shards,
         )
 
     def from_second(d):
@@ -1523,39 +1573,50 @@
         )
 
     if quick:
-        sums, dg, feat_far = tie(sums, dg, feat_far)
+        sums, dg, feat_far, small_recv = tie(sums, dg, feat_far, small_recv)
         feat_both = jnp.concatenate([feat_near, feat_far], 0)
-        feat_other = swap(feat_both, 1)
         split = dg.reshape(lines, 2, -1)
-        dg_other = swap(at(split, 1 - core, 1), 1)
-        parts_three = sum_parts(sums)
-        *parts_three, dg_other, feat_other = tie(*parts_three, dg_other, feat_other)
-        split = jnp.concatenate([at(split, core, 1), dg_other], 0).reshape(2 * lines, 2, -1)
+        dg_send = at(split, 1 - core, 1)
+
+        def core_filler(gate):
+            source, other = tie(dg_send, feat_both, gate)[:2]
+            grads["dg"] = swap(source, 1)
+            grads["feat"] = swap(other, 1)
+            return [grads["dg"], grads["feat"]]
+
+        grads = {}
+        parts_three = sum_parts(sums, ((), (core_filler,)))
+        feat_other = grads["feat"]
+        split = jnp.concatenate([at(split, core, 1), grads["dg"]], 0).reshape(2 * lines, 2, -1)
         dg_here, dg_there = at(split, side, 1), at(split, 1 - side, 1)
         *parts_three, dg_here, dg_there = tie(*parts_three, dg_here, dg_there)
         dg_far, dg_near, dg_both = swap(dg_there, 2), swap(dg_here, near), swap(dg_there, 2 + near)
-        d_three, dy, sums = from_third(parts_three)
-        sums, dy, d_three, dg_far, dg_near, dg_both = tie(sums, dy, d_three, dg_far, dg_near, dg_both)
-        grads = {}
+        dy, sums, out_send, out_keep = from_third(send_half, parts_three)
+        sums, dy, out_send, dg_far, dg_near, dg_both = tie(
+            sums, dy, out_send, dg_far, dg_near, dg_both
+        )
+        small = [small_keep, small_recv]
 
         def out_filler(gate):
-            source = tie(d_three, gate)[0]
-            grads["out"] = out_grad(send_half, act_two, source, shards)
+            grads["out"] = swap(tie(out_send, gate)[0], 1)
             return [grads["out"]]
 
         def head_filler(gate):
-            grads["out_recv"] = swap(grads["out"][0], 1)
             source = tie(dg_near, gate)[0]
             grads["head"] = factor_grad(feat_both, feat_other, dg_here, dg_far, source, dg_both)
-            return [grads["head"], grads["out_recv"]]
-
-        parts_two = sum_parts(sums, ((), (out_filler,), (head_filler,)))
-
-        small = [array.reshape(shards, -1, array.shape[-1]) for array in small]
-        early = [[grads["out"][1], grads["out_recv"]], small]
-        early_out = first_send(scalars, early)
-        *parts_two, early_out, partial = tie(*parts_two, early_out, grads["head"])
-        came = core_swap(early_out, near, 2)
+            return [grads["head"]]
+
+        def early_filler(gate):
+            source = tie(grads["out"], gate)[0]
+            grads["early"] = [[out_keep, source], small]
+            grads["early_out"] = first_send(scalars, grads["early"])
+            return [grads["early_out"]]
+
+        parts_two = sum_parts(sums, ((), (out_filler,), (head_filler, early_filler)))
+
+        early = grads["early"]
+        *parts_two, early_out, partial = tie(*parts_two, grads["early_out"], grads["head"])
+        early_came = core_swap(early_out, near, 2)
         partial = partial.reshape(2, 2, -1, partial.shape[1])
         head = dp_halves([partial], far[0], 1)
         d_two, mid_send = mid_grad(
@@ -1566,14 +1627,14 @@
             act_one,
             True,
         )
-        d_two, mid_send, early_came, head[-1] = tie(d_two, mid_send, came, head[-1])
+        d_two, mid_send, early_came = tie(d_two, mid_send, early_came)
         mid_recv = swap(mid_send, 1)
-        early_send, early_keep = second_send(scalars, early, early_came)
-        early_came = core_swap(early_send, 2, near)
+        early_out, early_keep = second_send(scalars, early, early_came)
+        early_came = core_swap(early_out, 2, near)
         mid_keep = mid_grad(
             "mid_second", mid_second_body, keep_half, [d_two, act_one], act_one, False
         )
-        mid_keep, mid_recv, early_came = tie(mid_keep, mid_recv, early_came)
+        mid_keep, mid_recv, early_came, head[-1] = tie(mid_keep, mid_recv, early_came, head[-1])
 
         def sharded(array):
             return array.reshape(shards, -1, array.shape[-1])
@@ -1582,37 +1643,54 @@
             return array.reshape((2, 2) + array.shape[1:])
 
         late = [[sharded(mid_keep), sharded(mid_recv)]]
-        mid_came = core_swap(first_send(scalars, late), near, 2)
-        early = dp_halves([by_bits(early_keep), by_bits(early_came)], far[0], 1)
-        d_two = tie(d_two, mid_keep)[0]
+        mid_out = first_send(scalars, late)
+        d_two, mid_out = tie(d_two, mid_out)
+        mid_came = core_swap(mid_out, near, 2)
+        head = dp_halves(head, far[1], 0)
         dy, sums = from_second(d_two)
-        dy, sums, mid_came, early[-1] = tie(dy, sums, mid_came, early[-1])
-        parts_one = sum_parts(sums)
-        mid_out, mid_keep = second_send(scalars, late, mid_came)
-        *parts_one, mid_out = tie(*parts_one, mid_out)
+        dy, sums, mid_came, head[-1], early_keep, early_came = tie(
+            dy, sums, mid_came, head[-1], early_keep, early_came
+        )
+        early = [by_bits(early_keep), by_bits(early_came)]
+
+        def early_z_filler(gate):
+            grads["z"] = dp_halves(early, far[0], 1)
+            return [grads["z"][-1]]
+
+        def mid_filler(gate):
+            source = tie(mid_came, gate)[0]
+            grads["mid"] = second_send(scalars, late, source)
+            return grads["mid"]
+
+        parts_one = sum_parts(sums, ((), (early_z_filler,), (mid_filler,)))
+        mid_out, mid_keep = grads["mid"]
+        *parts_one, mid_out, early_came = tie(*parts_one, mid_out, grads["z"][-1])
+        early = dp_halves(grads["z"][:-1] + [early_came], far[1], 0)
         mid_came = core_swap(mid_out, 2, near)
-        head = dp_halves(head, far[1], 0)
         d_one, in_send, in_keep = in_grad(send_half, parts_one, dy, *first_norm, x)
-        d_one, in_send, in_keep, mid_came, head[-1] = tie(d_one, in_send, in_keep, mid_came, head[-1])
+        d_one, in_send, in_keep, mid_came, early[-1] = tie(
+            d_one, in_send, in_keep, mid_came, early[-1]
+        )
         in_recv = swap(in_send, 1)
-        mid = dp_halves([by_bits(mid_keep), by_bits(mid_came)], far[0], 1)
-        early = dp_halves(early, far[1], 0)
         inner = [[sharded(in_keep), sharded(in_recv)]]
         in_out = first_send(scalars, inner)
+        mid = dp_halves([by_bits(mid_keep), by_bits(mid_came)], far[0], 1)
+        early_mine = jnp.concatenate([sum(early), sum(head)], 0)
+        d_one, in_out, early_mine = tie(d_one, in_out, early_mine)
         in_came = core_swap(in_out, near, 2)
-        d_one = tie(d_one, in_out)[0]
+        early_far = swap(early_mine, 2)
+        early_core = swap(early_mine, 1)
         grad_x = pixels_grad(d_one, conv_in, wide, slope, micro)
-        grad_x, in_came, mid[-1], early[-1] = tie(grad_x, in_came, mid[-1], early[-1])
+        grad_x, in_came, mid[-1], early_core = tie(grad_x, in_came, mid[-1], early_core)
         in_out, in_keep = second_send(scalars, inner, in_came)
         in_came = core_swap(in_out, 2, near)
         mid = dp_halves(mid, far[1], 0)
-        early_pieces = gathered(jnp.concatenate([sum(early), sum(head)], 0))
         inner = dp_halves([by_bits(in_keep), by_bits(in_came)], far[0], 1)
+        early_far = tie(early_far, inner[-1])[0]
+        early_pieces = [early_mine, early_far, early_core, swap(early_far, 1)]
         inner = dp_halves(inner, far[1], 0)
-        late_pieces = gathered(jnp.concatenate([sum(mid), sum(inner)], 0))
-
         channel = channels // shards
-        grad_conv_out, grad_embed, grad_protos, grad_head = placed_pieces(
+        early_grads = placed_pieces(
             place_early_body,
             scalars,
             early_pieces,
@@ -1623,11 +1701,16 @@
                 shape((channel, head_weight.shape[1])),
             ],
         )
+        late_mine = jnp.concatenate([sum(mid), sum(inner)], 0)
+        late_far = swap(late_mine, 2)
+        late_core = swap(late_mine, 1)
+        late_far, late_core, *early_grads = tie(late_far, late_core, *early_grads)
+        grad_conv_out, grad_embed, grad_protos, grad_head = early_grads
         grad_protos = grad_protos[:, :protos]
         grad_conv_mid, grad_conv_in = placed_pieces(
             place_late_body,
             scalars,
-            late_pieces,
+            [late_mine, late_far, late_core, swap(late_far, 1)],
             [
                 shape((conv_mid.shape[0] // shards, conv_mid.shape[1])),
                 shape((channel, conv_in.shape[1])),
@@ -1640,7 +1723,7 @@
             return lax.psum(lax.psum_scatter(array, "dp", scatter_dimension=0, tiled=True), "hst")
 
         parts_three = sum_parts(sums)
-        d_three, dy, sums = from_third(parts_three)
+        dy, sums, out_low, out_high = from_third(low, parts_three)
         parts_two = sum_parts(sums)
         ins = [*parts_two, dy, *second_norm, act_one]
         d_two, mid_low = mid_grad("mid_first", mid_first_body, low, ins, act_one, True)
@@ -1649,9 +1732,11 @@
         parts_one = sum_parts(sums)
         d_one, in_low, in_high = in_grad(low, parts_one, dy, *first_norm, x)
         grad_x = pixels_grad(d_one, conv_in, wide, slope, micro)
-        out = out_grad(low, act_two, d_three, shards)
+        out = jnp.stack([out_low, out_high])
         out = out.reshape(2, shards, -1, conv_out.shape[0] // shards, out.shape[-1])
-        small_protos, small_embed = unpack_small(packed, table.shape, embed_weight.shape)
+        small_protos, small_embed = unpack_small(
+            [small_keep, small_send], table.shape, embed_weight.shape
+        )
         grad_conv_out = reduced(out.transpose(1, 3, 0, 2, 4).reshape(conv_out.shape))
         grad_conv_mid = reduced(jnp.concatenate([mid_low, mid_high], 1))
         grad_conv_in = reduced(jnp.concatenate([in_low, in_high], 1))

time: 574 us -> 526 us (0.916)
  Pallas kernels: 252 us -> 226 us
  local copies, waits for them, and re-layouts: 36.8 us -> 26.3 us
  waiting for transfers between devices: 144 us -> 135 us
    pallas_call x7 -> x6, Pallas kernels: 45.2 us -> 24.5 us  [the longest x3 13.1 us: second_send(): run(named('second_send', body), (shards // 4,), specs, [out, out], [shape...]
    ppermute x102, waiting for transfers between devices: 130 us -> 111 us  [swap(): return lax.ppermute(value, AXES, [(i, i ^ mask) for i in range(count)])]
    ppermute x6, waiting for transfers between devices: 14.1 us -> 23.3 us  [core_swap(): return lax.ppermute(value, AXES, pairs)]
    unnamed x204 -> x192, local copies, waits for them, and re-layouts: 16.9 us -> 9.98 us
  transfers between devices with their start and end apart: 108 -> 108, of which waited for: 59 -> 64; matrix products, arithmetic and copies ran while one was open for 2% -> 4% of each run, Pallas kernels for 26% -> 28%
where the time goes in v3:
time: 526 us; the launch traced here: 516 us
  Pallas kernels  226 us (43%)
  waiting for transfers between devices  135 us (26%)
  starting transfers between devices  109 us (21%)
  local copies, waits for them, and re-layouts  26.3 us (5%)
  other arithmetic  17.4 us (3%)
    ppermute x102, waiting for transfers between devices, swap(): return lax.ppermute(value, AXES, [(i, i ^ mask) for i in range(count)])  111 us
    ppermute x102, starting transfers between devices, swap(): return lax.ppermute(value, AXES, [(i, i ^ mask) for i in range(count)])  103 us
    pallas_call x2, Pallas kernels, mid_grad(): run(named(name, body, *([len(ins) - 7] if with_d else [])), (TAPS,), [who...  26.2 us
    ppermute x6, waiting for transfers between devices, core_swap(): return lax.ppermute(value, AXES, pairs)  23.3 us
    pallas_call x4, Pallas kernels, slope_part(): run(slope_body, (channels // width,), [tile, tile, pl.BlockSpec((rows, 1)...  23.2 us
    pallas_call x1, Pallas kernels, third_back(): run(named('third_back', third_back_body, len(parts)), (micro,), [per_micr...  18.9 us
    pallas_call x1, Pallas kernels, second_back(): run(second_back_body, (micro,), [mid, whole(weight), pl.BlockSpec((rows,...  17.2 us
    pallas_call x1, Pallas kernels, second_product(): run(named('second_product', second_body, len(parts)), (micro,), [per_micr...  16.6 us
  transfers between devices with their start and end apart: 108, of which 64 were waited for; matrix products, arithmetic and copies ran while one was open for 4% of the time, Pallas kernels for 28%

profile of v3, /device:TPU:0, one launch (start us, length us, event | category | flops | bytes accessed | tf_op | source)
XLA Modules:
  0.0 515.7 jit_solution(2165823900925232752)
XLA Ops:
  2.7 9.3 %first_body.1 = (f32[2048,512]{1,0:T(8,128)}, f32[4,3,512]{2,1,0:T(4,128)}) custom-call(bf16[2048,2048]{1,0:T(8,128)(2,1)} %bitcast.157, bf16[2048,512]{1,0:T(8,128)(2,1)} %w_ref.7, f32[2048,1]{1,0:T(8,128)} %copy.139.v_ref.refs_5_.refs_9_.refs_10_.refs_2_.refs_8_.refs_7_), custom_call_target="tpu_custom_call" | custom-call | flops 4294967296 | bytes 8388608 | tf_op jit(solution)/shard_map/first_body/pallas_call | solution.py:247
  19.0 4.6 collective-permute-done.3
  23.7 3.7 collective-permute-start.6
  32.8 16.6 %second_product.1 = (bf16[2048,512]{1,0:T(8,128)(2,1)}, f32[2048,512]{1,0:T(8,128)}, f32[4,2,512]{2,1,0:T(2,128)}, f32[4,3,512]{2,1,0:T(4,128)}) custom-call(f32[4,3,512]{2,1,0:T(4,128)} %copy-done.47, f32[4,3,512]{2,1,0:T(4,128)} %copy-done.80, f32[4,3,512]{2,1,0:T(4,128)} %copy-done.79, f32[4,3,512]{2,1,0:T(4,128)} %copy-done.78, ...), custom_call_target="tpu_custom_call" | custom-call | flops 9663676416 | bytes 10485760 | tf_op jit(solution)/shard_map/second_product/pallas_call | solution.py:319
  64.7 12.1 %third_product.1 = (bf16[2048,512]{1,0:T(8,128)(2,1)}, bf16[2048,2048]{1,0:T(8,128)(2,1)}, f32[4,2,2048]{2,1,0:T(2,128)}, f32[4,2,512]{2,1,0:T(2,128)}) custom-call(f32[4,2,512]{2,1,0:T(2,128)} %copy-done.88, f32[4,2,512]{2,1,0:T(2,128)} %copy-done.91, f32[4,2,512]{2,1,0:T(2,128)} %copy-done.90, f32[4,2,512]{2,1,0:T(2,128)} %copy-done.89, ...), custom_call_target="tpu_custom_call" | custom-call | flops 4294967296 | bytes 16777216 | tf_op jit(solution)/shard_map/third_product/pallas_call | solution.py:370
  96.7 13.3 %pool.1 = (f32[64,2048]{1,0:T(8,128)}, f32[4,2,2048]{2,1,0:T(2,128)}) custom-call(f32[4,2,2048]{2,1,0:T(2,128)} %copy-done.35, f32[4,2,2048]{2,1,0:T(2,128)} %copy-done.50, f32[4,2,2048]{2,1,0:T(2,128)} %copy-done.49, f32[4,2,2048]{2,1,0:T(2,128)} %copy-done.48, f32[4,3,512]{2,1,0:T(4,128)} %copy-done.47, f32[4,3,512]{2,1,0:T(4,128)} %copy-done.80, ...), custom_call_target="tpu_custom_call" | custom-call | flops 83886080 | bytes 16777216 | tf_op jit(solution)/shard_map/pool/pallas_call | solution.py:446
  113.5 6.3 %head_body.1 = (f32[64,2048]{1,0:T(8,128)}, f32[4,2,2048]{2,1,0:T(2,128)}) custom-call(f32[64,2048]{1,0:T(8,128)} %get-tuple-element.214.feat_ref, bf16[2048,2048]{1,0:T(8,128)(2,1)} %refs_8_.3), custom_call_target="tpu_custom_call" | custom-call | flops 536870912 | bytes 8388608 | tf_op jit(solution)/shard_map/head_body/pallas_call | solution.py:544
  126.9 5.8 %slope_body.4 = (bf16[2048,2048]{1,0:T(8,128)(2,1)}, f32[64,2048]{1,0:T(8,128)}, f32[64,2048]{1,0:T(8,128)}) custom-call(bf16[2048,2048]{1,0:T(8,128)(2,1)} %get-tuple-element.244.refs_8_.refs_0_.refs_7_, bf16[2048,2048]{1,0:T(8,128)(2,1)} %bitcast.159, f32[2048,1]{1,0:T(8,128)} %copy.139.v_ref.refs_5_.refs_9_.refs_10_.refs_2_.refs_8_.refs_7_, ...), custom_call_target="tpu_custom_call" | custom-call | flops 31457280 | bytes 6291456 | tf_op jit(solution)/shard_map/slope_body/pallas_call | solution.py:503
  138.8 5.7 %slope_body.5 = (bf16[2048,2048]{1,0:T(8,128)(2,1)}, f32[64,2048]{1,0:T(8,128)}, f32[64,2048]{1,0:T(8,128)}) custom-call(bf16[2048,2048]{1,0:T(8,128)(2,1)} %get-tuple-element.244.refs_8_.refs_0_.refs_7_, bf16[2048,2048]{1,0:T(8,128)(2,1)} %bitcast.160, ...), custom_call_target="tpu_custom_call", output_to_operand_aliasing={{0}: (6, {}), {1}: (7, {}), {2}: (8, {})} | custom-call | flops 31457280 | bytes 6291456 | tf_op jit(solution)/shard_map/slope_body/pallas_call | solution.py:503
  154.6 5.8 %slope_body.6 = (bf16[2048,2048]{1,0:T(8,128)(2,1)}, f32[64,2048]{1,0:T(8,128)}, f32[64,2048]{1,0:T(8,128)}) custom-call(bf16[2048,2048]{1,0:T(8,128)(2,1)} %get-tuple-element.244.refs_8_.refs_0_.refs_7_, bf16[2048,2048]{1,0:T(8,128)(2,1)} %bitcast.161, ...), custom_call_target="tpu_custom_call", output_to_operand_aliasing={{0}: (6, {}), {1}: (7, {}), {2}: (8, {})} | custom-call | flops 31457280 | bytes 6291456 | tf_op jit(solution)/shard_map/slope_body/pallas_call | solution.py:503
  164.9 5.9 %slope_body.7 = (bf16[2048,2048]{1,0:T(8,128)(2,1)}, f32[64,2048]{1,0:T(8,128)}, f32[64,2048]{1,0:T(8,128)}) custom-call(bf16[2048,2048]{1,0:T(8,128)(2,1)} %get-tuple-element.244.refs_8_.refs_0_.refs_7_, bf16[2048,2048]{1,0:T(8,128)(2,1)} %bitcast.162, ...), custom_call_target="tpu_custom_call", output_to_operand_aliasing={{0}: (6, {}), {1}: (7, {}), {2}: (8, {})} | custom-call | flops 31457280 | bytes 6291456 | tf_op jit(solution)/shard_map/slope_body/pallas_call | solution.py:503
  211.2 6.4 %loss.1 = (f32[8,80,512]{2,1,0:T(8,128)}, f32[8,80,512]{2,1,0:T(8,128)}, f32[64,2048]{1,0:T(8,128)}, f32[8,2304]{1,0:T(8,128)}) custom-call(s32[1]{0:T(128)} %bitcast.refs_0_, f32[4,3072]{1,0:T(4,128)} %copy-done.42, f32[4,3072]{1,0:T(4,128)} %copy-done.71, f32[4,3072]{1,0:T(4,128)} %copy-done.70, f32[4,3072]{1,0:T(4,128)} %copy-done.69, ...), custom_call_target="tpu_custom_call" | custom-call | flops 201326592 | bytes 3145728 | tf_op jit(solution)/shard_map/loss/pallas_call | solution.py:1215
  238.3 7.8 %head_back.1 = (f32[64,2048]{1,0:T(8,128)}, f32[256,2048]{1,0:T(8,128)}, f32[4,2,2048]{2,1,0:T(2,128)}) custom-call(f32[8,2304]{1,0:T(8,128)} %copy-done.19, f32[8,2304]{1,0:T(8,128)} %copy-done.33, f32[8,2304]{1,0:T(8,128)} %copy-done.31, f32[8,2304]{1,0:T(8,128)} %copy-done.29, f32[64,2048]{1,0:T(8,128)} %get-tuple-element.272.refs_4_, ...), custom_call_target="tpu_custom_call" | custom-call | flops 536870912 | bytes 8388608 | tf_op jit(solution)/shard_map/head_back/pallas_call | solution.py:601
  246.2 5.7 %collective-permute-done.57 = f32[128,1024]{1,0:T(8,128)S(1)} collective-permute-done((f32[128,1024]{1,0:T(8,128)}, f32[128,1024]{1,0:T(8,128)S(1)}, u32[]{:S(2)}, u32[]{:S(2)}) %collective-permute-start.57) | collective-permute-done | bytes 524320 | tf_op jit(solution)/shard_map/ppermute | solution.py:32
  275.8 18.9 %third_back.1 = (f32[2048,512]{1,0:T(8,128)}, f32[4,2,512]{2,1,0:T(2,128)}, f32[8,128,512]{2,1,0:T(8,128)}, f32[8,128,512]{2,1,0:T(8,128)}) custom-call(s32[1]{0:T(128)S(6)} %sub.184.refs_0_, f32[4,2,2048]{2,1,0:T(2,128)} %bitcast.209, f32[4,2,2048]{2,1,0:T(2,128)} %copy-done.55, f32[4,2,2048]{2,1,0:T(2,128)} %copy-done.53, f32[4,2,2048]{2,1,0:T(2,128)} %copy-done.51, ...), custom_call_target="tpu_custom_call" | custom-call | flops 8589934592 | bytes 25165824 | tf_op jit(solution)/shard_map/third_back/pallas_call | solution.py:703
  311.5 3.9 first_send.3
  316.4 14.8 %mid_first.1 = (bf16[2048,512]{1,0:T(8,128)(2,1)}, f32[4608,256]{1,0:T(8,128)}) custom-call(s32[1]{0:T(128)S(6)} %sub.184.refs_0_, f32[4,2,512]{2,1,0:T(2,128)} %bitcast.241, f32[4,2,512]{2,1,0:T(2,128)} %copy-done.86, f32[4,2,512]{2,1,0:T(2,128)} %copy-done.84, f32[4,2,512]{2,1,0:T(2,128)} %copy-done.82, f32[2048,512]{1,0:T(8,128)} %get-tuple-element.327.refs_5_, ...), custom_call_target="tpu_custom_call" | custom-call | flops 4831838208 | bytes 4718592 | tf_op jit(solution)/shard_map/mid_first/pallas_call | solution.py:816
  331.2 6.4 %collective-permute-done.79.refs_17_.refs_18_.refs_19_.refs_20_ = f32[8,104,512]{2,1,0:T(8,128)S(1)} collective-permute-done((f32[8,104,512]{2,1,0:T(8,128)}, f32[8,104,512]{2,1,0:T(8,128)S(1)}, u32[]{:S(2)}, u32[]{:S(2)}) %collective-permute-start.79) | collective-permute-done | bytes 1703968 | tf_op jit(solution)/shard_map/ppermute | solution.py:126
  339.5 4.5 second_send.3
  345.1 11.3 %mid_second.1 = f32[4608,256]{1,0:T(8,128)} custom-call(s32[1]{0:T(128)} %bitcast.refs_0_, bf16[2048,512]{1,0:T(8,128)(2,1)} %get-tuple-element.339.refs_1_.d_ref, bf16[2048,512]{1,0:T(8,128)(2,1)} %get-tuple-element.328.refs_11_.refs_2_), custom_call_target="tpu_custom_call" | custom-call | flops 4831838208 | bytes 4718592 | tf_op jit(solution)/shard_map/mid_second/pallas_call | solution.py:816
  356.5 8.0 %collective-permute-done.82 = f32[2,256,512]{2,1,0:T(8,128)S(1)} collective-permute-done((f32[2,256,512]{2,1,0:T(8,128)S(1)}, f32[2,256,512]{2,1,0:T(8,128)S(1)}, u32[]{:S(2)}, u32[]{:S(2)}) %collective-permute-start.82) | collective-permute-done | bytes 1048608 | tf_op jit(solution)/shard_map/ppermute | solution.py:32
  364.5 4.2 first_send.4
  371.6 17.2 %second_back_body.1 = (f32[2048,512]{1,0:T(8,128)}, f32[4,2,512]{2,1,0:T(2,128)}) custom-call(bf16[2048,512]{1,0:T(8,128)(2,1)} %get-tuple-element.339.refs_1_.d_ref, bf16[4608,512]{1,0:T(8,128)(2,1)} %w_ref.6, f32[2048,1]{1,0:T(8,128)} %copy.139.v_ref.refs_5_.refs_9_.refs_10_.refs_2_.refs_8_.refs_7_, f32[2048,512]{1,0:T(8,128)} %get-tuple-element.209.refs_4_.h1_ref.refs_6_, ...), custom_call_target="tpu_custom_call" | custom-call | flops 9663676416 | bytes 10485760 | tf_op jit(solution)/shard_map/second_back_body/pallas_call | solution.py:901
  388.8 6.9 %collective-permute-done.84 = f32[256,512]{1,0:T(8,128)S(1)} collective-permute-done((f32[256,512]{1,0:T(8,128)S(1)}, f32[256,512]{1,0:T(8,128)S(1)}, u32[]{:S(2)}, u32[]{:S(2)}) %collective-permute-start.84) | collective-permute-done | bytes 524320 | tf_op jit(solution)/shard_map/ppermute | solution.py:32
  412.3 5.0 second_send.4
  419.1 12.7 %in_grad.1 = (bf16[2048,512]{1,0:T(8,128)(2,1)}, f32[2048,256]{1,0:T(8,128)}, f32[2048,256]{1,0:T(8,128)}) custom-call(s32[1]{0:T(128)S(6)} %sub.184.refs_0_, f32[4,2,512]{2,1,0:T(2,128)} %bitcast.228, f32[4,2,512]{2,1,0:T(2,128)} %copy-done.67, f32[4,2,512]{2,1,0:T(2,128)} %copy-done.65, f32[4,2,512]{2,1,0:T(2,128)} %copy-done.63, ...), custom_call_target="tpu_custom_call" | custom-call | flops 4294967296 | bytes 23068672 | tf_op jit(solution)/shard_map/in_grad/pallas_call | solution.py:857
  445.3 11.5 %pixels_body.1 = bf16[2048,2048]{1,0:T(8,128)(2,1)} custom-call(bf16[2048,512]{1,0:T(8,128)(2,1)} %get-tuple-element.376.d_ref, bf16[2048,512]{1,0:T(8,128)(2,1)} %w_ref.7, f32[256,2048]{1,0:T(8,128)} %get-tuple-element.291.refs_5_.wide_ref, bf16[2048,2048]{1,0:T(8,128)(2,1)} %get-tuple-element.245.refs_6_.slope_ref), custom_call_target="tpu_custom_call" | custom-call | flops 4294967296 | bytes 16777216 | tf_op jit(solution)/shard_map/pixels_body/pallas_call | solution.py:941
  467.3 12.7 %collective-permute-done.100 = f32[4,128,256]{2,1,0:T(8,128)S(1)} collective-permute-done((f32[4,128,256]{2,1,0:T(8,128)}, f32[4,128,256]{2,1,0:T(8,128)S(1)}, u32[]{:S(2)}, u32[]{:S(2)}) %collective-permute-start.100) | collective-permute-done | bytes 524320 | tf_op jit(solution)/shard_map/ppermute | solution.py:126
  484.4 5.7 %collective-permute-done.101 = f32[2,128,256]{2,1,0:T(8,128)S(1)} collective-permute-done((f32[2,128,256]{2,1,0:T(8,128)S(1)}, f32[2,128,256]{2,1,0:T(8,128)S(1)}, u32[]{:S(2)}, u32[]{:S(2)}) %collective-permute-start.101) | collective-permute-done | bytes 262176 | tf_op jit(solution)/shard_map/ppermute | solution.py:32
  490.2 5.3 %collective-permute-done.99 = f32[288,256]{1,0:T(8,128)S(1)} collective-permute-done((f32[288,256]{1,0:T(8,128)S(1)}, f32[288,256]{1,0:T(8,128)S(1)}, u32[]{:S(2)}, u32[]{:S(2)}) %collective-permute-start.99) | collective-permute-done | bytes 294944 | tf_op jit(solution)/shard_map/ppermute | solution.py:32
  499.2 4.2 place_early_body.1
  503.4 6.0 %collective-permute-done.103.far_ref = f32[416,256]{1,0:T(8,128)S(1)} collective-permute-done((f32[416,256]{1,0:T(8,128)S(1)}, f32[416,256]{1,0:T(8,128)S(1)}, u32[]{:S(2)}, u32[]{:S(2)}) %collective-permute-start.103) | collective-permute-done | bytes 426016 | tf_op jit(solution)/shard_map/ppermute | solution.py:32
  (489 shorter events, 245.0 us)
Async XLA Ops:
  123.4 9.4 %collective-permute-start.25 = (f32[4,2,2048]{2,1,0:T(2,128)S(1)}, f32[4,2,2048]{2,1,0:T(2,128)S(1)}, u32[]{:S(2)}, u32[]{:S(2)}) collective-permute-start(f32[4,2,2048]{2,1,0:T(2,128)S(1)} %pad_maximum_fusion.5), channel_id=1, source_target_pairs={{0,6},{1,7},{2,4},{3,5},{4,2},{5,3},{6,0},{7,1},{8,14},{9,15},{10,... | collective-permute-start | bytes 196616 | tf_op jit(solution)/shard_map/ppermute | solution.py:32
  133.1 11.4 %collective-permute-start.28 = (f32[4,2,2048]{2,1,0:T(2,128)S(1)}, f32[4,2,2048]{2,1,0:T(2,128)S(1)}, u32[]{:S(2)}, u32[]{:S(2)}) collective-permute-start(f32[4,2,2048]{2,1,0:T(2,128)S(1)} %pad_maximum_fusion.6.refs_0_), channel_id=1, source_target_pairs={{0,24},{1,25},{2,26},{3,27},{4,28},{5,29},{6,30},{7,31},{8,16},{9,... | collective-permute-start | bytes 196616 | tf_op jit(solution)/shard_map/ppermute | solution.py:32
  135.0 9.5 %collective-permute-start.27 = (f32[4,2,2048]{2,1,0:T(2,128)S(1)}, f32[4,2,2048]{2,1,0:T(2,128)S(1)}, u32[]{:S(2)}, u32[]{:S(2)}) collective-permute-start(f32[4,2,2048]{2,1,0:T(2,128)S(1)} %pad_maximum_fusion.6.refs_0_), channel_id=1, source_target_pairs={{0,16},{1,17},{2,18},{3,19},{4,20},{5,21},{6,22},{7,23},{8,24},{9,... | collective-permute-start | bytes 196616 | tf_op jit(solution)/shard_map/ppermute | solution.py:32
  135.0 9.6 %collective-permute-start.26 = (f32[4,2,2048]{2,1,0:T(2,128)S(1)}, f32[4,2,2048]{2,1,0:T(2,128)S(1)}, u32[]{:S(2)}, u32[]{:S(2)}) collective-permute-start(f32[4,2,2048]{2,1,0:T(2,128)S(1)} %pad_maximum_fusion.6.refs_0_), channel_id=1, source_target_pairs={{0,8},{1,9},{2,10},{3,11},{4,12},{5,13},{6,14},{7,15},{8,0},{9,1},... | collective-permute-start | bytes 196616 | tf_op jit(solution)/shard_map/ppermute | solution.py:32
  151.1 9.3 %collective-permute-start.32 = (f32[4,3072]{1,0:T(4,128)S(1)}, f32[4,3072]{1,0:T(4,128)S(1)}, u32[]{:S(2)}, u32[]{:S(2)}) collective-permute-start(f32[4,3072]{1,0:T(4,128)S(1)} %add.767), channel_id=1, source_target_pairs={{0,6},{1,7},{2,4},{3,5},{4,2},{5,3},{6,0},{7,1},{8,14},{9,15},{10,... | collective-permute-start | bytes 147464 | tf_op jit(solution)/shard_map/ppermute | solution.py:32
  160.5 10.3 %collective-permute-start.35 = (f32[4,3072]{1,0:T(4,128)S(1)}, f32[4,3072]{1,0:T(4,128)S(1)}, u32[]{:S(2)}, u32[]{:S(2)}) collective-permute-start(f32[4,3072]{1,0:T(4,128)S(1)} %add_add_fusion.6.refs_0_), channel_id=1, source_target_pairs={{0,24},{1,25},{2,26},{3,27},{4,28},{5,29},{6,30},{7,31},{8,16},{9,... | collective-permute-start | bytes 147464 | tf_op jit(solution)/shard_map/ppermute | solution.py:32
  236.4 15.4 %collective-permute-start.58 = (f32[8,80,512]{2,1,0:T(8,128)}, f32[8,80,512]{2,1,0:T(8,128)S(1)}, u32[]{:S(2)}, u32[]{:S(2)}) collective-permute-start(f32[8,80,512]{2,1,0:T(8,128)} %get-tuple-element.277), channel_id=1, source_target_pairs={{0,1},{1,0},{2,3},{3,2},{4,5},{5,4},{6,7},{7,6},{8,9},{9,8},{10,11... | collective-permute-start | bytes 3932168 | tf_op jit(solution)/shard_map/ppermute | solution.py:32
  237.3 14.5 %collective-permute-start.57 = (f32[128,1024]{1,0:T(8,128)}, f32[128,1024]{1,0:T(8,128)S(1)}, u32[]{:S(2)}, u32[]{:S(2)}) collective-permute-start(f32[128,1024]{1,0:T(8,128)} %pad_maximum_fusion.1), channel_id=1, source_target_pairs={{0,2},{1,3},{2,0},{3,1},{4,6},{5,7},{6,4},{7,5},{8,10},{9,11},{10,... | collective-permute-start | bytes 1572872 | tf_op jit(solution)/shard_map/ppermute | solution.py:32
  272.3 22.5 %collective-permute-start.70 = (f32[128,512]{1,0:T(8,128)S(1)}, f32[128,512]{1,0:T(8,128)S(1)}, u32[]{:S(2)}, u32[]{:S(2)}) collective-permute-start(f32[128,512]{1,0:T(8,128)S(1)} %get-tuple-element.298), channel_id=1, source_target_pairs={{0,6},{1,7},{2,4},{3,5},{4,2},{5,3},{6,0},{7,1},{8,14},{9,15},{10,... | collective-permute-start | bytes 786440 | tf_op jit(solution)/shard_map/ppermute | solution.py:32
  273.6 21.2 %collective-permute-start.68 = (f32[128,512]{1,0:T(8,128)S(1)}, f32[128,512]{1,0:T(8,128)S(1)}, u32[]{:S(2)}, u32[]{:S(2)}) collective-permute-start(f32[128,512]{1,0:T(8,128)S(1)} %get-tuple-element.298), channel_id=1, source_target_pairs={{0,2},{1,3},{2,0},{3,1},{4,6},{5,7},{6,4},{7,5},{8,10},{9,11},{10,... | collective-permute-start | bytes 786440 | tf_op jit(solution)/shard_map/ppermute | solution.py:32
  274.6 20.3 %collective-permute-start.69 = (f32[128,512]{1,0:T(8,128)S(1)}, f32[128,512]{1,0:T(8,128)S(1)}, u32[]{:S(2)}, u32[]{:S(2)}) collective-permute-start(f32[128,512]{1,0:T(8,128)S(1)} %get-tuple-element.299.dg_ref), channel_id=1, source_target_pairs={{0,4},{1,5},{2,6},{3,7},{4,0},{5,1},{6,2},{7,3},{8,12},{9,13},{10,... | collective-permute-start | bytes 786440 | tf_op jit(solution)/shard_map/ppermute | solution.py:32
  303.5 11.9 %collective-permute-start.78 = (f32[4,2,512]{2,1,0:T(2,128)S(1)}, f32[4,2,512]{2,1,0:T(2,128)S(1)}, u32[]{:S(2)}, u32[]{:S(2)}) collective-permute-start(f32[4,2,512]{2,1,0:T(2,128)S(1)} %bitcast.238), channel_id=1, source_target_pairs={{0,24},{1,25},{2,26},{3,27},{4,28},{5,29},{6,30},{7,31},{8,16},{9,... | collective-permute-start | bytes 49160 | tf_op jit(solution)/shard_map/ppermute | solution.py:32
  305.5 9.8 %collective-permute-start.77 = (f32[4,2,512]{2,1,0:T(2,128)S(1)}, f32[4,2,512]{2,1,0:T(2,128)S(1)}, u32[]{:S(2)}, u32[]{:S(2)}) collective-permute-start(f32[4,2,512]{2,1,0:T(2,128)S(1)} %bitcast.239), channel_id=1, source_target_pairs={{0,16},{1,17},{2,18},{3,19},{4,20},{5,21},{6,22},{7,23},{8,24},{9,... | collective-permute-start | bytes 49160 | tf_op jit(solution)/shard_map/ppermute | solution.py:32
  305.6 9.8 %collective-permute-start.76 = (f32[4,2,512]{2,1,0:T(2,128)S(1)}, f32[4,2,512]{2,1,0:T(2,128)S(1)}, u32[]{:S(2)}, u32[]{:S(2)}) collective-permute-start(f32[4,2,512]{2,1,0:T(2,128)S(1)} %bitcast.240), channel_id=1, source_target_pairs={{0,8},{1,9},{2,10},{3,11},{4,12},{5,13},{6,14},{7,15},{8,0},{9,1},... | collective-permute-start | bytes 49160 | tf_op jit(solution)/shard_map/ppermute | solution.py:32
  315.4 22.1 %collective-permute-start.79 = (f32[8,104,512]{2,1,0:T(8,128)}, f32[8,104,512]{2,1,0:T(8,128)S(1)}, u32[]{:S(2)}, u32[]{:S(2)}) collective-permute-start(f32[8,104,512]{2,1,0:T(8,128)} %first_send.3), channel_id=1, source_target_pairs={{0,4},{1,3},{2,6},{3,1},{4,0},{5,7},{6,2},{7,5},{8,12},{9,11},{10,... | collective-permute-start | bytes 5111816 | tf_op jit(solution)/shard_map/ppermute | solution.py:126
  337.5 26.9 %collective-permute-start.80 = (f32[4608,256]{1,0:T(8,128)}, f32[4608,256]{1,0:T(8,128)}, u32[]{:S(2)}, u32[]{:S(2)}) collective-permute-start(f32[4608,256]{1,0:T(8,128)} %get-tuple-element.333), channel_id=1, source_target_pairs={{0,1},{1,0},{2,3},{3,2},{4,5},{5,4},{6,7},{7,6},{8,9},{9,8},{10,11... | collective-permute-start | bytes 14155784 | tf_op jit(solution)/shard_map/ppermute | solution.py:32
  339.4 25.0 %collective-permute-start.82 = (f32[2,256,512]{2,1,0:T(8,128)S(1)}, f32[2,256,512]{2,1,0:T(8,128)S(1)}, u32[]{:S(2)}, u32[]{:S(2)}) collective-permute-start(f32[2,256,512]{2,1,0:T(8,128)S(1)} %dynamic-slice_bitcast_fusion), channel_id=1, source_target_pairs={{0,8},{1,9},{2,10},{3,11},{4,12},{5,13},{6,14},{7,15},{8,0},{9,1},... | collective-permute-start | bytes 3145736 | tf_op jit(solution)/shard_map/ppermute | solution.py:32
  344.0 20.5 %collective-permute-start.81 = (f32[4,104,512]{2,1,0:T(8,128)}, f32[4,104,512]{2,1,0:T(8,128)S(1)}, u32[]{:S(2)}, u32[]{:S(2)}) collective-permute-start(f32[4,104,512]{2,1,0:T(8,128)} %get-tuple-element.335), channel_id=1, source_target_pairs={{0,2},{1,5},{2,0},{3,7},{4,6},{5,1},{6,4},{7,3},{8,10},{9,13},{10,... | collective-permute-start | bytes 2555912 | tf_op jit(solution)/shard_map/ppermute | solution.py:126
  368.7 29.1 %collective-permute-start.83 = (f32[8,288,256]{2,1,0:T(8,128)}, f32[8,288,256]{2,1,0:T(8,128)S(1)}, u32[]{:S(2)}, u32[]{:S(2)}) collective-permute-start(f32[8,288,256]{2,1,0:T(8,128)} %first_send.4), channel_id=1, source_target_pairs={{0,4},{1,3},{2,6},{3,1},{4,0},{5,7},{6,2},{7,5},{8,12},{9,11},{10,... | collective-permute-start | bytes 7077896 | tf_op jit(solution)/shard_map/ppermute | solution.py:126
  370.7 24.9 %collective-permute-start.84 = (f32[256,512]{1,0:T(8,128)S(1)}, f32[256,512]{1,0:T(8,128)S(1)}, u32[]{:S(2)}, u32[]{:S(2)}) collective-permute-start(f32[256,512]{1,0:T(8,128)S(1)} %bitcast_add_fusion.1), channel_id=1, source_target_pairs={{0,16},{1,17},{2,18},{3,19},{4,20},{5,21},{6,22},{7,23},{8,24},{9,... | collective-permute-start | bytes 1572872 | tf_op jit(solution)/shard_map/ppermute | solution.py:32
  397.9 10.0 %collective-permute-start.89 = (f32[2,104,512]{2,1,0:T(8,128)S(1)}, f32[2,104,512]{2,1,0:T(8,128)S(1)}, u32[]{:S(2)}, u32[]{:S(2)}) collective-permute-start(f32[2,104,512]{2,1,0:T(8,128)S(1)} %add_bitcast_fusion.1), channel_id=1, source_target_pairs={{0,8},{1,9},{2,10},{3,11},{4,12},{5,13},{6,14},{7,15},{8,0},{9,1},... | collective-permute-start | bytes 1277960 | tf_op jit(solution)/shard_map/ppermute | solution.py:32
  407.9 9.5 %collective-permute-start.92 = (f32[4,2,512]{2,1,0:T(2,128)S(1)}, f32[4,2,512]{2,1,0:T(2,128)S(1)}, u32[]{:S(2)}, u32[]{:S(2)}) collective-permute-start(f32[4,2,512]{2,1,0:T(2,128)S(1)} %bitcast.225), channel_id=1, source_target_pairs={{0,24},{1,25},{2,26},{3,27},{4,28},{5,29},{6,30},{7,31},{8,16},{9,... | collective-permute-start | bytes 49160 | tf_op jit(solution)/shard_map/ppermute | solution.py:32
  417.4 16.5 %collective-permute-start.93 = (f32[4,288,256]{2,1,0:T(8,128)}, f32[4,288,256]{2,1,0:T(8,128)S(1)}, u32[]{:S(2)}, u32[]{:S(2)}) collective-permute-start(f32[4,288,256]{2,1,0:T(8,128)} %get-tuple-element.369), channel_id=1, source_target_pairs={{0,2},{1,5},{2,0},{3,7},{4,6},{5,1},{6,4},{7,3},{8,10},{9,13},{10,... | collective-permute-start | bytes 3538952 | tf_op jit(solution)/shard_map/ppermute | solution.py:126
  418.5 13.2 %collective-permute-start.94 = (f32[104,512]{1,0:T(8,128)S(1)}, f32[104,512]{1,0:T(8,128)S(1)}, u32[]{:S(2)}, u32[]{:S(2)}) collective-permute-start(f32[104,512]{1,0:T(8,128)S(1)} %bitcast_add_fusion.5), channel_id=1, source_target_pairs={{0,16},{1,17},{2,18},{3,19},{4,20},{5,21},{6,22},{7,23},{8,24},{9,... | collective-permute-start | bytes 638984 | tf_op jit(solution)/shard_map/ppermute | solution.py:32
  443.0 17.3 %collective-permute-start.96 = (f32[8,128,256]{2,1,0:T(8,128)}, f32[8,128,256]{2,1,0:T(8,128)S(1)}, u32[]{:S(2)}, u32[]{:S(2)}) collective-permute-start(f32[8,128,256]{2,1,0:T(8,128)} %first_send.5), channel_id=1, source_target_pairs={{0,4},{1,3},{2,6},{3,1},{4,0},{5,7},{6,2},{7,5},{8,12},{9,11},{10,... | collective-permute-start | bytes 3145736 | tf_op jit(solution)/shard_map/ppermute | solution.py:126
  444.4 15.9 %collective-permute-start.98 = (f32[360,512]{1,0:T(8,128)S(1)}, f32[360,512]{1,0:T(8,128)S(1)}, u32[]{:S(2)}, u32[]{:S(2)}) collective-permute-start(f32[360,512]{1,0:T(8,128)S(1)} %pad_maximum_fusion.mine_ref), channel_id=1, source_target_pairs={{0,1},{1,0},{2,3},{3,2},{4,5},{5,4},{6,7},{7,6},{8,9},{9,8},{10,11... | collective-permute-start | bytes 2211848 | tf_op jit(solution)/shard_map/ppermute | solution.py:32
  444.6 15.8 %collective-permute-start.97 = (f32[2,288,256]{2,1,0:T(8,128)S(1)}, f32[2,288,256]{2,1,0:T(8,128)S(1)}, u32[]{:S(2)}, u32[]{:S(2)}) collective-permute-start(f32[2,288,256]{2,1,0:T(8,128)S(1)} %add_bitcast_fusion), channel_id=1, source_target_pairs={{0,8},{1,9},{2,10},{3,11},{4,12},{5,13},{6,14},{7,15},{8,0},{9,1},... | collective-permute-start | bytes 1769480 | tf_op jit(solution)/shard_map/ppermute | solution.py:32
  465.0 15.1 %collective-permute-start.100 = (f32[4,128,256]{2,1,0:T(8,128)}, f32[4,128,256]{2,1,0:T(8,128)S(1)}, u32[]{:S(2)}, u32[]{:S(2)}) collective-permute-start(f32[4,128,256]{2,1,0:T(8,128)} %get-tuple-element.384), channel_id=1, source_target_pairs={{0,2},{1,5},{2,0},{3,7},{4,6},{5,1},{6,4},{7,3},{8,10},{9,13},{10,... | collective-permute-start | bytes 1572872 | tf_op jit(solution)/shard_map/ppermute | solution.py:126
  466.2 29.4 %collective-permute-start.105 = (f32[360,512]{1,0:T(8,128)S(1)}, f32[360,512]{1,0:T(8,128)S(1)}, u32[]{:S(2)}, u32[]{:S(2)}) collective-permute-start(f32[360,512]{1,0:T(8,128)S(1)} %pad_maximum_fusion.mine_ref), channel_id=1, source_target_pairs={{0,2},{1,3},{2,0},{3,1},{4,6},{5,7},{6,4},{7,5},{8,10},{9,11},{10,... | collective-permute-start | bytes 2211848 | tf_op jit(solution)/shard_map/ppermute | solution.py:32
  481.1 9.0 %collective-permute-start.101 = (f32[2,128,256]{2,1,0:T(8,128)S(1)}, f32[2,128,256]{2,1,0:T(8,128)S(1)}, u32[]{:S(2)}, u32[]{:S(2)}) collective-permute-start(f32[2,128,256]{2,1,0:T(8,128)S(1)} %add_bitcast_fusion.2), channel_id=1, source_target_pairs={{0,8},{1,9},{2,10},{3,11},{4,12},{5,13},{6,14},{7,15},{8,0},{9,1},... | collective-permute-start | bytes 786440 | tf_op jit(solution)/shard_map/ppermute | solution.py:32
  481.5 14.0 %collective-permute-start.99 = (f32[288,256]{1,0:T(8,128)S(1)}, f32[288,256]{1,0:T(8,128)S(1)}, u32[]{:S(2)}, u32[]{:S(2)}) collective-permute-start(f32[288,256]{1,0:T(8,128)S(1)} %bitcast_add_fusion.2), channel_id=1, source_target_pairs={{0,16},{1,17},{2,18},{3,19},{4,20},{5,21},{6,22},{7,23},{8,24},{9,... | collective-permute-start | bytes 884744 | tf_op jit(solution)/shard_map/ppermute | solution.py:32
  497.1 12.2 %collective-permute-start.103 = (f32[416,256]{1,0:T(8,128)S(1)}, f32[416,256]{1,0:T(8,128)S(1)}, u32[]{:S(2)}, u32[]{:S(2)}) collective-permute-start(f32[416,256]{1,0:T(8,128)S(1)} %pad_maximum_fusion.2.mine_ref), channel_id=1, source_target_pairs={{0,2},{1,3},{2,0},{3,1},{4,6},{5,7},{6,4},{7,5},{8,10},{9,11},{10,... | collective-permute-start | bytes 1277960 | tf_op jit(solution)/shard_map/ppermute | solution.py:32
  (168 other events, 1055.6 us)

commit v4 on v3

--- a/solution.py
+++ b/solution.py
@@ -146,7 +146,7 @@
         name=body.__name__,
         input_output_aliases=aliases or {},
         compiler_params=pltpu.CompilerParams(
-            vmem_limit_bytes=56 * MIB, dimension_semantics=("arbitrary",) * len(grid)
+            vmem_limit_bytes=52 * MIB, dimension_semantics=("arbitrary",) * len(grid)
         ),
         cost_estimate=pl.CostEstimate(
             flops=flops, bytes_accessed=bytes_accessed, transcendentals=0
@@ -410,119 +410,86 @@
         ref[(*index, (first + j) // LANES, place, slice(None))] = value[:, j : j + LANES]
 
 
-def pool_body(counts, refs):
-    part_refs, count_refs = refs[:counts], refs[counts : 2 * counts]
-    h_ref, x_ref, v_ref, gain_ref, shift_ref, size_ref, feat_ref, info_ref, sums_ref = refs[2 * counts :]
+def pool_body(counts, split, refs):
+    scalars_ref, part_refs, count_refs = refs[0], refs[1 : 1 + counts], refs[1 + counts : 1 + 2 * counts]
+    h_ref, x_ref, v_ref, gain_ref, shift_ref, size_ref = refs[1 + 2 * counts : 7 + 2 * counts]
+    feat_ref, info_ref, slope_ref, first_ref, second_ref = refs[7 + 2 * counts : 12 + 2 * counts]
+    sums_ref = refs[-1]
     rows, width = h_ref.shape
     mean, scaled = norm_of(part_refs, counts_of(count_refs))
     info_ref[0, 0:1, :] = mean
     info_ref[0, 1:2, :] = scaled
     factor = scaled * gain_ref[...]
     shift = shift_ref[...]
-    for j in range(0, width, 512):
-        lane = slice(j, j + 512)
+    chunk = 256
+    for j in range(0, width, chunk):
+        lane = slice(j, j + chunk)
         for k in range(rows // PIX):
-            acc = jnp.zeros((COLS, 512), F32)
+            acc = jnp.zeros((COLS, chunk), F32)
+            acc_first = jnp.zeros((COLS, chunk), F32)
+            acc_second = jnp.zeros((COLS, chunk), F32)
             for r in range(ROWS):
                 at = pl.ds(k * PIX + r * COLS, COLS)
-                resid = (
-                    (h_ref[at, lane].astype(F32) - mean[:, lane]) * factor[:, lane]
-                    + shift[:, lane]
-                    + x_ref[at, lane].astype(F32)
-                )
-                out = resid * (sigmoid(resid) * v_ref[at, :])
+                centred = h_ref[at, lane].astype(F32) - mean[:, lane]
+                resid = centred * factor[:, lane] + shift[:, lane] + x_ref[at, lane].astype(F32)
+                sig = sigmoid(resid)
+                kept = sig * v_ref[at, :]
+                out = resid * kept
                 acc += out.astype(BF16).astype(F32)
-            put_lanes(sums_ref, pl.ds(k * COLS, COLS), j, acc)
-    feat_ref[...] = (crop_sums(sums_ref) / size_ref[...]).astype(BF16).astype(F32)
-
-
-def pool(parts, members, h3, x, valid, gain, shift, sizes, micro):
+                slope = kept + out * (1.0 - sig)
+                acc_first += slope
+                acc_second += slope * centred
+                slope_ref[at, lane] = slope.astype(BF16)
+            place = pl.ds(k * COLS, COLS)
+            put_lanes(sums_ref, place, j, acc, 0)
+            put_lanes(sums_ref, place, j, acc_first, 1)
+            put_lanes(sums_ref, place, j, acc_second * scaled[:, lane], 2)
+    feat = (crop_sums(sums_ref, 0) / size_ref[...]).astype(BF16).astype(F32)
+    feat_ref[...] = feat
+    first_ref[...] = crop_sums(sums_ref, 1)
+    second_ref[...] = crop_sums(sums_ref, 2)
+    if split:
+        keep_ref, send_ref = refs[12 + 2 * counts : 14 + 2 * counts]
+        low = scalars_ref[1] == 0
+        for i in range(0, width, 2 * split):
+            one, two = feat[:, i : i + split], feat[:, i + split : i + 2 * split]
+            place = slice(i // 2, i // 2 + split)
+            keep_ref[:, place] = jnp.where(low, one, two)
+            send_ref[:, place] = jnp.where(low, two, one)
+
+
+def pool(scalars, parts, members, h3, x, valid, gain, shift, sizes, micro, split):
     rows, channels = h3.shape[0] // micro, h3.shape[1]
     crops = sizes.shape[0] // micro
     width = 1024
-    tile = pl.BlockSpec((rows, width), lambda m, c: (m, c))
-    line = pl.BlockSpec((1, width), lambda m, c: (0, c))
-    pair = pl.BlockSpec((1, 2, width), lambda m, c: (m, 0, c))
+    tile = pl.BlockSpec((rows, width), lambda m, c, w: (m, c))
+    line = pl.BlockSpec((1, width), lambda m, c, w: (0, c))
+    pair = pl.BlockSpec((1, 2, width), lambda m, c, w: (m, 0, c))
+    small = pl.BlockSpec((crops, width), lambda m, c, w: (m, c))
+    part = pl.BlockSpec((crops, width // 2), lambda m, c, w: (m, c))
+    lines = shape((micro * crops, channels))
+    half = shape((micro * crops, channels // 2))
     return run(
-        named("pool", pool_body, len(parts)),
+        named("pool", pool_body, len(parts), split),
         (micro, channels // width),
         [pair] * len(parts)
         + [per_micro(part) for part in members]
         + [
             tile,
             tile,
-            pl.BlockSpec((rows, 1), lambda m, c: (m, 0)),
+            pl.BlockSpec((rows, 1), lambda m, c, w: (m, 0)),
             line,
             line,
-            pl.BlockSpec((crops, 1), lambda m, c: (m, 0)),
-        ],
-        [pl.BlockSpec((crops, width), lambda m, c: (m, c)), pair],
-        [shape((micro * crops, channels)), shape((micro, 2, channels))],
-        [pltpu.VMEM((width // LANES, rows // ROWS, LANES), F32)],
+            pl.BlockSpec((crops, 1), lambda m, c, w: (m, 0)),
+        ],
+        [small, pair, tile, small, small] + ([part, part] if split else []),
+        [lines, shape((micro, 2, channels)), shape(h3.shape, BF16), lines, lines]
+        + ([half, half] if split else []),
+        [pltpu.VMEM((3, width // LANES, rows // ROWS, LANES), F32)],
         flops=20 * h3.size,
         bytes_accessed=4 * h3.size,
-    )(*parts, *members, h3, x, valid, gain, shift, sizes)
-
-
-def slope_body(*refs):
-    h_ref, x_ref, v_ref, info_ref, gain_ref, shift_ref = refs[:6]
-    slope_ref, first_ref, second_ref, sums_ref = refs[-4:]
-    rows, width = h_ref.shape
-    mean = info_ref[0, 0:1, :]
-    scaled = info_ref[0, 1:2, :]
-    factor = scaled * gain_ref[...]
-    shift = shift_ref[...]
-    for j in range(0, width, 512):
-        lane = slice(j, j + 512)
-        for k in range(rows // PIX):
-            acc_first = jnp.zeros((COLS, 512), F32)
-            acc_second = jnp.zeros((COLS, 512), F32)
-            for r in range(ROWS):
-                at = pl.ds(k * PIX + r * COLS, COLS)
-                centred = h_ref[at, lane].astype(F32) - mean[:, lane]
-                resid = centred * factor[:, lane] + shift[:, lane] + x_ref[at, lane].astype(F32)
-                sig = sigmoid(resid)
-                kept = sig * v_ref[at, :]
-                slope = kept + resid * kept * (1.0 - sig)
-                acc_first += slope
-                acc_second += slope * centred
-                slope_ref[at, lane] = slope.astype(BF16)
-            place = pl.ds(k * COLS, COLS)
-            put_lanes(sums_ref, place, j, acc_first, 0)
-            put_lanes(sums_ref, place, j, acc_second * scaled[:, lane], 1)
-    first_ref[...] = crop_sums(sums_ref, 0)
-    second_ref[...] = crop_sums(sums_ref, 1)
-
-
-def slope_part(h3, x, valid, info, gain, shift, micro, index, earlier):
-    rows, channels = h3.shape[0] // micro, h3.shape[1]
-    crops = rows // PIX * SLOTS
-    width = 1024
-    tile = pl.BlockSpec((rows, width), lambda c: (index, c))
-    small = pl.BlockSpec((crops, width), lambda c: (index, c))
-    return run(
-        slope_body,
-        (channels // width,),
-        [
-            tile,
-            tile,
-            pl.BlockSpec((rows, 1), lambda c: (index, 0)),
-            pl.BlockSpec((1, 2, width), lambda c: (index, 0, c)),
-            pl.BlockSpec((1, width), lambda c: (0, c)),
-            pl.BlockSpec((1, width), lambda c: (0, c)),
-        ]
-        + [pl.BlockSpec(memory_space=pl.ANY)] * len(earlier),
-        [tile, small, small],
-        [
-            shape(h3.shape, BF16),
-            shape((micro * crops, channels)),
-            shape((micro * crops, channels)),
-        ],
-        [pltpu.VMEM((2, width // LANES, rows // ROWS, LANES), F32)],
-        flops=30 * rows * channels,
-        bytes_accessed=6 * rows * channels,
-        aliases={6 + i: i for i in range(len(earlier))},
-    )(h3, x, valid, info, gain, shift, *earlier)
+        prefetch=1,
+    )(scalars, *parts, *members, h3, x, valid, gain, shift, sizes)
 
 
 def head_body(feat_ref, w_ref, g_ref, stats_ref):
@@ -559,8 +526,8 @@
 
 
 def head_back_body(total_crops, counts, refs):
-    part_refs = refs[:counts]
-    dy_ref, g_ref, info_ref, gain_ref, w_ref, size_ref, first_ref, second_ref, dg_ref, wide_ref, stats_ref, low_ref, spread_ref = refs[counts:]
+    which_ref, part_refs = refs[0], refs[1 : 1 + counts]
+    dy_ref, g_ref, info_ref, gain_ref, w_ref, size_ref, first_ref, second_ref, send_ref, keep_ref, wide_ref, stats_ref, low_ref, spread_ref = refs[1 + counts :]
     micro = stats_ref.shape[0]
     lines, width = dy_ref.shape
     crops = lines // micro
@@ -576,7 +543,9 @@
             dg = gain_ref[...] * scaled * (dy_ref[at, :] - (one + normal * two))
             low = dg.astype(BF16)
             low_ref[at, :] = low
-            dg_ref[at, :] = low.astype(F32)
+            left, right = [low[:, i : i + width // 2].astype(F32) for i in (0, width // 2)]
+            send_ref[at, :] = jnp.where(which_ref[0] == 0, right, left)
+            keep_ref[at, :] = jnp.where(which_ref[0] == 0, left, right)
 
     per_crop = nt_dot(low_ref[...], w_ref[...]) / size_ref[...]
     for j in range(wide_ref.shape[1] // LANES):
@@ -592,12 +561,13 @@
         stats_ref[m, 1:2, :] = jnp.sum(two[at], axis=0, keepdims=True)
 
 
-def head_back(parts, dy, g, info, gain, weight, sizes, first, second, total_crops):
+def head_back(which, parts, dy, g, info, gain, weight, sizes, first, second, total_crops):
     lines, width = dy.shape
     channels = weight.shape[0]
     micro = info.shape[0]
     tile = 512
-    part = pl.BlockSpec((lines, tile), lambda c: (0, c))
+    part = pl.BlockSpec((lines, tile), lambda c, w: (0, c))
+    half = shape((lines, width // 2))
     return run(
         named("head_back", head_back_body, total_crops, len(parts)),
         (channels // tile,),
@@ -607,24 +577,26 @@
             whole(g),
             whole(info),
             whole(gain),
-            pl.BlockSpec((tile, width), lambda c: (c, 0)),
+            pl.BlockSpec((tile, width), lambda c, w: (c, 0)),
             whole(sizes),
             part,
             part,
         ],
         [
-            whole(dy),
-            pl.BlockSpec((lines * CELL, tile), lambda c: (0, c)),
-            pl.BlockSpec((micro, 2, tile), lambda c: (0, 0, c)),
-        ],
-        [shape((lines, width)), shape((lines * CELL, channels)), shape((micro, 2, channels))],
+            whole(half),
+            whole(half),
+            pl.BlockSpec((lines * CELL, tile), lambda c, w: (0, c)),
+            pl.BlockSpec((micro, 2, tile), lambda c, w: (0, 0, c)),
+        ],
+        [half, half, shape((lines * CELL, channels)), shape((micro, 2, channels))],
         [
             pltpu.VMEM((lines, width), BF16),
             pltpu.VMEM((tile // LANES, lines * CELL, LANES), F32),
         ],
         flops=2 * lines * weight.size,
         bytes_accessed=2 * weight.size,
-    )(*parts, dy, g, info, gain, weight, sizes, first, second)
+        prefetch=1,
+    )(which, *parts, dy, g, info, gain, weight, sizes, first, second)
 
 
 def third_back_body(counts, refs):
@@ -1444,20 +1416,27 @@
         parts, members, h2, valid, row(gain_two), row(shift_two), conv_out, micro
     )
     parts = moment_parts(stats, counts)
-    feat, info_three = pool(
-        parts, members, h3, x, valid, row(gain_three), row(shift_three), sizes, micro
+    feat, info_three, slope, slope_first, slope_second, *feat_halves = pool(
+        scalars,
+        parts,
+        members,
+        h3,
+        x,
+        valid,
+        row(gain_three),
+        row(shift_three),
+        sizes,
+        micro,
+        channels // shards if quick else 0,
     )
 
     lines = feat.shape[0]
     if quick:
-        by_bit = feat.reshape(lines, shards // 2, 2, -1)
-        bit = bit_of(near)
-        feat_keep = at(by_bit, bit, 2).reshape(lines, -1)
-        feat_send = at(by_bit, 1 - bit, 2).reshape(lines, -1)
-        feat_near = swap(feat_send, near)
+        feat_keep, feat_send = feat_halves
+        feat_near, feat_far = swap(feat_send, near), swap(feat_keep, 2)
     g, stats = head_product(feat, head_weight, micro)
     if quick:
-        stats, feat_near = tie(stats, feat_near)
+        stats, feat_near, feat_far = tie(stats, feat_near, feat_far)
 
     crop_counts = []
     crop_members = []
@@ -1466,19 +1445,7 @@
         crop_members = [number] * (len(group) + 1)
         crop_counts.append(crop_members)
         number = number * (len(group) + 1)
-    slopes = []
-
-    def slope_filler(index):
-        def fill(gate):
-            source = tie(h3, gate)[0]
-            slopes[:] = slope_part(
-                source, x, valid, info_three, row(gain_three), row(shift_three), micro, index, slopes
-            )
-            return slopes
-
-        return fill
-
-    parts = moment_parts(stats, crop_counts, ((), (slope_filler(0),), (slope_filler(1),)))
+    parts = moment_parts(stats, crop_counts)
 
     act_four, embedded, inverse, unit_rows, logits, batch, queue, column, info_four = embed_product(
         parts,
@@ -1492,13 +1459,10 @@
         table,
         queue_rows,
     )
-    fillers = ((), (slope_filler(2),), (slope_filler(3),))
     for _ in range(SINK_ITERS - 1):
-        parts = sum_parts(column, fillers)
-        fillers = ()
+        parts = sum_parts(column)
         batch, queue, column = sweep(parts, protos, batch, queue, queue_rows.shape[0])
-    parts = sum_parts(column, fillers)
-    slope, slope_first, slope_second = slopes
+    parts = sum_parts(column)
     which = (1 - send_half) if quick else jnp.zeros((1,), jnp.int32)
     small_send, small_keep, dy_four, payload = loss_grads(
         which,
@@ -1527,11 +1491,11 @@
     grad_bias, total_loss = extra[: embed_bias.shape[0]], extra[embed_bias.shape[0]]
 
     if quick:
-        feat_keep, feat_near, small_send, *parts = tie(feat_keep, feat_near, small_send, *parts)
-        feat_near = jnp.concatenate([feat_keep, feat_near], 0)
-        feat_far = swap(feat_near, 2)
+        feat_near, small_send, *parts = tie(feat_near, small_send, *parts)
+        feat_both = swap(feat_near, 2)
         small_recv = swap(small_send, 1)
-    dg, wide, sums = head_back(
+    dg_send, dg_keep, wide, sums = head_back(
+        which,
         parts,
         dy_four,
         g,
@@ -1573,10 +1537,8 @@
         )
 
     if quick:
-        sums, dg, feat_far, small_recv = tie(sums, dg, feat_far, small_recv)
-        feat_both = jnp.concatenate([feat_near, feat_far], 0)
-        split = dg.reshape(lines, 2, -1)
-        dg_send = at(split, 1 - core, 1)
+        sums, dg_send, feat_both, small_recv = tie(sums, dg_send, feat_both, small_recv)
+        feat_both = jnp.concatenate([feat_keep, feat_near, feat_far, feat_both], 0)
 
         def core_filler(gate):
             source, other = tie(dg_send, feat_both, gate)[:2]
@@ -1587,8 +1549,18 @@
         grads = {}
         parts_three = sum_parts(sums, ((), (core_filler,)))
         feat_other = grads["feat"]
-        split = jnp.concatenate([at(split, core, 1), grads["dg"]], 0).reshape(2 * lines, 2, -1)
-        dg_here, dg_there = at(split, side, 1), at(split, 1 - side, 1)
+        quarter = dg_keep.shape[1] // 2
+
+        def quarter_of(place):
+            return jnp.concatenate(
+                [
+                    lax.dynamic_slice_in_dim(array, place * quarter, quarter, 1)
+                    for array in (dg_keep, grads["dg"])
+                ],
+                0,
+            )
+
+        dg_here, dg_there = quarter_of(side), quarter_of(1 - side)
         *parts_three, dg_here, dg_there = tie(*parts_three, dg_here, dg_there)
         dg_far, dg_near, dg_both = swap(dg_there, 2), swap(dg_here, near), swap(dg_there, 2 + near)
         dy, sums, out_send, out_keep = from_third(send_half, parts_three)
@@ -1617,8 +1589,8 @@
         early = grads["early"]
         *parts_two, early_out, partial = tie(*parts_two, grads["early_out"], grads["head"])
         early_came = core_swap(early_out, near, 2)
-        partial = partial.reshape(2, 2, -1, partial.shape[1])
-        head = dp_halves([partial], far[0], 1)
+        partial = partial.reshape(2, 2, 2, -1, partial.shape[1])
+        heads = [dp_halves([partial[:, :, 0]], far[0], 1)]
         d_two, mid_send = mid_grad(
             "mid_first",
             mid_first_body,
@@ -1627,14 +1599,19 @@
             act_one,
             True,
         )
-        d_two, mid_send, early_came = tie(d_two, mid_send, early_came)
+        d_two, mid_send, early_came, heads[0][-1] = tie(
+            d_two, mid_send, early_came, heads[0][-1]
+        )
+        heads.append(dp_halves([partial[:, :, 1]], far[0], 1))
         mid_recv = swap(mid_send, 1)
         early_out, early_keep = second_send(scalars, early, early_came)
         early_came = core_swap(early_out, 2, near)
         mid_keep = mid_grad(
             "mid_second", mid_second_body, keep_half, [d_two, act_one], act_one, False
         )
-        mid_keep, mid_recv, early_came, head[-1] = tie(mid_keep, mid_recv, early_came, head[-1])
+        mid_keep, mid_recv, early_came, heads[1][-1] = tie(
+            mid_keep, mid_recv, early_came, heads[1][-1]
+        )
 
         def sharded(array):
             return array.reshape(shards, -1, array.shape[-1])
@@ -1646,10 +1623,10 @@
         mid_out = first_send(scalars, late)
         d_two, mid_out = tie(d_two, mid_out)
         mid_came = core_swap(mid_out, near, 2)
-        head = dp_halves(head, far[1], 0)
+        heads = [dp_halves(head, far[1], 0) for head in heads]
         dy, sums = from_second(d_two)
-        dy, sums, mid_came, head[-1], early_keep, early_came = tie(
-            dy, sums, mid_came, head[-1], early_keep, early_came
+        dy, sums, mid_came, heads[0][-1], heads[1][-1], early_keep, early_came = tie(
+            dy, sums, mid_came, heads[0][-1], heads[1][-1], early_keep, early_came
         )
         early = [by_bits(early_keep), by_bits(early_came)]
 
@@ -1675,20 +1652,21 @@
         inner = [[sharded(in_keep), sharded(in_recv)]]
         in_out = first_send(scalars, inner)
         mid = dp_halves([by_bits(mid_keep), by_bits(mid_came)], far[0], 1)
-        early_mine = jnp.concatenate([sum(early), sum(head)], 0)
+        early_mine = jnp.concatenate([sum(early), sum(heads[0]), sum(heads[1])], 0)
         d_one, in_out, early_mine = tie(d_one, in_out, early_mine)
         in_came = core_swap(in_out, near, 2)
-        early_far = swap(early_mine, 2)
         early_core = swap(early_mine, 1)
         grad_x = pixels_grad(d_one, conv_in, wide, slope, micro)
         grad_x, in_came, mid[-1], early_core = tie(grad_x, in_came, mid[-1], early_core)
+        mid = dp_halves(mid, far[1], 0)
         in_out, in_keep = second_send(scalars, inner, in_came)
         in_came = core_swap(in_out, 2, near)
-        mid = dp_halves(mid, far[1], 0)
+        in_came, mid[-1], early_mine = tie(in_came, mid[-1], early_mine)
         inner = dp_halves([by_bits(in_keep), by_bits(in_came)], far[0], 1)
-        early_far = tie(early_far, inner[-1])[0]
+        early_far = swap(early_mine, 2)
+        inner = dp_halves(inner, far[1], 0)
+        early_far, inner[-1] = tie(early_far, inner[-1])
         early_pieces = [early_mine, early_far, early_core, swap(early_far, 1)]
-        inner = dp_halves(inner, far[1], 0)
         channel = channels // shards
         early_grads = placed_pieces(
             place_early_body,
@@ -1740,9 +1718,8 @@
         grad_conv_out = reduced(out.transpose(1, 3, 0, 2, 4).reshape(conv_out.shape))
         grad_conv_mid = reduced(jnp.concatenate([mid_low, mid_high], 1))
         grad_conv_in = reduced(jnp.concatenate([in_low, in_high], 1))
-        grad_head = reduced(
-            jnp.dot(feat.astype(BF16).T, dg.astype(BF16), preferred_element_type=F32)
-        )
+        dg = jnp.concatenate([dg_keep, dg_send], 1).astype(BF16)
+        grad_head = reduced(jnp.dot(feat.astype(BF16).T, dg, preferred_element_type=F32))
         grad_embed = reduced(small_embed)
         grad_protos = reduced(small_protos)[:, :protos]
 

time: 526 us -> 481 us (0.914)
  Pallas kernels: 226 us -> 197 us
  local copies, waits for them, and re-layouts: 26.3 us -> 16.8 us
  other arithmetic: 17.4 us -> 8.56 us
    pallas_call x5 -> x1, Pallas kernels: 36.5 us -> 17.4 us  [pool(): run(named('pool', pool_body, len(parts), split), (micro, channels // widt...]
    ppermute x102 -> x105, waiting for transfers between devices: 111 us -> 128 us  [swap(): return lax.ppermute(value, AXES, [(i, i ^ mask) for i in range(count)])]
    ppermute x6, waiting for transfers between devices: 23.3 us -> 8.41 us  [core_swap(): return lax.ppermute(value, AXES, pairs)]
    add x27, other arithmetic: 9.12 us -> 1.8 us  [tree(): parts = [parts[i] + parts[i + 1] for i in range(0, len(parts), 2)]]
    ppermute x102 -> x105, starting transfers between devices: 103 us -> 106 us  [swap(): return lax.ppermute(value, AXES, [(i, i ^ mask) for i in range(count)])]
  transfers between devices with their start and end apart: 108 -> 111, of which waited for: 64 -> 77; matrix products, arithmetic and copies ran while one was open for 4% -> 3% of each run, Pallas kernels for 28% -> 25%
where the time goes in v4:
time: 481 us; the launch traced here: 472 us
  Pallas kernels  197 us (41%)
  waiting for transfers between devices  136 us (28%)
  starting transfers between devices  112 us (23%)
  local copies, waits for them, and re-layouts  16.8 us (3%)
  other arithmetic  8.56 us (2%)
    ppermute x105, waiting for transfers between devices, swap(): return lax.ppermute(value, AXES, [(i, i ^ mask) for i in range(count)])  128 us
    ppermute x105, starting transfers between devices, swap(): return lax.ppermute(value, AXES, [(i, i ^ mask) for i in range(count)])  106 us
    pallas_call x2, Pallas kernels, mid_grad(): run(named(name, body, *([len(ins) - 7] if with_d else [])), (TAPS,), [who...  25.7 us
    pallas_call x1, Pallas kernels, third_back(): run(named('third_back', third_back_body, len(parts)), (micro,), [per_micr...  19.4 us
    pallas_call x1, Pallas kernels, pool(): run(named('pool', pool_body, len(parts), split), (micro, channels // widt...  17.4 us
    pallas_call x1, Pallas kernels, second_back(): run(second_back_body, (micro,), [mid, whole(weight), pl.BlockSpec((rows,...  17.3 us
    pallas_call x1, Pallas kernels, second_product(): run(named('second_product', second_body, len(parts)), (micro,), [per_micr...  16.2 us
    pallas_call x1, Pallas kernels, in_grad(): run(named('in_grad', in_grad_body, len(parts)), (depth // tile,), [whole(...  12.1 us
  transfers between devices with their start and end apart: 111, of which 77 were waited for; matrix products, arithmetic and copies ran while one was open for 3% of the time, Pallas kernels for 25%

profile of v4, /device:TPU:0, one launch (start us, length us, event | category | flops | bytes accessed | tf_op | source)
XLA Modules:
  0.0 472.2 jit_solution(12670831133353483520)
XLA Ops:
  1.8 9.6 %first_body.1 = (f32[2048,512]{1,0:T(8,128)}, f32[4,3,512]{2,1,0:T(4,128)S(1)}) custom-call(bf16[2048,2048]{1,0:T(8,128)(2,1)} %bitcast.220, bf16[2048,512]{1,0:T(8,128)(2,1)} %w_ref.7, f32[2048,1]{1,0:T(8,128)S(1)} %copy.114.v_ref.refs_5_.refs_9_.refs_11_.refs_8_.refs_7_), custom_call_target="tpu_custom_call" | custom-call | flops 4294967296 | bytes 8388608 | tf_op jit(solution)/shard_map/first_body/pallas_call | solution.py:247
  12.8 2.9 collective-permute-start.1
  17.5 4.6 collective-permute-done.3
  22.3 3.7 collective-permute-start.6
  30.8 16.2 %second_product.1 = (bf16[2048,512]{1,0:T(8,128)(2,1)}, f32[2048,512]{1,0:T(8,128)}, f32[4,2,512]{2,1,0:T(2,128)S(1)}, f32[4,3,512]{2,1,0:T(4,128)S(1)}) custom-call(f32[4,3,512]{2,1,0:T(4,128)S(1)} %pad_maximum_fusion.8.refs_0_.refs_4_.refs_5_, f32[4,3,512]{2,1,0:T(4,128)S(1)} %collective-permute-done.4.refs_1_.refs_5_.refs_6_, ...), custom_call_target="tpu_custom_call" | custom-call | flops 9663676416 | bytes 10485760 | tf_op jit(solution)/shard_map/second_product/pallas_call | solution.py:319
  60.7 11.6 %third_product.1 = (bf16[2048,512]{1,0:T(8,128)(2,1)}, bf16[2048,2048]{1,0:T(8,128)(2,1)}, f32[4,2,2048]{2,1,0:T(2,128)S(1)}, f32[4,2,512]{2,1,0:T(2,128)S(1)}) custom-call(f32[4,2,512]{2,1,0:T(2,128)S(1)} %pad_maximum_fusion.11.refs_0_, f32[4,2,512]{2,1,0:T(2,128)S(1)} %collective-permute-done.11.refs_1_, f32[4,2,512]{2,1,0:T(2,128)S(1)} %collective-permute-done.12.refs_2_, ...), custom_call_target="tpu_custom_call" | custom-call | flops 4294967296 | bytes 16777216 | tf_op jit(solution)/shard_map/third_product/pallas_call | solution.py:370
  90.3 17.4 %pool.1 = (f32[64,2048]{1,0:T(8,128)S(1)}, f32[4,2,2048]{2,1,0:T(2,128)S(1)}, bf16[2048,2048]{1,0:T(8,128)(2,1)}, f32[64,2048]{1,0:T(8,128)}, f32[64,2048]{1,0:T...) custom-call(s32[3]{0:T(128)S(1)} %pad_add_fusion.refs_0_.scalars_ref, ...), custom_call_target="tpu_custom_call" | custom-call | flops 83886080 | bytes 16777216 | tf_op jit(solution)/shard_map/pool/pallas_call | solution.py:472
  109.4 5.2 %head_body.1 = (f32[64,2048]{1,0:T(8,128)S(1)}, f32[4,2,2048]{2,1,0:T(2,128)S(1)}) custom-call(f32[64,2048]{1,0:T(8,128)S(1)} %get-tuple-element.194.feat_ref, bf16[2048,2048]{1,0:T(8,128)(2,1)} %refs_9_.1), custom_call_target="tpu_custom_call" | custom-call | flops 536870912 | bytes 8388608 | tf_op jit(solution)/shard_map/head_body/pallas_call | solution.py:511
  132.6 3.0 embed.1
  188.8 6.1 %loss.1 = (f32[8,80,512]{2,1,0:T(8,128)}, f32[8,80,512]{2,1,0:T(8,128)}, f32[64,2048]{1,0:T(8,128)S(1)}, f32[8,2304]{1,0:T(8,128)S(1)}) custom-call(s32[1]{0:T(128)} %bitcast.refs_0_, f32[4,3072]{1,0:T(4,128)S(1)} %add_add_fusion.4.refs_1_, f32[4,3072]{1,0:T(4,128)S(1)} %collective-permute-done.48.refs_2_, f32[4,3072]{1,0:T(4,128)S(1)} %collective-permute-done.49.refs_3_, ...), custom_call_target="tpu_custom_call" | custom-call | flops 201326592 | bytes 3145728 | tf_op jit(solution)/shard_map/loss/pallas_call | solution.py:1187
  213.7 7.5 %head_back.1 = (f32[64,1024]{1,0:T(8,128)S(1)}, f32[64,1024]{1,0:T(8,128)S(1)}, f32[256,2048]{1,0:T(8,128)}, f32[4,2,2048]{2,1,0:T(2,128)S(1)}) custom-call(s32[1]{0:T(128)} %bitcast.refs_0_, f32[8,2304]{1,0:T(8,128)S(1)} %add_add_fusion.1.refs_1_, f32[8,2304]{1,0:T(8,128)S(1)} %collective-permute-done.55.refs_2_, ...), custom_call_target="tpu_custom_call" | custom-call | flops 536870912 | bytes 8388608 | tf_op jit(solution)/shard_map/head_back/pallas_call | solution.py:571
  241.6 19.4 %third_back.1 = (f32[2048,512]{1,0:T(8,128)}, f32[4,2,512]{2,1,0:T(2,128)S(1)}, f32[8,128,512]{2,1,0:T(8,128)}, f32[8,128,512]{2,1,0:T(8,128)}) custom-call(s32[1]{0:T(128)S(6)} %sub.184.refs_0_, f32[4,2,2048]{2,1,0:T(2,128)S(1)} %bitcast.159, f32[4,2,2048]{2,1,0:T(2,128)S(1)} %collective-permute-done.66.refs_2_, ...), custom_call_target="tpu_custom_call" | custom-call | flops 8589934592 | bytes 25165824 | tf_op jit(solution)/shard_map/third_back/pallas_call | solution.py:675
  273.3 3.1 factor_body.1
  276.4 3.5 first_send.3
  283.9 14.3 %mid_first.1 = (bf16[2048,512]{1,0:T(8,128)(2,1)}, f32[4608,256]{1,0:T(8,128)}) custom-call(s32[1]{0:T(128)S(6)} %sub.184.refs_0_, f32[4,2,512]{2,1,0:T(2,128)S(1)} %bitcast.173, f32[4,2,512]{2,1,0:T(2,128)S(1)} %collective-permute-done.77.refs_2_, f32[4,2,512]{2,1,0:T(2,128)S(1)} %collective-permute-done.78.refs_3_, ...), custom_call_target="tpu_custom_call" | custom-call | flops 4831838208 | bytes 4718592 | tf_op jit(solution)/shard_map/mid_first/pallas_call | solution.py:788
  298.3 3.9 collective-permute-done.80.refs_17_.refs_18_.refs_19_.refs_20_
  302.2 3.6 second_send.3
  307.0 11.4 %mid_second.1 = f32[4608,256]{1,0:T(8,128)} custom-call(s32[1]{0:T(128)} %bitcast.refs_0_, bf16[2048,512]{1,0:T(8,128)(2,1)} %get-tuple-element.293.refs_1_.d_ref, bf16[2048,512]{1,0:T(8,128)(2,1)} %get-tuple-element.282.refs_11_.refs_2_), custom_call_target="tpu_custom_call" | custom-call | flops 4831838208 | bytes 4718592 | tf_op jit(solution)/shard_map/mid_second/pallas_call | solution.py:788
  318.3 2.8 collective-permute-done.84
  323.4 4.1 first_send.4
  333.6 17.3 %second_back_body.1 = (f32[2048,512]{1,0:T(8,128)}, f32[4,2,512]{2,1,0:T(2,128)S(1)}) custom-call(bf16[2048,512]{1,0:T(8,128)(2,1)} %get-tuple-element.293.refs_1_.d_ref, bf16[4608,512]{1,0:T(8,128)(2,1)} %w_ref.6, f32[2048,1]{1,0:T(8,128)S(1)} %copy-done.2, f32[2048,512]{1,0:T(8,128)} %get-tuple-element.189.refs_4_.h1_ref.refs_6_, ...), custom_call_target="tpu_custom_call" | custom-call | flops 9663676416 | bytes 10485760 | tf_op jit(solution)/shard_map/second_back_body/pallas_call | solution.py:873
  351.0 3.9 collective-permute-done.87
  371.7 4.7 second_send.4
  377.9 12.1 %in_grad.1 = (bf16[2048,512]{1,0:T(8,128)(2,1)}, f32[2048,256]{1,0:T(8,128)}, f32[2048,256]{1,0:T(8,128)}) custom-call(s32[1]{0:T(128)S(6)} %sub.184.refs_0_, f32[4,2,512]{2,1,0:T(2,128)S(1)} %bitcast.163, f32[4,2,512]{2,1,0:T(2,128)S(1)} %collective-permute-done.93.refs_2_, f32[4,2,512]{2,1,0:T(2,128)S(1)} %collective-permute-done.94.refs_3_, ...), custom_call_target="tpu_custom_call" | custom-call | flops 4294967296 | bytes 23068672 | tf_op jit(solution)/shard_map/in_grad/pallas_call | solution.py:829
  403.0 11.5 %pixels_body.1 = bf16[2048,2048]{1,0:T(8,128)(2,1)} custom-call(bf16[2048,512]{1,0:T(8,128)(2,1)} %get-tuple-element.332.d_ref, bf16[2048,512]{1,0:T(8,128)(2,1)} %w_ref.7, f32[256,2048]{1,0:T(8,128)} %get-tuple-element.243.refs_5_.wide_ref, bf16[2048,2048]{1,0:T(8,128)(2,1)} %get-tuple-element.244.refs_6_.slope_ref), custom_call_target="tpu_custom_call" | custom-call | flops 4294967296 | bytes 16777216 | tf_op jit(solution)/shard_map/pixels_body/pallas_call | solution.py:913
  414.6 3.2 collective-permute-done.100
  418.8 2.8 second_send.5
  423.7 13.6 %collective-permute-done.103 = f32[288,256]{1,0:T(8,128)S(1)} collective-permute-done((f32[288,256]{1,0:T(8,128)S(1)}, f32[288,256]{1,0:T(8,128)S(1)}, u32[]{:S(2)}, u32[]{:S(2)}) %collective-permute-start.103) | collective-permute-done | bytes 294944 | tf_op jit(solution)/shard_map/ppermute | solution.py:32
  438.9 7.2 %collective-permute-done.104 = f32[2,128,256]{2,1,0:T(8,128)S(1)} collective-permute-done((f32[2,128,256]{2,1,0:T(8,128)S(1)}, f32[2,128,256]{2,1,0:T(8,128)S(1)}, u32[]{:S(2)}, u32[]{:S(2)}) %collective-permute-start.104) | collective-permute-done | bytes 262176 | tf_op jit(solution)/shard_map/ppermute | solution.py:32
  447.5 6.7 %collective-permute-done.106 = f32[128,256]{1,0:T(8,128)S(1)} collective-permute-done((f32[128,256]{1,0:T(8,128)S(1)}, f32[128,256]{1,0:T(8,128)S(1)}, u32[]{:S(2)}, u32[]{:S(2)}) %collective-permute-start.106) | collective-permute-done | bytes 131104 | tf_op jit(solution)/shard_map/ppermute | solution.py:32
  458.7 3.6 place_early_body.1
  462.4 5.8 %collective-permute-done.107.far_ref = f32[416,256]{1,0:T(8,128)S(1)} collective-permute-done((f32[416,256]{1,0:T(8,128)S(1)}, f32[416,256]{1,0:T(8,128)S(1)}, u32[]{:S(2)}, u32[]{:S(2)}) %collective-permute-start.107) | collective-permute-done | bytes 426016 | tf_op jit(solution)/shard_map/ppermute | solution.py:32
  (387 shorter events, 223.7 us)
Async XLA Ops:
  107.7 7.6 %collective-permute-start.21 = (f32[64,1024]{1,0:T(8,128)S(1)}, f32[64,1024]{1,0:T(8,128)S(1)}, u32[]{:S(2)}, u32[]{:S(2)}) collective-permute-start(f32[64,1024]{1,0:T(8,128)S(1)} %get-tuple-element.196), channel_id=1, source_target_pairs={{0,4},{1,5},{2,6},{3,7},{4,0},{5,1},{6,2},{7,3},{8,12},{9,13},{10,... | collective-permute-start | bytes 786440 | tf_op jit(solution)/shard_map/ppermute | solution.py:32
  108.1 7.3 %collective-permute-start.22 = (f32[64,1024]{1,0:T(8,128)S(1)}, f32[64,1024]{1,0:T(8,128)S(1)}, u32[]{:S(2)}, u32[]{:S(2)}) collective-permute-start(f32[64,1024]{1,0:T(8,128)S(1)} %get-tuple-element.197), channel_id=1, source_target_pairs={{0,2},{1,3},{2,0},{3,1},{4,6},{5,7},{6,4},{7,5},{8,10},{9,11},{10,... | collective-permute-start | bytes 786440 | tf_op jit(solution)/shard_map/ppermute | solution.py:32
  212.5 8.8 %collective-permute-start.59 = (f32[8,80,512]{2,1,0:T(8,128)}, f32[8,80,512]{2,1,0:T(8,128)S(1)}, u32[]{:S(2)}, u32[]{:S(2)}) collective-permute-start(f32[8,80,512]{2,1,0:T(8,128)} %get-tuple-element.227), channel_id=1, source_target_pairs={{0,1},{1,0},{2,3},{3,2},{4,5},{5,4},{6,7},{7,6},{8,9},{9,8},{10,11... | collective-permute-start | bytes 3932168 | tf_op jit(solution)/shard_map/ppermute | solution.py:32
  212.5 8.8 %collective-permute-start.58 = (f32[64,1024]{1,0:T(8,128)S(1)}, f32[64,1024]{1,0:T(8,128)S(1)}, u32[]{:S(2)}, u32[]{:S(2)}) collective-permute-start(f32[64,1024]{1,0:T(8,128)S(1)} %copy-done.37), channel_id=1, source_target_pairs={{0,2},{1,3},{2,0},{3,1},{4,6},{5,7},{6,4},{7,5},{8,10},{9,11},{10,... | collective-permute-start | bytes 786440 | tf_op jit(solution)/shard_map/ppermute | solution.py:32
  222.7 7.5 %collective-permute-start.65 = (f32[256,1024]{1,0:T(8,128)S(1)}, f32[256,1024]{1,0:T(8,128)}, u32[]{:S(2)}, u32[]{:S(2)}) collective-permute-start(f32[256,1024]{1,0:T(8,128)S(1)} %constant_dynamic-update-slice_fusion.feat_ref), channel_id=1, source_target_pairs={{0,1},{1,0},{2,3},{3,2},{4,5},{5,4},{6,7},{7,6},{8,9},{9,8},{10,11... | collective-permute-start | bytes 3145736 | tf_op jit(solution)/shard_map/ppermute | solution.py:32
  238.1 22.9 %collective-permute-start.71 = (f32[128,512]{1,0:T(8,128)S(1)}, f32[128,512]{1,0:T(8,128)S(1)}, u32[]{:S(2)}, u32[]{:S(2)}) collective-permute-start(f32[128,512]{1,0:T(8,128)S(1)} %get-tuple-element.252), channel_id=1, source_target_pairs={{0,6},{1,7},{2,4},{3,5},{4,2},{5,3},{6,0},{7,1},{8,14},{9,15},{10,... | collective-permute-start | bytes 786440 | tf_op jit(solution)/shard_map/ppermute | solution.py:32
  239.7 21.3 %collective-permute-start.69 = (f32[128,512]{1,0:T(8,128)S(1)}, f32[128,512]{1,0:T(8,128)S(1)}, u32[]{:S(2)}, u32[]{:S(2)}) collective-permute-start(f32[128,512]{1,0:T(8,128)S(1)} %get-tuple-element.252), channel_id=1, source_target_pairs={{0,2},{1,3},{2,0},{3,1},{4,6},{5,7},{6,4},{7,5},{8,10},{9,11},{10,... | collective-permute-start | bytes 786440 | tf_op jit(solution)/shard_map/ppermute | solution.py:32
  240.8 20.3 %collective-permute-start.70 = (f32[128,512]{1,0:T(8,128)S(1)}, f32[128,512]{1,0:T(8,128)S(1)}, u32[]{:S(2)}, u32[]{:S(2)}) collective-permute-start(f32[128,512]{1,0:T(8,128)S(1)} %get-tuple-element.253.dg_ref), channel_id=1, source_target_pairs={{0,4},{1,5},{2,6},{3,7},{4,0},{5,1},{6,2},{7,3},{8,12},{9,13},{10,... | collective-permute-start | bytes 786440 | tf_op jit(solution)/shard_map/ppermute | solution.py:32
  268.8 11.1 %collective-permute-start.79 = (f32[4,2,512]{2,1,0:T(2,128)S(1)}, f32[4,2,512]{2,1,0:T(2,128)S(1)}, u32[]{:S(2)}, u32[]{:S(2)}) collective-permute-start(f32[4,2,512]{2,1,0:T(2,128)S(1)} %bitcast.170), channel_id=1, source_target_pairs={{0,24},{1,25},{2,26},{3,27},{4,28},{5,29},{6,30},{7,31},{8,16},{9,... | collective-permute-start | bytes 49160 | tf_op jit(solution)/shard_map/ppermute | solution.py:32
  270.9 9.1 %collective-permute-start.78 = (f32[4,2,512]{2,1,0:T(2,128)S(1)}, f32[4,2,512]{2,1,0:T(2,128)S(1)}, u32[]{:S(2)}, u32[]{:S(2)}) collective-permute-start(f32[4,2,512]{2,1,0:T(2,128)S(1)} %bitcast.171), channel_id=1, source_target_pairs={{0,16},{1,17},{2,18},{3,19},{4,20},{5,21},{6,22},{7,23},{8,24},{9,... | collective-permute-start | bytes 49160 | tf_op jit(solution)/shard_map/ppermute | solution.py:32
  271.0 8.9 %collective-permute-start.77 = (f32[4,2,512]{2,1,0:T(2,128)S(1)}, f32[4,2,512]{2,1,0:T(2,128)S(1)}, u32[]{:S(2)}, u32[]{:S(2)}) collective-permute-start(f32[4,2,512]{2,1,0:T(2,128)S(1)} %bitcast.172), channel_id=1, source_target_pairs={{0,8},{1,9},{2,10},{3,11},{4,12},{5,13},{6,14},{7,15},{8,0},{9,1},... | collective-permute-start | bytes 49160 | tf_op jit(solution)/shard_map/ppermute | solution.py:32
  280.0 22.2 %collective-permute-start.80 = (f32[8,104,512]{2,1,0:T(8,128)}, f32[8,104,512]{2,1,0:T(8,128)}, u32[]{:S(2)}, u32[]{:S(2)}) collective-permute-start(f32[8,104,512]{2,1,0:T(8,128)} %first_send.3), channel_id=1, source_target_pairs={{0,4},{1,3},{2,6},{3,1},{4,0},{5,7},{6,2},{7,5},{8,12},{9,11},{10,... | collective-permute-start | bytes 5111816 | tf_op jit(solution)/shard_map/ppermute | solution.py:126
  283.9 14.4 %collective-permute-start.81 = (f32[2,128,512]{2,1,0:T(8,128)S(1)}, f32[2,128,512]{2,1,0:T(8,128)S(1)}, u32[]{:S(2)}, u32[]{:S(2)}) collective-permute-start(f32[2,128,512]{2,1,0:T(8,128)S(1)} %dynamic-slice_bitcast_fusion.1), channel_id=1, source_target_pairs={{0,8},{1,9},{2,10},{3,11},{4,12},{5,13},{6,14},{7,15},{8,0},{9,1},... | collective-permute-start | bytes 1572872 | tf_op jit(solution)/shard_map/ppermute | solution.py:32
  302.2 19.0 %collective-permute-start.82 = (f32[4608,256]{1,0:T(8,128)}, f32[4608,256]{1,0:T(8,128)S(1)}, u32[]{:S(2)}, u32[]{:S(2)}) collective-permute-start(f32[4608,256]{1,0:T(8,128)} %get-tuple-element.288), channel_id=1, source_target_pairs={{0,1},{1,0},{2,3},{3,2},{4,5},{5,4},{6,7},{7,6},{8,9},{9,8},{10,11... | collective-permute-start | bytes 14155784 | tf_op jit(solution)/shard_map/ppermute | solution.py:32
  305.8 15.4 %collective-permute-start.83 = (f32[4,104,512]{2,1,0:T(8,128)S(1)}, f32[4,104,512]{2,1,0:T(8,128)S(1)}, u32[]{:S(2)}, u32[]{:S(2)}) collective-permute-start(f32[4,104,512]{2,1,0:T(8,128)S(1)} %get-tuple-element.290), channel_id=1, source_target_pairs={{0,2},{1,5},{2,0},{3,7},{4,6},{5,1},{6,4},{7,3},{8,10},{9,13},{10,... | collective-permute-start | bytes 2555912 | tf_op jit(solution)/shard_map/ppermute | solution.py:126
  306.9 14.3 %collective-permute-start.84 = (f32[2,128,512]{2,1,0:T(8,128)S(1)}, f32[2,128,512]{2,1,0:T(8,128)S(1)}, u32[]{:S(2)}, u32[]{:S(2)}) collective-permute-start(f32[2,128,512]{2,1,0:T(8,128)S(1)} %dynamic-slice_bitcast_fusion), channel_id=1, source_target_pairs={{0,8},{1,9},{2,10},{3,11},{4,12},{5,13},{6,14},{7,15},{8,0},{9,1},... | collective-permute-start | bytes 1572872 | tf_op jit(solution)/shard_map/ppermute | solution.py:32
  327.5 29.2 %collective-permute-start.85 = (f32[8,288,256]{2,1,0:T(8,128)}, f32[8,288,256]{2,1,0:T(8,128)}, u32[]{:S(2)}, u32[]{:S(2)}) collective-permute-start(f32[8,288,256]{2,1,0:T(8,128)} %first_send.4), channel_id=1, source_target_pairs={{0,4},{1,3},{2,6},{3,1},{4,0},{5,7},{6,2},{7,5},{8,12},{9,11},{10,... | collective-permute-start | bytes 7077896 | tf_op jit(solution)/shard_map/ppermute | solution.py:126
  329.5 21.5 %collective-permute-start.86 = (f32[128,512]{1,0:T(8,128)S(1)}, f32[128,512]{1,0:T(8,128)S(1)}, u32[]{:S(2)}, u32[]{:S(2)}) collective-permute-start(f32[128,512]{1,0:T(8,128)S(1)} %bitcast_add_fusion.5), channel_id=1, source_target_pairs={{0,16},{1,17},{2,18},{3,19},{4,20},{5,21},{6,22},{7,23},{8,24},{9,... | collective-permute-start | bytes 786440 | tf_op jit(solution)/shard_map/ppermute | solution.py:32
  331.5 23.4 %collective-permute-start.87 = (f32[128,512]{1,0:T(8,128)S(1)}, f32[128,512]{1,0:T(8,128)S(1)}, u32[]{:S(2)}, u32[]{:S(2)}) collective-permute-start(f32[128,512]{1,0:T(8,128)S(1)} %bitcast_add_fusion.4), channel_id=1, source_target_pairs={{0,16},{1,17},{2,18},{3,19},{4,20},{5,21},{6,22},{7,23},{8,24},{9,... | collective-permute-start | bytes 786440 | tf_op jit(solution)/shard_map/ppermute | solution.py:32
  356.8 10.5 %collective-permute-start.92 = (f32[2,104,512]{2,1,0:T(8,128)S(1)}, f32[2,104,512]{2,1,0:T(8,128)S(1)}, u32[]{:S(2)}, u32[]{:S(2)}) collective-permute-start(f32[2,104,512]{2,1,0:T(8,128)S(1)} %add_bitcast_fusion.1), channel_id=1, source_target_pairs={{0,8},{1,9},{2,10},{3,11},{4,12},{5,13},{6,14},{7,15},{8,0},{9,1},... | collective-permute-start | bytes 1277960 | tf_op jit(solution)/shard_map/ppermute | solution.py:32
  367.3 9.1 %collective-permute-start.95 = (f32[4,2,512]{2,1,0:T(2,128)S(1)}, f32[4,2,512]{2,1,0:T(2,128)S(1)}, u32[]{:S(2)}, u32[]{:S(2)}) collective-permute-start(f32[4,2,512]{2,1,0:T(2,128)S(1)} %bitcast.160), channel_id=1, source_target_pairs={{0,24},{1,25},{2,26},{3,27},{4,28},{5,29},{6,30},{7,31},{8,16},{9,... | collective-permute-start | bytes 49160 | tf_op jit(solution)/shard_map/ppermute | solution.py:32
  376.4 16.3 %collective-permute-start.96 = (f32[4,288,256]{2,1,0:T(8,128)S(1)}, f32[4,288,256]{2,1,0:T(8,128)S(1)}, u32[]{:S(2)}, u32[]{:S(2)}) collective-permute-start(f32[4,288,256]{2,1,0:T(8,128)S(1)} %get-tuple-element.324), channel_id=1, source_target_pairs={{0,2},{1,5},{2,0},{3,7},{4,6},{5,1},{6,4},{7,3},{8,10},{9,13},{10,... | collective-permute-start | bytes 3538952 | tf_op jit(solution)/shard_map/ppermute | solution.py:126
  377.6 12.4 %collective-permute-start.97 = (f32[104,512]{1,0:T(8,128)S(1)}, f32[104,512]{1,0:T(8,128)S(1)}, u32[]{:S(2)}, u32[]{:S(2)}) collective-permute-start(f32[104,512]{1,0:T(8,128)S(1)} %bitcast_add_fusion.7), channel_id=1, source_target_pairs={{0,16},{1,17},{2,18},{3,19},{4,20},{5,21},{6,22},{7,23},{8,24},{9,... | collective-permute-start | bytes 638984 | tf_op jit(solution)/shard_map/ppermute | solution.py:32
  400.7 17.1 %collective-permute-start.99 = (f32[8,128,256]{2,1,0:T(8,128)S(1)}, f32[8,128,256]{2,1,0:T(8,128)S(1)}, u32[]{:S(2)}, u32[]{:S(2)}) collective-permute-start(f32[8,128,256]{2,1,0:T(8,128)S(1)} %first_send.5), channel_id=1, source_target_pairs={{0,4},{1,3},{2,6},{3,1},{4,0},{5,7},{6,2},{7,5},{8,12},{9,11},{10,... | collective-permute-start | bytes 3145736 | tf_op jit(solution)/shard_map/ppermute | solution.py:126
  401.9 15.9 %collective-permute-start.101 = (f32[360,512]{1,0:T(8,128)S(1)}, f32[360,512]{1,0:T(8,128)S(1)}, u32[]{:S(2)}, u32[]{:S(2)}) collective-permute-start(f32[360,512]{1,0:T(8,128)S(1)} %pad_maximum_fusion.mine_ref), channel_id=1, source_target_pairs={{0,1},{1,0},{2,3},{3,2},{4,5},{5,4},{6,7},{7,6},{8,9},{9,8},{10,11... | collective-permute-start | bytes 2211848 | tf_op jit(solution)/shard_map/ppermute | solution.py:32
  402.3 15.5 %collective-permute-start.100 = (f32[2,288,256]{2,1,0:T(8,128)S(1)}, f32[2,288,256]{2,1,0:T(8,128)S(1)}, u32[]{:S(2)}, u32[]{:S(2)}) collective-permute-start(f32[2,288,256]{2,1,0:T(8,128)S(1)} %add_bitcast_fusion), channel_id=1, source_target_pairs={{0,8},{1,9},{2,10},{3,11},{4,12},{5,13},{6,14},{7,15},{8,0},{9,1},... | collective-permute-start | bytes 1769480 | tf_op jit(solution)/shard_map/ppermute | solution.py:32
  421.7 15.6 %collective-permute-start.103 = (f32[288,256]{1,0:T(8,128)S(1)}, f32[288,256]{1,0:T(8,128)S(1)}, u32[]{:S(2)}, u32[]{:S(2)}) collective-permute-start(f32[288,256]{1,0:T(8,128)S(1)} %bitcast_add_fusion), channel_id=1, source_target_pairs={{0,16},{1,17},{2,18},{3,19},{4,20},{5,21},{6,22},{7,23},{8,24},{9,... | collective-permute-start | bytes 884744 | tf_op jit(solution)/shard_map/ppermute | solution.py:32
  422.7 14.5 %collective-permute-start.102 = (f32[4,128,256]{2,1,0:T(8,128)S(1)}, f32[4,128,256]{2,1,0:T(8,128)S(1)}, u32[]{:S(2)}, u32[]{:S(2)}) collective-permute-start(f32[4,128,256]{2,1,0:T(8,128)S(1)} %get-tuple-element.339), channel_id=1, source_target_pairs={{0,2},{1,5},{2,0},{3,7},{4,6},{5,1},{6,4},{7,3},{8,10},{9,13},{10,... | collective-permute-start | bytes 1572872 | tf_op jit(solution)/shard_map/ppermute | solution.py:126
  437.3 18.4 %collective-permute-start.105 = (f32[360,512]{1,0:T(8,128)S(1)}, f32[360,512]{1,0:T(8,128)S(1)}, u32[]{:S(2)}, u32[]{:S(2)}) collective-permute-start(f32[360,512]{1,0:T(8,128)S(1)} %pad_maximum_fusion.mine_ref), channel_id=1, source_target_pairs={{0,2},{1,3},{2,0},{3,1},{4,6},{5,7},{6,4},{7,5},{8,10},{9,11},{10,... | collective-permute-start | bytes 2211848 | tf_op jit(solution)/shard_map/ppermute | solution.py:32
  438.2 8.0 %collective-permute-start.104 = (f32[2,128,256]{2,1,0:T(8,128)S(1)}, f32[2,128,256]{2,1,0:T(8,128)S(1)}, u32[]{:S(2)}, u32[]{:S(2)}) collective-permute-start(f32[2,128,256]{2,1,0:T(8,128)S(1)} %add_bitcast_fusion.2), channel_id=1, source_target_pairs={{0,8},{1,9},{2,10},{3,11},{4,12},{5,13},{6,14},{7,15},{8,0},{9,1},... | collective-permute-start | bytes 786440 | tf_op jit(solution)/shard_map/ppermute | solution.py:32
  446.2 8.0 %collective-permute-start.106 = (f32[128,256]{1,0:T(8,128)S(1)}, f32[128,256]{1,0:T(8,128)S(1)}, u32[]{:S(2)}, u32[]{:S(2)}) collective-permute-start(f32[128,256]{1,0:T(8,128)S(1)} %bitcast_add_fusion.8), channel_id=1, source_target_pairs={{0,16},{1,17},{2,18},{3,19},{4,20},{5,21},{6,22},{7,23},{8,24},{9,... | collective-permute-start | bytes 393224 | tf_op jit(solution)/shard_map/ppermute | solution.py:32
  456.3 11.8 %collective-permute-start.107 = (f32[416,256]{1,0:T(8,128)S(1)}, f32[416,256]{1,0:T(8,128)S(1)}, u32[]{:S(2)}, u32[]{:S(2)}) collective-permute-start(f32[416,256]{1,0:T(8,128)S(1)} %pad_maximum_fusion.1.mine_ref), channel_id=1, source_target_pairs={{0,2},{1,3},{2,0},{3,1},{4,6},{5,7},{6,4},{7,5},{8,10},{9,11},{10,... | collective-permute-start | bytes 1277960 | tf_op jit(solution)/shard_map/ppermute | solution.py:32
  (122 other events, 1023.8 us)

commit v5 on v4

--- a/solution.py
+++ b/solution.py
@@ -126,10 +126,21 @@
     return lax.ppermute(value, AXES, pairs)
 
 
-def dp_halves(addends, mask, axis):
+def dp_split(addends, mask, axis):
     bit = bit_of(mask)
     send = sum(at(array, 1 - bit, axis) for array in addends)
-    return [at(array, bit, axis) for array in addends] + [swap(send, mask)]
+    return [at(array, bit, axis) for array in addends], send
+
+
+def dp_halves(addends, mask, axis):
+    keep, send = dp_split(addends, mask, axis)
+    return keep + [swap(send, mask)]
+
+
+VMEM_MIB = {
+    "third_back": 58,
+    "second_back_body": 58,
+}
 
 
 def run(body, grid, in_specs, out_specs, out_shape, scratch=(), flops=0, bytes_accessed=0, prefetch=0, aliases=None):
@@ -146,7 +157,7 @@
         name=body.__name__,
         input_output_aliases=aliases or {},
         compiler_params=pltpu.CompilerParams(
-            vmem_limit_bytes=52 * MIB, dimension_semantics=("arbitrary",) * len(grid)
+            vmem_limit_bytes=VMEM_MIB.get(body.__name__, 44) * MIB, dimension_semantics=("arbitrary",) * len(grid)
         ),
         cost_estimate=pl.CostEstimate(
             flops=flops, bytes_accessed=bytes_accessed, transcendentals=0
@@ -359,8 +370,10 @@
         pre = (h_ref[at, :] - mean) * factor + shift
         a_ref[at, :] = (pre * sigmoid(pre) * v_ref[at, :]).astype(BF16)
     wide_ref[...] = jnp.dot(a_ref[...], w_ref[...], preferred_element_type=F32)
-    h3_ref[...] = wide_ref[...].astype(BF16)
     put_moments(stats_ref, wide_ref, v_ref, False)
+    for i in range(0, rows, 32):
+        at = slice(i, i + 32)
+        h3_ref[at, :] = (wide_ref[at, :] - stats_ref[0, 0:1, :]).astype(BF16)
 
 
 def third_product(parts, members, h2, valid, gain, shift, weight, micro):
@@ -412,11 +425,12 @@
 
 def pool_body(counts, split, refs):
     scalars_ref, part_refs, count_refs = refs[0], refs[1 : 1 + counts], refs[1 + counts : 1 + 2 * counts]
-    h_ref, x_ref, v_ref, gain_ref, shift_ref, size_ref = refs[1 + 2 * counts : 7 + 2 * counts]
-    feat_ref, info_ref, slope_ref, first_ref, second_ref = refs[7 + 2 * counts : 12 + 2 * counts]
+    base_ref, h_ref, x_ref, v_ref, gain_ref, shift_ref, size_ref = refs[1 + 2 * counts : 8 + 2 * counts]
+    feat_ref, info_ref, slope_ref, first_ref, second_ref = refs[8 + 2 * counts : 13 + 2 * counts]
     sums_ref = refs[-1]
     rows, width = h_ref.shape
     mean, scaled = norm_of(part_refs, counts_of(count_refs))
+    mean = mean - base_ref[0, 0:1, :]
     info_ref[0, 0:1, :] = mean
     info_ref[0, 1:2, :] = scaled
     factor = scaled * gain_ref[...]
@@ -449,7 +463,7 @@
     first_ref[...] = crop_sums(sums_ref, 1)
     second_ref[...] = crop_sums(sums_ref, 2)
     if split:
-        keep_ref, send_ref = refs[12 + 2 * counts : 14 + 2 * counts]
+        keep_ref, send_ref = refs[13 + 2 * counts : 15 + 2 * counts]
         low = scalars_ref[1] == 0
         for i in range(0, width, 2 * split):
             one, two = feat[:, i : i + split], feat[:, i + split : i + 2 * split]
@@ -458,7 +472,7 @@
             send_ref[:, place] = jnp.where(low, two, one)
 
 
-def pool(scalars, parts, members, h3, x, valid, gain, shift, sizes, micro, split):
+def pool(scalars, parts, members, base, h3, x, valid, gain, shift, sizes, micro, split):
     rows, channels = h3.shape[0] // micro, h3.shape[1]
     crops = sizes.shape[0] // micro
     width = 1024
@@ -475,6 +489,7 @@
         [pair] * len(parts)
         + [per_micro(part) for part in members]
         + [
+            pair,
             tile,
             tile,
             pl.BlockSpec((rows, 1), lambda m, c, w: (m, 0)),
@@ -489,7 +504,7 @@
         flops=20 * h3.size,
         bytes_accessed=4 * h3.size,
         prefetch=1,
-    )(scalars, *parts, *members, h3, x, valid, gain, shift, sizes)
+    )(scalars, *parts, *members, base, h3, x, valid, gain, shift, sizes)
 
 
 def head_body(feat_ref, w_ref, g_ref, stats_ref):
@@ -1308,43 +1323,47 @@
     )(scalars, *(flat * 4), *([came] * 4))
 
 
-def place_early_body(scalars_ref, mine_ref, far_ref, mine_core_ref, far_core_ref, out_ref, embed_ref, protos_ref, head_ref):
+def four_places(scalars_ref, refs):
+    core, side = scalars_ref[0], scalars_ref[2]
+    return [
+        (core, side, refs[0]),
+        (core, 1 - side, refs[1]),
+        (1 - core, side, refs[2]),
+        (1 - core, 1 - side, refs[3]),
+    ]
+
+
+def place_early_body(scalars_ref, *refs):
+    out_ref, embed_ref, protos_ref, head_ref = refs[8:]
     lines = out_ref.shape[0]
     rows = protos_ref.shape[0] // 2
     wide = 512
     groups = protos_ref.shape[1] // 2 // wide
     lane = embed_ref.shape[1]
     below = embed_ref.shape[0] // 4 // (wide // lane)
-    start = lines + groups * rows + below
-    for c, y, ref in ((0, 0, mine_ref), (0, 1, far_ref), (1, 0, mine_core_ref), (1, 1, far_core_ref)):
-        c = scalars_ref[0] if c == 0 else 1 - scalars_ref[0]
-        y = scalars_ref[2] if y == 0 else 1 - scalars_ref[2]
-        column = pl.multiple_of((2 * c + y) * wide, wide)
-        out_ref[:, pl.ds(column, wide)] = ref[0:lines, :]
-        head_ref[:, pl.ds(column, wide)] = ref[start:, :]
+    start = lines + groups * rows
+    for c, y, ref in four_places(scalars_ref, refs[:4]):
+        out_ref[:, pl.ds(pl.multiple_of((2 * c + y) * wide, wide), wide)] = ref[0:lines, :]
         at = pl.ds(pl.multiple_of(y * rows, rows), rows)
         for q in range(groups):
             column = pl.multiple_of((c * groups + q) * wide, wide)
             protos_ref[at, pl.ds(column, wide)] = ref[lines + q * rows : lines + (q + 1) * rows, :]
         for q in range(wide // lane):
             first = pl.multiple_of(((2 * c + y) * (wide // lane) + q) * below, below)
-            embed_ref[pl.ds(first, below), :] = ref[
-                lines + groups * rows : start, q * lane : (q + 1) * lane
-            ]
-
-
-def place_late_body(scalars_ref, mine_ref, far_ref, mine_core_ref, far_core_ref, *out_refs):
-    for c, y, ref in ((0, 0, mine_ref), (0, 1, far_ref), (1, 0, mine_core_ref), (1, 1, far_core_ref)):
-        c = scalars_ref[0] if c == 0 else 1 - scalars_ref[0]
-        y = scalars_ref[2] if y == 0 else 1 - scalars_ref[2]
-        start = 0
-        for out_ref in out_refs:
-            rows, width = out_ref.shape[0] // 2, out_ref.shape[1] // 2
+            embed_ref[pl.ds(first, below), :] = ref[start:, q * lane : (q + 1) * lane]
+    for c, y, ref in four_places(scalars_ref, refs[4:8]):
+        head_ref[:, pl.ds(pl.multiple_of((2 * c + y) * wide, wide), wide)] = ref[...]
+
+
+def place_late_body(scalars_ref, *refs):
+    outs = refs[8:]
+    for out_ref, pieces in zip(outs, (refs[:4], refs[4:8])):
+        rows, width = out_ref.shape[0] // 2, out_ref.shape[1] // 2
+        for c, y, ref in four_places(scalars_ref, pieces):
             out_ref[
                 pl.ds(pl.multiple_of(y * rows, rows), rows),
                 pl.ds(pl.multiple_of(c * width, width), width),
-            ] = ref[start : start + rows, :]
-            start += rows
+            ] = ref[...]
 
 
 def placed_pieces(body, scalars, pieces, outs):
@@ -1415,11 +1434,13 @@
     act_two, h3, stats, info_two = third_product(
         parts, members, h2, valid, row(gain_two), row(shift_two), conv_out, micro
     )
+    base = stats
     parts = moment_parts(stats, counts)
     feat, info_three, slope, slope_first, slope_second, *feat_halves = pool(
         scalars,
         parts,
         members,
+        base,
         h3,
         x,
         valid,
@@ -1623,10 +1644,11 @@
         mid_out = first_send(scalars, late)
         d_two, mid_out = tie(d_two, mid_out)
         mid_came = core_swap(mid_out, near, 2)
-        heads = [dp_halves(head, far[1], 0) for head in heads]
+        halves = [dp_split(head, far[1], 0) for head in heads]
+        head_came = swap(jnp.concatenate([send for _, send in halves], 0), far[1])
         dy, sums = from_second(d_two)
-        dy, sums, mid_came, heads[0][-1], heads[1][-1], early_keep, early_came = tie(
-            dy, sums, mid_came, heads[0][-1], heads[1][-1], early_keep, early_came
+        dy, sums, mid_came, head_came, early_keep, early_came = tie(
+            dy, sums, mid_came, head_came, early_keep, early_came
         )
         early = [by_bits(early_keep), by_bits(early_came)]
 
@@ -1652,26 +1674,35 @@
         inner = [[sharded(in_keep), sharded(in_recv)]]
         in_out = first_send(scalars, inner)
         mid = dp_halves([by_bits(mid_keep), by_bits(mid_came)], far[0], 1)
-        early_mine = jnp.concatenate([sum(early), sum(heads[0]), sum(heads[1])], 0)
-        d_one, in_out, early_mine = tie(d_one, in_out, early_mine)
+        d_one, in_out = tie(d_one, in_out)
         in_came = core_swap(in_out, near, 2)
-        early_core = swap(early_mine, 1)
+        early_mine, head_mine = sum(early), jnp.concatenate([sum(keep) for keep, _ in halves], 0) + head_came
+        early_core, head_core = swap(early_mine, 1), swap(head_mine, 1)
         grad_x = pixels_grad(d_one, conv_in, wide, slope, micro)
-        grad_x, in_came, mid[-1], early_core = tie(grad_x, in_came, mid[-1], early_core)
-        mid = dp_halves(mid, far[1], 0)
+        grad_x, in_came, mid[-1], early_mine, early_core, head_mine, head_core = tie(
+            grad_x, in_came, mid[-1], early_mine, early_core, head_mine, head_core
+        )
+        mid_keep, mid_out = dp_split(mid, far[1], 0)
+        in_came, mid_out = tie(in_came, mid_out)
+        mid_came = swap(mid_out, far[1])
         in_out, in_keep = second_send(scalars, inner, in_came)
         in_came = core_swap(in_out, 2, near)
-        in_came, mid[-1], early_mine = tie(in_came, mid[-1], early_mine)
+        head_far = swap(head_mine, 2)
+        in_came, mid_came, head_far = tie(in_came, mid_came, head_far)
         inner = dp_halves([by_bits(in_keep), by_bits(in_came)], far[0], 1)
-        early_far = swap(early_mine, 2)
+        mid_mine = sum(mid_keep) + mid_came
+        early_far, mid_core, head_both = swap(early_mine, 2), swap(mid_mine, 1), swap(head_far, 1)
+        inner[-1], early_far, mid_mine, mid_core, head_both = tie(
+            inner[-1], early_far, mid_mine, mid_core, head_both
+        )
         inner = dp_halves(inner, far[1], 0)
-        early_far, inner[-1] = tie(early_far, inner[-1])
-        early_pieces = [early_mine, early_far, early_core, swap(early_far, 1)]
+        mid_far, early_both = swap(mid_mine, 2), swap(early_far, 1)
         channel = channels // shards
         early_grads = placed_pieces(
             place_early_body,
             scalars,
-            early_pieces,
+            [early_mine, early_far, early_core, early_both]
+            + [head_mine, head_far, head_core, head_both],
             [
                 shape((conv_out.shape[0] // shards, channels)),
                 shape((embed_weight.shape[0] // shards, embed_weight.shape[1])),
@@ -1679,16 +1710,15 @@
                 shape((channel, head_weight.shape[1])),
             ],
         )
-        late_mine = jnp.concatenate([sum(mid), sum(inner)], 0)
-        late_far = swap(late_mine, 2)
-        late_core = swap(late_mine, 1)
-        late_far, late_core, *early_grads = tie(late_far, late_core, *early_grads)
+        inner[-1], mid_far, *early_grads = tie(inner[-1], mid_far, *early_grads)
+        in_mine = sum(inner)
+        in_far, in_core, mid_both = swap(in_mine, 2), swap(in_mine, 1), swap(mid_far, 1)
         grad_conv_out, grad_embed, grad_protos, grad_head = early_grads
         grad_protos = grad_protos[:, :protos]
         grad_conv_mid, grad_conv_in = placed_pieces(
             place_late_body,
             scalars,
-            [late_mine, late_far, late_core, swap(late_far, 1)],
+            [mid_mine, mid_far, mid_core, mid_both, in_mine, in_far, in_core, swap(in_far, 1)],
             [
                 shape((conv_mid.shape[0] // shards, conv_mid.shape[1])),
                 shape((channel, conv_in.shape[1])),

time: 481 us -> 469 us (0.975)
  Pallas kernels: 197 us -> 166 us
  local copies, waits for them, and re-layouts: 16.8 us -> 24.8 us
  starting transfers between devices: 112 us -> 118 us
    unnamed x90 -> x218, local copies, waits for them, and re-layouts: 10.4 us -> 19.1 us
    ppermute x105 -> x110, starting transfers between devices: 106 us -> 112 us  [swap(): return lax.ppermute(value, AXES, [(i, i ^ mask) for i in range(count)])]
    pallas_call x2, Pallas kernels: 25.7 us -> 20.6 us  [mid_grad(): run(named(name, body, *([len(ins) - 7] if with_d else [])), (TAPS,), [who...]
    ppermute x105 -> x110, waiting for transfers between devices: 128 us -> 132 us  [swap(): return lax.ppermute(value, AXES, [(i, i ^ mask) for i in range(count)])]
  transfers between devices with their start and end apart: 111 -> 116, of which waited for: 77 -> 79; matrix products, arithmetic and copies ran while one was open for 3% -> 3% of each run, Pallas kernels for 25% -> 22%
where the time goes in v5:
time: 469 us; the launch traced here: 461 us
  Pallas kernels  166 us (35%)
  waiting for transfers between devices  136 us (29%)
  starting transfers between devices  118 us (25%)
  local copies, waits for them, and re-layouts  24.8 us (5%)
  other arithmetic  13 us (3%)
    ppermute x110, waiting for transfers between devices, swap(): return lax.ppermute(value, AXES, [(i, i ^ mask) for i in range(count)])  132 us
    ppermute x110, starting transfers between devices, swap(): return lax.ppermute(value, AXES, [(i, i ^ mask) for i in range(count)])  112 us
    pallas_call x2, Pallas kernels, mid_grad(): run(named(name, body, *([len(ins) - 7] if with_d else [])), (TAPS,), [who...  20.6 us
    unnamed x218, local copies, waits for them, and re-layouts  19.1 us
    pallas_call x1, Pallas kernels, third_back(): run(named('third_back', third_back_body, len(parts)), (micro,), [per_micr...  19 us
    pallas_call x1, Pallas kernels, pool(): run(named('pool', pool_body, len(parts), split), (micro, channels // widt...  17.4 us
    pallas_call x1, Pallas kernels, second_back(): run(second_back_body, (micro,), [mid, whole(weight), pl.BlockSpec((rows,...  17.3 us
    pallas_call x1, Pallas kernels, second_product(): run(named('second_product', second_body, len(parts)), (micro,), [per_micr...  15.4 us
  transfers between devices with their start and end apart: 116, of which 79 were waited for; matrix products, arithmetic and copies ran while one was open for 3% of the time, Pallas kernels for 22%

profile of v5, /device:TPU:0, one launch (start us, length us, event | category | flops | bytes accessed | tf_op | source)
XLA Modules:
  0.0 460.7 jit_solution(8139018625296235429)
XLA Ops:
  3.7 7.3 %first_body.1 = (f32[2048,512]{1,0:T(8,128)S(1)}, f32[4,3,512]{2,1,0:T(4,128)S(1)}) custom-call(bf16[2048,2048]{1,0:T(8,128)(2,1)} %bitcast.209, bf16[2048,512]{1,0:T(8,128)(2,1)S(1)} %copy-done.13, f32[2048,1]{1,0:T(8,128)S(1)} %copy.114.v_ref.refs_5_.refs_9_.refs_12_.refs_8_.refs_7_), custom_call_target="tpu_custom_call" | custom-call | flops 4294967296 | bytes 8388608 | tf_op jit(solution)/shard_map/first_body/pallas_call | solution.py:258
  14.5 2.9 collective-permute-start.1
  19.2 4.6 collective-permute-done.3
  24.0 3.7 collective-permute-start.6
  29.9 2.6 collective-permute-done.5.refs_2_.refs_6_.refs_7_
  32.5 15.4 %second_product.1 = (bf16[2048,512]{1,0:T(8,128)(2,1)S(1)}, f32[2048,512]{1,0:T(8,128)S(1)}, f32[4,2,512]{2,1,0:T(2,128)S(1)}, f32[4,3,512]{2,1,0:T(4,128)S(1)}) custom-call(f32[4,3,512]{2,1,0:T(4,128)S(1)} %pad_maximum_fusion.7.refs_0_.refs_4_.refs_5_, f32[4,3,512]{2,1,0:T(4,128)S(1)} %collective-permute-done.4.refs_1_.refs_5_.refs_6_, ...), custom_call_target="tpu_custom_call" | custom-call | flops 9663676416 | bytes 10485760 | tf_op jit(solution)/shard_map/second_product/pallas_call | solution.py:330
  62.9 10.4 %third_product.1 = (bf16[2048,512]{1,0:T(8,128)(2,1)S(1)}, bf16[2048,2048]{1,0:T(8,128)(2,1)}, f32[4,2,2048]{2,1,0:T(2,128)S(1)}, f32[4,2,512]{2,1,0:T(2,128)S(1)}) custom-call(f32[4,2,512]{2,1,0:T(2,128)S(1)} %pad_maximum_fusion.10.refs_0_, f32[4,2,512]{2,1,0:T(2,128)S(1)} %collective-permute-done.11.refs_1_, ...), custom_call_target="tpu_custom_call" | custom-call | flops 4294967296 | bytes 16777216 | tf_op jit(solution)/shard_map/third_product/pallas_call | solution.py:383
  93.3 17.4 %pool.1 = (f32[64,2048]{1,0:T(8,128)S(1)}, f32[4,2,2048]{2,1,0:T(2,128)S(1)}, bf16[2048,2048]{1,0:T(8,128)(2,1)}, f32[64,2048]{1,0:T(8,128)S(1)}, f32[64,2048]{1...) custom-call(s32[3]{0:T(128)S(1)} %pad_add_fusion.refs_0_.scalars_ref, ...), custom_call_target="tpu_custom_call" | custom-call | flops 83886080 | bytes 16777216 | tf_op jit(solution)/shard_map/pool/pallas_call | solution.py:486
  112.5 3.0 head_body.1
  115.6 2.8 collective-permute-done.21
  184.6 3.3 loss.1
  203.0 2.6 collective-permute-done.56.refs_3_
  206.9 6.7 %head_back.1 = (f32[64,1024]{1,0:T(8,128)}, f32[64,1024]{1,0:T(8,128)S(1)}, f32[256,2048]{1,0:T(8,128)S(1)}, f32[4,2,2048]{2,1,0:T(2,128)S(1)}) custom-call(s32[1]{0:T(128)} %bitcast.refs_0_, f32[8,2304]{1,0:T(8,128)S(1)} %add_add_fusion.1.refs_1_, f32[8,2304]{1,0:T(8,128)S(1)} %collective-permute-done.55.refs_2_, ...), custom_call_target="tpu_custom_call" | custom-call | flops 536870912 | bytes 8388608 | tf_op jit(solution)/shard_map/head_back/pallas_call | solution.py:586
  237.2 19.0 %third_back.1 = (f32[2048,512]{1,0:T(8,128)}, f32[4,2,512]{2,1,0:T(2,128)}, f32[8,128,512]{2,1,0:T(8,128)}, f32[8,128,512]{2,1,0:T(8,128)}) custom-call(s32[1]{0:T(128)S(6)} %sub.184.refs_0_, f32[4,2,2048]{2,1,0:T(2,128)} %bitcast.222, f32[4,2,2048]{2,1,0:T(2,128)} %copy-done.100, f32[4,2,2048]{2,1,0:T(2,128)} %copy-done.98, f32[4,2,2048]{2,1,0:T(2,128)} %copy-done.96, ...), custom_call_target="tpu_custom_call" | custom-call | flops 8589934592 | bytes 25165824 | tf_op jit(solution)/shard_map/third_back/pallas_call | solution.py:690
  282.1 12.4 %mid_first.1 = (bf16[2048,512]{1,0:T(8,128)(2,1)S(1)}, f32[4608,256]{1,0:T(8,128)}) custom-call(s32[1]{0:T(128)S(6)} %sub.184.refs_0_, f32[4,2,512]{2,1,0:T(2,128)S(1)} %bitcast.186, f32[4,2,512]{2,1,0:T(2,128)S(1)} %copy-done.54, f32[4,2,512]{2,1,0:T(2,128)S(1)} %copy-done.51, f32[4,2,512]{2,1,0:T(2,128)S(1)} %collective-permute-done.79.refs_4_, ...), custom_call_target="tpu_custom_call" | custom-call | flops 4831838208 | bytes 4718592 | tf_op jit(solution)/shard_map/mid_first/pallas_call | solution.py:803
  294.5 3.7 collective-permute-done.80.refs_17_.refs_18_.refs_19_.refs_20_
  301.7 8.3 %mid_second.1 = f32[4608,256]{1,0:T(8,128)S(1)} custom-call(s32[1]{0:T(128)} %bitcast.refs_0_, bf16[2048,512]{1,0:T(8,128)(2,1)S(1)} %get-tuple-element.299.refs_1_.d_ref, bf16[2048,512]{1,0:T(8,128)(2,1)S(1)} %copy-done.72), custom_call_target="tpu_custom_call" | custom-call | flops 4831838208 | bytes 4718592 | tf_op jit(solution)/shard_map/mid_second/pallas_call | solution.py:803
  310.0 6.0 %collective-permute-done.84 = f32[2,128,512]{2,1,0:T(8,128)S(1)} collective-permute-done((f32[2,128,512]{2,1,0:T(8,128)S(1)}, f32[2,128,512]{2,1,0:T(8,128)S(1)}, u32[]{:S(2)}, u32[]{:S(2)}) %collective-permute-start.84) | collective-permute-done | bytes 524320 | tf_op jit(solution)/shard_map/ppermute | solution.py:32
  316.0 3.6 first_send.4
  323.6 17.3 %second_back_body.1 = (f32[2048,512]{1,0:T(8,128)}, f32[4,2,512]{2,1,0:T(2,128)}) custom-call(bf16[2048,512]{1,0:T(8,128)(2,1)} %copy-done.73, bf16[4608,512]{1,0:T(8,128)(2,1)} %w_ref.6, f32[2048,1]{1,0:T(8,128)} %copy-done.7, f32[2048,512]{1,0:T(8,128)} %copy-done.11, f32[4,3,512]{2,1,0:T(4,128)} %copy-done.33, f32[1,512]{1,0:T(1,128)} %bitcast.198, ...), custom_call_target="tpu_custom_call" | custom-call | flops 9663676416 | bytes 10485760 | tf_op jit(solution)/shard_map/second_back_body/pallas_call | solution.py:888
  340.9 7.6 %collective-permute-done.86 = f32[256,512]{1,0:T(8,128)} collective-permute-done((f32[256,512]{1,0:T(8,128)}, f32[256,512]{1,0:T(8,128)}, u32[]{:S(2)}, u32[]{:S(2)}) %collective-permute-start.86) | collective-permute-done | bytes 524320 | tf_op jit(solution)/shard_map/ppermute | solution.py:32
  358.5 2.9 collective-permute-done.91
  363.3 2.6 collective-permute-start.92
  365.9 3.2 second_send.4
  372.1 11.6 %in_grad.1 = (bf16[2048,512]{1,0:T(8,128)(2,1)S(1)}, f32[2048,256]{1,0:T(8,128)}, f32[2048,256]{1,0:T(8,128)S(1)}) custom-call(s32[1]{0:T(128)S(6)} %sub.184.refs_0_, f32[4,2,512]{2,1,0:T(2,128)S(1)} %bitcast.179, f32[4,2,512]{2,1,0:T(2,128)S(1)} %collective-permute-done.92.refs_2_, f32[4,2,512]{2,1,0:T(2,128)S(1)} %collective-permute-done.93.refs_3_, ...), custom_call_target="tpu_custom_call" | custom-call | flops 4294967296 | bytes 23068672 | tf_op jit(solution)/shard_map/in_grad/pallas_call | solution.py:844
  387.5 3.5 collective-permute-done.97
  399.7 9.3 %pixels_body.1 = bf16[2048,2048]{1,0:T(8,128)(2,1)} custom-call(bf16[2048,512]{1,0:T(8,128)(2,1)S(1)} %copy-done.18, bf16[2048,512]{1,0:T(8,128)(2,1)S(1)} %copy-done.14, f32[256,2048]{1,0:T(8,128)S(1)} %copy-done.16, bf16[2048,2048]{1,0:T(8,128)(2,1)} %get-tuple-element.250.refs_6_.slope_ref), custom_call_target="tpu_custom_call" | custom-call | flops 4294967296 | bytes 16777216 | tf_op jit(solution)/shard_map/pixels_body/pallas_call | solution.py:928
  409.1 3.5 collective-permute-done.99
  420.7 11.8 %collective-permute-done.103 = f32[288,256]{1,0:T(8,128)S(1)} collective-permute-done((f32[288,256]{1,0:T(8,128)S(1)}, f32[288,256]{1,0:T(8,128)S(1)}, u32[]{:S(2)}, u32[]{:S(2)}) %collective-permute-start.103) | collective-permute-done | bytes 294944 | tf_op jit(solution)/shard_map/ppermute | solution.py:32
  432.5 4.7 %collective-permute-done.104.refs_5_ = f32[256,512]{1,0:T(8,128)S(1)} collective-permute-done((f32[256,512]{1,0:T(8,128)S(1)}, f32[256,512]{1,0:T(8,128)S(1)}, u32[]{:S(2)}, u32[]{:S(2)}) %collective-permute-start.104) | collective-permute-done | bytes 524320 | tf_op jit(solution)/shard_map/ppermute | solution.py:32
  439.5 4.2 collective-permute-done.105
  453.8 3.2 collective-permute-done.113.refs_5_
  (525 shorter events, 237.2 us)
Async XLA Ops:
  110.7 7.7 %collective-permute-start.21 = (f32[64,1024]{1,0:T(8,128)S(1)}, f32[64,1024]{1,0:T(8,128)S(1)}, u32[]{:S(2)}, u32[]{:S(2)}) collective-permute-start(f32[64,1024]{1,0:T(8,128)S(1)} %get-tuple-element.202), channel_id=1, source_target_pairs={{0,4},{1,5},{2,6},{3,7},{4,0},{5,1},{6,2},{7,3},{8,12},{9,13},{10,... | collective-permute-start | bytes 786440 | tf_op jit(solution)/shard_map/ppermute | solution.py:32
  111.1 7.3 %collective-permute-start.22 = (f32[64,1024]{1,0:T(8,128)S(1)}, f32[64,1024]{1,0:T(8,128)S(1)}, u32[]{:S(2)}, u32[]{:S(2)}) collective-permute-start(f32[64,1024]{1,0:T(8,128)S(1)} %get-tuple-element.203), channel_id=1, source_target_pairs={{0,2},{1,3},{2,0},{3,1},{4,6},{5,7},{6,4},{7,5},{8,10},{9,11},{10,... | collective-permute-start | bytes 786440 | tf_op jit(solution)/shard_map/ppermute | solution.py:32
  205.6 9.4 %collective-permute-start.59 = (f32[8,80,512]{2,1,0:T(8,128)S(1)}, f32[8,80,512]{2,1,0:T(8,128)S(1)}, u32[]{:S(2)}, u32[]{:S(2)}) collective-permute-start(f32[8,80,512]{2,1,0:T(8,128)S(1)} %get-tuple-element.233), channel_id=1, source_target_pairs={{0,1},{1,0},{2,3},{3,2},{4,5},{5,4},{6,7},{7,6},{8,9},{9,8},{10,11... | collective-permute-start | bytes 3932168 | tf_op jit(solution)/shard_map/ppermute | solution.py:32
  205.7 9.2 %collective-permute-start.58 = (f32[64,1024]{1,0:T(8,128)S(1)}, f32[64,1024]{1,0:T(8,128)S(1)}, u32[]{:S(2)}, u32[]{:S(2)}) collective-permute-start(f32[64,1024]{1,0:T(8,128)S(1)} %copy-done.91), channel_id=1, source_target_pairs={{0,2},{1,3},{2,0},{3,1},{4,6},{5,7},{6,4},{7,5},{8,10},{9,11},{10,... | collective-permute-start | bytes 786440 | tf_op jit(solution)/shard_map/ppermute | solution.py:32
  217.3 8.3 %collective-permute-start.65 = (f32[256,1024]{1,0:T(8,128)S(1)}, f32[256,1024]{1,0:T(8,128)}, u32[]{:S(2)}, u32[]{:S(2)}) collective-permute-start(f32[256,1024]{1,0:T(8,128)S(1)} %constant_dynamic-update-slice_fusion.feat_ref), channel_id=1, source_target_pairs={{0,1},{1,0},{2,3},{3,2},{4,5},{5,4},{6,7},{7,6},{8,9},{9,8},{10,11... | collective-permute-start | bytes 3145736 | tf_op jit(solution)/shard_map/ppermute | solution.py:32
  233.7 22.6 %collective-permute-start.71 = (f32[128,512]{1,0:T(8,128)S(1)}, f32[128,512]{1,0:T(8,128)S(1)}, u32[]{:S(2)}, u32[]{:S(2)}) collective-permute-start(f32[128,512]{1,0:T(8,128)S(1)} %get-tuple-element.258), channel_id=1, source_target_pairs={{0,6},{1,7},{2,4},{3,5},{4,2},{5,3},{6,0},{7,1},{8,14},{9,15},{10,... | collective-permute-start | bytes 786440 | tf_op jit(solution)/shard_map/ppermute | solution.py:32
  235.4 20.9 %collective-permute-start.69 = (f32[128,512]{1,0:T(8,128)S(1)}, f32[128,512]{1,0:T(8,128)S(1)}, u32[]{:S(2)}, u32[]{:S(2)}) collective-permute-start(f32[128,512]{1,0:T(8,128)S(1)} %get-tuple-element.258), channel_id=1, source_target_pairs={{0,2},{1,3},{2,0},{3,1},{4,6},{5,7},{6,4},{7,5},{8,10},{9,11},{10,... | collective-permute-start | bytes 786440 | tf_op jit(solution)/shard_map/ppermute | solution.py:32
  236.4 19.9 %collective-permute-start.70 = (f32[128,512]{1,0:T(8,128)S(1)}, f32[128,512]{1,0:T(8,128)S(1)}, u32[]{:S(2)}, u32[]{:S(2)}) collective-permute-start(f32[128,512]{1,0:T(8,128)S(1)} %get-tuple-element.259.dg_ref), channel_id=1, source_target_pairs={{0,4},{1,5},{2,6},{3,7},{4,0},{5,1},{6,2},{7,3},{8,12},{9,13},{10,... | collective-permute-start | bytes 786440 | tf_op jit(solution)/shard_map/ppermute | solution.py:32
  265.0 10.9 %collective-permute-start.79 = (f32[4,2,512]{2,1,0:T(2,128)S(1)}, f32[4,2,512]{2,1,0:T(2,128)S(1)}, u32[]{:S(2)}, u32[]{:S(2)}) collective-permute-start(f32[4,2,512]{2,1,0:T(2,128)S(1)} %bitcast.183), channel_id=1, source_target_pairs={{0,24},{1,25},{2,26},{3,27},{4,28},{5,29},{6,30},{7,31},{8,16},{9,... | collective-permute-start | bytes 49160 | tf_op jit(solution)/shard_map/ppermute | solution.py:32
  267.1 8.8 %collective-permute-start.78 = (f32[4,2,512]{2,1,0:T(2,128)S(1)}, f32[4,2,512]{2,1,0:T(2,128)S(1)}, u32[]{:S(2)}, u32[]{:S(2)}) collective-permute-start(f32[4,2,512]{2,1,0:T(2,128)S(1)} %bitcast.184), channel_id=1, source_target_pairs={{0,16},{1,17},{2,18},{3,19},{4,20},{5,21},{6,22},{7,23},{8,24},{9,... | collective-permute-start | bytes 49160 | tf_op jit(solution)/shard_map/ppermute | solution.py:32
  267.2 8.7 %collective-permute-start.77 = (f32[4,2,512]{2,1,0:T(2,128)S(1)}, f32[4,2,512]{2,1,0:T(2,128)S(1)}, u32[]{:S(2)}, u32[]{:S(2)}) collective-permute-start(f32[4,2,512]{2,1,0:T(2,128)S(1)} %bitcast.185), channel_id=1, source_target_pairs={{0,8},{1,9},{2,10},{3,11},{4,12},{5,13},{6,14},{7,15},{8,0},{9,1},... | collective-permute-start | bytes 49160 | tf_op jit(solution)/shard_map/ppermute | solution.py:32
  276.0 22.2 %collective-permute-start.80 = (f32[8,104,512]{2,1,0:T(8,128)}, f32[8,104,512]{2,1,0:T(8,128)}, u32[]{:S(2)}, u32[]{:S(2)}) collective-permute-start(f32[8,104,512]{2,1,0:T(8,128)} %first_send.3), channel_id=1, source_target_pairs={{0,4},{1,3},{2,6},{3,1},{4,0},{5,7},{6,2},{7,5},{8,12},{9,11},{10,... | collective-permute-start | bytes 5111816 | tf_op jit(solution)/shard_map/ppermute | solution.py:126
  279.3 15.2 %collective-permute-start.81 = (f32[2,128,512]{2,1,0:T(8,128)S(1)}, f32[2,128,512]{2,1,0:T(8,128)S(1)}, u32[]{:S(2)}, u32[]{:S(2)}) collective-permute-start(f32[2,128,512]{2,1,0:T(8,128)S(1)} %dynamic-slice_bitcast_fusion.1), channel_id=1, source_target_pairs={{0,8},{1,9},{2,10},{3,11},{4,12},{5,13},{6,14},{7,15},{8,0},{9,1},... | collective-permute-start | bytes 1572872 | tf_op jit(solution)/shard_map/ppermute | solution.py:32
  298.2 17.8 %collective-permute-start.82 = (f32[4608,256]{1,0:T(8,128)}, f32[4608,256]{1,0:T(8,128)}, u32[]{:S(2)}, u32[]{:S(2)}) collective-permute-start(f32[4608,256]{1,0:T(8,128)} %get-tuple-element.294), channel_id=1, source_target_pairs={{0,1},{1,0},{2,3},{3,2},{4,5},{5,4},{6,7},{7,6},{8,9},{9,8},{10,11... | collective-permute-start | bytes 14155784 | tf_op jit(solution)/shard_map/ppermute | solution.py:32
  300.5 15.5 %collective-permute-start.83 = (f32[4,104,512]{2,1,0:T(8,128)S(1)}, f32[4,104,512]{2,1,0:T(8,128)}, u32[]{:S(2)}, u32[]{:S(2)}) collective-permute-start(f32[4,104,512]{2,1,0:T(8,128)S(1)} %get-tuple-element.296), channel_id=1, source_target_pairs={{0,2},{1,5},{2,0},{3,7},{4,6},{5,1},{6,4},{7,3},{8,10},{9,13},{10,... | collective-permute-start | bytes 2555912 | tf_op jit(solution)/shard_map/ppermute | solution.py:126
  301.6 14.3 %collective-permute-start.84 = (f32[2,128,512]{2,1,0:T(8,128)S(1)}, f32[2,128,512]{2,1,0:T(8,128)S(1)}, u32[]{:S(2)}, u32[]{:S(2)}) collective-permute-start(f32[2,128,512]{2,1,0:T(8,128)S(1)} %dynamic-slice_bitcast_fusion), channel_id=1, source_target_pairs={{0,8},{1,9},{2,10},{3,11},{4,12},{5,13},{6,14},{7,15},{8,0},{9,1},... | collective-permute-start | bytes 1572872 | tf_op jit(solution)/shard_map/ppermute | solution.py:32
  319.5 29.2 %collective-permute-start.85 = (f32[8,288,256]{2,1,0:T(8,128)}, f32[8,288,256]{2,1,0:T(8,128)}, u32[]{:S(2)}, u32[]{:S(2)}) collective-permute-start(f32[8,288,256]{2,1,0:T(8,128)} %first_send.4), channel_id=1, source_target_pairs={{0,4},{1,3},{2,6},{3,1},{4,0},{5,7},{6,2},{7,5},{8,12},{9,11},{10,... | collective-permute-start | bytes 7077896 | tf_op jit(solution)/shard_map/ppermute | solution.py:126
  322.9 25.6 %collective-permute-start.86 = (f32[256,512]{1,0:T(8,128)}, f32[256,512]{1,0:T(8,128)}, u32[]{:S(2)}, u32[]{:S(2)}) collective-permute-start(f32[256,512]{1,0:T(8,128)} %pad_maximum_fusion), channel_id=1, source_target_pairs={{0,16},{1,17},{2,18},{3,19},{4,20},{5,21},{6,22},{7,23},{8,24},{9,... | collective-permute-start | bytes 1572872 | tf_op jit(solution)/shard_map/ppermute | solution.py:32
  349.8 11.7 %collective-permute-start.91 = (f32[2,104,512]{2,1,0:T(8,128)S(1)}, f32[2,104,512]{2,1,0:T(8,128)S(1)}, u32[]{:S(2)}, u32[]{:S(2)}) collective-permute-start(f32[2,104,512]{2,1,0:T(8,128)S(1)} %add_bitcast_fusion.1), channel_id=1, source_target_pairs={{0,8},{1,9},{2,10},{3,11},{4,12},{5,13},{6,14},{7,15},{8,0},{9,1},... | collective-permute-start | bytes 1277960 | tf_op jit(solution)/shard_map/ppermute | solution.py:32
  361.5 7.7 %collective-permute-start.94 = (f32[4,2,512]{2,1,0:T(2,128)S(1)}, f32[4,2,512]{2,1,0:T(2,128)S(1)}, u32[]{:S(2)}, u32[]{:S(2)}) collective-permute-start(f32[4,2,512]{2,1,0:T(2,128)S(1)} %bitcast.176), channel_id=1, source_target_pairs={{0,24},{1,25},{2,26},{3,27},{4,28},{5,29},{6,30},{7,31},{8,16},{9,... | collective-permute-start | bytes 49160 | tf_op jit(solution)/shard_map/ppermute | solution.py:32
  369.2 16.3 %collective-permute-start.95 = (f32[4,288,256]{2,1,0:T(8,128)S(1)}, f32[4,288,256]{2,1,0:T(8,128)S(1)}, u32[]{:S(2)}, u32[]{:S(2)}) collective-permute-start(f32[4,288,256]{2,1,0:T(8,128)S(1)} %get-tuple-element.330), channel_id=1, source_target_pairs={{0,2},{1,5},{2,0},{3,7},{4,6},{5,1},{6,4},{7,3},{8,10},{9,13},{10,... | collective-permute-start | bytes 3538952 | tf_op jit(solution)/shard_map/ppermute | solution.py:126
  371.4 13.7 %collective-permute-start.96 = (f32[104,512]{1,0:T(8,128)S(1)}, f32[104,512]{1,0:T(8,128)S(1)}, u32[]{:S(2)}, u32[]{:S(2)}) collective-permute-start(f32[104,512]{1,0:T(8,128)S(1)} %bitcast_add_fusion.7), channel_id=1, source_target_pairs={{0,16},{1,17},{2,18},{3,19},{4,20},{5,21},{6,22},{7,23},{8,24},{9,... | collective-permute-start | bytes 638984 | tf_op jit(solution)/shard_map/ppermute | solution.py:32
  393.4 19.2 %collective-permute-start.98 = (f32[8,128,256]{2,1,0:T(8,128)S(1)}, f32[8,128,256]{2,1,0:T(8,128)S(1)}, u32[]{:S(2)}, u32[]{:S(2)}) collective-permute-start(f32[8,128,256]{2,1,0:T(8,128)S(1)} %first_send.5), channel_id=1, source_target_pairs={{0,4},{1,3},{2,6},{3,1},{4,0},{5,7},{6,2},{7,5},{8,12},{9,11},{10,... | collective-permute-start | bytes 3145736 | tf_op jit(solution)/shard_map/ppermute | solution.py:126
  396.6 12.5 %collective-permute-start.101 = (f32[256,512]{1,0:T(8,128)S(1)}, f32[256,512]{1,0:T(8,128)S(1)}, u32[]{:S(2)}, u32[]{:S(2)}) collective-permute-start(f32[256,512]{1,0:T(8,128)S(1)} %maximum_add_fusion.refs_4_), channel_id=1, source_target_pairs={{0,1},{1,0},{2,3},{3,2},{4,5},{5,4},{6,7},{7,6},{8,9},{9,8},{10,11... | collective-permute-start | bytes 1572872 | tf_op jit(solution)/shard_map/ppermute | solution.py:32
  396.8 15.8 %collective-permute-start.99 = (f32[2,288,256]{2,1,0:T(8,128)S(1)}, f32[2,288,256]{2,1,0:T(8,128)S(1)}, u32[]{:S(2)}, u32[]{:S(2)}) collective-permute-start(f32[2,288,256]{2,1,0:T(8,128)S(1)} %add_bitcast_fusion), channel_id=1, source_target_pairs={{0,8},{1,9},{2,10},{3,11},{4,12},{5,13},{6,14},{7,15},{8,0},{9,1},... | collective-permute-start | bytes 1769480 | tf_op jit(solution)/shard_map/ppermute | solution.py:32
  399.5 9.6 %collective-permute-start.100 = (f32[104,512]{1,0:T(8,128)S(1)}, f32[104,512]{1,0:T(8,128)S(1)}, u32[]{:S(2)}, u32[]{:S(2)}) collective-permute-start(f32[104,512]{1,0:T(8,128)S(1)} %fusion.1.refs_0_), channel_id=1, source_target_pairs={{0,1},{1,0},{2,3},{3,2},{4,5},{5,4},{6,7},{7,6},{8,9},{9,8},{10,11... | collective-permute-start | bytes 638984 | tf_op jit(solution)/shard_map/ppermute | solution.py:32
  414.7 17.7 %collective-permute-start.102 = (f32[4,128,256]{2,1,0:T(8,128)S(1)}, f32[4,128,256]{2,1,0:T(8,128)S(1)}, u32[]{:S(2)}, u32[]{:S(2)}) collective-permute-start(f32[4,128,256]{2,1,0:T(8,128)S(1)} %get-tuple-element.345), channel_id=1, source_target_pairs={{0,2},{1,5},{2,0},{3,7},{4,6},{5,1},{6,4},{7,3},{8,10},{9,13},{10,... | collective-permute-start | bytes 1572872 | tf_op jit(solution)/shard_map/ppermute | solution.py:126
  415.8 21.4 %collective-permute-start.104 = (f32[256,512]{1,0:T(8,128)S(1)}, f32[256,512]{1,0:T(8,128)S(1)}, u32[]{:S(2)}, u32[]{:S(2)}) collective-permute-start(f32[256,512]{1,0:T(8,128)S(1)} %maximum_add_fusion.refs_4_), channel_id=1, source_target_pairs={{0,2},{1,3},{2,0},{3,1},{4,6},{5,7},{6,4},{7,5},{8,10},{9,11},{10,... | collective-permute-start | bytes 1572872 | tf_op jit(solution)/shard_map/ppermute | solution.py:32
  417.0 15.5 %collective-permute-start.103 = (f32[288,256]{1,0:T(8,128)S(1)}, f32[288,256]{1,0:T(8,128)S(1)}, u32[]{:S(2)}, u32[]{:S(2)}) collective-permute-start(f32[288,256]{1,0:T(8,128)S(1)} %bitcast_add_fusion.1), channel_id=1, source_target_pairs={{0,16},{1,17},{2,18},{3,19},{4,20},{5,21},{6,22},{7,23},{8,24},{9,... | collective-permute-start | bytes 884744 | tf_op jit(solution)/shard_map/ppermute | solution.py:32
  419.7 19.8 %collective-permute-start.106 = (f32[104,512]{1,0:T(8,128)S(1)}, f32[104,512]{1,0:T(8,128)S(1)}, u32[]{:S(2)}, u32[]{:S(2)}) collective-permute-start(f32[104,512]{1,0:T(8,128)S(1)} %fusion.1.refs_0_), channel_id=1, source_target_pairs={{0,2},{1,3},{2,0},{3,1},{4,6},{5,7},{6,4},{7,5},{8,10},{9,11},{10,... | collective-permute-start | bytes 638984 | tf_op jit(solution)/shard_map/ppermute | solution.py:32
  443.7 8.4 %collective-permute-start.110 = (f32[288,256]{1,0:T(8,128)S(1)}, f32[288,256]{1,0:T(8,128)S(1)}, u32[]{:S(2)}, u32[]{:S(2)}) collective-permute-start(f32[288,256]{1,0:T(8,128)S(1)} %fusion.refs_0_), channel_id=1, source_target_pairs={{0,2},{1,3},{2,0},{3,1},{4,6},{5,7},{6,4},{7,5},{8,10},{9,11},{10,... | collective-permute-start | bytes 884744 | tf_op jit(solution)/shard_map/ppermute | solution.py:32
  444.7 7.3 %collective-permute-start.109 = (f32[128,256]{1,0:T(8,128)S(1)}, f32[128,256]{1,0:T(8,128)S(1)}, u32[]{:S(2)}, u32[]{:S(2)}) collective-permute-start(f32[128,256]{1,0:T(8,128)S(1)} %bitcast_add_fusion.9), channel_id=1, source_target_pairs={{0,16},{1,17},{2,18},{3,19},{4,20},{5,21},{6,22},{7,23},{8,24},{9,... | collective-permute-start | bytes 393224 | tf_op jit(solution)/shard_map/ppermute | solution.py:32
  (191 other events, 2050.8 us)

commit v6 on v5

--- a/solution.py
+++ b/solution.py
@@ -1610,8 +1610,9 @@
         early = grads["early"]
         *parts_two, early_out, partial = tie(*parts_two, grads["early_out"], grads["head"])
         early_came = core_swap(early_out, near, 2)
-        partial = partial.reshape(2, 2, 2, -1, partial.shape[1])
-        heads = [dp_halves([partial[:, :, 0]], far[0], 1)]
+        partial = partial.reshape(2, 2, -1, partial.shape[1])
+        most = partial.shape[2] * 3 // 4
+        heads = [dp_halves([partial[:, :, :most]], far[0], 1)]
         d_two, mid_send = mid_grad(
             "mid_first",
             mid_first_body,
@@ -1623,7 +1624,7 @@
         d_two, mid_send, early_came, heads[0][-1] = tie(
             d_two, mid_send, early_came, heads[0][-1]
         )
-        heads.append(dp_halves([partial[:, :, 1]], far[0], 1))
+        heads.append(dp_halves([partial[:, :, most:]], far[0], 1))
         mid_recv = swap(mid_send, 1)
         early_out, early_keep = second_send(scalars, early, early_came)
         early_came = core_swap(early_out, 2, near)
@@ -1676,24 +1677,27 @@
         mid = dp_halves([by_bits(mid_keep), by_bits(mid_came)], far[0], 1)
         d_one, in_out = tie(d_one, in_out)
         in_came = core_swap(in_out, near, 2)
-        early_mine, head_mine = sum(early), jnp.concatenate([sum(keep) for keep, _ in halves], 0) + head_came
-        early_core, head_core = swap(early_mine, 1), swap(head_mine, 1)
         grad_x = pixels_grad(d_one, conv_in, wide, slope, micro)
-        grad_x, in_came, mid[-1], early_mine, early_core, head_mine, head_core = tie(
-            grad_x, in_came, mid[-1], early_mine, early_core, head_mine, head_core
-        )
+        grad_x, in_came, mid[-1], early[-1], head_came = tie(
+            grad_x, in_came, mid[-1], early[-1], head_came
+        )
+        head_mine = jnp.concatenate([sum(keep) for keep, _ in halves], 0) + head_came
         mid_keep, mid_out = dp_split(mid, far[1], 0)
         in_came, mid_out = tie(in_came, mid_out)
         mid_came = swap(mid_out, far[1])
         in_out, in_keep = second_send(scalars, inner, in_came)
         in_came = core_swap(in_out, 2, near)
-        head_far = swap(head_mine, 2)
-        in_came, mid_came, head_far = tie(in_came, mid_came, head_far)
+        head_far, head_core = swap(head_mine, 2), swap(head_mine, 1)
+        early_mine = sum(early)
+        in_came, mid_came, head_far, head_core, early_mine = tie(
+            in_came, mid_came, head_far, head_core, early_mine
+        )
         inner = dp_halves([by_bits(in_keep), by_bits(in_came)], far[0], 1)
         mid_mine = sum(mid_keep) + mid_came
-        early_far, mid_core, head_both = swap(early_mine, 2), swap(mid_mine, 1), swap(head_far, 1)
-        inner[-1], early_far, mid_mine, mid_core, head_both = tie(
-            inner[-1], early_far, mid_mine, mid_core, head_both
+        early_far, early_core = swap(early_mine, 2), swap(early_mine, 1)
+        mid_core, head_both = swap(mid_mine, 1), swap(head_far, 1)
+        inner[-1], early_far, early_core, mid_mine, mid_core, head_both = tie(
+            inner[-1], early_far, early_core, mid_mine, mid_core, head_both
         )
         inner = dp_halves(inner, far[1], 0)
         mid_far, early_both = swap(mid_mine, 2), swap(early_far, 1)

time: 469 us -> 465 us (level)
  waiting for transfers between devices: 136 us -> 130 us
    ppermute x110, waiting for transfers between devices: 132 us -> 125 us  [swap(): return lax.ppermute(value, AXES, [(i, i ^ mask) for i in range(count)])]
    unnamed x218 -> x216, local copies, waits for them, and re-layouts: 19.1 us -> 19.7 us
  transfers between devices with their start and end apart: 116 -> 116, of which waited for: 79 -> 79; matrix products, arithmetic and copies ran while one was open for 3% -> 4% of each run, Pallas kernels for 22% -> 22%
where the time goes in v6:
time: 465 us; the launch traced here: 457 us
  Pallas kernels  165 us (35%)
  waiting for transfers between devices  130 us (28%)
  starting transfers between devices  119 us (26%)
  local copies, waits for them, and re-layouts  26.3 us (6%)
  other arithmetic  13.9 us (3%)
    ppermute x110, waiting for transfers between devices, swap(): return lax.ppermute(value, AXES, [(i, i ^ mask) for i in range(count)])  125 us
    ppermute x110, starting transfers between devices, swap(): return lax.ppermute(value, AXES, [(i, i ^ mask) for i in range(count)])  111 us
    pallas_call x2, Pallas kernels, mid_grad(): run(named(name, body, *([len(ins) - 7] if with_d else [])), (TAPS,), [who...  20.6 us
    unnamed x216, local copies, waits for them, and re-layouts  19.7 us
    pallas_call x1, Pallas kernels, third_back(): run(named('third_back', third_back_body, len(parts)), (micro,), [per_micr...  19 us
    pallas_call x1, Pallas kernels, pool(): run(named('pool', pool_body, len(parts), split), (micro, channels // widt...  17.4 us
    pallas_call x1, Pallas kernels, second_back(): run(second_back_body, (micro,), [mid, whole(weight), pl.BlockSpec((rows,...  17.2 us
    pallas_call x1, Pallas kernels, second_product(): run(named('second_product', second_body, len(parts)), (micro,), [per_micr...  15.4 us
  transfers between devices with their start and end apart: 116, of which 79 were waited for; matrix products, arithmetic and copies ran while one was open for 4% of the time, Pallas kernels for 22%

profile of v6, /device:TPU:0, one launch (start us, length us, event | category | flops | bytes accessed | tf_op | source)
XLA Modules:
  0.0 456.6 jit_solution(14845465550896109548)
XLA Ops:
  3.7 7.3 %first_body.1 = (f32[2048,512]{1,0:T(8,128)S(1)}, f32[4,3,512]{2,1,0:T(4,128)S(1)}) custom-call(bf16[2048,2048]{1,0:T(8,128)(2,1)} %bitcast.210, bf16[2048,512]{1,0:T(8,128)(2,1)S(1)} %copy-done.13, f32[2048,1]{1,0:T(8,128)S(1)} %copy.114.v_ref.refs_5_.refs_9_.refs_12_.refs_8_.refs_7_), custom_call_target="tpu_custom_call" | custom-call | flops 4294967296 | bytes 8388608 | tf_op jit(solution)/shard_map/first_body/pallas_call | solution.py:258
  14.5 2.9 collective-permute-start.1
  19.2 4.6 %collective-permute-done.3 = f32[4,3,512]{2,1,0:T(4,128)S(1)} collective-permute-done((f32[4,3,512]{2,1,0:T(4,128)S(1)}, f32[4,3,512]{2,1,0:T(4,128)S(1)}, u32[]{:S(2)}, u32[]{:S(2)}) %collective-permute-start.3) | collective-permute-done | bytes 24608 | tf_op jit(solution)/shard_map/ppermute | solution.py:32
  24.0 3.7 collective-permute-start.6
  29.9 2.6 collective-permute-done.5.refs_2_.refs_6_.refs_7_
  32.5 15.4 %second_product.1 = (bf16[2048,512]{1,0:T(8,128)(2,1)S(1)}, f32[2048,512]{1,0:T(8,128)S(1)}, f32[4,2,512]{2,1,0:T(2,128)S(1)}, f32[4,3,512]{2,1,0:T(4,128)S(1)}) custom-call(f32[4,3,512]{2,1,0:T(4,128)S(1)} %pad_maximum_fusion.7.refs_0_.refs_4_.refs_5_, f32[4,3,512]{2,1,0:T(4,128)S(1)} %collective-permute-done.4.refs_1_.refs_5_.refs_6_, ...), custom_call_target="tpu_custom_call" | custom-call | flops 9663676416 | bytes 10485760 | tf_op jit(solution)/shard_map/second_product/pallas_call | solution.py:330
  62.9 10.4 %third_product.1 = (bf16[2048,512]{1,0:T(8,128)(2,1)S(1)}, bf16[2048,2048]{1,0:T(8,128)(2,1)}, f32[4,2,2048]{2,1,0:T(2,128)S(1)}, f32[4,2,512]{2,1,0:T(2,128)S(1)}) custom-call(f32[4,2,512]{2,1,0:T(2,128)S(1)} %pad_maximum_fusion.10.refs_0_, f32[4,2,512]{2,1,0:T(2,128)S(1)} %collective-permute-done.11.refs_1_, ...), custom_call_target="tpu_custom_call" | custom-call | flops 4294967296 | bytes 16777216 | tf_op jit(solution)/shard_map/third_product/pallas_call | solution.py:383
  84.6 2.5 collective-permute-start.20
  93.3 17.4 %pool.1 = (f32[64,2048]{1,0:T(8,128)S(1)}, f32[4,2,2048]{2,1,0:T(2,128)S(1)}, bf16[2048,2048]{1,0:T(8,128)(2,1)}, f32[64,2048]{1,0:T(8,128)S(1)}, f32[64,2048]{1...) custom-call(s32[3]{0:T(128)S(1)} %pad_add_fusion.refs_0_.scalars_ref, ...), custom_call_target="tpu_custom_call" | custom-call | flops 83886080 | bytes 16777216 | tf_op jit(solution)/shard_map/pool/pallas_call | solution.py:486
  112.5 3.0 head_body.1
  115.6 2.8 collective-permute-done.21
  144.3 2.4 collective-permute-start.36
  184.6 3.3 loss.1
  192.8 2.4 collective-permute-done.54
  202.9 2.6 collective-permute-done.56.refs_3_
  206.8 6.7 %head_back.1 = (f32[64,1024]{1,0:T(8,128)}, f32[64,1024]{1,0:T(8,128)S(1)}, f32[256,2048]{1,0:T(8,128)S(1)}, f32[4,2,2048]{2,1,0:T(2,128)S(1)}) custom-call(s32[1]{0:T(128)} %bitcast.refs_0_, f32[8,2304]{1,0:T(8,128)S(1)} %add_add_fusion.1.refs_1_, f32[8,2304]{1,0:T(8,128)S(1)} %collective-permute-done.55.refs_2_, ...), custom_call_target="tpu_custom_call" | custom-call | flops 536870912 | bytes 8388608 | tf_op jit(solution)/shard_map/head_back/pallas_call | solution.py:586
  237.2 19.0 %third_back.1 = (f32[2048,512]{1,0:T(8,128)}, f32[4,2,512]{2,1,0:T(2,128)}, f32[8,128,512]{2,1,0:T(8,128)}, f32[8,128,512]{2,1,0:T(8,128)}) custom-call(s32[1]{0:T(128)S(6)} %sub.184.refs_0_, f32[4,2,2048]{2,1,0:T(2,128)} %bitcast.223, f32[4,2,2048]{2,1,0:T(2,128)} %copy-done.99, f32[4,2,2048]{2,1,0:T(2,128)} %copy-done.97, f32[4,2,2048]{2,1,0:T(2,128)} %copy-done.95, ...), custom_call_target="tpu_custom_call" | custom-call | flops 8589934592 | bytes 25165824 | tf_op jit(solution)/shard_map/third_back/pallas_call | solution.py:690
  282.5 12.4 %mid_first.1 = (bf16[2048,512]{1,0:T(8,128)(2,1)S(1)}, f32[4608,256]{1,0:T(8,128)}) custom-call(s32[1]{0:T(128)S(6)} %sub.184.refs_0_, f32[4,2,512]{2,1,0:T(2,128)S(1)} %bitcast.187, f32[4,2,512]{2,1,0:T(2,128)S(1)} %copy-done.54, f32[4,2,512]{2,1,0:T(2,128)S(1)} %copy-done.51, f32[4,2,512]{2,1,0:T(2,128)S(1)} %collective-permute-done.79.refs_4_, ...), custom_call_target="tpu_custom_call" | custom-call | flops 4831838208 | bytes 4718592 | tf_op jit(solution)/shard_map/mid_first/pallas_call | solution.py:803
  302.9 8.3 %mid_second.1 = f32[4608,256]{1,0:T(8,128)S(1)} custom-call(s32[1]{0:T(128)} %bitcast.refs_0_, bf16[2048,512]{1,0:T(8,128)(2,1)S(1)} %get-tuple-element.300.refs_1_.d_ref, bf16[2048,512]{1,0:T(8,128)(2,1)S(1)} %copy-done.72), custom_call_target="tpu_custom_call" | custom-call | flops 4831838208 | bytes 4718592 | tf_op jit(solution)/shard_map/mid_second/pallas_call | solution.py:803
  313.5 3.4 first_send.4
  323.3 17.2 %second_back_body.1 = (f32[2048,512]{1,0:T(8,128)}, f32[4,2,512]{2,1,0:T(2,128)}) custom-call(bf16[2048,512]{1,0:T(8,128)(2,1)} %copy-done.73, bf16[4608,512]{1,0:T(8,128)(2,1)} %w_ref.6, f32[2048,1]{1,0:T(8,128)} %copy-done.7, f32[2048,512]{1,0:T(8,128)} %copy-done.11, f32[4,3,512]{2,1,0:T(4,128)} %copy-done.33, f32[1,512]{1,0:T(1,128)} %bitcast.199, ...), custom_call_target="tpu_custom_call" | custom-call | flops 9663676416 | bytes 10485760 | tf_op jit(solution)/shard_map/second_back_body/pallas_call | solution.py:888
  340.6 6.5 %collective-permute-done.86 = f32[256,512]{1,0:T(8,128)} collective-permute-done((f32[256,512]{1,0:T(8,128)}, f32[256,512]{1,0:T(8,128)}, u32[]{:S(2)}, u32[]{:S(2)}) %collective-permute-start.86) | collective-permute-done | bytes 524320 | tf_op jit(solution)/shard_map/ppermute | solution.py:32
  363.2 3.2 second_send.4
  369.6 11.6 %in_grad.1 = (bf16[2048,512]{1,0:T(8,128)(2,1)S(1)}, f32[2048,256]{1,0:T(8,128)}, f32[2048,256]{1,0:T(8,128)S(1)}) custom-call(s32[1]{0:T(128)S(6)} %sub.184.refs_0_, f32[4,2,512]{2,1,0:T(2,128)S(1)} %bitcast.180, f32[4,2,512]{2,1,0:T(2,128)S(1)} %collective-permute-done.92.refs_2_, f32[4,2,512]{2,1,0:T(2,128)S(1)} %collective-permute-done.93.refs_3_, ...), custom_call_target="tpu_custom_call" | custom-call | flops 4294967296 | bytes 23068672 | tf_op jit(solution)/shard_map/in_grad/pallas_call | solution.py:844
  385.8 2.4 collective-permute-done.97
  393.7 9.5 %pixels_body.1 = bf16[2048,2048]{1,0:T(8,128)(2,1)} custom-call(bf16[2048,512]{1,0:T(8,128)(2,1)S(1)} %copy-done.18, bf16[2048,512]{1,0:T(8,128)(2,1)S(1)} %copy-done.14, f32[256,2048]{1,0:T(8,128)S(1)} %copy-done.16, bf16[2048,2048]{1,0:T(8,128)(2,1)} %get-tuple-element.251.refs_6_.slope_ref), custom_call_target="tpu_custom_call" | custom-call | flops 4294967296 | bytes 16777216 | tf_op jit(solution)/shard_map/pixels_body/pallas_call | solution.py:928
  403.1 3.7 collective-permute-done.99
  416.1 12.7 %collective-permute-done.101 = f32[288,256]{1,0:T(8,128)S(1)} collective-permute-done((f32[288,256]{1,0:T(8,128)S(1)}, f32[288,256]{1,0:T(8,128)S(1)}, u32[]{:S(2)}, u32[]{:S(2)}) %collective-permute-start.101) | collective-permute-done | bytes 294944 | tf_op jit(solution)/shard_map/ppermute | solution.py:32
  431.5 5.1 %collective-permute-done.105.refs_1_ = f32[104,512]{1,0:T(8,128)S(1)} collective-permute-done((f32[104,512]{1,0:T(8,128)S(1)}, f32[104,512]{1,0:T(8,128)S(1)}, u32[]{:S(2)}, u32[]{:S(2)}) %collective-permute-start.105) | collective-permute-done | bytes 213024 | tf_op jit(solution)/shard_map/ppermute | solution.py:32
  442.2 2.4 place_early_body.1
  444.5 3.3 collective-permute-done.109
  449.6 3.3 collective-permute-done.113.refs_5_
  (524 shorter events, 239.9 us)
Async XLA Ops:
  110.7 7.7 %collective-permute-start.21 = (f32[64,1024]{1,0:T(8,128)S(1)}, f32[64,1024]{1,0:T(8,128)S(1)}, u32[]{:S(2)}, u32[]{:S(2)}) collective-permute-start(f32[64,1024]{1,0:T(8,128)S(1)} %get-tuple-element.203), channel_id=1, source_target_pairs={{0,4},{1,5},{2,6},{3,7},{4,0},{5,1},{6,2},{7,3},{8,12},{9,13},{10,... | collective-permute-start | bytes 786440 | tf_op jit(solution)/shard_map/ppermute | solution.py:32
  205.6 9.4 %collective-permute-start.59 = (f32[8,80,512]{2,1,0:T(8,128)S(1)}, f32[8,80,512]{2,1,0:T(8,128)S(1)}, u32[]{:S(2)}, u32[]{:S(2)}) collective-permute-start(f32[8,80,512]{2,1,0:T(8,128)S(1)} %get-tuple-element.234), channel_id=1, source_target_pairs={{0,1},{1,0},{2,3},{3,2},{4,5},{5,4},{6,7},{7,6},{8,9},{9,8},{10,11... | collective-permute-start | bytes 3932168 | tf_op jit(solution)/shard_map/ppermute | solution.py:32
  205.7 9.2 %collective-permute-start.58 = (f32[64,1024]{1,0:T(8,128)S(1)}, f32[64,1024]{1,0:T(8,128)S(1)}, u32[]{:S(2)}, u32[]{:S(2)}) collective-permute-start(f32[64,1024]{1,0:T(8,128)S(1)} %copy-done.89), channel_id=1, source_target_pairs={{0,2},{1,3},{2,0},{3,1},{4,6},{5,7},{6,4},{7,5},{8,10},{9,11},{10,... | collective-permute-start | bytes 786440 | tf_op jit(solution)/shard_map/ppermute | solution.py:32
  217.3 8.3 %collective-permute-start.65 = (f32[256,1024]{1,0:T(8,128)S(1)}, f32[256,1024]{1,0:T(8,128)}, u32[]{:S(2)}, u32[]{:S(2)}) collective-permute-start(f32[256,1024]{1,0:T(8,128)S(1)} %constant_dynamic-update-slice_fusion.feat_ref), channel_id=1, source_target_pairs={{0,1},{1,0},{2,3},{3,2},{4,5},{5,4},{6,7},{7,6},{8,9},{9,8},{10,11... | collective-permute-start | bytes 3145736 | tf_op jit(solution)/shard_map/ppermute | solution.py:32
  233.7 22.6 %collective-permute-start.71 = (f32[128,512]{1,0:T(8,128)S(1)}, f32[128,512]{1,0:T(8,128)S(1)}, u32[]{:S(2)}, u32[]{:S(2)}) collective-permute-start(f32[128,512]{1,0:T(8,128)S(1)} %get-tuple-element.259), channel_id=1, source_target_pairs={{0,6},{1,7},{2,4},{3,5},{4,2},{5,3},{6,0},{7,1},{8,14},{9,15},{10,... | collective-permute-start | bytes 786440 | tf_op jit(solution)/shard_map/ppermute | solution.py:32
  235.4 20.9 %collective-permute-start.69 = (f32[128,512]{1,0:T(8,128)S(1)}, f32[128,512]{1,0:T(8,128)S(1)}, u32[]{:S(2)}, u32[]{:S(2)}) collective-permute-start(f32[128,512]{1,0:T(8,128)S(1)} %get-tuple-element.259), channel_id=1, source_target_pairs={{0,2},{1,3},{2,0},{3,1},{4,6},{5,7},{6,4},{7,5},{8,10},{9,11},{10,... | collective-permute-start | bytes 786440 | tf_op jit(solution)/shard_map/ppermute | solution.py:32
  236.4 19.9 %collective-permute-start.70 = (f32[128,512]{1,0:T(8,128)S(1)}, f32[128,512]{1,0:T(8,128)S(1)}, u32[]{:S(2)}, u32[]{:S(2)}) collective-permute-start(f32[128,512]{1,0:T(8,128)S(1)} %get-tuple-element.260.dg_ref), channel_id=1, source_target_pairs={{0,4},{1,5},{2,6},{3,7},{4,0},{5,1},{6,2},{7,3},{8,12},{9,13},{10,... | collective-permute-start | bytes 786440 | tf_op jit(solution)/shard_map/ppermute | solution.py:32
  265.0 11.0 %collective-permute-start.79 = (f32[4,2,512]{2,1,0:T(2,128)S(1)}, f32[4,2,512]{2,1,0:T(2,128)S(1)}, u32[]{:S(2)}, u32[]{:S(2)}) collective-permute-start(f32[4,2,512]{2,1,0:T(2,128)S(1)} %bitcast.184), channel_id=1, source_target_pairs={{0,24},{1,25},{2,26},{3,27},{4,28},{5,29},{6,30},{7,31},{8,16},{9,... | collective-permute-start | bytes 49160 | tf_op jit(solution)/shard_map/ppermute | solution.py:32
  267.1 8.9 %collective-permute-start.78 = (f32[4,2,512]{2,1,0:T(2,128)S(1)}, f32[4,2,512]{2,1,0:T(2,128)S(1)}, u32[]{:S(2)}, u32[]{:S(2)}) collective-permute-start(f32[4,2,512]{2,1,0:T(2,128)S(1)} %bitcast.185), channel_id=1, source_target_pairs={{0,16},{1,17},{2,18},{3,19},{4,20},{5,21},{6,22},{7,23},{8,24},{9,... | collective-permute-start | bytes 49160 | tf_op jit(solution)/shard_map/ppermute | solution.py:32
  267.2 8.8 %collective-permute-start.77 = (f32[4,2,512]{2,1,0:T(2,128)S(1)}, f32[4,2,512]{2,1,0:T(2,128)S(1)}, u32[]{:S(2)}, u32[]{:S(2)}) collective-permute-start(f32[4,2,512]{2,1,0:T(2,128)S(1)} %bitcast.186), channel_id=1, source_target_pairs={{0,8},{1,9},{2,10},{3,11},{4,12},{5,13},{6,14},{7,15},{8,0},{9,1},... | collective-permute-start | bytes 49160 | tf_op jit(solution)/shard_map/ppermute | solution.py:32
  276.1 22.2 %collective-permute-start.80 = (f32[8,104,512]{2,1,0:T(8,128)}, f32[8,104,512]{2,1,0:T(8,128)}, u32[]{:S(2)}, u32[]{:S(2)}) collective-permute-start(f32[8,104,512]{2,1,0:T(8,128)} %first_send.3), channel_id=1, source_target_pairs={{0,4},{1,3},{2,6},{3,1},{4,0},{5,7},{6,2},{7,5},{8,12},{9,11},{10,... | collective-permute-start | bytes 5111816 | tf_op jit(solution)/shard_map/ppermute | solution.py:126
  279.2 16.8 %collective-permute-start.81 = (f32[2,192,512]{2,1,0:T(8,128)S(1)}, f32[2,192,512]{2,1,0:T(8,128)S(1)}, u32[]{:S(2)}, u32[]{:S(2)}) collective-permute-start(f32[2,192,512]{2,1,0:T(8,128)S(1)} %dynamic-slice_bitcast_fusion), channel_id=1, source_target_pairs={{0,8},{1,9},{2,10},{3,11},{4,12},{5,13},{6,14},{7,15},{8,0},{9,1},... | collective-permute-start | bytes 2359304 | tf_op jit(solution)/shard_map/ppermute | solution.py:32
  298.3 15.2 %collective-permute-start.82 = (f32[4608,256]{1,0:T(8,128)}, f32[4608,256]{1,0:T(8,128)}, u32[]{:S(2)}, u32[]{:S(2)}) collective-permute-start(f32[4608,256]{1,0:T(8,128)} %get-tuple-element.295), channel_id=1, source_target_pairs={{0,1},{1,0},{2,3},{3,2},{4,5},{5,4},{6,7},{7,6},{8,9},{9,8},{10,11... | collective-permute-start | bytes 14155784 | tf_op jit(solution)/shard_map/ppermute | solution.py:32
  300.6 12.9 %collective-permute-start.83 = (f32[4,104,512]{2,1,0:T(8,128)S(1)}, f32[4,104,512]{2,1,0:T(8,128)}, u32[]{:S(2)}, u32[]{:S(2)}) collective-permute-start(f32[4,104,512]{2,1,0:T(8,128)S(1)} %get-tuple-element.297), channel_id=1, source_target_pairs={{0,2},{1,5},{2,0},{3,7},{4,6},{5,1},{6,4},{7,3},{8,10},{9,13},{10,... | collective-permute-start | bytes 2555912 | tf_op jit(solution)/shard_map/ppermute | solution.py:126
  302.8 8.7 %collective-permute-start.84 = (f32[2,64,512]{2,1,0:T(8,128)S(1)}, f32[2,64,512]{2,1,0:T(8,128)S(1)}, u32[]{:S(2)}, u32[]{:S(2)}) collective-permute-start(f32[2,64,512]{2,1,0:T(8,128)S(1)} %dynamic-slice_bitcast_fusion.1), channel_id=1, source_target_pairs={{0,8},{1,9},{2,10},{3,11},{4,12},{5,13},{6,14},{7,15},{8,0},{9,1},... | collective-permute-start | bytes 786440 | tf_op jit(solution)/shard_map/ppermute | solution.py:32
  316.9 30.2 %collective-permute-start.85 = (f32[8,288,256]{2,1,0:T(8,128)}, f32[8,288,256]{2,1,0:T(8,128)}, u32[]{:S(2)}, u32[]{:S(2)}) collective-permute-start(f32[8,288,256]{2,1,0:T(8,128)} %first_send.4), channel_id=1, source_target_pairs={{0,4},{1,3},{2,6},{3,1},{4,0},{5,7},{6,2},{7,5},{8,12},{9,11},{10,... | collective-permute-start | bytes 7077896 | tf_op jit(solution)/shard_map/ppermute | solution.py:126
  321.5 25.6 %collective-permute-start.86 = (f32[256,512]{1,0:T(8,128)}, f32[256,512]{1,0:T(8,128)}, u32[]{:S(2)}, u32[]{:S(2)}) collective-permute-start(f32[256,512]{1,0:T(8,128)} %pad_maximum_fusion), channel_id=1, source_target_pairs={{0,16},{1,17},{2,18},{3,19},{4,20},{5,21},{6,22},{7,23},{8,24},{9,... | collective-permute-start | bytes 1572872 | tf_op jit(solution)/shard_map/ppermute | solution.py:32
  348.1 10.5 %collective-permute-start.91 = (f32[2,104,512]{2,1,0:T(8,128)S(1)}, f32[2,104,512]{2,1,0:T(8,128)S(1)}, u32[]{:S(2)}, u32[]{:S(2)}) collective-permute-start(f32[2,104,512]{2,1,0:T(8,128)S(1)} %add_bitcast_fusion.1), channel_id=1, source_target_pairs={{0,8},{1,9},{2,10},{3,11},{4,12},{5,13},{6,14},{7,15},{8,0},{9,1},... | collective-permute-start | bytes 1277960 | tf_op jit(solution)/shard_map/ppermute | solution.py:32
  358.7 7.7 %collective-permute-start.94 = (f32[4,2,512]{2,1,0:T(2,128)S(1)}, f32[4,2,512]{2,1,0:T(2,128)S(1)}, u32[]{:S(2)}, u32[]{:S(2)}) collective-permute-start(f32[4,2,512]{2,1,0:T(2,128)S(1)} %bitcast.177), channel_id=1, source_target_pairs={{0,24},{1,25},{2,26},{3,27},{4,28},{5,29},{6,30},{7,31},{8,16},{9,... | collective-permute-start | bytes 49160 | tf_op jit(solution)/shard_map/ppermute | solution.py:32
  366.4 16.3 %collective-permute-start.95 = (f32[4,288,256]{2,1,0:T(8,128)S(1)}, f32[4,288,256]{2,1,0:T(8,128)S(1)}, u32[]{:S(2)}, u32[]{:S(2)}) collective-permute-start(f32[4,288,256]{2,1,0:T(8,128)S(1)} %get-tuple-element.331), channel_id=1, source_target_pairs={{0,2},{1,5},{2,0},{3,7},{4,6},{5,1},{6,4},{7,3},{8,10},{9,13},{10,... | collective-permute-start | bytes 3538952 | tf_op jit(solution)/shard_map/ppermute | solution.py:126
  368.6 13.9 %collective-permute-start.96 = (f32[104,512]{1,0:T(8,128)S(1)}, f32[104,512]{1,0:T(8,128)S(1)}, u32[]{:S(2)}, u32[]{:S(2)}) collective-permute-start(f32[104,512]{1,0:T(8,128)S(1)} %bitcast_add_fusion.5), channel_id=1, source_target_pairs={{0,16},{1,17},{2,18},{3,19},{4,20},{5,21},{6,22},{7,23},{8,24},{9,... | collective-permute-start | bytes 638984 | tf_op jit(solution)/shard_map/ppermute | solution.py:32
  390.5 16.3 %collective-permute-start.98 = (f32[8,128,256]{2,1,0:T(8,128)S(1)}, f32[8,128,256]{2,1,0:T(8,128)S(1)}, u32[]{:S(2)}, u32[]{:S(2)}) collective-permute-start(f32[8,128,256]{2,1,0:T(8,128)S(1)} %first_send.5), channel_id=1, source_target_pairs={{0,4},{1,3},{2,6},{3,1},{4,0},{5,7},{6,2},{7,5},{8,12},{9,11},{10,... | collective-permute-start | bytes 3145736 | tf_op jit(solution)/shard_map/ppermute | solution.py:126
  392.1 14.7 %collective-permute-start.99 = (f32[2,288,256]{2,1,0:T(8,128)S(1)}, f32[2,288,256]{2,1,0:T(8,128)S(1)}, u32[]{:S(2)}, u32[]{:S(2)}) collective-permute-start(f32[2,288,256]{2,1,0:T(8,128)S(1)} %add_bitcast_fusion), channel_id=1, source_target_pairs={{0,8},{1,9},{2,10},{3,11},{4,12},{5,13},{6,14},{7,15},{8,0},{9,1},... | collective-permute-start | bytes 1769480 | tf_op jit(solution)/shard_map/ppermute | solution.py:32
  408.0 20.9 %collective-permute-start.103 = (f32[256,512]{1,0:T(8,128)S(1)}, f32[256,512]{1,0:T(8,128)S(1)}, u32[]{:S(2)}, u32[]{:S(2)}) collective-permute-start(f32[256,512]{1,0:T(8,128)S(1)} %maximum_add_fusion.refs_4_), channel_id=1, source_target_pairs={{0,1},{1,0},{2,3},{3,2},{4,5},{5,4},{6,7},{7,6},{8,9},{9,8},{10,11... | collective-permute-start | bytes 1572872 | tf_op jit(solution)/shard_map/ppermute | solution.py:32
  408.1 20.8 %collective-permute-start.102 = (f32[256,512]{1,0:T(8,128)S(1)}, f32[256,512]{1,0:T(8,128)S(1)}, u32[]{:S(2)}, u32[]{:S(2)}) collective-permute-start(f32[256,512]{1,0:T(8,128)S(1)} %maximum_add_fusion.refs_4_), channel_id=1, source_target_pairs={{0,2},{1,3},{2,0},{3,1},{4,6},{5,7},{6,4},{7,5},{8,10},{9,11},{10,... | collective-permute-start | bytes 1572872 | tf_op jit(solution)/shard_map/ppermute | solution.py:32
  411.3 17.6 %collective-permute-start.100 = (f32[4,128,256]{2,1,0:T(8,128)S(1)}, f32[4,128,256]{2,1,0:T(8,128)S(1)}, u32[]{:S(2)}, u32[]{:S(2)}) collective-permute-start(f32[4,128,256]{2,1,0:T(8,128)S(1)} %get-tuple-element.346), channel_id=1, source_target_pairs={{0,2},{1,5},{2,0},{3,7},{4,6},{5,1},{6,4},{7,3},{8,10},{9,13},{10,... | collective-permute-start | bytes 1572872 | tf_op jit(solution)/shard_map/ppermute | solution.py:126
  412.4 16.4 %collective-permute-start.101 = (f32[288,256]{1,0:T(8,128)S(1)}, f32[288,256]{1,0:T(8,128)S(1)}, u32[]{:S(2)}, u32[]{:S(2)}) collective-permute-start(f32[288,256]{1,0:T(8,128)S(1)} %bitcast_add_fusion.3), channel_id=1, source_target_pairs={{0,16},{1,17},{2,18},{3,19},{4,20},{5,21},{6,22},{7,23},{8,24},{9,... | collective-permute-start | bytes 884744 | tf_op jit(solution)/shard_map/ppermute | solution.py:32
  430.1 8.4 %collective-permute-start.104 = (f32[2,128,256]{2,1,0:T(8,128)S(1)}, f32[2,128,256]{2,1,0:T(8,128)S(1)}, u32[]{:S(2)}, u32[]{:S(2)}) collective-permute-start(f32[2,128,256]{2,1,0:T(8,128)S(1)} %add_bitcast_fusion.2), channel_id=1, source_target_pairs={{0,8},{1,9},{2,10},{3,11},{4,12},{5,13},{6,14},{7,15},{8,0},{9,1},... | collective-permute-start | bytes 786440 | tf_op jit(solution)/shard_map/ppermute | solution.py:32
  430.8 7.8 %collective-permute-start.108 = (f32[256,512]{1,0:T(8,128)S(1)}, f32[256,512]{1,0:T(8,128)S(1)}, u32[]{:S(2)}, u32[]{:S(2)}) collective-permute-start(f32[256,512]{1,0:T(8,128)S(1)} %collective-permute-done.102.refs_5_), channel_id=1, source_target_pairs={{0,1},{1,0},{2,3},{3,2},{4,5},{5,4},{6,7},{7,6},{8,9},{9,8},{10,11... | collective-permute-start | bytes 1572872 | tf_op jit(solution)/shard_map/ppermute | solution.py:32
  430.9 7.7 %collective-permute-start.107 = (f32[288,256]{1,0:T(8,128)S(1)}, f32[288,256]{1,0:T(8,128)S(1)}, u32[]{:S(2)}, u32[]{:S(2)}) collective-permute-start(f32[288,256]{1,0:T(8,128)S(1)} %fusion.refs_0_), channel_id=1, source_target_pairs={{0,1},{1,0},{2,3},{3,2},{4,5},{5,4},{6,7},{7,6},{8,9},{9,8},{10,11... | collective-permute-start | bytes 884744 | tf_op jit(solution)/shard_map/ppermute | solution.py:32
  438.5 9.3 %collective-permute-start.110 = (f32[288,256]{1,0:T(8,128)S(1)}, f32[288,256]{1,0:T(8,128)S(1)}, u32[]{:S(2)}, u32[]{:S(2)}) collective-permute-start(f32[288,256]{1,0:T(8,128)S(1)} %fusion.refs_0_), channel_id=1, source_target_pairs={{0,2},{1,3},{2,0},{3,1},{4,6},{5,7},{6,4},{7,5},{8,10},{9,11},{10,... | collective-permute-start | bytes 884744 | tf_op jit(solution)/shard_map/ppermute | solution.py:32
  439.6 8.2 %collective-permute-start.109 = (f32[128,256]{1,0:T(8,128)S(1)}, f32[128,256]{1,0:T(8,128)S(1)}, u32[]{:S(2)}, u32[]{:S(2)}) collective-permute-start(f32[128,256]{1,0:T(8,128)S(1)} %bitcast_add_fusion.7), channel_id=1, source_target_pairs={{0,16},{1,17},{2,18},{3,19},{4,20},{5,21},{6,22},{7,23},{8,24},{9,... | collective-permute-start | bytes 393224 | tf_op jit(solution)/shard_map/ppermute | solution.py:32
  (190 other events, 1996.9 us)

commit v7 on v6

--- a/solution.py
+++ b/solution.py
@@ -1682,6 +1682,12 @@
             grad_x, in_came, mid[-1], early[-1], head_came
         )
         head_mine = jnp.concatenate([sum(keep) for keep, _ in halves], 0) + head_came
+        in_came, *later = tie(
+            in_came, *parts_one, *parts_two, *parts_three, first_four, second_four
+        )
+        steps = len(parts_one)
+        parts_one, parts_two, parts_three = [later[i * steps : (i + 1) * steps] for i in range(3)]
+        first_four, second_four = later[3 * steps :]
         mid_keep, mid_out = dp_split(mid, far[1], 0)
         in_came, mid_out = tie(in_came, mid_out)
         mid_came = swap(mid_out, far[1])

time: 465 us -> 471 us (1.013)
    unnamed x216 -> x222, local copies, waits for them, and re-layouts: 19.7 us -> 20.4 us
where the time goes in v7:
time: 471 us; the launch traced here: 463 us
  Pallas kernels  167 us (35%)
  waiting for transfers between devices  128 us (27%)
  starting transfers between devices  120 us (25%)
  local copies, waits for them, and re-layouts  27 us (6%)
  other arithmetic  18 us (4%)
    ppermute x110, waiting for transfers between devices, swap(): return lax.ppermute(value, AXES, [(i, i ^ mask) for i in range(count)])  124 us
    ppermute x110, starting transfers between devices, swap(): return lax.ppermute(value, AXES, [(i, i ^ mask) for i in range(count)])  112 us
    pallas_call x2, Pallas kernels, mid_grad(): run(named(name, body, *([len(ins) - 7] if with_d else [])), (TAPS,), [who...  20.6 us
    unnamed x222, local copies, waits for them, and re-layouts  20.4 us
    pallas_call x1, Pallas kernels, third_back(): run(named('third_back', third_back_body, len(parts)), (micro,), [per_micr...  19 us
    pallas_call x1, Pallas kernels, pool(): run(named('pool', pool_body, len(parts), split), (micro, channels // widt...  17.4 us
    pallas_call x1, Pallas kernels, second_back(): run(second_back_body, (micro,), [mid, whole(weight), pl.BlockSpec((rows,...  17.2 us
    pallas_call x1, Pallas kernels, second_product(): run(named('second_product', second_body, len(parts)), (micro,), [per_micr...  15.4 us
  transfers between devices with their start and end apart: 116, of which 79 were waited for; matrix products, arithmetic and copies ran while one was open for 4% of the time, Pallas kernels for 22%

profile of v7, /device:TPU:0, one launch (start us, length us, event | category | flops | bytes accessed | tf_op | source)
XLA Modules:
  0.0 462.6 jit_solution(1020149468678516665)
XLA Ops:
  3.7 7.3 %first_body.1 = (f32[2048,512]{1,0:T(8,128)S(1)}, f32[4,3,512]{2,1,0:T(4,128)S(1)}) custom-call(bf16[2048,2048]{1,0:T(8,128)(2,1)} %bitcast.210, bf16[2048,512]{1,0:T(8,128)(2,1)S(1)} %copy-done.13, f32[2048,1]{1,0:T(8,128)S(1)} %copy.114.v_ref.refs_5_.refs_9_.refs_12_.refs_8_.refs_7_), custom_call_target="tpu_custom_call" | custom-call | flops 4294967296 | bytes 8388608 | tf_op jit(solution)/shard_map/first_body/pallas_call | solution.py:258
  14.4 2.9 collective-permute-start.1
  19.2 4.6 collective-permute-done.3
  24.0 3.7 collective-permute-start.6
  29.8 2.6 collective-permute-done.5.refs_2_.refs_6_.refs_7_
  32.5 15.4 %second_product.1 = (bf16[2048,512]{1,0:T(8,128)(2,1)S(1)}, f32[2048,512]{1,0:T(8,128)S(1)}, f32[4,2,512]{2,1,0:T(2,128)S(1)}, f32[4,3,512]{2,1,0:T(4,128)S(1)}) custom-call(f32[4,3,512]{2,1,0:T(4,128)S(1)} %pad_maximum_fusion.7.refs_0_.refs_4_.refs_5_, f32[4,3,512]{2,1,0:T(4,128)S(1)} %collective-permute-done.4.refs_1_.refs_5_.refs_6_, ...), custom_call_target="tpu_custom_call" | custom-call | flops 9663676416 | bytes 10485760 | tf_op jit(solution)/shard_map/second_product/pallas_call | solution.py:330
  62.9 10.4 %third_product.1 = (bf16[2048,512]{1,0:T(8,128)(2,1)S(1)}, bf16[2048,2048]{1,0:T(8,128)(2,1)}, f32[4,2,2048]{2,1,0:T(2,128)S(1)}, f32[4,2,512]{2,1,0:T(2,128)S(1)}) custom-call(f32[4,2,512]{2,1,0:T(2,128)S(1)} %pad_maximum_fusion.10.refs_0_, f32[4,2,512]{2,1,0:T(2,128)S(1)} %collective-permute-done.11.refs_1_, ...), custom_call_target="tpu_custom_call" | custom-call | flops 4294967296 | bytes 16777216 | tf_op jit(solution)/shard_map/third_product/pallas_call | solution.py:383
  84.6 2.5 collective-permute-start.20
  93.3 17.4 %pool.1 = (f32[64,2048]{1,0:T(8,128)S(1)}, f32[4,2,2048]{2,1,0:T(2,128)S(1)}, bf16[2048,2048]{1,0:T(8,128)(2,1)}, f32[64,2048]{1,0:T(8,128)S(1)}, f32[64,2048]{1...) custom-call(s32[3]{0:T(128)S(1)} %pad_add_fusion.refs_0_.scalars_ref, ...), custom_call_target="tpu_custom_call" | custom-call | flops 83886080 | bytes 16777216 | tf_op jit(solution)/shard_map/pool/pallas_call | solution.py:486
  112.5 3.0 head_body.1
  115.6 2.8 collective-permute-done.21
  184.6 3.3 loss.1
  202.9 2.6 collective-permute-done.56.refs_3_
  206.8 6.7 %head_back.1 = (f32[64,1024]{1,0:T(8,128)}, f32[64,1024]{1,0:T(8,128)S(1)}, f32[256,2048]{1,0:T(8,128)S(1)}, f32[4,2,2048]{2,1,0:T(2,128)S(1)}) custom-call(s32[1]{0:T(128)} %bitcast.refs_0_, f32[8,2304]{1,0:T(8,128)S(1)} %add_add_fusion.1.refs_1_, f32[8,2304]{1,0:T(8,128)S(1)} %collective-permute-done.55.refs_2_, ...), custom_call_target="tpu_custom_call" | custom-call | flops 536870912 | bytes 8388608 | tf_op jit(solution)/shard_map/head_back/pallas_call | solution.py:586
  237.2 19.0 %third_back.1 = (f32[2048,512]{1,0:T(8,128)}, f32[4,2,512]{2,1,0:T(2,128)}, f32[8,128,512]{2,1,0:T(8,128)}, f32[8,128,512]{2,1,0:T(8,128)}) custom-call(s32[1]{0:T(128)S(6)} %sub.184.refs_0_, f32[4,2,2048]{2,1,0:T(2,128)} %bitcast.223, f32[4,2,2048]{2,1,0:T(2,128)} %copy-done.102, f32[4,2,2048]{2,1,0:T(2,128)} %copy-done.100, f32[4,2,2048]{2,1,0:T(2,128)} %copy-done.98, ...), custom_call_target="tpu_custom_call" | custom-call | flops 8589934592 | bytes 25165824 | tf_op jit(solution)/shard_map/third_back/pallas_call | solution.py:690
  282.5 12.4 %mid_first.1 = (bf16[2048,512]{1,0:T(8,128)(2,1)S(1)}, f32[4608,256]{1,0:T(8,128)}) custom-call(s32[1]{0:T(128)S(6)} %sub.184.refs_0_, f32[4,2,512]{2,1,0:T(2,128)S(1)} %bitcast.187, f32[4,2,512]{2,1,0:T(2,128)S(1)} %copy-done.57, f32[4,2,512]{2,1,0:T(2,128)S(1)} %copy-done.54, f32[4,2,512]{2,1,0:T(2,128)S(1)} %collective-permute-done.79.refs_4_, ...), custom_call_target="tpu_custom_call" | custom-call | flops 4831838208 | bytes 4718592 | tf_op jit(solution)/shard_map/mid_first/pallas_call | solution.py:803
  302.8 8.3 %mid_second.1 = f32[4608,256]{1,0:T(8,128)S(1)} custom-call(s32[1]{0:T(128)} %bitcast.refs_0_, bf16[2048,512]{1,0:T(8,128)(2,1)S(1)} %get-tuple-element.315.refs_1_.d_ref, bf16[2048,512]{1,0:T(8,128)(2,1)S(1)} %copy-done.75), custom_call_target="tpu_custom_call" | custom-call | flops 4831838208 | bytes 4718592 | tf_op jit(solution)/shard_map/mid_second/pallas_call | solution.py:803
  313.4 3.4 first_send.4
  323.3 17.2 %second_back_body.1 = (f32[2048,512]{1,0:T(8,128)}, f32[4,2,512]{2,1,0:T(2,128)}) custom-call(bf16[2048,512]{1,0:T(8,128)(2,1)} %copy-done.76, bf16[4608,512]{1,0:T(8,128)(2,1)} %w_ref.6, f32[2048,1]{1,0:T(8,128)} %copy-done.7, f32[2048,512]{1,0:T(8,128)} %copy-done.11, f32[4,3,512]{2,1,0:T(4,128)} %copy-done.36, f32[1,512]{1,0:T(1,128)} %bitcast.199, ...), custom_call_target="tpu_custom_call" | custom-call | flops 9663676416 | bytes 10485760 | tf_op jit(solution)/shard_map/second_back_body/pallas_call | solution.py:888
  340.5 6.5 %collective-permute-done.86 = f32[256,512]{1,0:T(8,128)} collective-permute-done((f32[256,512]{1,0:T(8,128)}, f32[256,512]{1,0:T(8,128)}, u32[]{:S(2)}, u32[]{:S(2)}) %collective-permute-start.86) | collective-permute-done | bytes 524320 | tf_op jit(solution)/shard_map/ppermute | solution.py:32
  363.1 3.2 second_send.4
  369.5 11.7 %in_grad.1 = (bf16[2048,512]{1,0:T(8,128)(2,1)S(1)}, f32[2048,256]{1,0:T(8,128)}, f32[2048,256]{1,0:T(8,128)S(1)}) custom-call(s32[1]{0:T(128)S(6)} %sub.184.refs_0_, f32[4,2,512]{2,1,0:T(2,128)S(1)} %bitcast.180, f32[4,2,512]{2,1,0:T(2,128)S(1)} %collective-permute-done.92.refs_2_, f32[4,2,512]{2,1,0:T(2,128)S(1)} %collective-permute-done.93.refs_3_, ...), custom_call_target="tpu_custom_call" | custom-call | flops 4294967296 | bytes 23068672 | tf_op jit(solution)/shard_map/in_grad/pallas_call | solution.py:844
  384.6 3.6 collective-permute-done.97
  394.5 9.5 %pixels_body.1 = bf16[2048,2048]{1,0:T(8,128)(2,1)} custom-call(bf16[2048,512]{1,0:T(8,128)(2,1)S(1)} %copy-done.18, bf16[2048,512]{1,0:T(8,128)(2,1)S(1)} %copy-done.14, f32[256,2048]{1,0:T(8,128)S(1)} %copy-done.16, bf16[2048,2048]{1,0:T(8,128)(2,1)} %get-tuple-element.266.refs_6_.slope_ref), custom_call_target="tpu_custom_call" | custom-call | flops 4294967296 | bytes 16777216 | tf_op jit(solution)/shard_map/pixels_body/pallas_call | solution.py:928
  404.0 2.7 collective-permute-done.99
  411.0 2.7 second_send.5
  419.1 11.9 %collective-permute-done.101 = f32[288,256]{1,0:T(8,128)S(1)} collective-permute-done((f32[288,256]{1,0:T(8,128)}, f32[288,256]{1,0:T(8,128)S(1)}, u32[]{:S(2)}, u32[]{:S(2)}) %collective-permute-start.101) | collective-permute-done | bytes 294944 | tf_op jit(solution)/shard_map/ppermute | solution.py:32
  435.5 6.2 %collective-permute-done.105.refs_1_ = f32[104,512]{1,0:T(8,128)S(1)} collective-permute-done((f32[104,512]{1,0:T(8,128)S(1)}, f32[104,512]{1,0:T(8,128)S(1)}, u32[]{:S(2)}, u32[]{:S(2)}) %collective-permute-start.105) | collective-permute-done | bytes 213024 | tf_op jit(solution)/shard_map/ppermute | solution.py:32
  441.8 2.5 collective-permute-start.109
  445.9 3.4 place_early_body.1
  450.6 3.1 collective-permute-done.110.refs_1_
  455.5 3.4 collective-permute-done.113.refs_5_
  (532 shorter events, 244.2 us)
Async XLA Ops:
  110.7 7.7 %collective-permute-start.21 = (f32[64,1024]{1,0:T(8,128)S(1)}, f32[64,1024]{1,0:T(8,128)S(1)}, u32[]{:S(2)}, u32[]{:S(2)}) collective-permute-start(f32[64,1024]{1,0:T(8,128)S(1)} %get-tuple-element.218), channel_id=1, source_target_pairs={{0,4},{1,5},{2,6},{3,7},{4,0},{5,1},{6,2},{7,3},{8,12},{9,13},{10,... | collective-permute-start | bytes 786440 | tf_op jit(solution)/shard_map/ppermute | solution.py:32
  205.6 9.4 %collective-permute-start.59 = (f32[8,80,512]{2,1,0:T(8,128)S(1)}, f32[8,80,512]{2,1,0:T(8,128)S(1)}, u32[]{:S(2)}, u32[]{:S(2)}) collective-permute-start(f32[8,80,512]{2,1,0:T(8,128)S(1)} %get-tuple-element.249), channel_id=1, source_target_pairs={{0,1},{1,0},{2,3},{3,2},{4,5},{5,4},{6,7},{7,6},{8,9},{9,8},{10,11... | collective-permute-start | bytes 3932168 | tf_op jit(solution)/shard_map/ppermute | solution.py:32
  205.7 9.2 %collective-permute-start.58 = (f32[64,1024]{1,0:T(8,128)S(1)}, f32[64,1024]{1,0:T(8,128)S(1)}, u32[]{:S(2)}, u32[]{:S(2)}) collective-permute-start(f32[64,1024]{1,0:T(8,128)S(1)} %copy-done.93), channel_id=1, source_target_pairs={{0,2},{1,3},{2,0},{3,1},{4,6},{5,7},{6,4},{7,5},{8,10},{9,11},{10,... | collective-permute-start | bytes 786440 | tf_op jit(solution)/shard_map/ppermute | solution.py:32
  217.3 8.3 %collective-permute-start.65 = (f32[256,1024]{1,0:T(8,128)S(1)}, f32[256,1024]{1,0:T(8,128)}, u32[]{:S(2)}, u32[]{:S(2)}) collective-permute-start(f32[256,1024]{1,0:T(8,128)S(1)} %constant_dynamic-update-slice_fusion.feat_ref), channel_id=1, source_target_pairs={{0,1},{1,0},{2,3},{3,2},{4,5},{5,4},{6,7},{7,6},{8,9},{9,8},{10,11... | collective-permute-start | bytes 3145736 | tf_op jit(solution)/shard_map/ppermute | solution.py:32
  233.7 22.6 %collective-permute-start.71 = (f32[128,512]{1,0:T(8,128)S(1)}, f32[128,512]{1,0:T(8,128)S(1)}, u32[]{:S(2)}, u32[]{:S(2)}) collective-permute-start(f32[128,512]{1,0:T(8,128)S(1)} %get-tuple-element.274), channel_id=1, source_target_pairs={{0,6},{1,7},{2,4},{3,5},{4,2},{5,3},{6,0},{7,1},{8,14},{9,15},{10,... | collective-permute-start | bytes 786440 | tf_op jit(solution)/shard_map/ppermute | solution.py:32
  235.4 20.9 %collective-permute-start.69 = (f32[128,512]{1,0:T(8,128)S(1)}, f32[128,512]{1,0:T(8,128)S(1)}, u32[]{:S(2)}, u32[]{:S(2)}) collective-permute-start(f32[128,512]{1,0:T(8,128)S(1)} %get-tuple-element.274), channel_id=1, source_target_pairs={{0,2},{1,3},{2,0},{3,1},{4,6},{5,7},{6,4},{7,5},{8,10},{9,11},{10,... | collective-permute-start | bytes 786440 | tf_op jit(solution)/shard_map/ppermute | solution.py:32
  236.4 19.9 %collective-permute-start.70 = (f32[128,512]{1,0:T(8,128)S(1)}, f32[128,512]{1,0:T(8,128)S(1)}, u32[]{:S(2)}, u32[]{:S(2)}) collective-permute-start(f32[128,512]{1,0:T(8,128)S(1)} %get-tuple-element.275.dg_ref), channel_id=1, source_target_pairs={{0,4},{1,5},{2,6},{3,7},{4,0},{5,1},{6,2},{7,3},{8,12},{9,13},{10,... | collective-permute-start | bytes 786440 | tf_op jit(solution)/shard_map/ppermute | solution.py:32
  264.9 11.0 %collective-permute-start.79 = (f32[4,2,512]{2,1,0:T(2,128)S(1)}, f32[4,2,512]{2,1,0:T(2,128)S(1)}, u32[]{:S(2)}, u32[]{:S(2)}) collective-permute-start(f32[4,2,512]{2,1,0:T(2,128)S(1)} %bitcast.184), channel_id=1, source_target_pairs={{0,24},{1,25},{2,26},{3,27},{4,28},{5,29},{6,30},{7,31},{8,16},{9,... | collective-permute-start | bytes 49160 | tf_op jit(solution)/shard_map/ppermute | solution.py:32
  267.1 8.9 %collective-permute-start.78 = (f32[4,2,512]{2,1,0:T(2,128)S(1)}, f32[4,2,512]{2,1,0:T(2,128)S(1)}, u32[]{:S(2)}, u32[]{:S(2)}) collective-permute-start(f32[4,2,512]{2,1,0:T(2,128)S(1)} %bitcast.185), channel_id=1, source_target_pairs={{0,16},{1,17},{2,18},{3,19},{4,20},{5,21},{6,22},{7,23},{8,24},{9,... | collective-permute-start | bytes 49160 | tf_op jit(solution)/shard_map/ppermute | solution.py:32
  267.2 8.8 %collective-permute-start.77 = (f32[4,2,512]{2,1,0:T(2,128)S(1)}, f32[4,2,512]{2,1,0:T(2,128)S(1)}, u32[]{:S(2)}, u32[]{:S(2)}) collective-permute-start(f32[4,2,512]{2,1,0:T(2,128)S(1)} %bitcast.186), channel_id=1, source_target_pairs={{0,8},{1,9},{2,10},{3,11},{4,12},{5,13},{6,14},{7,15},{8,0},{9,1},... | collective-permute-start | bytes 49160 | tf_op jit(solution)/shard_map/ppermute | solution.py:32
  276.0 22.2 %collective-permute-start.80 = (f32[8,104,512]{2,1,0:T(8,128)}, f32[8,104,512]{2,1,0:T(8,128)}, u32[]{:S(2)}, u32[]{:S(2)}) collective-permute-start(f32[8,104,512]{2,1,0:T(8,128)} %first_send.3), channel_id=1, source_target_pairs={{0,4},{1,3},{2,6},{3,1},{4,0},{5,7},{6,2},{7,5},{8,12},{9,11},{10,... | collective-permute-start | bytes 5111816 | tf_op jit(solution)/shard_map/ppermute | solution.py:126
  279.2 16.8 %collective-permute-start.81 = (f32[2,192,512]{2,1,0:T(8,128)S(1)}, f32[2,192,512]{2,1,0:T(8,128)S(1)}, u32[]{:S(2)}, u32[]{:S(2)}) collective-permute-start(f32[2,192,512]{2,1,0:T(8,128)S(1)} %dynamic-slice_bitcast_fusion), channel_id=1, source_target_pairs={{0,8},{1,9},{2,10},{3,11},{4,12},{5,13},{6,14},{7,15},{8,0},{9,1},... | collective-permute-start | bytes 2359304 | tf_op jit(solution)/shard_map/ppermute | solution.py:32
  298.2 15.2 %collective-permute-start.82 = (f32[4608,256]{1,0:T(8,128)}, f32[4608,256]{1,0:T(8,128)}, u32[]{:S(2)}, u32[]{:S(2)}) collective-permute-start(f32[4608,256]{1,0:T(8,128)} %get-tuple-element.310), channel_id=1, source_target_pairs={{0,1},{1,0},{2,3},{3,2},{4,5},{5,4},{6,7},{7,6},{8,9},{9,8},{10,11... | collective-permute-start | bytes 14155784 | tf_op jit(solution)/shard_map/ppermute | solution.py:32
  300.5 12.9 %collective-permute-start.83 = (f32[4,104,512]{2,1,0:T(8,128)S(1)}, f32[4,104,512]{2,1,0:T(8,128)}, u32[]{:S(2)}, u32[]{:S(2)}) collective-permute-start(f32[4,104,512]{2,1,0:T(8,128)S(1)} %get-tuple-element.312), channel_id=1, source_target_pairs={{0,2},{1,5},{2,0},{3,7},{4,6},{5,1},{6,4},{7,3},{8,10},{9,13},{10,... | collective-permute-start | bytes 2555912 | tf_op jit(solution)/shard_map/ppermute | solution.py:126
  302.7 8.7 %collective-permute-start.84 = (f32[2,64,512]{2,1,0:T(8,128)S(1)}, f32[2,64,512]{2,1,0:T(8,128)S(1)}, u32[]{:S(2)}, u32[]{:S(2)}) collective-permute-start(f32[2,64,512]{2,1,0:T(8,128)S(1)} %dynamic-slice_bitcast_fusion.1), channel_id=1, source_target_pairs={{0,8},{1,9},{2,10},{3,11},{4,12},{5,13},{6,14},{7,15},{8,0},{9,1},... | collective-permute-start | bytes 786440 | tf_op jit(solution)/shard_map/ppermute | solution.py:32
  316.8 30.2 %collective-permute-start.85 = (f32[8,288,256]{2,1,0:T(8,128)}, f32[8,288,256]{2,1,0:T(8,128)}, u32[]{:S(2)}, u32[]{:S(2)}) collective-permute-start(f32[8,288,256]{2,1,0:T(8,128)} %first_send.4), channel_id=1, source_target_pairs={{0,4},{1,3},{2,6},{3,1},{4,0},{5,7},{6,2},{7,5},{8,12},{9,11},{10,... | collective-permute-start | bytes 7077896 | tf_op jit(solution)/shard_map/ppermute | solution.py:126
  321.4 25.5 %collective-permute-start.86 = (f32[256,512]{1,0:T(8,128)}, f32[256,512]{1,0:T(8,128)}, u32[]{:S(2)}, u32[]{:S(2)}) collective-permute-start(f32[256,512]{1,0:T(8,128)} %pad_maximum_fusion), channel_id=1, source_target_pairs={{0,16},{1,17},{2,18},{3,19},{4,20},{5,21},{6,22},{7,23},{8,24},{9,... | collective-permute-start | bytes 1572872 | tf_op jit(solution)/shard_map/ppermute | solution.py:32
  348.1 10.5 %collective-permute-start.91 = (f32[2,104,512]{2,1,0:T(8,128)S(1)}, f32[2,104,512]{2,1,0:T(8,128)S(1)}, u32[]{:S(2)}, u32[]{:S(2)}) collective-permute-start(f32[2,104,512]{2,1,0:T(8,128)S(1)} %add_bitcast_fusion.1), channel_id=1, source_target_pairs={{0,8},{1,9},{2,10},{3,11},{4,12},{5,13},{6,14},{7,15},{8,0},{9,1},... | collective-permute-start | bytes 1277960 | tf_op jit(solution)/shard_map/ppermute | solution.py:32
  358.6 7.7 %collective-permute-start.94 = (f32[4,2,512]{2,1,0:T(2,128)S(1)}, f32[4,2,512]{2,1,0:T(2,128)S(1)}, u32[]{:S(2)}, u32[]{:S(2)}) collective-permute-start(f32[4,2,512]{2,1,0:T(2,128)S(1)} %bitcast.177), channel_id=1, source_target_pairs={{0,24},{1,25},{2,26},{3,27},{4,28},{5,29},{6,30},{7,31},{8,16},{9,... | collective-permute-start | bytes 49160 | tf_op jit(solution)/shard_map/ppermute | solution.py:32
  366.4 16.3 %collective-permute-start.95 = (f32[4,288,256]{2,1,0:T(8,128)S(1)}, f32[4,288,256]{2,1,0:T(8,128)S(1)}, u32[]{:S(2)}, u32[]{:S(2)}) collective-permute-start(f32[4,288,256]{2,1,0:T(8,128)S(1)} %get-tuple-element.346), channel_id=1, source_target_pairs={{0,2},{1,5},{2,0},{3,7},{4,6},{5,1},{6,4},{7,3},{8,10},{9,13},{10,... | collective-permute-start | bytes 3538952 | tf_op jit(solution)/shard_map/ppermute | solution.py:126
  368.6 14.0 %collective-permute-start.96 = (f32[104,512]{1,0:T(8,128)S(1)}, f32[104,512]{1,0:T(8,128)S(1)}, u32[]{:S(2)}, u32[]{:S(2)}) collective-permute-start(f32[104,512]{1,0:T(8,128)S(1)} %bitcast_add_fusion.5), channel_id=1, source_target_pairs={{0,16},{1,17},{2,18},{3,19},{4,20},{5,21},{6,22},{7,23},{8,24},{9,... | collective-permute-start | bytes 638984 | tf_op jit(solution)/shard_map/ppermute | solution.py:32
  390.4 16.3 %collective-permute-start.98 = (f32[8,128,256]{2,1,0:T(8,128)S(1)}, f32[8,128,256]{2,1,0:T(8,128)S(1)}, u32[]{:S(2)}, u32[]{:S(2)}) collective-permute-start(f32[8,128,256]{2,1,0:T(8,128)S(1)} %first_send.5), channel_id=1, source_target_pairs={{0,4},{1,3},{2,6},{3,1},{4,0},{5,7},{6,2},{7,5},{8,12},{9,11},{10,... | collective-permute-start | bytes 3145736 | tf_op jit(solution)/shard_map/ppermute | solution.py:126
  392.0 14.8 %collective-permute-start.99 = (f32[2,288,256]{2,1,0:T(8,128)S(1)}, f32[2,288,256]{2,1,0:T(8,128)S(1)}, u32[]{:S(2)}, u32[]{:S(2)}) collective-permute-start(f32[2,288,256]{2,1,0:T(8,128)S(1)} %add_bitcast_fusion), channel_id=1, source_target_pairs={{0,8},{1,9},{2,10},{3,11},{4,12},{5,13},{6,14},{7,15},{8,0},{9,1},... | collective-permute-start | bytes 1769480 | tf_op jit(solution)/shard_map/ppermute | solution.py:32
  408.1 23.0 %collective-permute-start.103 = (f32[256,512]{1,0:T(8,128)S(1)}, f32[256,512]{1,0:T(8,128)S(1)}, u32[]{:S(2)}, u32[]{:S(2)}) collective-permute-start(f32[256,512]{1,0:T(8,128)S(1)} %maximum_add_fusion.refs_4_), channel_id=1, source_target_pairs={{0,1},{1,0},{2,3},{3,2},{4,5},{5,4},{6,7},{7,6},{8,9},{9,8},{10,11... | collective-permute-start | bytes 1572872 | tf_op jit(solution)/shard_map/ppermute | solution.py:32
  408.2 22.9 %collective-permute-start.102 = (f32[256,512]{1,0:T(8,128)S(1)}, f32[256,512]{1,0:T(8,128)}, u32[]{:S(2)}, u32[]{:S(2)}) collective-permute-start(f32[256,512]{1,0:T(8,128)S(1)} %maximum_add_fusion.refs_4_), channel_id=1, source_target_pairs={{0,2},{1,3},{2,0},{3,1},{4,6},{5,7},{6,4},{7,5},{8,10},{9,11},{10,... | collective-permute-start | bytes 1572872 | tf_op jit(solution)/shard_map/ppermute | solution.py:32
  414.5 16.6 %collective-permute-start.101 = (f32[288,256]{1,0:T(8,128)}, f32[288,256]{1,0:T(8,128)S(1)}, u32[]{:S(2)}, u32[]{:S(2)}) collective-permute-start(f32[288,256]{1,0:T(8,128)} %bitcast_add_fusion.3), channel_id=1, source_target_pairs={{0,16},{1,17},{2,18},{3,19},{4,20},{5,21},{6,22},{7,23},{8,24},{9,... | collective-permute-start | bytes 884744 | tf_op jit(solution)/shard_map/ppermute | solution.py:32
  416.6 14.5 %collective-permute-start.100 = (f32[4,128,256]{2,1,0:T(8,128)}, f32[4,128,256]{2,1,0:T(8,128)S(1)}, u32[]{:S(2)}, u32[]{:S(2)}) collective-permute-start(f32[4,128,256]{2,1,0:T(8,128)} %get-tuple-element.362), channel_id=1, source_target_pairs={{0,2},{1,5},{2,0},{3,7},{4,6},{5,1},{6,4},{7,3},{8,10},{9,13},{10,... | collective-permute-start | bytes 1572872 | tf_op jit(solution)/shard_map/ppermute | solution.py:126
  432.1 9.6 %collective-permute-start.104 = (f32[2,128,256]{2,1,0:T(8,128)S(1)}, f32[2,128,256]{2,1,0:T(8,128)S(1)}, u32[]{:S(2)}, u32[]{:S(2)}) collective-permute-start(f32[2,128,256]{2,1,0:T(8,128)S(1)} %add_bitcast_fusion.2), channel_id=1, source_target_pairs={{0,8},{1,9},{2,10},{3,11},{4,12},{5,13},{6,14},{7,15},{8,0},{9,1},... | collective-permute-start | bytes 786440 | tf_op jit(solution)/shard_map/ppermute | solution.py:32
  432.2 9.5 %collective-permute-start.108 = (f32[256,512]{1,0:T(8,128)}, f32[256,512]{1,0:T(8,128)S(1)}, u32[]{:S(2)}, u32[]{:S(2)}) collective-permute-start(f32[256,512]{1,0:T(8,128)} %collective-permute-done.102.refs_5_), channel_id=1, source_target_pairs={{0,1},{1,0},{2,3},{3,2},{4,5},{5,4},{6,7},{7,6},{8,9},{9,8},{10,11... | collective-permute-start | bytes 1572872 | tf_op jit(solution)/shard_map/ppermute | solution.py:32
  433.4 8.3 %collective-permute-start.107 = (f32[288,256]{1,0:T(8,128)S(1)}, f32[288,256]{1,0:T(8,128)S(1)}, u32[]{:S(2)}, u32[]{:S(2)}) collective-permute-start(f32[288,256]{1,0:T(8,128)S(1)} %fusion.refs_0_), channel_id=1, source_target_pairs={{0,1},{1,0},{2,3},{3,2},{4,5},{5,4},{6,7},{7,6},{8,9},{9,8},{10,11... | collective-permute-start | bytes 884744 | tf_op jit(solution)/shard_map/ppermute | solution.py:32
  441.8 8.8 %collective-permute-start.109 = (f32[128,256]{1,0:T(8,128)S(1)}, f32[128,256]{1,0:T(8,128)S(1)}, u32[]{:S(2)}, u32[]{:S(2)}) collective-permute-start(f32[128,256]{1,0:T(8,128)S(1)} %bitcast_add_fusion.7), channel_id=1, source_target_pairs={{0,16},{1,17},{2,18},{3,19},{4,20},{5,21},{6,22},{7,23},{8,24},{9,... | collective-permute-start | bytes 393224 | tf_op jit(solution)/shard_map/ppermute | solution.py:32
  444.3 9.4 %collective-permute-start.110 = (f32[288,256]{1,0:T(8,128)S(1)}, f32[288,256]{1,0:T(8,128)S(1)}, u32[]{:S(2)}, u32[]{:S(2)}) collective-permute-start(f32[288,256]{1,0:T(8,128)S(1)} %fusion.refs_0_), channel_id=1, source_target_pairs={{0,2},{1,3},{2,0},{3,1},{4,6},{5,7},{6,4},{7,5},{8,10},{9,11},{10,... | collective-permute-start | bytes 884744 | tf_op jit(solution)/shard_map/ppermute | solution.py:32
  (193 other events, 2000.8 us)
